TPU v7x, 32 devices: a whole 2x2x4 slice. The times are simulated.
32 devices in a mesh: group: 4 (over z), expert: 8 (over y, x, core).
Axes of the slice: x: 2, y: 2, z: 4, core: 2. Of those that a mesh axis runs over, the one named last changes fastest.
Arguments:
- tokens: bfloat16 [512, 3584], P(('group', 'expert')), parts along dimension 0, may hold values from -6 to 6
- w_in: bfloat16 [2, 3584, 4096], P(None, None, ('group', 'expert')), parts along dimension 2, may hold values from -0.09375 to 0.09375
- w_down: bfloat16 [4096, 3584], P(('group', 'expert')), parts along dimension 0, may hold values from -0.5 to 0.5
- old_place: int32 [32], P('group'), parts along dimension 0, may hold values from 0 to 5, as said below
- new_place: int32 [32], P('group'), parts along dimension 0, may hold values from 0 to 5, as said below
- expert_ids: int32 [512, 2], P(('group', 'expert')), parts along dimension 0, may hold values from 0 to 5, all different within a row
- replica: int32 [512, 2], P(('group', 'expert')), parts along dimension 0, may hold values from 0 to 1
- combine: float32 [512, 2], P(('group', 'expert')), parts along dimension 0, may hold values from 0.2 to 1
Outputs:
- mixed: bfloat16 [512, 3584], P(('group', 'expert')), parts along dimension 0
There are 4 independent parts, one for each index of `group`. A program takes and returns all parts, laid end to end along the dimension named above; each array names one. Nothing has to cross between parts.
Inputs may be any that keep to these rules, and one draw needn't show every extreme that they name: Each of the 6 experts is held by one or two slots of old_place; exactly two experts are held twice. new_place is old_place with the entries of some pairs of slots 2 i and 2 i + 1 exchanged.
All inputs are finite; a program needn't handle non-finite values.
Results may differ from a plain program's by a relative error of at most 0.0057.
Values may be sent and summed in bfloat16 or wider, within the bound.
No kernel may reach another device: no remote copies, remote signals or barrier semaphores. Data moves between devices by JAX's collectives and lax.ppermute only.
A program may use at most 64 MiB of HBM per device.

v0:
```python
import jax
import jax.numpy as jnp
from jax import lax
from jax.sharding import PartitionSpec as P

SLOTS = 8
EXPERTS = 6
CAP = 4


def from_partner(value, axis, distance):
    return lax.ppermute(value, axis, [(i, i ^ 1 << distance) for i in range(lax.axis_size(axis))])


def routing(new_place, expert_ids, replica):
    slot_ids = jnp.arange(SLOTS, dtype=jnp.int32)
    experts = jnp.arange(EXPERTS, dtype=jnp.int32)
    holders = (new_place[None, :] == experts[:, None]).astype(jnp.int32)
    counts = jnp.sum(holders, axis=1)
    before = jnp.cumsum(holders, axis=1) - holders
    expert_hot = (expert_ids[..., None] == experts).astype(jnp.int32)
    count_sel = jnp.sum(expert_hot * counts, axis=-1)
    wanted = replica % jnp.maximum(count_sel, 1)
    holder_sel = jnp.sum(expert_hot[..., None] * holders, axis=2)
    rank_sel = jnp.sum(expert_hot[..., None] * before, axis=2)
    chosen = holder_sel * (rank_sel == wanted[..., None]).astype(jnp.int32)
    return (chosen, jnp.sum(chosen * slot_ids, axis=-1))


def body(tokens, w_in, w_down, old_place, new_place, expert_ids, replica, combine):
    devices = lax.axis_size("expert")
    shards = devices // SLOTS
    model_width = tokens.shape[1]
    chosen, dest_slot = routing(new_place, expert_ids, replica)
    flat_chosen = chosen.reshape(-1, SLOTS)
    position = (jnp.cumsum(flat_chosen, axis=0) - flat_chosen).reshape(chosen.shape)
    position = jnp.sum(chosen * position, axis=-1)
    is_kept = position < CAP
    target = jnp.where(is_kept, dest_slot * CAP + position, -1)
    columns = jnp.arange(SLOTS * CAP, dtype=jnp.int32)
    matches = target[..., None] == columns
    selector = jnp.sum(matches.astype(jnp.int32), axis=1).astype(jnp.bfloat16)
    combiner = jnp.sum(combine[..., None] * matches.astype(jnp.float32), axis=1)
    buffer = jnp.einsum("rj,rd->jd", selector, tokens, preferred_element_type=jnp.float32)
    buffer = buffer.astype(jnp.bfloat16).reshape(SLOTS, CAP, model_width)
    slot_mine = lax.axis_index("expert") // shards
    pair_bit = shards.bit_length() - 1
    other_in, other_down = from_partner((w_in, w_down), "expert", pair_bit)
    keep_mine = new_place[slot_mine] == old_place[slot_mine]
    weights_in = jnp.where(keep_mine, w_in, other_in)
    weights_down = jnp.where(keep_mine, w_down, other_down)
    blocks = jnp.broadcast_to(buffer[:, None], (SLOTS, shards, CAP, model_width)).reshape(
        devices, CAP, model_width
    )
    received = lax.all_to_all(blocks, "expert", split_axis=0, concat_axis=0, tiled=True)
    flat_rows = received.reshape(-1, model_width)
    gate_up = jnp.einsum("rd,gdh->grh", flat_rows, weights_in, preferred_element_type=jnp.float32)
    hidden = (jax.nn.silu(gate_up[0]) * gate_up[1]).astype(jnp.bfloat16)
    partial_value = jnp.dot(hidden, weights_down, preferred_element_type=jnp.float32).astype(
        jnp.bfloat16
    )
    returned = lax.all_to_all(
        partial_value.reshape(received.shape), "expert", split_axis=0, concat_axis=0, tiled=True
    )
    returned = returned.reshape(SLOTS, shards, CAP, model_width)
    summed = jnp.sum(returned.astype(jnp.float32), axis=1).reshape(SLOTS * CAP, model_width)
    mixed = jnp.dot(
        combiner, summed, precision=lax.Precision.HIGHEST, preferred_element_type=jnp.float32
    )
    return mixed.astype(jnp.bfloat16)


def solution(mesh):
    placed = (
        P(("group", "expert"), None),
        P(None, None, ("group", "expert")),
        P(("group", "expert"), None),
        P("group"),
        P("group"),
        P(("group", "expert"), None),
        P(("group", "expert"), None),
        P(("group", "expert"), None),
    )
    return jax.shard_map(
        body, mesh=mesh, in_specs=placed, out_specs=P(("group", "expert"), None), check_vma=False
    )
```

profile of v0, /device:TPU:0, one launch (start us, length us, event | category | flops | bytes accessed | tf_op | source)
XLA Modules:
  0.0 32.2 jit_solution(9558663320971807193)
XLA Ops:
  0.0 0.0 copy-start
  0.0 0.0 copy-start.1
  0.0 0.5 %collective-permute-start = (bf16[2,3584,128]{2,1,0:T(8,128)(2,1)}, bf16[2,3584,128]{2,1,0:T(8,128)(2,1)}, u32[]{:S(2)}, u32[]{:S(2)}) collective-permute-start(bf16[2,3584,128]{2,1,0:T(8,128)(2,1)} %param.9), channel_id=1, source_target_pairs={{0,1},{1,0},{2,3},{3,2},{4,5},{5,4},{6,7},{7,6},{8,9},{9,8},{10,11... | collective-permute-start | bytes 5505032 | tf_op jit(solution)/shard_map/ppermute | solution.py:12
  0.5 0.1 collective-permute-start.1
  0.5 0.8 %fusion.13 = s32[16,2,6]{0,1,2:T(2,128)S(1)} fusion(s32[16,2]{0,1:T(2,128)} %param.13), kind=kLoop, calls=%fused_computation.26 | loop fusion | flops 384 | bytes 896 | tf_op jit(solution)/shard_map/convert_element_type | solution.py:21
  1.3 0.7 %fusion.15 = s32[6,8]{1,0:T(8,128)S(1)} fusion(s32[8]{0:T(128)} %param.12), kind=kLoop, calls=%fused_computation.29 | loop fusion | flops 96 | bytes 224 | tf_op jit(solution)/shard_map/convert_element_type | solution.py:18
  2.0 0.2 reduce_window_sum.24
  2.1 0.8 %fusion.16 = (s32[6]{0:T(128)S(1)}, s32[6,8]{1,0:T(8,128)S(1)}) fusion(s32[8]{0:T(128)} %param.12, s32[6,8]{1,0:T(8,128)S(1)} %reduce_window_sum.24), kind=kLoop, calls=%fused_computation.31 | loop fusion | flops 186 | bytes 440 | tf_op jit(solution)/shard_map/reduce_sum | solution.py:19
  2.9 0.1 multiply_reduce_fusion.1
  3.0 0.1 copy.21
  3.0 0.1 copy.23
  3.1 0.8 %select_reduce_fusion.1 = s32[16,2]{0,1:T(2,128)S(1)} fusion(s32[6]{0:T(128)S(1)} %get-tuple-element.9, s32[16,2]{0,1:T(2,128)} %param.13), kind=kLoop, calls=%fused_computation.24 | loop fusion | flops 544 | bytes 280 | tf_op jit(solution)/shard_map/reduce_sum | solution.py:22
  3.9 0.8 %and_select_fusion = s32[16,2]{0,1:T(2,128)S(1)} fusion(s32[16,2]{0,1:T(2,128)} %param.14, s32[16,2]{0,1:T(2,128)S(1)} %select_reduce_fusion.1), kind=kLoop, calls=%fused_computation.34 | loop fusion | flops 288 | bytes 384 | tf_op jit(solution)/shard_map/jit(remainder)/select_n | solution.py:23
  4.7 0.1 copy.22
  4.8 0.1 eq.94
  4.9 0.1 compare_select_fusion
  5.0 0.1 reduce_window_sum.25
  5.0 0.1 copy.24
  5.1 0.1 convert_reduce_fusion
  5.2 0.0 copy-done
  5.2 0.2 convolution_convert_fusion.1
  5.4 0.8 %reshape_broadcast_in_dim_reshape.3 = bf16[8,4,3584]{2,1,0:T(4,128)(2,1)} reshape(bf16[32,3584]{1,0:T(8,128)(2,1)S(1)} %convolution_convert_fusion.1) | data formatting | bytes 458752 | tf_op jit(solution)/shard_map/reshape;broadcast_in_dim;reshape | solution.py:52
  6.2 5.2 %all-to-all-start = ((bf16[8,4,3584]{2,1,0:T(4,128)(2,1)}), bf16[8,4,3584]{2,1,0:T(4,128)(2,1)S(1)}, u32[]{:S(2)}, u32[]{:S(2)}) async-start(bf16[8,4,3584]{2,1,0:T(4,128)(2,1)} %reshape_broadcast_in_dim_reshape.3), calls=%async_computation | async-start | bytes 458752 | tf_op jit(solution)/shard_map/all_to_all | solution.py:55
  11.4 1.2 %dynamic_slice.6 = s32[1]{0:T(128)} dynamic-slice(s32[8]{0:T(128)} %param.12, s32[]{:T(128)S(6)} %select_n.43), dynamic_slice_sizes={1} | dynamic-slice | bytes 12 | tf_op jit(solution)/shard_map/dynamic_slice | solution.py:49
  12.6 1.2 %dynamic_slice.7 = s32[1]{0:T(128)} dynamic-slice(s32[8]{0:T(128)} %param.11, s32[]{:T(128)S(6)} %select_n.43), dynamic_slice_sizes={1} | dynamic-slice | bytes 12 | tf_op jit(solution)/shard_map/dynamic_slice | solution.py:49
  15.1 2.9 %all-to-all-done = bf16[8,4,3584]{2,1,0:T(4,128)(2,1)S(1)} async-done(((bf16[8,4,3584]{2,1,0:T(4,128)(2,1)}), bf16[8,4,3584]{2,1,0:T(4,128)(2,1)S(1)}, u32[]{:S(2)}, u32[]{:S(2)}) %all-to-all-start) | async-done | bytes 229408 | tf_op jit(solution)/shard_map/all_to_all | solution.py:55
  18.0 0.1 reshape.139
  18.0 0.0 collective-permute-done
  18.0 0.0 copy-done.1
  18.0 0.0 copy-start.2
  18.1 2.2 %fusion.3 = f32[2,32,128]{2,1,0:T(8,128)S(1)} fusion(bf16[32,3584,1]{1,0,2:T(8,128)(2,1)S(1)} %reshape.139, bf16[2,3584,128]{2,1,0:T(8,128)(2,1)S(1)} %copy-done.1, bf16[2,3584,128]{2,1,0:T(8,128)(2,1)} %collective-permute-done, pred[]{:T(512)} %bitcast.3), kind=kOutput, calls=%fused_computation.6 | convolution fusion | flops 59637760 | bytes 3932161 | tf_op jit(solution)/shard_map/rd,gdh->grh/dot_general | solution.py:57
  20.2 0.0 copy-start.3
  20.2 0.0 collective-permute-done.1
  20.3 0.0 copy-done.2
  20.3 0.3 convolution_convert_fusion
  20.6 0.8 %reshape.137 = bf16[8,4,3584]{2,1,0:T(4,128)(2,1)} reshape(bf16[32,3584]{1,0:T(8,128)(2,1)S(1)} %convolution_convert_fusion) | data formatting | bytes 458752 | tf_op jit(solution)/shard_map/reshape | solution.py:63
  21.3 3.4 %all-to-all-start.1 = ((bf16[8,4,3584]{2,1,0:T(4,128)(2,1)}), bf16[8,4,3584]{2,1,0:T(4,128)(2,1)S(1)}, u32[]{:S(2)}, u32[]{:S(2)}) async-start(bf16[8,4,3584]{2,1,0:T(4,128)(2,1)} %reshape.137), calls=%async_computation.1 | async-start | bytes 458752 | tf_op jit(solution)/shard_map/all_to_all | solution.py:62
  24.7 0.0 copy-done.3
  24.8 0.1 select_reduce_fusion
  24.8 6.4 %all-to-all-done.1 = bf16[8,4,3584]{2,1,0:T(4,128)(2,1)S(1)} async-done(((bf16[8,4,3584]{2,1,0:T(4,128)(2,1)}), bf16[8,4,3584]{2,1,0:T(4,128)(2,1)S(1)}, u32[]{:S(2)}, u32[]{:S(2)}) %all-to-all-start.1) | async-done | bytes 229408 | tf_op jit(solution)/shard_map/all_to_all | solution.py:62
  31.3 0.1 reshape.138
  31.3 0.9 %convolution_convert_fusion.2 = bf16[16,3584]{1,0:T(8,128)(2,1)} fusion(f32[16,32]{1,0:T(8,128)S(1)} %select_reduce_fusion, bf16[32,3584]{1,0:T(8,128)(2,1)S(1)} %reshape.138), kind=kOutput, calls=%fused_computation.2 | convolution fusion | flops 22077440 | bytes 346112 | tf_op jit(solution)/shard_map/dot_general | solution.py:67
  (3 shorter events, 0.0 us)
Async XLA Ops:
  0.0 5.2 %copy-start = (bf16[16,3584]{1,0:T(8,128)(2,1)S(1)}, bf16[16,3584]{1,0:T(8,128)(2,1)}, u32[]{:S(2)}) copy-start(bf16[16,3584]{1,0:T(8,128)(2,1)} %param.8) | copy-start | bytes 344068
  0.0 18.0 %copy-start.1 = (bf16[2,3584,128]{2,1,0:T(8,128)(2,1)S(1)}, bf16[2,3584,128]{2,1,0:T(8,128)(2,1)}, u32[]{:S(2)}) copy-start(bf16[2,3584,128]{2,1,0:T(8,128)(2,1)} %param.9) | copy-start | bytes 5505028
  0.0 18.0 %collective-permute-start = (bf16[2,3584,128]{2,1,0:T(8,128)(2,1)}, bf16[2,3584,128]{2,1,0:T(8,128)(2,1)}, u32[]{:S(2)}, u32[]{:S(2)}) collective-permute-start(bf16[2,3584,128]{2,1,0:T(8,128)(2,1)} %param.9), channel_id=1, source_target_pairs={{0,1},{1,0},{2,3},{3,2},{4,5},{5,4},{6,7},{7,6},{8,9},{9,8},{10,11... | collective-permute-start | bytes 5505032 | tf_op jit(solution)/shard_map/ppermute | solution.py:12
  0.5 19.8 %collective-permute-start.1 = (bf16[128,3584]{1,0:T(8,128)(2,1)}, bf16[128,3584]{1,0:T(8,128)(2,1)S(1)}, u32[]{:S(2)}, u32[]{:S(2)}) collective-permute-start(bf16[128,3584]{1,0:T(8,128)(2,1)} %param.10), channel_id=1, source_target_pairs={{0,1},{1,0},{2,3},{3,2},{4,5},{5,4},{6,7},{7,6},{8,9},{9,8},{10,11... | collective-permute-start | bytes 2752520 | tf_op jit(solution)/shard_map/ppermute | solution.py:12
  6.2 11.8 %all-to-all-start = ((bf16[8,4,3584]{2,1,0:T(4,128)(2,1)}), bf16[8,4,3584]{2,1,0:T(4,128)(2,1)S(1)}, u32[]{:S(2)}, u32[]{:S(2)}) async-start(bf16[8,4,3584]{2,1,0:T(4,128)(2,1)} %reshape_broadcast_in_dim_reshape.3), calls=%async_computation | async-start | bytes 458752 | tf_op jit(solution)/shard_map/all_to_all | solution.py:55
  18.0 2.2 %copy-start.2 = (bf16[128,3584]{1,0:T(8,128)(2,1)S(1)}, bf16[128,3584]{1,0:T(8,128)(2,1)}, u32[]{:S(2)}) copy-start(bf16[128,3584]{1,0:T(8,128)(2,1)} %param.10) | copy-start | bytes 2752516
  20.2 4.5 %copy-start.3 = (f32[16,2]{0,1:T(2,128)S(1)}, f32[16,2]{0,1:T(2,128)}, u32[]{:S(2)}) copy-start(f32[16,2]{0,1:T(2,128)} %param.15) | copy-start | bytes 388
  21.3 9.9 %all-to-all-start.1 = ((bf16[8,4,3584]{2,1,0:T(4,128)(2,1)}), bf16[8,4,3584]{2,1,0:T(4,128)(2,1)S(1)}, u32[]{:S(2)}, u32[]{:S(2)}) async-start(bf16[8,4,3584]{2,1,0:T(4,128)(2,1)} %reshape.137), calls=%async_computation.1 | async-start | bytes 458752 | tf_op jit(solution)/shard_map/all_to_all | solution.py:62
where the time goes:
time: 32.1 us; the launch traced here: 32.2 us
  waiting for transfers between devices  9.34 us (29%)
  starting transfers between devices  9.1 us (28%)
  local copies, waits for them, and re-layouts  4.52 us (14%)
  other arithmetic  4.3 us (13%)
  matrix products  3.62 us (11%)
  between operations  1.33 us (4%)
    all_to_all x1, waiting for transfers between devices, body(): lax.all_to_all(partial_value.reshape(received.shape), 'expert', split_axi...  6.43 us
    all_to_all x1, starting transfers between devices, body(): lax.all_to_all(blocks, 'expert', split_axis=0, concat_axis=0, tiled=True)  5.17 us
    all_to_all x1, starting transfers between devices, body(): lax.all_to_all(partial_value.reshape(received.shape), 'expert', split_axi...  3.4 us
    all_to_all x1, waiting for transfers between devices, body(): lax.all_to_all(blocks, 'expert', split_axis=0, concat_axis=0, tiled=True)  2.9 us
    dynamic_slice x2, local copies, waits for them, and re-layouts, body(): keep_mine = new_place[slot_mine] == old_place[slot_mine]  2.47 us
    dot_general x1, matrix products, body(): jnp.einsum('rd,gdh->grh', flat_rows, weights_in, preferred_element_type=j...  2.18 us
    dot_general x1, matrix products, body(): jnp.dot(combiner, summed, precision=lax.Precision.HIGHEST, preferred_elem...  0.89 us
    select_n x1, other arithmetic, routing(): wanted = replica % jnp.maximum(count_sel, 1)  0.8 us
  transfers between devices with their start and end apart: 4, of which 2 were waited for; matrix products, arithmetic and copies ran while one was open for 32% of the time, Pallas kernels for 0%

commit v1 on v0

v1 whole, which is shorter than its diff:
```python
import functools

import jax
import jax.numpy as jnp
from jax import lax
from jax.experimental import pallas as pl
from jax.experimental.pallas import tpu as pltpu
from jax.sharding import PartitionSpec as P

SLOTS = 8
CAP = 4

VMEM = pl.BlockSpec(memory_space=pltpu.VMEM)


def targets(shards, new_ref, old_ref, ids_ref, replica_ref):
    new, old = new_ref[...], old_ref[...]
    slots = new.shape[1]
    rows = ids_ref.shape[1]
    me = lax.axis_index("expert") // shards
    down = lax.broadcasted_iota(jnp.int32, (slots, slots), 0)
    across = lax.broadcasted_iota(jnp.int32, (slots, slots), 1)
    new_full = jnp.broadcast_to(new, (slots, slots)).astype(jnp.float32)
    source = jnp.where(new == old, across, across ^ 1)
    base = (CAP * (source ^ me)).astype(jnp.float32)
    diagonal = down == across
    mine = jnp.sum(jnp.where(diagonal, new_full, 0.0), axis=1, keepdims=True)
    line = jnp.sum(jnp.where(diagonal, base, 0.0), axis=1, keepdims=True)
    same = jnp.where(mine == new_full, 1.0, 0.0)
    count = jnp.sum(same, axis=1, keepdims=True).astype(jnp.int32)
    rank = jnp.sum(jnp.where(across < down, same, 0.0), axis=1, keepdims=True).astype(jnp.int32)
    expert = mine.astype(jnp.int32)
    chosen = []
    for k in range(ids_ref.shape[0]):
        wanted = replica_ref[k : k + 1, :] & (count - 1)
        hit = (ids_ref[k : k + 1, :] == expert) & (rank == wanted)
        chosen.append(jnp.where(hit, 1.0, 0.0))
    earlier = lax.broadcasted_iota(jnp.int32, (rows, rows), 0) < lax.broadcasted_iota(
        jnp.int32, (rows, rows), 1
    )
    any_choice = functools.reduce(jnp.add, chosen)
    position = jnp.dot(
        any_choice.astype(jnp.bfloat16),
        jnp.where(earlier, 1.0, 0.0).astype(jnp.bfloat16),
        preferred_element_type=jnp.float32,
    )
    found = []
    for hit in chosen:
        place = jnp.where(position < CAP, line + position + 1.0, 0.0)
        found.append((jnp.sum(hit * place, axis=0, keepdims=True) - 1.0).astype(jnp.int32))
        position = position + hit
    return found


def dispatch_kernel(shards, new_ref, old_ref, ids_ref, replica_ref, tokens_ref, *block_refs):
    found = targets(shards, new_ref, old_ref, ids_ref, replica_ref)
    lines = CAP * len(block_refs)
    line = lax.broadcasted_iota(jnp.int32, (lines, tokens_ref.shape[0]), 0)
    picked = functools.reduce(jnp.logical_or, [line == target for target in found])
    selector = jnp.where(picked, 1.0, 0.0).astype(jnp.bfloat16)
    buffer = jnp.dot(selector, tokens_ref[...], preferred_element_type=jnp.float32)
    for b, block_ref in enumerate(block_refs):
        block_ref[...] = buffer[CAP * b : CAP * (b + 1)].astype(jnp.bfloat16)


def combine_kernel(shards, new_ref, old_ref, ids_ref, replica_ref, combine_ref, weight_ref):
    found = targets(shards, new_ref, old_ref, ids_ref, replica_ref)
    line = lax.broadcasted_iota(jnp.int32, weight_ref.shape, 0)
    weight_ref[...] = functools.reduce(
        jnp.add,
        [
            jnp.where(line == target, combine_ref[k : k + 1, :], 0.0)
            for k, target in enumerate(found)
        ],
    )


def stack(refs):
    return jnp.concatenate([ref[...].astype(jnp.float32) for ref in refs], axis=0)


def expert_kernel(devices, w_in_ref, w_down_ref, *refs):
    rows = stack(refs[:devices]).astype(jnp.bfloat16)
    gate = jnp.dot(rows, w_in_ref[0], preferred_element_type=jnp.float32)
    up = jnp.dot(rows, w_in_ref[1], preferred_element_type=jnp.float32)
    hidden = (jax.nn.silu(gate) * up).astype(jnp.bfloat16)
    piece = jnp.dot(hidden, w_down_ref[...], preferred_element_type=jnp.float32)
    for b, out_ref in enumerate(refs[devices:]):
        out_ref[...] = piece[CAP * b : CAP * (b + 1)].astype(jnp.bfloat16)


def mix_kernel(shards, weight_ref, *refs):
    out_ref = refs[-1]
    total = functools.reduce(jnp.add, [stack(refs[j:-1:shards]) for j in range(shards)])
    weight = weight_ref[...]
    out_ref[...] = lax.dot_general(
        weight,
        total,
        (((0,), (0,)), ((), ())),
        precision=lax.Precision.HIGHEST,
        preferred_element_type=jnp.float32,
    ).astype(jnp.bfloat16)


def call(kernel, outs, args):
    return pl.pallas_call(
        kernel,
        out_shape=outs,
        in_specs=[VMEM] * len(args),
        out_specs=jax.tree.map(lambda _: VMEM, outs),
    )(*args)


def from_each(blocks, devices):
    return [
        block if b == 0 else lax.ppermute(block, "expert", [(i, i ^ b) for i in range(devices)])
        for b, block in enumerate(blocks)
    ]


def body(tokens, w_in, w_down, old_place, new_place, expert_ids, replica, combine):
    devices = lax.axis_size("expert")
    shards = devices // SLOTS
    rows, width = tokens.shape
    routing = (new_place[None], old_place[None], expert_ids.T, replica.T)
    block = jax.ShapeDtypeStruct((CAP, width), jnp.bfloat16)
    blocks = call(
        functools.partial(dispatch_kernel, shards), [block] * SLOTS, (*routing, tokens)
    )
    received = from_each([blocks[b // shards] for b in range(devices)], devices)
    weight = call(
        functools.partial(combine_kernel, shards),
        jax.ShapeDtypeStruct((SLOTS * CAP, rows), jnp.float32),
        (*routing, combine.T),
    )
    pieces = call(
        functools.partial(expert_kernel, devices), [block] * devices, (w_in, w_down, *received)
    )
    returned = from_each(pieces, devices)
    return call(
        functools.partial(mix_kernel, shards),
        jax.ShapeDtypeStruct((rows, width), jnp.bfloat16),
        (weight, *returned),
    )


def solution(mesh):
    placed = (
        P(("group", "expert"), None),
        P(None, None, ("group", "expert")),
        P(("group", "expert"), None),
        P("group"),
        P("group"),
        P(("group", "expert"), None),
        P(("group", "expert"), None),
        P(("group", "expert"), None),
    )
    return jax.shard_map(
        body, mesh=mesh, in_specs=placed, out_specs=P(("group", "expert"), None), check_vma=False
    )
```

time: 32.1 us -> 29.6 us (0.922); the launches traced: 32.2 us -> 29.4 us
  Pallas kernels: 0 us -> 8.9 us
  starting transfers between devices: 9.1 us -> 13.9 us
  other arithmetic: 4.3 us -> 0 us
  waiting for transfers between devices: 9.34 us -> 5.23 us
  matrix products: 3.62 us -> 0 us
  local copies, waits for them, and re-layouts: 4.52 us -> 1.16 us
  between operations: 1.33 us -> 0.13 us
    ppermute x2 -> x14, starting transfers between devices: 0.53 us -> 13.9 us  [from_each(): lax.ppermute(block, 'expert', [(i, i ^ b) for i in range(devices)])]
    all_to_all x2 -> x0, waiting for transfers between devices: 9.33 us -> none  [the longest x1 6.43 us: body(): lax.all_to_all(partial_value.reshape(received.shape), 'expert', split_axi...]
    pallas_call x0 -> x4, Pallas kernels: none -> 8.9 us  [call(): pl.pallas_call(kernel, out_shape=outs, in_specs=[VMEM] * len(args), out_s...]
    all_to_all x2 -> x0, starting transfers between devices: 8.57 us -> none  [the longest x1 5.17 us: body(): lax.all_to_all(blocks, 'expert', split_axis=0, concat_axis=0, tiled=True)]
    ppermute x2 -> x14, waiting for transfers between devices: 0.01 us -> 5.23 us  [from_each(): lax.ppermute(block, 'expert', [(i, i ^ b) for i in range(devices)])]
    dot_general x4 -> x0, matrix products: 3.62 us -> none  [the longest x1 2.18 us: body(): jnp.einsum('rd,gdh->grh', flat_rows, weights_in, preferred_element_type=j...]
    dynamic_slice x2 -> x0, local copies, waits for them, and re-layouts: 2.47 us -> none  [body(): keep_mine = new_place[slot_mine] == old_place[slot_mine]]
    reduce_sum x6 -> x0, other arithmetic: 1.79 us -> none  [the longest x1 0.77 us: routing(): counts = jnp.sum(holders, axis=1)]
  transfers between devices with their start and end apart: 4 -> 14, of which waited for: 2 -> 4; matrix products, arithmetic and copies ran while one was open for 32% -> 0% of each run, Pallas kernels for 0% -> 6%
where the time goes in v1:
time: 29.6 us; the launch traced here: 29.4 us
  starting transfers between devices  13.9 us (47%)
  Pallas kernels  8.9 us (30%)
  waiting for transfers between devices  5.23 us (18%)
  local copies, waits for them, and re-layouts  1.16 us (4%)
    ppermute x14, starting transfers between devices, from_each(): lax.ppermute(block, 'expert', [(i, i ^ b) for i in range(devices)])  13.9 us
    pallas_call x4, Pallas kernels, call(): pl.pallas_call(kernel, out_shape=outs, in_specs=[VMEM] * len(args), out_s...  8.9 us
    ppermute x14, waiting for transfers between devices, from_each(): lax.ppermute(block, 'expert', [(i, i ^ b) for i in range(devices)])  5.23 us
    unnamed x28, local copies, waits for them, and re-layouts  1.16 us
  transfers between devices with their start and end apart: 14, of which 4 were waited for; matrix products, arithmetic and copies ran while one was open for 0% of the time, Pallas kernels for 6%

profile of v1, /device:TPU:0, one launch (start us, length us, event | category | flops | bytes accessed | tf_op | source)
XLA Modules:
  0.0 29.4 jit_solution(18107787093889456191)
XLA Ops:
  0.0 2.1 %shard_map.83 = (bf16[4,3584]{1,0:T(4,128)(2,1)}, bf16[4,3584]{1,0:T(4,128)(2,1)}, bf16[4,3584]{1,0:T(4,128)(2,1)}, bf16[4,3584]{1,0:T(4,128)(2,1)}, bf16[4,3584...) custom-call(s32[1,8]{1,0:T(1,128)} %bitcast.9, s32[1,8]{1,0:T(1,128)} %bitcast.11, ...), custom_call_target="tpu_custom_call" | custom-call | tf_op jit(solution)/shard_map/pallas_call | solution.py:106
  2.1 0.5 %collective-permute-start = (bf16[4,3584]{1,0:T(4,128)(2,1)}, bf16[4,3584]{1,0:T(4,128)(2,1)S(1)}, u32[]{:S(2)}, u32[]{:S(2)}) collective-permute-start(bf16[4,3584]{1,0:T(4,128)(2,1)} %get-tuple-element.22), channel_id=1, source_target_pairs={{0,1},{1,0},{2,3},{3,2},{4,5},{5,4},{6,7},{7,6},{8,9},{9,8},{10,11... | collective-permute-start | bytes 86024 | tf_op jit(solution)/shard_map/ppermute | solution.py:116
  2.6 2.6 %collective-permute-start.1 = (bf16[4,3584]{1,0:T(4,128)(2,1)}, bf16[4,3584]{1,0:T(4,128)(2,1)S(1)}, u32[]{:S(2)}, u32[]{:S(2)}) collective-permute-start(bf16[4,3584]{1,0:T(4,128)(2,1)} %get-tuple-element.23), channel_id=1, source_target_pairs={{0,2},{1,3},{2,0},{3,1},{4,6},{5,7},{6,4},{7,5},{8,10},{9,11},{10,... | collective-permute-start | bytes 86024 | tf_op jit(solution)/shard_map/ppermute | solution.py:116
  5.2 0.1 collective-permute-start.2
  5.2 1.8 %collective-permute-start.3 = (bf16[4,3584]{1,0:T(4,128)(2,1)}, bf16[4,3584]{1,0:T(4,128)(2,1)S(1)}, u32[]{:S(2)}, u32[]{:S(2)}) collective-permute-start(bf16[4,3584]{1,0:T(4,128)(2,1)} %get-tuple-element.25), channel_id=1, source_target_pairs={{0,4},{1,5},{2,6},{3,7},{4,0},{5,1},{6,2},{7,3},{8,12},{9,13},{10,... | collective-permute-start | bytes 86024 | tf_op jit(solution)/shard_map/ppermute | solution.py:116
  7.0 0.0 collective-permute-start.4
  7.0 0.0 collective-permute-done.refs_1_
  7.0 0.0 copy-start
  7.0 2.6 %collective-permute-start.5 = (bf16[4,3584]{1,0:T(4,128)(2,1)}, bf16[4,3584]{1,0:T(4,128)(2,1)S(1)}, u32[]{:S(2)}, u32[]{:S(2)}) collective-permute-start(bf16[4,3584]{1,0:T(4,128)(2,1)} %get-tuple-element.27), channel_id=1, source_target_pairs={{0,6},{1,7},{2,4},{3,5},{4,2},{5,3},{6,0},{7,1},{8,14},{9,15},{10,... | collective-permute-start | bytes 86024 | tf_op jit(solution)/shard_map/ppermute | solution.py:116
  9.6 0.0 collective-permute-done.1.refs_2_
  9.6 0.0 copy-start.1
  9.6 0.1 collective-permute-start.6
  9.7 0.0 collective-permute-done.2.refs_3_
  9.8 0.0 copy-start.2
  9.8 0.0 collective-permute-done.3.refs_4_
  9.8 0.0 copy-start.3
  9.8 0.8 %collective-permute-done.4.refs_5_ = bf16[4,3584]{1,0:T(4,128)(2,1)S(1)} collective-permute-done((bf16[4,3584]{1,0:T(4,128)(2,1)}, bf16[4,3584]{1,0:T(4,128)(2,1)S(1)}, u32[]{:S(2)}, u32[]{:S(2)}) %collective-permute-start.4) | collective-permute-done | bytes 28704 | tf_op jit(solution)/shard_map/ppermute | solution.py:116
  10.6 0.0 copy-start.4
  10.6 1.5 %collective-permute-done.5.refs_6_ = bf16[4,3584]{1,0:T(4,128)(2,1)S(1)} collective-permute-done((bf16[4,3584]{1,0:T(4,128)(2,1)}, bf16[4,3584]{1,0:T(4,128)(2,1)S(1)}, u32[]{:S(2)}, u32[]{:S(2)}) %collective-permute-start.5) | collective-permute-done | bytes 28704 | tf_op jit(solution)/shard_map/ppermute | solution.py:116
  12.0 0.0 copy-start.5
  12.0 2.0 %collective-permute-done.6.refs_7_ = bf16[4,3584]{1,0:T(4,128)(2,1)S(1)} collective-permute-done((bf16[4,3584]{1,0:T(4,128)(2,1)}, bf16[4,3584]{1,0:T(4,128)(2,1)S(1)}, u32[]{:S(2)}, u32[]{:S(2)}) %collective-permute-start.6) | collective-permute-done | bytes 28704 | tf_op jit(solution)/shard_map/ppermute | solution.py:116
  14.0 0.0 copy-start.6
  14.0 0.0 copy-done
  14.0 0.0 copy-done.1
  14.0 0.0 copy-done.2
  14.0 0.0 copy-done.3
  14.0 0.0 copy-done.4
  14.1 0.0 copy-done.5
  14.1 0.6 %copy-done.6 = bf16[4,3584]{1,0:T(4,128)(2,1)} copy-done((bf16[4,3584]{1,0:T(4,128)(2,1)}, bf16[4,3584]{1,0:T(4,128)(2,1)S(1)}, u32[]{:S(2)}) %copy-start.6) | copy-done | bytes 28696
  14.6 3.2 %shard_map.84 = (bf16[4,3584]{1,0:T(4,128)(2,1)}, bf16[4,3584]{1,0:T(4,128)(2,1)}, bf16[4,3584]{1,0:T(4,128)(2,1)}, bf16[4,3584]{1,0:T(4,128)(2,1)}, bf16[4,3584...) custom-call(bf16[2,3584,128]{2,1,0:T(8,128)(2,1)} %w_in_ref.1, ...), custom_call_target="tpu_custom_call" | custom-call | tf_op jit(solution)/shard_map/pallas_call | solution.py:106
  17.8 0.5 %collective-permute-start.10 = (bf16[4,3584]{1,0:T(4,128)(2,1)}, bf16[4,3584]{1,0:T(4,128)(2,1)S(1)}, u32[]{:S(2)}, u32[]{:S(2)}) collective-permute-start(bf16[4,3584]{1,0:T(4,128)(2,1)} %get-tuple-element.33), channel_id=1, source_target_pairs={{0,4},{1,5},{2,6},{3,7},{4,0},{5,1},{6,2},{7,3},{8,12},{9,13},{10,... | collective-permute-start | bytes 86024 | tf_op jit(solution)/shard_map/ppermute | solution.py:116
  18.4 1.0 %collective-permute-start.11 = (bf16[4,3584]{1,0:T(4,128)(2,1)}, bf16[4,3584]{1,0:T(4,128)(2,1)S(1)}, u32[]{:S(2)}, u32[]{:S(2)}) collective-permute-start(bf16[4,3584]{1,0:T(4,128)(2,1)} %get-tuple-element.34), channel_id=1, source_target_pairs={{0,5},{1,4},{2,7},{3,6},{4,1},{5,0},{6,3},{7,2},{8,13},{9,12},{10,... | collective-permute-start | bytes 86024 | tf_op jit(solution)/shard_map/ppermute | solution.py:116
  19.4 1.1 %collective-permute-start.12 = (bf16[4,3584]{1,0:T(4,128)(2,1)}, bf16[4,3584]{1,0:T(4,128)(2,1)S(1)}, u32[]{:S(2)}, u32[]{:S(2)}) collective-permute-start(bf16[4,3584]{1,0:T(4,128)(2,1)} %get-tuple-element.35), channel_id=1, source_target_pairs={{0,6},{1,7},{2,4},{3,5},{4,2},{5,3},{6,0},{7,1},{8,14},{9,15},{10,... | collective-permute-start | bytes 86024 | tf_op jit(solution)/shard_map/ppermute | solution.py:116
  20.5 1.8 %collective-permute-start.13 = (bf16[4,3584]{1,0:T(4,128)(2,1)}, bf16[4,3584]{1,0:T(4,128)(2,1)S(1)}, u32[]{:S(2)}, u32[]{:S(2)}) collective-permute-start(bf16[4,3584]{1,0:T(4,128)(2,1)} %get-tuple-element.36), channel_id=1, source_target_pairs={{0,7},{1,6},{2,5},{3,4},{4,3},{5,2},{6,1},{7,0},{8,15},{9,14},{10,... | collective-permute-start | bytes 86024 | tf_op jit(solution)/shard_map/ppermute | solution.py:116
  22.3 0.1 collective-permute-start.7
  22.4 0.0 collective-permute-done.10.refs_4_
  22.4 0.0 copy-start.7
  22.4 0.5 %collective-permute-start.8 = (bf16[4,3584]{1,0:T(4,128)(2,1)}, bf16[4,3584]{1,0:T(4,128)(2,1)S(1)}, u32[]{:S(2)}, u32[]{:S(2)}) collective-permute-start(bf16[4,3584]{1,0:T(4,128)(2,1)} %get-tuple-element.31), channel_id=1, source_target_pairs={{0,2},{1,3},{2,0},{3,1},{4,6},{5,7},{6,4},{7,5},{8,10},{9,11},{10,... | collective-permute-start | bytes 86024 | tf_op jit(solution)/shard_map/ppermute | solution.py:116
  23.0 0.0 collective-permute-done.11.refs_5_
  23.0 0.0 copy-start.8
  23.0 1.2 %collective-permute-start.9 = (bf16[4,3584]{1,0:T(4,128)(2,1)}, bf16[4,3584]{1,0:T(4,128)(2,1)S(1)}, u32[]{:S(2)}, u32[]{:S(2)}) collective-permute-start(bf16[4,3584]{1,0:T(4,128)(2,1)} %get-tuple-element.32), channel_id=1, source_target_pairs={{0,3},{1,2},{2,1},{3,0},{4,7},{5,6},{6,5},{7,4},{8,11},{9,10},{10,... | collective-permute-start | bytes 86024 | tf_op jit(solution)/shard_map/ppermute | solution.py:116
  24.1 1.6 %shard_map.82.weight_ref = f32[32,16]{1,0:T(8,128)} custom-call(s32[1,8]{1,0:T(1,128)} %bitcast.10, s32[1,8]{1,0:T(1,128)} %bitcast.12, s32[2,16]{1,0:T(2,128)} %bitcast.6, s32[2,16]{1,0:T(2,128)} %bitcast.8, f32[2,16]{1,0:T(2,128)} %bitcast.13), custom_call_target="tpu_custom_call" | custom-call | tf_op jit(solution)/shard_map/pallas_call | solution.py:106
  25.8 0.0 collective-permute-done.12.refs_6_
  25.8 0.0 copy-start.9
  25.8 0.0 collective-permute-done.13.refs_7_
  25.8 0.0 copy-start.10
  25.8 0.0 collective-permute-done.7.refs_1_
  25.8 0.0 copy-start.11
  25.8 1.0 %collective-permute-done.8.refs_2_ = bf16[4,3584]{1,0:T(4,128)(2,1)S(1)} collective-permute-done((bf16[4,3584]{1,0:T(4,128)(2,1)}, bf16[4,3584]{1,0:T(4,128)(2,1)S(1)}, u32[]{:S(2)}, u32[]{:S(2)}) %collective-permute-start.8) | collective-permute-done | bytes 28704 | tf_op jit(solution)/shard_map/ppermute | solution.py:116
  26.8 0.0 copy-start.12
  26.8 0.0 collective-permute-done.9.refs_3_
  26.8 0.0 copy-start.13
  26.8 0.0 copy-done.7
  26.8 0.0 copy-done.8
  26.8 0.0 copy-done.9
  26.8 0.0 copy-done.10
  26.8 0.0 copy-done.11
  26.8 0.5 %copy-done.12 = bf16[4,3584]{1,0:T(4,128)(2,1)} copy-done((bf16[4,3584]{1,0:T(4,128)(2,1)}, bf16[4,3584]{1,0:T(4,128)(2,1)S(1)}, u32[]{:S(2)}) %copy-start.12) | copy-done | bytes 28696
  27.4 0.0 copy-done.13
  27.4 2.0 %shard_map.85 = bf16[16,3584]{1,0:T(8,128)(2,1)} custom-call(f32[32,16]{1,0:T(8,128)} %shard_map.82.weight_ref, bf16[4,3584]{1,0:T(4,128)(2,1)} %get-tuple-element.29.refs_0_, bf16[4,3584]{1,0:T(4,128)(2,1)} %copy-done.11, bf16[4,3584]{1,0:T(4,128)(2,1)} %copy-done.12, bf16[4,3584]{1,0:T(4,128)(2,1)} %copy-done.13, bf16[4,3584]{1,0:T(4,128)(2,1)} %copy-done.7, ...), custom_call_target="tpu_custom_call" | custom-call | tf_op jit(solution)/shard_map/pallas_call | solution.py:106
Async XLA Ops:
  2.1 4.9 %collective-permute-start = (bf16[4,3584]{1,0:T(4,128)(2,1)}, bf16[4,3584]{1,0:T(4,128)(2,1)S(1)}, u32[]{:S(2)}, u32[]{:S(2)}) collective-permute-start(bf16[4,3584]{1,0:T(4,128)(2,1)} %get-tuple-element.22), channel_id=1, source_target_pairs={{0,1},{1,0},{2,3},{3,2},{4,5},{5,4},{6,7},{7,6},{8,9},{9,8},{10,11... | collective-permute-start | bytes 86024 | tf_op jit(solution)/shard_map/ppermute | solution.py:116
  2.6 7.0 %collective-permute-start.1 = (bf16[4,3584]{1,0:T(4,128)(2,1)}, bf16[4,3584]{1,0:T(4,128)(2,1)S(1)}, u32[]{:S(2)}, u32[]{:S(2)}) collective-permute-start(bf16[4,3584]{1,0:T(4,128)(2,1)} %get-tuple-element.23), channel_id=1, source_target_pairs={{0,2},{1,3},{2,0},{3,1},{4,6},{5,7},{6,4},{7,5},{8,10},{9,11},{10,... | collective-permute-start | bytes 86024 | tf_op jit(solution)/shard_map/ppermute | solution.py:116
  5.2 4.6 %collective-permute-start.2 = (bf16[4,3584]{1,0:T(4,128)(2,1)}, bf16[4,3584]{1,0:T(4,128)(2,1)S(1)}, u32[]{:S(2)}, u32[]{:S(2)}) collective-permute-start(bf16[4,3584]{1,0:T(4,128)(2,1)} %get-tuple-element.24), channel_id=1, source_target_pairs={{0,3},{1,2},{2,1},{3,0},{4,7},{5,6},{6,5},{7,4},{8,11},{9,10},{10,... | collective-permute-start | bytes 86024 | tf_op jit(solution)/shard_map/ppermute | solution.py:116
  5.2 4.5 %collective-permute-start.3 = (bf16[4,3584]{1,0:T(4,128)(2,1)}, bf16[4,3584]{1,0:T(4,128)(2,1)S(1)}, u32[]{:S(2)}, u32[]{:S(2)}) collective-permute-start(bf16[4,3584]{1,0:T(4,128)(2,1)} %get-tuple-element.25), channel_id=1, source_target_pairs={{0,4},{1,5},{2,6},{3,7},{4,0},{5,1},{6,2},{7,3},{8,12},{9,13},{10,... | collective-permute-start | bytes 86024 | tf_op jit(solution)/shard_map/ppermute | solution.py:116
  7.0 3.6 %collective-permute-start.4 = (bf16[4,3584]{1,0:T(4,128)(2,1)}, bf16[4,3584]{1,0:T(4,128)(2,1)S(1)}, u32[]{:S(2)}, u32[]{:S(2)}) collective-permute-start(bf16[4,3584]{1,0:T(4,128)(2,1)} %get-tuple-element.26), channel_id=1, source_target_pairs={{0,5},{1,4},{2,7},{3,6},{4,1},{5,0},{6,3},{7,2},{8,13},{9,12},{10,... | collective-permute-start | bytes 86024 | tf_op jit(solution)/shard_map/ppermute | solution.py:116
  7.0 7.0 %copy-start = (bf16[4,3584]{1,0:T(4,128)(2,1)}, bf16[4,3584]{1,0:T(4,128)(2,1)S(1)}, u32[]{:S(2)}) copy-start(bf16[4,3584]{1,0:T(4,128)(2,1)S(1)} %collective-permute-done.refs_1_) | copy-start | bytes 86020
  7.0 5.0 %collective-permute-start.5 = (bf16[4,3584]{1,0:T(4,128)(2,1)}, bf16[4,3584]{1,0:T(4,128)(2,1)S(1)}, u32[]{:S(2)}, u32[]{:S(2)}) collective-permute-start(bf16[4,3584]{1,0:T(4,128)(2,1)} %get-tuple-element.27), channel_id=1, source_target_pairs={{0,6},{1,7},{2,4},{3,5},{4,2},{5,3},{6,0},{7,1},{8,14},{9,15},{10,... | collective-permute-start | bytes 86024 | tf_op jit(solution)/shard_map/ppermute | solution.py:116
  9.6 4.4 %copy-start.1 = (bf16[4,3584]{1,0:T(4,128)(2,1)}, bf16[4,3584]{1,0:T(4,128)(2,1)S(1)}, u32[]{:S(2)}) copy-start(bf16[4,3584]{1,0:T(4,128)(2,1)S(1)} %collective-permute-done.1.refs_2_) | copy-start | bytes 86020
  9.6 4.4 %collective-permute-start.6 = (bf16[4,3584]{1,0:T(4,128)(2,1)}, bf16[4,3584]{1,0:T(4,128)(2,1)S(1)}, u32[]{:S(2)}, u32[]{:S(2)}) collective-permute-start(bf16[4,3584]{1,0:T(4,128)(2,1)} %get-tuple-element.28), channel_id=1, source_target_pairs={{0,7},{1,6},{2,5},{3,4},{4,3},{5,2},{6,1},{7,0},{8,15},{9,14},{10,... | collective-permute-start | bytes 86024 | tf_op jit(solution)/shard_map/ppermute | solution.py:116
  9.8 4.3 %copy-start.2 = (bf16[4,3584]{1,0:T(4,128)(2,1)}, bf16[4,3584]{1,0:T(4,128)(2,1)S(1)}, u32[]{:S(2)}) copy-start(bf16[4,3584]{1,0:T(4,128)(2,1)S(1)} %collective-permute-done.2.refs_3_) | copy-start | bytes 86020
  9.8 4.3 %copy-start.3 = (bf16[4,3584]{1,0:T(4,128)(2,1)}, bf16[4,3584]{1,0:T(4,128)(2,1)S(1)}, u32[]{:S(2)}) copy-start(bf16[4,3584]{1,0:T(4,128)(2,1)S(1)} %collective-permute-done.3.refs_4_) | copy-start | bytes 86020
  10.6 3.5 %copy-start.4 = (bf16[4,3584]{1,0:T(4,128)(2,1)}, bf16[4,3584]{1,0:T(4,128)(2,1)S(1)}, u32[]{:S(2)}) copy-start(bf16[4,3584]{1,0:T(4,128)(2,1)S(1)} %collective-permute-done.4.refs_5_) | copy-start | bytes 86020
  12.0 2.0 %copy-start.5 = (bf16[4,3584]{1,0:T(4,128)(2,1)}, bf16[4,3584]{1,0:T(4,128)(2,1)S(1)}, u32[]{:S(2)}) copy-start(bf16[4,3584]{1,0:T(4,128)(2,1)S(1)} %collective-permute-done.5.refs_6_) | copy-start | bytes 86020
  14.0 0.6 %copy-start.6 = (bf16[4,3584]{1,0:T(4,128)(2,1)}, bf16[4,3584]{1,0:T(4,128)(2,1)S(1)}, u32[]{:S(2)}) copy-start(bf16[4,3584]{1,0:T(4,128)(2,1)S(1)} %collective-permute-done.6.refs_7_) | copy-start | bytes 86020
  17.8 4.6 %collective-permute-start.10 = (bf16[4,3584]{1,0:T(4,128)(2,1)}, bf16[4,3584]{1,0:T(4,128)(2,1)S(1)}, u32[]{:S(2)}, u32[]{:S(2)}) collective-permute-start(bf16[4,3584]{1,0:T(4,128)(2,1)} %get-tuple-element.33), channel_id=1, source_target_pairs={{0,4},{1,5},{2,6},{3,7},{4,0},{5,1},{6,2},{7,3},{8,12},{9,13},{10,... | collective-permute-start | bytes 86024 | tf_op jit(solution)/shard_map/ppermute | solution.py:116
  18.4 4.6 %collective-permute-start.11 = (bf16[4,3584]{1,0:T(4,128)(2,1)}, bf16[4,3584]{1,0:T(4,128)(2,1)S(1)}, u32[]{:S(2)}, u32[]{:S(2)}) collective-permute-start(bf16[4,3584]{1,0:T(4,128)(2,1)} %get-tuple-element.34), channel_id=1, source_target_pairs={{0,5},{1,4},{2,7},{3,6},{4,1},{5,0},{6,3},{7,2},{8,13},{9,12},{10,... | collective-permute-start | bytes 86024 | tf_op jit(solution)/shard_map/ppermute | solution.py:116
  19.4 6.4 %collective-permute-start.12 = (bf16[4,3584]{1,0:T(4,128)(2,1)}, bf16[4,3584]{1,0:T(4,128)(2,1)S(1)}, u32[]{:S(2)}, u32[]{:S(2)}) collective-permute-start(bf16[4,3584]{1,0:T(4,128)(2,1)} %get-tuple-element.35), channel_id=1, source_target_pairs={{0,6},{1,7},{2,4},{3,5},{4,2},{5,3},{6,0},{7,1},{8,14},{9,15},{10,... | collective-permute-start | bytes 86024 | tf_op jit(solution)/shard_map/ppermute | solution.py:116
  20.5 5.3 %collective-permute-start.13 = (bf16[4,3584]{1,0:T(4,128)(2,1)}, bf16[4,3584]{1,0:T(4,128)(2,1)S(1)}, u32[]{:S(2)}, u32[]{:S(2)}) collective-permute-start(bf16[4,3584]{1,0:T(4,128)(2,1)} %get-tuple-element.36), channel_id=1, source_target_pairs={{0,7},{1,6},{2,5},{3,4},{4,3},{5,2},{6,1},{7,0},{8,15},{9,14},{10,... | collective-permute-start | bytes 86024 | tf_op jit(solution)/shard_map/ppermute | solution.py:116
  22.3 3.5 %collective-permute-start.7 = (bf16[4,3584]{1,0:T(4,128)(2,1)}, bf16[4,3584]{1,0:T(4,128)(2,1)S(1)}, u32[]{:S(2)}, u32[]{:S(2)}) collective-permute-start(bf16[4,3584]{1,0:T(4,128)(2,1)} %get-tuple-element.30), channel_id=1, source_target_pairs={{0,1},{1,0},{2,3},{3,2},{4,5},{5,4},{6,7},{7,6},{8,9},{9,8},{10,11... | collective-permute-start | bytes 86024 | tf_op jit(solution)/shard_map/ppermute | solution.py:116
  22.4 4.4 %copy-start.7 = (bf16[4,3584]{1,0:T(4,128)(2,1)}, bf16[4,3584]{1,0:T(4,128)(2,1)S(1)}, u32[]{:S(2)}) copy-start(bf16[4,3584]{1,0:T(4,128)(2,1)S(1)} %collective-permute-done.10.refs_4_) | copy-start | bytes 86020
  22.4 4.4 %collective-permute-start.8 = (bf16[4,3584]{1,0:T(4,128)(2,1)}, bf16[4,3584]{1,0:T(4,128)(2,1)S(1)}, u32[]{:S(2)}, u32[]{:S(2)}) collective-permute-start(bf16[4,3584]{1,0:T(4,128)(2,1)} %get-tuple-element.31), channel_id=1, source_target_pairs={{0,2},{1,3},{2,0},{3,1},{4,6},{5,7},{6,4},{7,5},{8,10},{9,11},{10,... | collective-permute-start | bytes 86024 | tf_op jit(solution)/shard_map/ppermute | solution.py:116
  23.0 3.8 %copy-start.8 = (bf16[4,3584]{1,0:T(4,128)(2,1)}, bf16[4,3584]{1,0:T(4,128)(2,1)S(1)}, u32[]{:S(2)}) copy-start(bf16[4,3584]{1,0:T(4,128)(2,1)S(1)} %collective-permute-done.11.refs_5_) | copy-start | bytes 86020
  23.0 3.8 %collective-permute-start.9 = (bf16[4,3584]{1,0:T(4,128)(2,1)}, bf16[4,3584]{1,0:T(4,128)(2,1)S(1)}, u32[]{:S(2)}, u32[]{:S(2)}) collective-permute-start(bf16[4,3584]{1,0:T(4,128)(2,1)} %get-tuple-element.32), channel_id=1, source_target_pairs={{0,3},{1,2},{2,1},{3,0},{4,7},{5,6},{6,5},{7,4},{8,11},{9,10},{10,... | collective-permute-start | bytes 86024 | tf_op jit(solution)/shard_map/ppermute | solution.py:116
  25.8 1.0 %copy-start.9 = (bf16[4,3584]{1,0:T(4,128)(2,1)}, bf16[4,3584]{1,0:T(4,128)(2,1)S(1)}, u32[]{:S(2)}) copy-start(bf16[4,3584]{1,0:T(4,128)(2,1)S(1)} %collective-permute-done.12.refs_6_) | copy-start | bytes 86020
  25.8 1.0 %copy-start.10 = (bf16[4,3584]{1,0:T(4,128)(2,1)}, bf16[4,3584]{1,0:T(4,128)(2,1)S(1)}, u32[]{:S(2)}) copy-start(bf16[4,3584]{1,0:T(4,128)(2,1)S(1)} %collective-permute-done.13.refs_7_) | copy-start | bytes 86020
  25.8 1.0 %copy-start.11 = (bf16[4,3584]{1,0:T(4,128)(2,1)}, bf16[4,3584]{1,0:T(4,128)(2,1)S(1)}, u32[]{:S(2)}) copy-start(bf16[4,3584]{1,0:T(4,128)(2,1)S(1)} %collective-permute-done.7.refs_1_) | copy-start | bytes 86020
  26.8 0.6 %copy-start.12 = (bf16[4,3584]{1,0:T(4,128)(2,1)}, bf16[4,3584]{1,0:T(4,128)(2,1)S(1)}, u32[]{:S(2)}) copy-start(bf16[4,3584]{1,0:T(4,128)(2,1)S(1)} %collective-permute-done.8.refs_2_) | copy-start | bytes 86020
  26.8 0.6 %copy-start.13 = (bf16[4,3584]{1,0:T(4,128)(2,1)}, bf16[4,3584]{1,0:T(4,128)(2,1)S(1)}, u32[]{:S(2)}) copy-start(bf16[4,3584]{1,0:T(4,128)(2,1)S(1)} %collective-permute-done.9.refs_3_) | copy-start | bytes 86020

commit v2 on v1

--- a/solution.py
+++ b/solution.py
@@ -54,93 +54,123 @@
 
 def dispatch_kernel(shards, new_ref, old_ref, ids_ref, replica_ref, tokens_ref, *block_refs):
     found = targets(shards, new_ref, old_ref, ids_ref, replica_ref)
-    lines = CAP * len(block_refs)
+    lines = sum(ref.shape[0] for ref in block_refs)
     line = lax.broadcasted_iota(jnp.int32, (lines, tokens_ref.shape[0]), 0)
     picked = functools.reduce(jnp.logical_or, [line == target for target in found])
     selector = jnp.where(picked, 1.0, 0.0).astype(jnp.bfloat16)
     buffer = jnp.dot(selector, tokens_ref[...], preferred_element_type=jnp.float32)
+    size = block_refs[0].shape[0]
     for b, block_ref in enumerate(block_refs):
-        block_ref[...] = buffer[CAP * b : CAP * (b + 1)].astype(jnp.bfloat16)
+        block_ref[...] = buffer[size * b : size * (b + 1)].astype(jnp.bfloat16)
 
 
 def combine_kernel(shards, new_ref, old_ref, ids_ref, replica_ref, combine_ref, weight_ref):
     found = targets(shards, new_ref, old_ref, ids_ref, replica_ref)
-    line = lax.broadcasted_iota(jnp.int32, weight_ref.shape, 0)
-    weight_ref[...] = functools.reduce(
+    line = lax.broadcasted_iota(jnp.int32, (weight_ref.shape[1], ids_ref.shape[1]), 0)
+    weight = functools.reduce(
         jnp.add,
         [
             jnp.where(line == target, combine_ref[k : k + 1, :], 0.0)
             for k, target in enumerate(found)
         ],
-    )
+    ).T
+    high = weight.astype(jnp.bfloat16)
+    low = (weight - high.astype(jnp.float32)).astype(jnp.bfloat16)
+    weight_ref[...] = jnp.concatenate([high, low], axis=0)
 
 
 def stack(refs):
     return jnp.concatenate([ref[...].astype(jnp.float32) for ref in refs], axis=0)
 
 
-def expert_kernel(devices, w_in_ref, w_down_ref, *refs):
-    rows = stack(refs[:devices]).astype(jnp.bfloat16)
-    gate = jnp.dot(rows, w_in_ref[0], preferred_element_type=jnp.float32)
-    up = jnp.dot(rows, w_in_ref[1], preferred_element_type=jnp.float32)
-    hidden = (jax.nn.silu(gate) * up).astype(jnp.bfloat16)
-    piece = jnp.dot(hidden, w_down_ref[...], preferred_element_type=jnp.float32)
-    for b, out_ref in enumerate(refs[devices:]):
-        out_ref[...] = piece[CAP * b : CAP * (b + 1)].astype(jnp.bfloat16)
+def expert_kernel(split, in_ref, down_ref, twin_in_ref, twin_down_ref, *refs):
+    count = len(refs) // 2
+    rows = stack(refs[:count]).astype(jnp.bfloat16)
+    size = refs[0].shape[0]
+    hidden = []
+    for half, ref in enumerate((in_ref, twin_in_ref)):
+        gate = jnp.dot(rows, ref[0], preferred_element_type=jnp.float32)
+        up = jnp.dot(rows, ref[1], preferred_element_type=jnp.float32)
+        value = jax.nn.silu(gate) * up
+        if split:
+            place = lax.broadcasted_iota(jnp.int32, value.shape, 0) & (size - 1)
+            value = jnp.where((place >= size // 2) == bool(half), value, 0.0)
+        hidden.append(value.astype(jnp.bfloat16))
+    piece = jnp.dot(
+        jnp.concatenate(hidden, axis=1),
+        jnp.concatenate([down_ref[...], twin_down_ref[...]], axis=0),
+        preferred_element_type=jnp.float32,
+    )
+    for b, out_ref in enumerate(refs[count:]):
+        out_ref[...] = piece[size * b : size * (b + 1)].astype(jnp.bfloat16)
 
 
-def mix_kernel(shards, weight_ref, *refs):
+def mix_kernel(repeats, weight_ref, *refs):
     out_ref = refs[-1]
-    total = functools.reduce(jnp.add, [stack(refs[j:-1:shards]) for j in range(shards)])
-    weight = weight_ref[...]
-    out_ref[...] = lax.dot_general(
-        weight,
-        total,
-        (((0,), (0,)), ((), ())),
-        precision=lax.Precision.HIGHEST,
-        preferred_element_type=jnp.float32,
-    ).astype(jnp.bfloat16)
+    total = functools.reduce(jnp.add, [stack(refs[j:-1:repeats]) for j in range(repeats)])
+    high = total.astype(jnp.bfloat16)
+    mixed = jnp.dot(weight_ref[...], high, preferred_element_type=jnp.float32)
+    if repeats > 1:
+        low = (total - high.astype(jnp.float32)).astype(jnp.bfloat16)
+        mixed += jnp.dot(weight_ref[...], low, preferred_element_type=jnp.float32)
+    rows = out_ref.shape[0]
+    out_ref[...] = (mixed[:rows] + mixed[rows:]).astype(jnp.bfloat16)
 
 
-def call(kernel, outs, args):
+def call(kernel, outs, args, flops=0):
+    nbytes = sum(x.size * x.dtype.itemsize for x in jax.tree.leaves((outs, args)))
     return pl.pallas_call(
         kernel,
         out_shape=outs,
         in_specs=[VMEM] * len(args),
         out_specs=jax.tree.map(lambda _: VMEM, outs),
+        compiler_params=pltpu.CompilerParams(vmem_limit_bytes=16 << 20),
+        cost_estimate=pl.CostEstimate(flops=flops, bytes_accessed=nbytes, transcendentals=0),
     )(*args)
 
 
-def from_each(blocks, devices):
-    return [
-        block if b == 0 else lax.ppermute(block, "expert", [(i, i ^ b) for i in range(devices)])
-        for b, block in enumerate(blocks)
-    ]
+def swap(block, distance):
+    if distance == 0:
+        return block
+    pairs = [(i, i ^ distance) for i in range(lax.axis_size("expert"))]
+    return lax.ppermute(block, "expert", pairs)
 
 
 def body(tokens, w_in, w_down, old_place, new_place, expert_ids, replica, combine):
     devices = lax.axis_size("expert")
     shards = devices // SLOTS
+    split = shards == 1
+    repeats = max(shards // 2, 1)
     rows, width = tokens.shape
+    hidden = w_down.shape[0]
+    twin_in, twin_down = swap(w_in, 1), swap(w_down, 1)
     routing = (new_place[None], old_place[None], expert_ids.T, replica.T)
-    block = jax.ShapeDtypeStruct((CAP, width), jnp.bfloat16)
+    block = jax.ShapeDtypeStruct((CAP * (2 if split else 1), width), jnp.bfloat16)
     blocks = call(
-        functools.partial(dispatch_kernel, shards), [block] * SLOTS, (*routing, tokens)
+        functools.partial(dispatch_kernel, shards),
+        [block] * (devices // 2 // repeats),
+        (*routing, tokens),
+        2 * SLOTS * CAP * rows * width,
     )
-    received = from_each([blocks[b // shards] for b in range(devices)], devices)
+    distances = range(0, devices, 2)
+    received = [swap(blocks[c // repeats], d) for c, d in enumerate(distances)]
     weight = call(
         functools.partial(combine_kernel, shards),
-        jax.ShapeDtypeStruct((SLOTS * CAP, rows), jnp.float32),
+        jax.ShapeDtypeStruct((2 * rows, SLOTS * CAP), jnp.bfloat16),
         (*routing, combine.T),
     )
     pieces = call(
-        functools.partial(expert_kernel, devices), [block] * devices, (w_in, w_down, *received)
+        functools.partial(expert_kernel, split),
+        [block] * len(distances),
+        (w_in, w_down, twin_in, twin_down, *received),
+        12 * len(distances) * block.shape[0] * hidden * width,
     )
-    returned = from_each(pieces, devices)
+    returned = [swap(piece, d) for piece, d in zip(pieces, distances)]
     return call(
-        functools.partial(mix_kernel, shards),
+        functools.partial(mix_kernel, repeats),
         jax.ShapeDtypeStruct((rows, width), jnp.bfloat16),
         (weight, *returned),
+        4 * SLOTS * CAP * rows * width,
     )
 
 

time: 29.6 us -> 24.8 us (0.84)
  Pallas kernels: 8.9 us -> 2.69 us
  starting transfers between devices: 13.9 us -> 8.59 us
  local copies, waits for them, and re-layouts: 1.16 us -> 6.26 us
  waiting for transfers between devices: 5.23 us -> 6.99 us
    pallas_call x4, Pallas kernels: 8.9 us -> 2.69 us  [call(): pl.pallas_call(kernel, out_shape=outs, in_specs=[VMEM] * len(args), out_s...]
    ppermute x14 -> x8, starting transfers between devices: 13.9 us -> 8.59 us  [swap(): return lax.ppermute(block, 'expert', pairs)]
    unnamed x28 -> x24, local copies, waits for them, and re-layouts: 1.16 us -> 6.26 us
    ppermute x14 -> x8, waiting for transfers between devices: 5.23 us -> 6.99 us  [swap(): return lax.ppermute(block, 'expert', pairs)]
  transfers between devices with their start and end apart: 14 -> 8, of which waited for: 4 -> 6; matrix products, arithmetic and copies ran while one was open for 0% -> 0% of each run, Pallas kernels for 6% -> 3%
where the time goes in v2:
time: 24.8 us; the launch traced here: 24.6 us
  starting transfers between devices  8.59 us (35%)
  waiting for transfers between devices  6.99 us (28%)
  local copies, waits for them, and re-layouts  6.26 us (25%)
  Pallas kernels  2.69 us (11%)
    ppermute x8, starting transfers between devices, swap(): return lax.ppermute(block, 'expert', pairs)  8.59 us
    ppermute x8, waiting for transfers between devices, swap(): return lax.ppermute(block, 'expert', pairs)  6.99 us
    unnamed x24, local copies, waits for them, and re-layouts  6.26 us
    pallas_call x4, Pallas kernels, call(): pl.pallas_call(kernel, out_shape=outs, in_specs=[VMEM] * len(args), out_s...  2.69 us
  transfers between devices with their start and end apart: 8, of which 6 were waited for; matrix products, arithmetic and copies ran while one was open for 0% of the time, Pallas kernels for 3%

profile of v2, /device:TPU:0, one launch (start us, length us, event | category | flops | bytes accessed | tf_op | source)
XLA Modules:
  0.0 24.6 jit_solution(11953703465287749588)
XLA Ops:
  0.0 0.5 %collective-permute-start = (bf16[2,3584,128]{2,1,0:T(8,128)(2,1)}, bf16[2,3584,128]{2,1,0:T(8,128)(2,1)S(1)}, u32[]{:S(2)}, u32[]{:S(2)}) collective-permute-start(bf16[2,3584,128]{2,1,0:T(8,128)(2,1)} %in_ref.1), channel_id=1, source_target_pairs={{0,1},{1,0},{2,3},{3,2},{4,5},{5,4},{6,7},{7,6},{8,9},{9,8},{10,11... | collective-permute-start | bytes 5505032 | tf_op jit(solution)/shard_map/ppermute | solution.py:136
  0.5 0.1 collective-permute-start.1
  0.5 0.0 copy-start.2
  0.5 0.9 %copy-done.2 = bf16[16,3584]{1,0:T(8,128)(2,1)S(1)} copy-done((bf16[16,3584]{1,0:T(8,128)(2,1)S(1)}, bf16[16,3584]{1,0:T(8,128)(2,1)}, u32[]{:S(2)}) %copy-start.2) | copy-done | bytes 114712
  1.4 0.0 copy-start.3
  1.4 0.7 %copy-done.3 = s32[16,2]{0,1:T(2,128)S(1)} copy-done((s32[16,2]{0,1:T(2,128)S(1)}, s32[16,2]{0,1:T(2,128)}, u32[]{:S(2)}) %copy-start.3) | copy-done | bytes 152
  2.1 0.0 copy-start.5
  2.1 0.7 %copy-done.5 = s32[16,2]{0,1:T(2,128)S(1)} copy-done((s32[16,2]{0,1:T(2,128)S(1)}, s32[16,2]{0,1:T(2,128)}, u32[]{:S(2)}) %copy-start.5) | copy-done | bytes 152
  2.8 0.0 copy-start.7
  2.8 0.7 %copy-done.7 = s32[8]{0:T(128)S(1)} copy-done((s32[8]{0:T(128)S(1)}, s32[8]{0:T(128)}, u32[]{:S(2)}) %copy-start.7) | copy-done | bytes 56
  3.4 0.0 copy-start.9
  3.4 0.7 %copy-done.9 = s32[8]{0:T(128)S(1)} copy-done((s32[8]{0:T(128)S(1)}, s32[8]{0:T(128)}, u32[]{:S(2)}) %copy-start.9) | copy-done | bytes 56
  4.1 0.5 %shard_map.83 = (bf16[8,3584]{1,0:T(8,128)(2,1)S(1)}, bf16[8,3584]{1,0:T(8,128)(2,1)S(1)}, bf16[8,3584]{1,0:T(8,128)(2,1)S(1)}, bf16[8,3584]{1,0:T(8,128)(2,1)S(1)}) custom-call(s32[1,8]{1,0:T(1,128)S(1)} %bitcast.9, s32[1,8]{1,0:T(1,128)S(1)} %bitcast.11, s32[2,16]{1,0:T(2,128)S(1)} %bitcast.5, s32[2,16]{1,0:T(2,128)S(1)} %bitcast.7, ...), custom_call_target="tpu_custom_call" | custom-call | flops 3670016 | bytes 344384 | tf_op jit(solution)/shard_map/pallas_call | solution.py:122
  4.6 3.0 %collective-permute-start.2 = (bf16[8,3584]{1,0:T(8,128)(2,1)S(1)}, bf16[8,3584]{1,0:T(8,128)(2,1)S(1)}, u32[]{:S(2)}, u32[]{:S(2)}) collective-permute-start(bf16[8,3584]{1,0:T(8,128)(2,1)S(1)} %get-tuple-element.14), channel_id=1, source_target_pairs={{0,2},{1,3},{2,0},{3,1},{4,6},{5,7},{6,4},{7,5},{8,10},{9,11},{10,... | collective-permute-start | bytes 172040 | tf_op jit(solution)/shard_map/ppermute | solution.py:136
  7.6 1.5 %collective-permute-start.3 = (bf16[8,3584]{1,0:T(8,128)(2,1)S(1)}, bf16[8,3584]{1,0:T(8,128)(2,1)S(1)}, u32[]{:S(2)}, u32[]{:S(2)}) collective-permute-start(bf16[8,3584]{1,0:T(8,128)(2,1)S(1)} %get-tuple-element.15), channel_id=1, source_target_pairs={{0,4},{1,5},{2,6},{3,7},{4,0},{5,1},{6,2},{7,3},{8,12},{9,13},{10,... | collective-permute-start | bytes 172040 | tf_op jit(solution)/shard_map/ppermute | solution.py:136
  9.1 0.0 collective-permute-start.4
  9.1 0.6 %collective-permute-done.2.refs_1_ = bf16[8,3584]{1,0:T(8,128)(2,1)S(1)} collective-permute-done((bf16[8,3584]{1,0:T(8,128)(2,1)S(1)}, bf16[8,3584]{1,0:T(8,128)(2,1)S(1)}, u32[]{:S(2)}, u32[]{:S(2)}) %collective-permute-start.2) | collective-permute-done | bytes 57376 | tf_op jit(solution)/shard_map/ppermute | solution.py:136
  9.7 2.0 %collective-permute-done.3.refs_2_ = bf16[8,3584]{1,0:T(8,128)(2,1)S(1)} collective-permute-done((bf16[8,3584]{1,0:T(8,128)(2,1)S(1)}, bf16[8,3584]{1,0:T(8,128)(2,1)S(1)}, u32[]{:S(2)}, u32[]{:S(2)}) %collective-permute-start.3) | collective-permute-done | bytes 57376 | tf_op jit(solution)/shard_map/ppermute | solution.py:136
  11.7 2.4 %collective-permute-done.4.refs_3_ = bf16[8,3584]{1,0:T(8,128)(2,1)S(1)} collective-permute-done((bf16[8,3584]{1,0:T(8,128)(2,1)S(1)}, bf16[8,3584]{1,0:T(8,128)(2,1)S(1)}, u32[]{:S(2)}, u32[]{:S(2)}) %collective-permute-start.4) | collective-permute-done | bytes 57376 | tf_op jit(solution)/shard_map/ppermute | solution.py:136
  14.2 0.0 collective-permute-done.1.twin_down_ref
  14.2 0.0 collective-permute-done.twin_in_ref
  14.2 0.0 copy-start
  14.2 1.5 %copy-done = bf16[2,3584,128]{2,1,0:T(8,128)(2,1)S(1)} copy-done((bf16[2,3584,128]{2,1,0:T(8,128)(2,1)S(1)}, bf16[2,3584,128]{2,1,0:T(8,128)(2,1)}, u32[]{:S(2)}) %copy-start) | copy-done | bytes 1835032
  15.7 0.0 copy-start.1
  15.7 1.2 %copy-done.1 = bf16[128,3584]{1,0:T(8,128)(2,1)S(1)} copy-done((bf16[128,3584]{1,0:T(8,128)(2,1)S(1)}, bf16[128,3584]{1,0:T(8,128)(2,1)}, u32[]{:S(2)}) %copy-start.1) | copy-done | bytes 917528
  16.8 0.0 copy-start.4
  16.9 0.0 copy-start.6
  16.9 0.0 copy-start.8
  16.9 0.0 copy-start.10
  16.9 0.0 copy-start.11
  16.9 1.0 %shard_map.84 = (bf16[8,3584]{1,0:T(8,128)(2,1)S(1)}, bf16[8,3584]{1,0:T(8,128)(2,1)S(1)}, bf16[8,3584]{1,0:T(8,128)(2,1)S(1)}, bf16[8,3584]{1,0:T(8,128)(2,1)S(1)}) custom-call(bf16[2,3584,128]{2,1,0:T(8,128)(2,1)S(1)} %copy-done, bf16[128,3584]{1,0:T(8,128)(2,1)S(1)} %copy-done.1, bf16[2,3584,128]{2,1,0:T(8,128)(2,1)S(1)} %collective-permute-done.twin_in_ref, ...), custom_call_target="tpu_custom_call" | custom-call | flops 176160768 | bytes 5963776 | tf_op jit(solution)/shard_map/pallas_call | solution.py:122
  17.9 0.6 %collective-permute-start.5 = (bf16[8,3584]{1,0:T(8,128)(2,1)S(1)}, bf16[8,3584]{1,0:T(8,128)(2,1)S(1)}, u32[]{:S(2)}, u32[]{:S(2)}) collective-permute-start(bf16[8,3584]{1,0:T(8,128)(2,1)S(1)} %get-tuple-element.18), channel_id=1, source_target_pairs={{0,2},{1,3},{2,0},{3,1},{4,6},{5,7},{6,4},{7,5},{8,10},{9,11},{10,... | collective-permute-start | bytes 172040 | tf_op jit(solution)/shard_map/ppermute | solution.py:136
  18.5 0.2 collective-permute-start.6
  18.7 2.8 %collective-permute-start.7 = (bf16[8,3584]{1,0:T(8,128)(2,1)S(1)}, bf16[8,3584]{1,0:T(8,128)(2,1)S(1)}, u32[]{:S(2)}, u32[]{:S(2)}) collective-permute-start(bf16[8,3584]{1,0:T(8,128)(2,1)S(1)} %get-tuple-element.20), channel_id=1, source_target_pairs={{0,6},{1,7},{2,4},{3,5},{4,2},{5,3},{6,0},{7,1},{8,14},{9,15},{10,... | collective-permute-start | bytes 172040 | tf_op jit(solution)/shard_map/ppermute | solution.py:136
  21.4 0.0 copy-done.4
  21.4 0.0 copy-done.6
  21.4 0.0 copy-done.8
  21.4 0.0 copy-done.10
  21.4 0.0 copy-done.11
  21.4 0.4 %shard_map.82.weight_ref = bf16[32,32]{1,0:T(8,128)(2,1)S(1)} custom-call(s32[1,8]{1,0:T(1,128)S(1)} %bitcast.10, s32[1,8]{1,0:T(1,128)S(1)} %bitcast.12, s32[2,16]{1,0:T(2,128)S(1)} %bitcast.6, s32[2,16]{1,0:T(2,128)S(1)} %bitcast.8, f32[2,16]{1,0:T(2,128)S(1)} %bitcast.13), custom_call_target="tpu_custom_call" | custom-call | bytes 2496 | tf_op jit(solution)/shard_map/pallas_call | solution.py:122
  21.8 0.3 %collective-permute-done.5.refs_1_ = bf16[8,3584]{1,0:T(8,128)(2,1)S(1)} collective-permute-done((bf16[8,3584]{1,0:T(8,128)(2,1)S(1)}, bf16[8,3584]{1,0:T(8,128)(2,1)S(1)}, u32[]{:S(2)}, u32[]{:S(2)}) %collective-permute-start.5) | collective-permute-done | bytes 57376 | tf_op jit(solution)/shard_map/ppermute | solution.py:136
  22.1 0.5 %collective-permute-done.6.refs_2_ = bf16[8,3584]{1,0:T(8,128)(2,1)S(1)} collective-permute-done((bf16[8,3584]{1,0:T(8,128)(2,1)S(1)}, bf16[8,3584]{1,0:T(8,128)(2,1)S(1)}, u32[]{:S(2)}, u32[]{:S(2)}) %collective-permute-start.6) | collective-permute-done | bytes 57376 | tf_op jit(solution)/shard_map/ppermute | solution.py:136
  22.6 1.1 %collective-permute-done.7.refs_3_ = bf16[8,3584]{1,0:T(8,128)(2,1)S(1)} collective-permute-done((bf16[8,3584]{1,0:T(8,128)(2,1)S(1)}, bf16[8,3584]{1,0:T(8,128)(2,1)S(1)}, u32[]{:S(2)}, u32[]{:S(2)}) %collective-permute-start.7) | collective-permute-done | bytes 57376 | tf_op jit(solution)/shard_map/ppermute | solution.py:136
  23.7 0.8 %shard_map.85 = bf16[16,3584]{1,0:T(8,128)(2,1)} custom-call(bf16[32,32]{1,0:T(8,128)(2,1)S(1)} %shard_map.82.weight_ref, bf16[8,3584]{1,0:T(8,128)(2,1)S(1)} %get-tuple-element.17.refs_0_, bf16[8,3584]{1,0:T(8,128)(2,1)S(1)} %collective-permute-done.5.refs_1_, bf16[8,3584]{1,0:T(8,128)(2,1)S(1)} %collective-permute-done.6.refs_2_, ...), custom_call_target="tpu_custom_call" | custom-call | flops 7340032 | bytes 346112 | tf_op jit(solution)/shard_map/pallas_call | solution.py:122
Async XLA Ops:
  0.0 14.2 %collective-permute-start = (bf16[2,3584,128]{2,1,0:T(8,128)(2,1)}, bf16[2,3584,128]{2,1,0:T(8,128)(2,1)S(1)}, u32[]{:S(2)}, u32[]{:S(2)}) collective-permute-start(bf16[2,3584,128]{2,1,0:T(8,128)(2,1)} %in_ref.1), channel_id=1, source_target_pairs={{0,1},{1,0},{2,3},{3,2},{4,5},{5,4},{6,7},{7,6},{8,9},{9,8},{10,11... | collective-permute-start | bytes 5505032 | tf_op jit(solution)/shard_map/ppermute | solution.py:136
  0.5 13.7 %collective-permute-start.1 = (bf16[128,3584]{1,0:T(8,128)(2,1)}, bf16[128,3584]{1,0:T(8,128)(2,1)S(1)}, u32[]{:S(2)}, u32[]{:S(2)}) collective-permute-start(bf16[128,3584]{1,0:T(8,128)(2,1)} %down_ref.1), channel_id=1, source_target_pairs={{0,1},{1,0},{2,3},{3,2},{4,5},{5,4},{6,7},{7,6},{8,9},{9,8},{10,11... | collective-permute-start | bytes 2752520 | tf_op jit(solution)/shard_map/ppermute | solution.py:136
  0.5 0.9 %copy-start.2 = (bf16[16,3584]{1,0:T(8,128)(2,1)S(1)}, bf16[16,3584]{1,0:T(8,128)(2,1)}, u32[]{:S(2)}) copy-start(bf16[16,3584]{1,0:T(8,128)(2,1)} %tokens_ref.1) | copy-start | bytes 344068
  1.4 0.7 %copy-start.3 = (s32[16,2]{0,1:T(2,128)S(1)}, s32[16,2]{0,1:T(2,128)}, u32[]{:S(2)}) copy-start(s32[16,2]{0,1:T(2,128)} %param.13) | copy-start | bytes 388
  2.1 0.7 %copy-start.5 = (s32[16,2]{0,1:T(2,128)S(1)}, s32[16,2]{0,1:T(2,128)}, u32[]{:S(2)}) copy-start(s32[16,2]{0,1:T(2,128)} %param.14) | copy-start | bytes 388
  2.8 0.7 %copy-start.7 = (s32[8]{0:T(128)S(1)}, s32[8]{0:T(128)}, u32[]{:S(2)}) copy-start(s32[8]{0:T(128)} %param.12) | copy-start | bytes 100
  3.4 0.7 %copy-start.9 = (s32[8]{0:T(128)S(1)}, s32[8]{0:T(128)}, u32[]{:S(2)}) copy-start(s32[8]{0:T(128)} %param.11) | copy-start | bytes 100
  4.6 5.2 %collective-permute-start.2 = (bf16[8,3584]{1,0:T(8,128)(2,1)S(1)}, bf16[8,3584]{1,0:T(8,128)(2,1)S(1)}, u32[]{:S(2)}, u32[]{:S(2)}) collective-permute-start(bf16[8,3584]{1,0:T(8,128)(2,1)S(1)} %get-tuple-element.14), channel_id=1, source_target_pairs={{0,2},{1,3},{2,0},{3,1},{4,6},{5,7},{6,4},{7,5},{8,10},{9,11},{10,... | collective-permute-start | bytes 172040 | tf_op jit(solution)/shard_map/ppermute | solution.py:136
  7.6 4.2 %collective-permute-start.3 = (bf16[8,3584]{1,0:T(8,128)(2,1)S(1)}, bf16[8,3584]{1,0:T(8,128)(2,1)S(1)}, u32[]{:S(2)}, u32[]{:S(2)}) collective-permute-start(bf16[8,3584]{1,0:T(8,128)(2,1)S(1)} %get-tuple-element.15), channel_id=1, source_target_pairs={{0,4},{1,5},{2,6},{3,7},{4,0},{5,1},{6,2},{7,3},{8,12},{9,13},{10,... | collective-permute-start | bytes 172040 | tf_op jit(solution)/shard_map/ppermute | solution.py:136
  9.1 5.1 %collective-permute-start.4 = (bf16[8,3584]{1,0:T(8,128)(2,1)S(1)}, bf16[8,3584]{1,0:T(8,128)(2,1)S(1)}, u32[]{:S(2)}, u32[]{:S(2)}) collective-permute-start(bf16[8,3584]{1,0:T(8,128)(2,1)S(1)} %get-tuple-element.16), channel_id=1, source_target_pairs={{0,6},{1,7},{2,4},{3,5},{4,2},{5,3},{6,0},{7,1},{8,14},{9,15},{10,... | collective-permute-start | bytes 172040 | tf_op jit(solution)/shard_map/ppermute | solution.py:136
  14.2 1.5 %copy-start = (bf16[2,3584,128]{2,1,0:T(8,128)(2,1)S(1)}, bf16[2,3584,128]{2,1,0:T(8,128)(2,1)}, u32[]{:S(2)}) copy-start(bf16[2,3584,128]{2,1,0:T(8,128)(2,1)} %in_ref.1) | copy-start | bytes 5505028
  15.7 1.2 %copy-start.1 = (bf16[128,3584]{1,0:T(8,128)(2,1)S(1)}, bf16[128,3584]{1,0:T(8,128)(2,1)}, u32[]{:S(2)}) copy-start(bf16[128,3584]{1,0:T(8,128)(2,1)} %down_ref.1) | copy-start | bytes 2752516
  16.8 4.6 %copy-start.4 = (s32[16,2]{0,1:T(2,128)S(1)}, s32[16,2]{0,1:T(2,128)}, u32[]{:S(2)}) copy-start(s32[16,2]{0,1:T(2,128)} %param.13) | copy-start | bytes 388
  16.9 4.6 %copy-start.6 = (s32[16,2]{0,1:T(2,128)S(1)}, s32[16,2]{0,1:T(2,128)}, u32[]{:S(2)}) copy-start(s32[16,2]{0,1:T(2,128)} %param.14) | copy-start | bytes 388
  16.9 4.6 %copy-start.8 = (s32[8]{0:T(128)S(1)}, s32[8]{0:T(128)}, u32[]{:S(2)}) copy-start(s32[8]{0:T(128)} %param.12) | copy-start | bytes 100
  16.9 4.6 %copy-start.10 = (s32[8]{0:T(128)S(1)}, s32[8]{0:T(128)}, u32[]{:S(2)}) copy-start(s32[8]{0:T(128)} %param.11) | copy-start | bytes 100
  16.9 4.6 %copy-start.11 = (f32[16,2]{0,1:T(2,128)S(1)}, f32[16,2]{0,1:T(2,128)}, u32[]{:S(2)}) copy-start(f32[16,2]{0,1:T(2,128)} %param.15) | copy-start | bytes 388
  17.9 4.2 %collective-permute-start.5 = (bf16[8,3584]{1,0:T(8,128)(2,1)S(1)}, bf16[8,3584]{1,0:T(8,128)(2,1)S(1)}, u32[]{:S(2)}, u32[]{:S(2)}) collective-permute-start(bf16[8,3584]{1,0:T(8,128)(2,1)S(1)} %get-tuple-element.18), channel_id=1, source_target_pairs={{0,2},{1,3},{2,0},{3,1},{4,6},{5,7},{6,4},{7,5},{8,10},{9,11},{10,... | collective-permute-start | bytes 172040 | tf_op jit(solution)/shard_map/ppermute | solution.py:136
  18.5 4.2 %collective-permute-start.6 = (bf16[8,3584]{1,0:T(8,128)(2,1)S(1)}, bf16[8,3584]{1,0:T(8,128)(2,1)S(1)}, u32[]{:S(2)}, u32[]{:S(2)}) collective-permute-start(bf16[8,3584]{1,0:T(8,128)(2,1)S(1)} %get-tuple-element.19), channel_id=1, source_target_pairs={{0,4},{1,5},{2,6},{3,7},{4,0},{5,1},{6,2},{7,3},{8,12},{9,13},{10,... | collective-permute-start | bytes 172040 | tf_op jit(solution)/shard_map/ppermute | solution.py:136
  18.7 5.1 %collective-permute-start.7 = (bf16[8,3584]{1,0:T(8,128)(2,1)S(1)}, bf16[8,3584]{1,0:T(8,128)(2,1)S(1)}, u32[]{:S(2)}, u32[]{:S(2)}) collective-permute-start(bf16[8,3584]{1,0:T(8,128)(2,1)S(1)} %get-tuple-element.20), channel_id=1, source_target_pairs={{0,6},{1,7},{2,4},{3,5},{4,2},{5,3},{6,0},{7,1},{8,14},{9,15},{10,... | collective-permute-start | bytes 172040 | tf_op jit(solution)/shard_map/ppermute | solution.py:136

commit v3 on v2

v3 whole, which is shorter than its diff:
```python
import functools

import jax
import jax.numpy as jnp
from jax import lax
from jax.experimental import pallas as pl
from jax.experimental.pallas import tpu as pltpu
from jax.sharding import PartitionSpec as P

SLOTS = 8
CAP = 4
CHIP_STEPS = ((0, 3, 1, 2), (0, 3, 2, 1))

VMEM = pl.BlockSpec(memory_space=pltpu.VMEM)
HBM = pl.BlockSpec(memory_space=pltpu.HBM)


def targets(shards, new, old, ids, replica):
    slots, rows = new.shape[1], ids.shape[1]
    device = lax.axis_index("expert")
    down = lax.broadcasted_iota(jnp.int32, (slots, slots), 0)
    across = lax.broadcasted_iota(jnp.int32, (slots, slots), 1)
    new_full = jnp.broadcast_to(new, (slots, slots)).astype(jnp.float32)
    away = jnp.where(new == old, across, across ^ 1) ^ (device // shards)
    if shards == 1:
        odd = device & 1
        chip = away >> 1
        step = sum(
            jnp.where(chip == jnp.where(odd == 1, c_odd, c_even), k, 0)
            for k, (c_even, c_odd) in enumerate(zip(*CHIP_STEPS))
        )
        away = (away & 1) | (step << 1)
    base = (CAP * away).astype(jnp.float32)
    diagonal = down == across
    mine = jnp.sum(jnp.where(diagonal, new_full, 0.0), axis=1, keepdims=True)
    line = jnp.sum(jnp.where(diagonal, base, 0.0), axis=1, keepdims=True)
    same = jnp.where(mine == new_full, 1.0, 0.0)
    count = jnp.sum(same, axis=1, keepdims=True).astype(jnp.int32)
    rank = jnp.sum(jnp.where(across < down, same, 0.0), axis=1, keepdims=True).astype(jnp.int32)
    expert = mine.astype(jnp.int32)
    chosen = []
    for k in range(ids.shape[0]):
        wanted = replica[k : k + 1] & (count - 1)
        hit = (ids[k : k + 1] == expert) & (rank == wanted)
        chosen.append(jnp.where(hit, 1.0, 0.0))
    earlier = lax.broadcasted_iota(jnp.int32, (rows, rows), 0) < lax.broadcasted_iota(
        jnp.int32, (rows, rows), 1
    )
    any_choice = functools.reduce(jnp.add, chosen)
    position = jnp.dot(
        any_choice.astype(jnp.bfloat16),
        jnp.where(earlier, 1.0, 0.0).astype(jnp.bfloat16),
        preferred_element_type=jnp.float32,
    )
    found = []
    for hit in chosen:
        place = jnp.where(position < CAP, line + position + 1.0, 0.0)
        found.append((jnp.sum(hit * place, axis=0, keepdims=True) - 1.0).astype(jnp.int32))
        position = position + hit
    return found


def start_copies(sources, buffers, sems):
    copies = [pltpu.make_async_copy(*pair, sems.at[i]) for i, pair in enumerate(zip(sources, buffers))]
    for copy in copies:
        copy.start()
    return copies


def dispatch_kernel(shards, *refs):
    sources, refs = refs[:5], refs[5:]
    found_ref, *block_refs = refs[:-6]
    buffers, sems = refs[-6:-1], refs[-1]
    copies = start_copies(sources, buffers, sems)
    for copy in copies[:-1]:
        copy.wait()
    found = targets(shards, *[ref[...] for ref in buffers[:-1]])
    found_ref[...] = jnp.concatenate(found, axis=0)
    tokens_ref = buffers[-1]
    size = block_refs[0].shape[0]
    line = lax.broadcasted_iota(jnp.int32, (size * len(block_refs), tokens_ref.shape[0]), 0)
    picked = functools.reduce(jnp.logical_or, [line == target for target in found])
    selector = jnp.where(picked, 1.0, 0.0).astype(jnp.bfloat16)
    copies[-1].wait()
    buffer = jnp.dot(selector, tokens_ref[...], preferred_element_type=jnp.float32)
    for b, block_ref in enumerate(block_refs):
        block_ref[...] = buffer[size * b : size * (b + 1)].astype(jnp.bfloat16)


def prepare_kernel(
    found_ref, combine_hbm, in_hbm, down_hbm, in_ref, down_ref, weight_ref, combine_ref, sems
):
    copies = start_copies(
        (combine_hbm, in_hbm, down_hbm), (combine_ref, in_ref, down_ref), sems
    )
    copies[0].wait()
    line = lax.broadcasted_iota(jnp.int32, (weight_ref.shape[1], combine_ref.shape[1]), 0)
    weight = functools.reduce(
        jnp.add,
        [
            jnp.where(line == found_ref[k : k + 1], combine_ref[k : k + 1], 0.0)
            for k in range(found_ref.shape[0])
        ],
    ).T
    high = weight.astype(jnp.bfloat16)
    low = (weight - high.astype(jnp.float32)).astype(jnp.bfloat16)
    weight_ref[...] = jnp.concatenate([high, low], axis=0)
    for copy in copies[1:]:
        copy.wait()


def stack(refs):
    return jnp.concatenate([ref[...].astype(jnp.float32) for ref in refs], axis=0)


def expert_kernel(split, in_ref, down_ref, twin_in_ref, twin_down_ref, *refs):
    count = len(refs) // 2
    rows = stack(refs[:count]).astype(jnp.bfloat16)
    size = refs[0].shape[0]
    hidden = []
    for half, ref in enumerate((in_ref, twin_in_ref)):
        gate = jnp.dot(rows, ref[0], preferred_element_type=jnp.float32)
        up = jnp.dot(rows, ref[1], preferred_element_type=jnp.float32)
        value = jax.nn.silu(gate) * up
        if split:
            place = lax.broadcasted_iota(jnp.int32, value.shape, 0) & (size - 1)
            value = jnp.where((place >= size // 2) == bool(half), value, 0.0)
        hidden.append(value.astype(jnp.bfloat16))
    piece = jnp.dot(
        jnp.concatenate(hidden, axis=1),
        jnp.concatenate([down_ref[...], twin_down_ref[...]], axis=0),
        preferred_element_type=jnp.float32,
    )
    for b, out_ref in enumerate(refs[count:]):
        out_ref[...] = piece[size * b : size * (b + 1)].astype(jnp.bfloat16)


def mix_kernel(repeats, weight_ref, *refs):
    out_hbm, out_ref, sems = refs[-3:]
    refs = refs[:-3]
    rows, width = out_ref.shape
    parts = sems.shape[0]
    step = width // parts
    copies = []
    for part in range(parts):
        columns = slice(part * step, (part + 1) * step)
        total = functools.reduce(
            jnp.add,
            [stack([ref.at[:, columns] for ref in refs[j::repeats]]) for j in range(repeats)],
        )
        high = total.astype(jnp.bfloat16)
        mixed = jnp.dot(weight_ref[...], high, preferred_element_type=jnp.float32)
        if repeats > 1:
            low = (total - high.astype(jnp.float32)).astype(jnp.bfloat16)
            mixed += jnp.dot(weight_ref[...], low, preferred_element_type=jnp.float32)
        out_ref[:, columns] = (mixed[:rows] + mixed[rows:]).astype(jnp.bfloat16)
        copies.append(
            pltpu.make_async_copy(out_ref.at[:, columns], out_hbm.at[:, columns], sems.at[part])
        )
        copies[-1].start()
    for copy in copies:
        copy.wait()


def call(kernel, outs, args, flops, arg_specs=None, out_specs=None, scratch=()):
    arg_specs = arg_specs or [VMEM] * len(args)
    nbytes = sum(x.size * x.dtype.itemsize for x in jax.tree.leaves((outs, args)))
    return pl.pallas_call(
        kernel,
        out_shape=outs,
        in_specs=arg_specs,
        out_specs=out_specs or jax.tree.map(lambda _: VMEM, outs),
        scratch_shapes=scratch,
        compiler_params=pltpu.CompilerParams(vmem_limit_bytes=16 << 20),
        cost_estimate=pl.CostEstimate(flops=flops, bytes_accessed=nbytes, transcendentals=0),
    )(*[pltpu.with_memory_space_constraint(x, s.memory_space) for x, s in zip(args, arg_specs)])


def shape_of(array):
    return jax.ShapeDtypeStruct(array.shape, array.dtype)


def scratch_for(*arrays):
    return [pltpu.VMEM(x.shape, x.dtype) for x in arrays] + [pltpu.SemaphoreType.DMA((len(arrays),))]


def swap(block, distance, odd_distance=None):
    if distance == 0:
        return block
    apart = (distance, distance if odd_distance is None else odd_distance)
    pairs = [(i, i ^ apart[i & 1]) for i in range(lax.axis_size("expert"))]
    return lax.ppermute(block, "expert", pairs)


def exchange(blocks, split):
    even, odd = CHIP_STEPS if split else (range(len(blocks)),) * 2
    return [swap(block, 2 * even[k], 2 * odd[k]) for k, block in enumerate(blocks)]


def body(tokens, w_in, w_down, old_place, new_place, expert_ids, replica, combine):
    devices = lax.axis_size("expert")
    shards = devices // SLOTS
    split = shards == 1
    repeats = max(shards // 2, 1)
    chips = devices // 2
    rows, width = tokens.shape
    hidden = w_down.shape[0]
    twin_in, twin_down = swap(w_in, 1), swap(w_down, 1)
    operands = (new_place[None], old_place[None], expert_ids.T, replica.T, tokens)
    combine = combine.T
    block = jax.ShapeDtypeStruct((CAP * (2 if split else 1), width), jnp.bfloat16)
    found, *blocks = call(
        functools.partial(dispatch_kernel, shards),
        [shape_of(operands[2])] + [block] * (chips // repeats),
        operands,
        2 * SLOTS * CAP * rows * width,
        [HBM] * len(operands),
        scratch=scratch_for(*operands),
    )
    received = exchange([blocks[c // repeats] for c in range(chips)], split)
    own_in, own_down, weight = call(
        prepare_kernel,
        [
            shape_of(w_in),
            shape_of(w_down),
            jax.ShapeDtypeStruct((2 * rows, SLOTS * CAP), jnp.bfloat16),
        ],
        (found, combine, w_in, w_down),
        0,
        [VMEM, HBM, HBM, HBM],
        scratch=[pltpu.VMEM(combine.shape, combine.dtype), pltpu.SemaphoreType.DMA((3,))],
    )
    pieces = call(
        functools.partial(expert_kernel, split),
        [block] * chips,
        (own_in, own_down, twin_in, twin_down, *received),
        12 * chips * block.shape[0] * hidden * width,
    )
    returned = exchange(pieces, split)
    parts = 4 if width % 512 == 0 else 1
    return call(
        functools.partial(mix_kernel, repeats),
        shape_of(tokens),
        (weight, *returned),
        4 * SLOTS * CAP * rows * width,
        out_specs=HBM,
        scratch=[pltpu.VMEM(tokens.shape, tokens.dtype), pltpu.SemaphoreType.DMA((parts,))],
    )


def solution(mesh):
    placed = (
        P(("group", "expert"), None),
        P(None, None, ("group", "expert")),
        P(("group", "expert"), None),
        P("group"),
        P("group"),
        P(("group", "expert"), None),
        P(("group", "expert"), None),
        P(("group", "expert"), None),
    )
    return jax.shard_map(
        body, mesh=mesh, in_specs=placed, out_specs=P(("group", "expert"), None), check_vma=False
    )
```

time: 24.8 us -> 18.7 us (0.75)
  local copies, waits for them, and re-layouts: 6.26 us -> 0 us
  Pallas kernels: 2.69 us -> 4.87 us
  waiting for transfers between devices: 6.99 us -> 5.02 us
    unnamed x24 -> x0, local copies, waits for them, and re-layouts: 6.26 us -> none
    pallas_call x4, Pallas kernels: 2.69 us -> 4.87 us  [call(): pl.pallas_call(kernel, out_shape=outs, in_specs=arg_specs, out_specs=out_...]
    ppermute x8, waiting for transfers between devices: 6.99 us -> 5.02 us  [swap(): return lax.ppermute(block, 'expert', pairs)]
  transfers between devices with their start and end apart: 8 -> 8, of which waited for: 6 -> 5; matrix products, arithmetic and copies ran while one was open for 0% -> 0% of each run, Pallas kernels for 3% -> 16%
where the time goes in v3:
time: 18.7 us; the launch traced here: 18.6 us
  starting transfers between devices  8.65 us (46%)
  waiting for transfers between devices  5.02 us (27%)
  Pallas kernels  4.87 us (26%)
    ppermute x8, starting transfers between devices, swap(): return lax.ppermute(block, 'expert', pairs)  8.65 us
    ppermute x8, waiting for transfers between devices, swap(): return lax.ppermute(block, 'expert', pairs)  5.02 us
    pallas_call x4, Pallas kernels, call(): pl.pallas_call(kernel, out_shape=outs, in_specs=arg_specs, out_specs=out_...  4.87 us
  transfers between devices with their start and end apart: 8, of which 5 were waited for; matrix products, arithmetic and copies ran while one was open for 0% of the time, Pallas kernels for 16%

profile of v3, /device:TPU:0, one launch (start us, length us, event | category | flops | bytes accessed | tf_op | source)
XLA Modules:
  0.0 18.6 jit_solution(13847140050691422704)
XLA Ops:
  0.0 0.5 %collective-permute-start = (bf16[2,3584,128]{2,1,0:T(8,128)(2,1)}, bf16[2,3584,128]{2,1,0:T(8,128)(2,1)S(1)}, u32[]{:S(2)}, u32[]{:S(2)}) collective-permute-start(bf16[2,3584,128]{2,1,0:T(8,128)(2,1)} %in_hbm.1), channel_id=1, source_target_pairs={{0,1},{1,0},{2,3},{3,2},{4,5},{5,4},{6,7},{7,6},{8,9},{9,8},{10,11... | collective-permute-start | bytes 5505032 | tf_op jit(solution)/shard_map/ppermute | solution.py:192
  0.5 0.1 collective-permute-start.1
  0.5 1.2 %shard_map.82 = (s32[2,16]{1,0:T(2,128)S(1)}, bf16[8,3584]{1,0:T(8,128)(2,1)S(1)}, bf16[8,3584]{1,0:T(8,128)(2,1)S(1)}, bf16[8,3584]{1,0:T(8,128)(2,1)S(1)}, bf16[8,3584]{1,0:T(8,128)(2,1)S(1)}) custom-call(s32[1,8]{1,0:T(1,128)} %bitcast.8, s32[1,8]{1,0:T(1,128)} %bitcast.9, s32[2,16]{1,0:T(2,128)} %bitcast.5, s32[2,16]{1,0:T(2,128)} %bitcast.6, ...), custom_call_target="tpu_custom_call" | custom-call | flops 3670016 | bytes 344512 | tf_op jit(solution)/shard_map/pallas_call | solution.py:168
  1.8 4.0 %collective-permute-start.2 = (bf16[8,3584]{1,0:T(8,128)(2,1)S(1)}, bf16[8,3584]{1,0:T(8,128)(2,1)S(1)}, u32[]{:S(2)}, u32[]{:S(2)}) collective-permute-start(bf16[8,3584]{1,0:T(8,128)(2,1)S(1)} %get-tuple-element.22), channel_id=1, source_target_pairs={{0,6},{1,7},{2,4},{3,5},{4,2},{5,3},{6,0},{7,1},{8,14},{9,15},{10,... | collective-permute-start | bytes 172040 | tf_op jit(solution)/shard_map/ppermute | solution.py:192
  5.7 0.5 %collective-permute-start.3 = (bf16[8,3584]{1,0:T(8,128)(2,1)S(1)}, bf16[8,3584]{1,0:T(8,128)(2,1)S(1)}, u32[]{:S(2)}, u32[]{:S(2)}) collective-permute-start(bf16[8,3584]{1,0:T(8,128)(2,1)S(1)} %get-tuple-element.23), channel_id=1, source_target_pairs={{0,2},{1,5},{2,0},{3,7},{4,6},{5,1},{6,4},{7,3},{8,10},{9,13},{10,... | collective-permute-start | bytes 172040 | tf_op jit(solution)/shard_map/ppermute | solution.py:192
  6.3 0.1 collective-permute-start.4
  6.4 1.8 %shard_map.83 = (bf16[2,3584,128]{2,1,0:T(8,128)(2,1)S(1)}, bf16[128,3584]{1,0:T(8,128)(2,1)S(1)}, bf16[32,32]{1,0:T(8,128)(2,1)S(1)}) custom-call(s32[2,16]{1,0:T(2,128)S(1)} %get-tuple-element.17.found_ref, f32[2,16]{1,0:T(2,128)} %bitcast.7, bf16[2,3584,128]{2,1,0:T(8,128)(2,1)} %in_hbm.1, bf16[128,3584]{1,0:T(8,128)(2,1)} %down_hbm.1), custom_call_target="tpu_custom_call" | custom-call | bytes 5507328 | tf_op jit(solution)/shard_map/pallas_call | solution.py:168
  8.2 0.0 collective-permute-done.2.refs_1_
  8.2 1.7 %collective-permute-done.3.refs_2_ = bf16[8,3584]{1,0:T(8,128)(2,1)S(1)} collective-permute-done((bf16[8,3584]{1,0:T(8,128)(2,1)S(1)}, bf16[8,3584]{1,0:T(8,128)(2,1)S(1)}, u32[]{:S(2)}, u32[]{:S(2)}) %collective-permute-start.3) | collective-permute-done | bytes 57376 | tf_op jit(solution)/shard_map/ppermute | solution.py:192
  9.9 0.5 %collective-permute-done.4.refs_3_ = bf16[8,3584]{1,0:T(8,128)(2,1)S(1)} collective-permute-done((bf16[8,3584]{1,0:T(8,128)(2,1)S(1)}, bf16[8,3584]{1,0:T(8,128)(2,1)S(1)}, u32[]{:S(2)}, u32[]{:S(2)}) %collective-permute-start.4) | collective-permute-done | bytes 57376 | tf_op jit(solution)/shard_map/ppermute | solution.py:192
  10.4 0.0 collective-permute-done.1.twin_down_ref
  10.4 0.0 collective-permute-done.twin_in_ref
  10.4 1.0 %shard_map.84 = (bf16[8,3584]{1,0:T(8,128)(2,1)S(1)}, bf16[8,3584]{1,0:T(8,128)(2,1)S(1)}, bf16[8,3584]{1,0:T(8,128)(2,1)S(1)}, bf16[8,3584]{1,0:T(8,128)(2,1)S(1)}) custom-call(bf16[2,3584,128]{2,1,0:T(8,128)(2,1)S(1)} %get-tuple-element.19.in_ref, bf16[128,3584]{1,0:T(8,128)(2,1)S(1)} %get-tuple-element.20.down_ref, ...), custom_call_target="tpu_custom_call" | custom-call | flops 176160768 | bytes 5963776 | tf_op jit(solution)/shard_map/pallas_call | solution.py:168
  11.5 1.5 %collective-permute-start.5 = (bf16[8,3584]{1,0:T(8,128)(2,1)S(1)}, bf16[8,3584]{1,0:T(8,128)(2,1)S(1)}, u32[]{:S(2)}, u32[]{:S(2)}) collective-permute-start(bf16[8,3584]{1,0:T(8,128)(2,1)S(1)} %get-tuple-element.26), channel_id=1, source_target_pairs={{0,6},{1,7},{2,4},{3,5},{4,2},{5,3},{6,0},{7,1},{8,14},{9,15},{10,... | collective-permute-start | bytes 172040 | tf_op jit(solution)/shard_map/ppermute | solution.py:192
  12.9 0.6 %collective-permute-start.6 = (bf16[8,3584]{1,0:T(8,128)(2,1)S(1)}, bf16[8,3584]{1,0:T(8,128)(2,1)S(1)}, u32[]{:S(2)}, u32[]{:S(2)}) collective-permute-start(bf16[8,3584]{1,0:T(8,128)(2,1)S(1)} %get-tuple-element.27), channel_id=1, source_target_pairs={{0,2},{1,5},{2,0},{3,7},{4,6},{5,1},{6,4},{7,3},{8,10},{9,13},{10,... | collective-permute-start | bytes 172040 | tf_op jit(solution)/shard_map/ppermute | solution.py:192
  13.6 1.4 %collective-permute-start.7 = (bf16[8,3584]{1,0:T(8,128)(2,1)S(1)}, bf16[8,3584]{1,0:T(8,128)(2,1)S(1)}, u32[]{:S(2)}, u32[]{:S(2)}) collective-permute-start(bf16[8,3584]{1,0:T(8,128)(2,1)S(1)} %get-tuple-element.28), channel_id=1, source_target_pairs={{0,4},{1,3},{2,6},{3,1},{4,0},{5,7},{6,2},{7,5},{8,12},{9,11},{10,... | collective-permute-start | bytes 172040 | tf_op jit(solution)/shard_map/ppermute | solution.py:192
  15.0 1.8 %collective-permute-done.5.refs_1_ = bf16[8,3584]{1,0:T(8,128)(2,1)S(1)} collective-permute-done((bf16[8,3584]{1,0:T(8,128)(2,1)S(1)}, bf16[8,3584]{1,0:T(8,128)(2,1)S(1)}, u32[]{:S(2)}, u32[]{:S(2)}) %collective-permute-start.5) | collective-permute-done | bytes 57376 | tf_op jit(solution)/shard_map/ppermute | solution.py:192
  16.8 0.3 %collective-permute-done.6.refs_2_ = bf16[8,3584]{1,0:T(8,128)(2,1)S(1)} collective-permute-done((bf16[8,3584]{1,0:T(8,128)(2,1)S(1)}, bf16[8,3584]{1,0:T(8,128)(2,1)S(1)}, u32[]{:S(2)}, u32[]{:S(2)}) %collective-permute-start.6) | collective-permute-done | bytes 57376 | tf_op jit(solution)/shard_map/ppermute | solution.py:192
  17.1 0.6 %collective-permute-done.7.refs_3_ = bf16[8,3584]{1,0:T(8,128)(2,1)S(1)} collective-permute-done((bf16[8,3584]{1,0:T(8,128)(2,1)S(1)}, bf16[8,3584]{1,0:T(8,128)(2,1)S(1)}, u32[]{:S(2)}, u32[]{:S(2)}) %collective-permute-start.7) | collective-permute-done | bytes 57376 | tf_op jit(solution)/shard_map/ppermute | solution.py:192
  17.7 0.8 %shard_map.85 = bf16[16,3584]{1,0:T(8,128)(2,1)} custom-call(bf16[32,32]{1,0:T(8,128)(2,1)S(1)} %get-tuple-element.18.weight_ref, bf16[8,3584]{1,0:T(8,128)(2,1)S(1)} %get-tuple-element.25.refs_0_, bf16[8,3584]{1,0:T(8,128)(2,1)S(1)} %collective-permute-done.5.refs_1_, bf16[8,3584]{1,0:T(8,128)(2,1)S(1)} %collective-permute-done.6.refs_2_, ...), custom_call_target="tpu_custom_call" | custom-call | flops 7340032 | bytes 346112 | tf_op jit(solution)/shard_map/pallas_call | solution.py:168
Async XLA Ops:
  0.0 10.4 %collective-permute-start = (bf16[2,3584,128]{2,1,0:T(8,128)(2,1)}, bf16[2,3584,128]{2,1,0:T(8,128)(2,1)S(1)}, u32[]{:S(2)}, u32[]{:S(2)}) collective-permute-start(bf16[2,3584,128]{2,1,0:T(8,128)(2,1)} %in_hbm.1), channel_id=1, source_target_pairs={{0,1},{1,0},{2,3},{3,2},{4,5},{5,4},{6,7},{7,6},{8,9},{9,8},{10,11... | collective-permute-start | bytes 5505032 | tf_op jit(solution)/shard_map/ppermute | solution.py:192
  0.5 10.0 %collective-permute-start.1 = (bf16[128,3584]{1,0:T(8,128)(2,1)}, bf16[128,3584]{1,0:T(8,128)(2,1)S(1)}, u32[]{:S(2)}, u32[]{:S(2)}) collective-permute-start(bf16[128,3584]{1,0:T(8,128)(2,1)} %down_hbm.1), channel_id=1, source_target_pairs={{0,1},{1,0},{2,3},{3,2},{4,5},{5,4},{6,7},{7,6},{8,9},{9,8},{10,11... | collective-permute-start | bytes 2752520 | tf_op jit(solution)/shard_map/ppermute | solution.py:192
  1.8 6.4 %collective-permute-start.2 = (bf16[8,3584]{1,0:T(8,128)(2,1)S(1)}, bf16[8,3584]{1,0:T(8,128)(2,1)S(1)}, u32[]{:S(2)}, u32[]{:S(2)}) collective-permute-start(bf16[8,3584]{1,0:T(8,128)(2,1)S(1)} %get-tuple-element.22), channel_id=1, source_target_pairs={{0,6},{1,7},{2,4},{3,5},{4,2},{5,3},{6,0},{7,1},{8,14},{9,15},{10,... | collective-permute-start | bytes 172040 | tf_op jit(solution)/shard_map/ppermute | solution.py:192
  5.7 4.2 %collective-permute-start.3 = (bf16[8,3584]{1,0:T(8,128)(2,1)S(1)}, bf16[8,3584]{1,0:T(8,128)(2,1)S(1)}, u32[]{:S(2)}, u32[]{:S(2)}) collective-permute-start(bf16[8,3584]{1,0:T(8,128)(2,1)S(1)} %get-tuple-element.23), channel_id=1, source_target_pairs={{0,2},{1,5},{2,0},{3,7},{4,6},{5,1},{6,4},{7,3},{8,10},{9,13},{10,... | collective-permute-start | bytes 172040 | tf_op jit(solution)/shard_map/ppermute | solution.py:192
  6.3 4.2 %collective-permute-start.4 = (bf16[8,3584]{1,0:T(8,128)(2,1)S(1)}, bf16[8,3584]{1,0:T(8,128)(2,1)S(1)}, u32[]{:S(2)}, u32[]{:S(2)}) collective-permute-start(bf16[8,3584]{1,0:T(8,128)(2,1)S(1)} %get-tuple-element.24), channel_id=1, source_target_pairs={{0,4},{1,3},{2,6},{3,1},{4,0},{5,7},{6,2},{7,5},{8,12},{9,11},{10,... | collective-permute-start | bytes 172040 | tf_op jit(solution)/shard_map/ppermute | solution.py:192
  11.5 5.4 %collective-permute-start.5 = (bf16[8,3584]{1,0:T(8,128)(2,1)S(1)}, bf16[8,3584]{1,0:T(8,128)(2,1)S(1)}, u32[]{:S(2)}, u32[]{:S(2)}) collective-permute-start(bf16[8,3584]{1,0:T(8,128)(2,1)S(1)} %get-tuple-element.26), channel_id=1, source_target_pairs={{0,6},{1,7},{2,4},{3,5},{4,2},{5,3},{6,0},{7,1},{8,14},{9,15},{10,... | collective-permute-start | bytes 172040 | tf_op jit(solution)/shard_map/ppermute | solution.py:192
  12.9 4.2 %collective-permute-start.6 = (bf16[8,3584]{1,0:T(8,128)(2,1)S(1)}, bf16[8,3584]{1,0:T(8,128)(2,1)S(1)}, u32[]{:S(2)}, u32[]{:S(2)}) collective-permute-start(bf16[8,3584]{1,0:T(8,128)(2,1)S(1)} %get-tuple-element.27), channel_id=1, source_target_pairs={{0,2},{1,5},{2,0},{3,7},{4,6},{5,1},{6,4},{7,3},{8,10},{9,13},{10,... | collective-permute-start | bytes 172040 | tf_op jit(solution)/shard_map/ppermute | solution.py:192
  13.6 4.2 %collective-permute-start.7 = (bf16[8,3584]{1,0:T(8,128)(2,1)S(1)}, bf16[8,3584]{1,0:T(8,128)(2,1)S(1)}, u32[]{:S(2)}, u32[]{:S(2)}) collective-permute-start(bf16[8,3584]{1,0:T(8,128)(2,1)S(1)} %get-tuple-element.28), channel_id=1, source_target_pairs={{0,4},{1,3},{2,6},{3,1},{4,0},{5,7},{6,2},{7,5},{8,12},{9,11},{10,... | collective-permute-start | bytes 172040 | tf_op jit(solution)/shard_map/ppermute | solution.py:192

commit v4 on v3

--- a/solution.py
+++ b/solution.py
@@ -21,7 +21,8 @@
     down = lax.broadcasted_iota(jnp.int32, (slots, slots), 0)
     across = lax.broadcasted_iota(jnp.int32, (slots, slots), 1)
     new_full = jnp.broadcast_to(new, (slots, slots)).astype(jnp.float32)
-    away = jnp.where(new == old, across, across ^ 1) ^ (device // shards)
+    source = jnp.where(new == old, across, across ^ 1)
+    away = source ^ (device // shards)
     if shards == 1:
         odd = device & 1
         chip = away >> 1
@@ -29,7 +30,7 @@
             jnp.where(chip == jnp.where(odd == 1, c_odd, c_even), k, 0)
             for k, (c_even, c_odd) in enumerate(zip(*CHIP_STEPS))
         )
-        away = (away & 1) | (step << 1)
+        away = (source & 1) | (step << 1)
     base = (CAP * away).astype(jnp.float32)
     diagonal = down == across
     mine = jnp.sum(jnp.where(diagonal, new_full, 0.0), axis=1, keepdims=True)
@@ -114,6 +115,7 @@
 
 
 def expert_kernel(split, in_ref, down_ref, twin_in_ref, twin_down_ref, *refs):
+    odd = lax.axis_index("expert") & 1
     count = len(refs) // 2
     rows = stack(refs[:count]).astype(jnp.bfloat16)
     size = refs[0].shape[0]
@@ -123,8 +125,8 @@
         up = jnp.dot(rows, ref[1], preferred_element_type=jnp.float32)
         value = jax.nn.silu(gate) * up
         if split:
-            place = lax.broadcasted_iota(jnp.int32, value.shape, 0) & (size - 1)
-            value = jnp.where((place >= size // 2) == bool(half), value, 0.0)
+            place = lax.broadcasted_iota(jnp.int32, value.shape, 0) // (size // 2)
+            value = jnp.where((place & 1) == (odd ^ half), value, 0.0)
         hidden.append(value.astype(jnp.bfloat16))
     piece = jnp.dot(
         jnp.concatenate(hidden, axis=1),
@@ -184,17 +186,23 @@
     return [pltpu.VMEM(x.shape, x.dtype) for x in arrays] + [pltpu.SemaphoreType.DMA((len(arrays),))]
 
 
-def swap(block, distance, odd_distance=None):
-    if distance == 0:
-        return block
-    apart = (distance, distance if odd_distance is None else odd_distance)
-    pairs = [(i, i ^ apart[i & 1]) for i in range(lax.axis_size("expert"))]
-    return lax.ppermute(block, "expert", pairs)
-
-
-def exchange(blocks, split):
-    even, odd = CHIP_STEPS if split else (range(len(blocks)),) * 2
-    return [swap(block, 2 * even[k], 2 * odd[k]) for k, block in enumerate(blocks)]
+def exchange(blocks, split, back=False):
+    devices = lax.axis_size("expert")
+    result = list(blocks)
+    for k in range(1, len(blocks)):
+        if split:
+            pairs = [(i, i ^ 1 ^ 2 * CHIP_STEPS[i & 1][k]) for i in range(devices)]
+        else:
+            pairs = [(i, i ^ 2 * k) for i in range(devices)]
+        if back:
+            pairs = [(target, source) for source, target in pairs]
+        result[k] = lax.ppermute(blocks[k], "expert", pairs)
+    return result
+
+
+def from_twin(array):
+    pairs = [(i, i ^ 1) for i in range(lax.axis_size("expert"))]
+    return lax.ppermute(array, "expert", pairs)
 
 
 def body(tokens, w_in, w_down, old_place, new_place, expert_ids, replica, combine):
@@ -205,7 +213,7 @@
     chips = devices // 2
     rows, width = tokens.shape
     hidden = w_down.shape[0]
-    twin_in, twin_down = swap(w_in, 1), swap(w_down, 1)
+    twin_in, twin_down = from_twin(w_in), from_twin(w_down)
     operands = (new_place[None], old_place[None], expert_ids.T, replica.T, tokens)
     combine = combine.T
     block = jax.ShapeDtypeStruct((CAP * (2 if split else 1), width), jnp.bfloat16)
@@ -236,7 +244,7 @@
         (own_in, own_down, twin_in, twin_down, *received),
         12 * chips * block.shape[0] * hidden * width,
     )
-    returned = exchange(pieces, split)
+    returned = exchange(pieces, split, back=True)
     parts = 4 if width % 512 == 0 else 1
     return call(
         functools.partial(mix_kernel, repeats),

time: 18.7 us -> 18.6 us (level)
  starting transfers between devices: 8.65 us -> 8.36 us
    ppermute x8, starting transfers between devices: 8.65 us -> 8.36 us  [the longest x6 7.85 us: exchange(): result[k] = lax.ppermute(blocks[k], 'expert', pairs)]
  transfers between devices with their start and end apart: 8 -> 8, of which waited for: 5 -> 4; matrix products, arithmetic and copies ran while one was open for 0% -> 0% of each run, Pallas kernels for 16% -> 16%
where the time goes in v4:
time: 18.6 us; the launch traced here: 18.4 us
  starting transfers between devices  8.36 us (45%)
  waiting for transfers between devices  5.14 us (28%)
  Pallas kernels  4.87 us (26%)
    ppermute x6, starting transfers between devices, exchange(): result[k] = lax.ppermute(blocks[k], 'expert', pairs)  7.85 us
    ppermute x6, waiting for transfers between devices, exchange(): result[k] = lax.ppermute(blocks[k], 'expert', pairs)  5.14 us
    pallas_call x4, Pallas kernels, call(): pl.pallas_call(kernel, out_shape=outs, in_specs=arg_specs, out_specs=out_...  4.87 us
    ppermute x2, starting transfers between devices, from_twin(): return lax.ppermute(array, 'expert', pairs)  0.51 us
  transfers between devices with their start and end apart: 8, of which 4 were waited for; matrix products, arithmetic and copies ran while one was open for 0% of the time, Pallas kernels for 16%

profile of v4, /device:TPU:0, one launch (start us, length us, event | category | flops | bytes accessed | tf_op | source)
XLA Modules:
  0.0 18.4 jit_solution(17619285719724270246)
XLA Ops:
  0.0 0.5 %collective-permute-start = (bf16[2,3584,128]{2,1,0:T(8,128)(2,1)}, bf16[2,3584,128]{2,1,0:T(8,128)(2,1)S(1)}, u32[]{:S(2)}, u32[]{:S(2)}) collective-permute-start(bf16[2,3584,128]{2,1,0:T(8,128)(2,1)} %in_hbm.1), channel_id=1, source_target_pairs={{0,1},{1,0},{2,3},{3,2},{4,5},{5,4},{6,7},{7,6},{8,9},{9,8},{10,11... | collective-permute-start | bytes 5505032 | tf_op jit(solution)/shard_map/ppermute | solution.py:205
  0.5 0.1 collective-permute-start.1
  0.5 1.2 %shard_map.82 = (s32[2,16]{1,0:T(2,128)S(1)}, bf16[8,3584]{1,0:T(8,128)(2,1)S(1)}, bf16[8,3584]{1,0:T(8,128)(2,1)S(1)}, bf16[8,3584]{1,0:T(8,128)(2,1)S(1)}, bf16[8,3584]{1,0:T(8,128)(2,1)S(1)}) custom-call(s32[1,8]{1,0:T(1,128)} %bitcast.8, s32[1,8]{1,0:T(1,128)} %bitcast.9, s32[2,16]{1,0:T(2,128)} %bitcast.5, s32[2,16]{1,0:T(2,128)} %bitcast.6, ...), custom_call_target="tpu_custom_call" | custom-call | flops 3670016 | bytes 344512 | tf_op jit(solution)/shard_map/pallas_call | solution.py:170
  1.8 3.6 %collective-permute-start.2 = (bf16[8,3584]{1,0:T(8,128)(2,1)S(1)}, bf16[8,3584]{1,0:T(8,128)(2,1)S(1)}, u32[]{:S(2)}, u32[]{:S(2)}) collective-permute-start(bf16[8,3584]{1,0:T(8,128)(2,1)S(1)} %get-tuple-element.22), channel_id=1, source_target_pairs={{0,7},{1,6},{2,5},{3,4},{4,3},{5,2},{6,1},{7,0},{8,15},{9,14},{10,... | collective-permute-start | bytes 172040 | tf_op jit(solution)/shard_map/ppermute | solution.py:199
  5.3 0.6 %collective-permute-start.3 = (bf16[8,3584]{1,0:T(8,128)(2,1)S(1)}, bf16[8,3584]{1,0:T(8,128)(2,1)S(1)}, u32[]{:S(2)}, u32[]{:S(2)}) collective-permute-start(bf16[8,3584]{1,0:T(8,128)(2,1)S(1)} %get-tuple-element.23), channel_id=1, source_target_pairs={{0,3},{1,4},{2,1},{3,6},{4,7},{5,0},{6,5},{7,2},{8,11},{9,12},{10,... | collective-permute-start | bytes 172040 | tf_op jit(solution)/shard_map/ppermute | solution.py:199
  6.0 1.1 %collective-permute-start.4 = (bf16[8,3584]{1,0:T(8,128)(2,1)S(1)}, bf16[8,3584]{1,0:T(8,128)(2,1)S(1)}, u32[]{:S(2)}, u32[]{:S(2)}) collective-permute-start(bf16[8,3584]{1,0:T(8,128)(2,1)S(1)} %get-tuple-element.24), channel_id=1, source_target_pairs={{0,5},{1,2},{2,7},{3,0},{4,1},{5,6},{6,3},{7,4},{8,13},{9,10},{10,... | collective-permute-start | bytes 172040 | tf_op jit(solution)/shard_map/ppermute | solution.py:199
  7.1 1.8 %shard_map.83 = (bf16[2,3584,128]{2,1,0:T(8,128)(2,1)S(1)}, bf16[128,3584]{1,0:T(8,128)(2,1)S(1)}, bf16[32,32]{1,0:T(8,128)(2,1)S(1)}) custom-call(s32[2,16]{1,0:T(2,128)S(1)} %get-tuple-element.17.found_ref, f32[2,16]{1,0:T(2,128)} %bitcast.7, bf16[2,3584,128]{2,1,0:T(8,128)(2,1)} %in_hbm.1, bf16[128,3584]{1,0:T(8,128)(2,1)} %down_hbm.1), custom_call_target="tpu_custom_call" | custom-call | bytes 5507328 | tf_op jit(solution)/shard_map/pallas_call | solution.py:170
  8.9 0.0 collective-permute-done.2.refs_1_
  8.9 0.1 collective-permute-done.3.refs_2_
  8.9 1.2 %collective-permute-done.4.refs_3_ = bf16[8,3584]{1,0:T(8,128)(2,1)S(1)} collective-permute-done((bf16[8,3584]{1,0:T(8,128)(2,1)S(1)}, bf16[8,3584]{1,0:T(8,128)(2,1)S(1)}, u32[]{:S(2)}, u32[]{:S(2)}) %collective-permute-start.4) | collective-permute-done | bytes 57376 | tf_op jit(solution)/shard_map/ppermute | solution.py:199
  10.2 0.0 collective-permute-done.1.twin_down_ref
  10.2 0.0 collective-permute-done.twin_in_ref
  10.2 1.0 %shard_map.84 = (bf16[8,3584]{1,0:T(8,128)(2,1)S(1)}, bf16[8,3584]{1,0:T(8,128)(2,1)S(1)}, bf16[8,3584]{1,0:T(8,128)(2,1)S(1)}, bf16[8,3584]{1,0:T(8,128)(2,1)S(1)}) custom-call(bf16[2,3584,128]{2,1,0:T(8,128)(2,1)S(1)} %get-tuple-element.19.in_ref, bf16[128,3584]{1,0:T(8,128)(2,1)S(1)} %get-tuple-element.20.down_ref, ...), custom_call_target="tpu_custom_call" | custom-call | flops 176160768 | bytes 5963776 | tf_op jit(solution)/shard_map/pallas_call | solution.py:170
  11.2 0.8 %collective-permute-start.5 = (bf16[8,3584]{1,0:T(8,128)(2,1)S(1)}, bf16[8,3584]{1,0:T(8,128)(2,1)S(1)}, u32[]{:S(2)}, u32[]{:S(2)}) collective-permute-start(bf16[8,3584]{1,0:T(8,128)(2,1)S(1)} %get-tuple-element.26), channel_id=1, source_target_pairs={{7,0},{6,1},{5,2},{4,3},{3,4},{2,5},{1,6},{0,7},{15,8},{14,9},{13,... | collective-permute-start | bytes 172040 | tf_op jit(solution)/shard_map/ppermute | solution.py:199
  11.9 1.5 %collective-permute-start.6 = (bf16[8,3584]{1,0:T(8,128)(2,1)S(1)}, bf16[8,3584]{1,0:T(8,128)(2,1)S(1)}, u32[]{:S(2)}, u32[]{:S(2)}) collective-permute-start(bf16[8,3584]{1,0:T(8,128)(2,1)S(1)} %get-tuple-element.27), channel_id=1, source_target_pairs={{3,0},{4,1},{1,2},{6,3},{7,4},{0,5},{5,6},{2,7},{11,8},{12,9},{9,1... | collective-permute-start | bytes 172040 | tf_op jit(solution)/shard_map/ppermute | solution.py:199
  13.4 0.3 %collective-permute-start.7 = (bf16[8,3584]{1,0:T(8,128)(2,1)S(1)}, bf16[8,3584]{1,0:T(8,128)(2,1)S(1)}, u32[]{:S(2)}, u32[]{:S(2)}) collective-permute-start(bf16[8,3584]{1,0:T(8,128)(2,1)S(1)} %get-tuple-element.28), channel_id=1, source_target_pairs={{5,0},{2,1},{7,2},{0,3},{1,4},{6,5},{3,6},{4,7},{13,8},{10,9},{15,... | collective-permute-start | bytes 172040 | tf_op jit(solution)/shard_map/ppermute | solution.py:199
  13.7 2.4 %collective-permute-done.5.refs_1_ = bf16[8,3584]{1,0:T(8,128)(2,1)S(1)} collective-permute-done((bf16[8,3584]{1,0:T(8,128)(2,1)S(1)}, bf16[8,3584]{1,0:T(8,128)(2,1)S(1)}, u32[]{:S(2)}, u32[]{:S(2)}) %collective-permute-start.5) | collective-permute-done | bytes 57376 | tf_op jit(solution)/shard_map/ppermute | solution.py:199
  16.1 0.0 collective-permute-done.6.refs_2_
  16.1 1.5 %collective-permute-done.7.refs_3_ = bf16[8,3584]{1,0:T(8,128)(2,1)S(1)} collective-permute-done((bf16[8,3584]{1,0:T(8,128)(2,1)S(1)}, bf16[8,3584]{1,0:T(8,128)(2,1)S(1)}, u32[]{:S(2)}, u32[]{:S(2)}) %collective-permute-start.7) | collective-permute-done | bytes 57376 | tf_op jit(solution)/shard_map/ppermute | solution.py:199
  17.6 0.8 %shard_map.85 = bf16[16,3584]{1,0:T(8,128)(2,1)} custom-call(bf16[32,32]{1,0:T(8,128)(2,1)S(1)} %get-tuple-element.18.weight_ref, bf16[8,3584]{1,0:T(8,128)(2,1)S(1)} %get-tuple-element.25.refs_0_, bf16[8,3584]{1,0:T(8,128)(2,1)S(1)} %collective-permute-done.5.refs_1_, bf16[8,3584]{1,0:T(8,128)(2,1)S(1)} %collective-permute-done.6.refs_2_, ...), custom_call_target="tpu_custom_call" | custom-call | flops 7340032 | bytes 346112 | tf_op jit(solution)/shard_map/pallas_call | solution.py:170
Async XLA Ops:
  0.0 10.2 %collective-permute-start = (bf16[2,3584,128]{2,1,0:T(8,128)(2,1)}, bf16[2,3584,128]{2,1,0:T(8,128)(2,1)S(1)}, u32[]{:S(2)}, u32[]{:S(2)}) collective-permute-start(bf16[2,3584,128]{2,1,0:T(8,128)(2,1)} %in_hbm.1), channel_id=1, source_target_pairs={{0,1},{1,0},{2,3},{3,2},{4,5},{5,4},{6,7},{7,6},{8,9},{9,8},{10,11... | collective-permute-start | bytes 5505032 | tf_op jit(solution)/shard_map/ppermute | solution.py:205
  0.5 9.7 %collective-permute-start.1 = (bf16[128,3584]{1,0:T(8,128)(2,1)}, bf16[128,3584]{1,0:T(8,128)(2,1)S(1)}, u32[]{:S(2)}, u32[]{:S(2)}) collective-permute-start(bf16[128,3584]{1,0:T(8,128)(2,1)} %down_hbm.1), channel_id=1, source_target_pairs={{0,1},{1,0},{2,3},{3,2},{4,5},{5,4},{6,7},{7,6},{8,9},{9,8},{10,11... | collective-permute-start | bytes 2752520 | tf_op jit(solution)/shard_map/ppermute | solution.py:205
  1.8 7.1 %collective-permute-start.2 = (bf16[8,3584]{1,0:T(8,128)(2,1)S(1)}, bf16[8,3584]{1,0:T(8,128)(2,1)S(1)}, u32[]{:S(2)}, u32[]{:S(2)}) collective-permute-start(bf16[8,3584]{1,0:T(8,128)(2,1)S(1)} %get-tuple-element.22), channel_id=1, source_target_pairs={{0,7},{1,6},{2,5},{3,4},{4,3},{5,2},{6,1},{7,0},{8,15},{9,14},{10,... | collective-permute-start | bytes 172040 | tf_op jit(solution)/shard_map/ppermute | solution.py:199
  5.3 3.6 %collective-permute-start.3 = (bf16[8,3584]{1,0:T(8,128)(2,1)S(1)}, bf16[8,3584]{1,0:T(8,128)(2,1)S(1)}, u32[]{:S(2)}, u32[]{:S(2)}) collective-permute-start(bf16[8,3584]{1,0:T(8,128)(2,1)S(1)} %get-tuple-element.23), channel_id=1, source_target_pairs={{0,3},{1,4},{2,1},{3,6},{4,7},{5,0},{6,5},{7,2},{8,11},{9,12},{10,... | collective-permute-start | bytes 172040 | tf_op jit(solution)/shard_map/ppermute | solution.py:199
  6.0 4.2 %collective-permute-start.4 = (bf16[8,3584]{1,0:T(8,128)(2,1)S(1)}, bf16[8,3584]{1,0:T(8,128)(2,1)S(1)}, u32[]{:S(2)}, u32[]{:S(2)}) collective-permute-start(bf16[8,3584]{1,0:T(8,128)(2,1)S(1)} %get-tuple-element.24), channel_id=1, source_target_pairs={{0,5},{1,2},{2,7},{3,0},{4,1},{5,6},{6,3},{7,4},{8,13},{9,10},{10,... | collective-permute-start | bytes 172040 | tf_op jit(solution)/shard_map/ppermute | solution.py:199
  11.2 4.9 %collective-permute-start.5 = (bf16[8,3584]{1,0:T(8,128)(2,1)S(1)}, bf16[8,3584]{1,0:T(8,128)(2,1)S(1)}, u32[]{:S(2)}, u32[]{:S(2)}) collective-permute-start(bf16[8,3584]{1,0:T(8,128)(2,1)S(1)} %get-tuple-element.26), channel_id=1, source_target_pairs={{7,0},{6,1},{5,2},{4,3},{3,4},{2,5},{1,6},{0,7},{15,8},{14,9},{13,... | collective-permute-start | bytes 172040 | tf_op jit(solution)/shard_map/ppermute | solution.py:199
  11.9 4.1 %collective-permute-start.6 = (bf16[8,3584]{1,0:T(8,128)(2,1)S(1)}, bf16[8,3584]{1,0:T(8,128)(2,1)S(1)}, u32[]{:S(2)}, u32[]{:S(2)}) collective-permute-start(bf16[8,3584]{1,0:T(8,128)(2,1)S(1)} %get-tuple-element.27), channel_id=1, source_target_pairs={{3,0},{4,1},{1,2},{6,3},{7,4},{0,5},{5,6},{2,7},{11,8},{12,9},{9,1... | collective-permute-start | bytes 172040 | tf_op jit(solution)/shard_map/ppermute | solution.py:199
  13.4 4.1 %collective-permute-start.7 = (bf16[8,3584]{1,0:T(8,128)(2,1)S(1)}, bf16[8,3584]{1,0:T(8,128)(2,1)S(1)}, u32[]{:S(2)}, u32[]{:S(2)}) collective-permute-start(bf16[8,3584]{1,0:T(8,128)(2,1)S(1)} %get-tuple-element.28), channel_id=1, source_target_pairs={{5,0},{2,1},{7,2},{0,3},{1,4},{6,5},{3,6},{4,7},{13,8},{10,9},{15,... | collective-permute-start | bytes 172040 | tf_op jit(solution)/shard_map/ppermute | solution.py:199

commit v5 on v4

--- a/solution.py
+++ b/solution.py
@@ -9,29 +9,18 @@
 
 SLOTS = 8
 CAP = 4
-CHIP_STEPS = ((0, 3, 1, 2), (0, 3, 2, 1))
 
 VMEM = pl.BlockSpec(memory_space=pltpu.VMEM)
 HBM = pl.BlockSpec(memory_space=pltpu.HBM)
 
 
-def targets(shards, new, old, ids, replica):
+def targets(new, old, ids, replica):
     slots, rows = new.shape[1], ids.shape[1]
-    device = lax.axis_index("expert")
     down = lax.broadcasted_iota(jnp.int32, (slots, slots), 0)
     across = lax.broadcasted_iota(jnp.int32, (slots, slots), 1)
     new_full = jnp.broadcast_to(new, (slots, slots)).astype(jnp.float32)
     source = jnp.where(new == old, across, across ^ 1)
-    away = source ^ (device // shards)
-    if shards == 1:
-        odd = device & 1
-        chip = away >> 1
-        step = sum(
-            jnp.where(chip == jnp.where(odd == 1, c_odd, c_even), k, 0)
-            for k, (c_even, c_odd) in enumerate(zip(*CHIP_STEPS))
-        )
-        away = (source & 1) | (step << 1)
-    base = (CAP * away).astype(jnp.float32)
+    base = (CAP * source).astype(jnp.float32)
     diagonal = down == across
     mine = jnp.sum(jnp.where(diagonal, new_full, 0.0), axis=1, keepdims=True)
     line = jnp.sum(jnp.where(diagonal, base, 0.0), axis=1, keepdims=True)
@@ -68,24 +57,20 @@
     return copies
 
 
-def dispatch_kernel(shards, *refs):
-    sources, refs = refs[:5], refs[5:]
-    found_ref, *block_refs = refs[:-6]
-    buffers, sems = refs[-6:-1], refs[-1]
+def dispatch_kernel(*refs):
+    sources, (found_ref, lines_ref), buffers, sems = refs[:5], refs[5:7], refs[7:-1], refs[-1]
     copies = start_copies(sources, buffers, sems)
     for copy in copies[:-1]:
         copy.wait()
-    found = targets(shards, *[ref[...] for ref in buffers[:-1]])
+    found = targets(*[ref[...] for ref in buffers[:-1]])
     found_ref[...] = jnp.concatenate(found, axis=0)
     tokens_ref = buffers[-1]
-    size = block_refs[0].shape[0]
-    line = lax.broadcasted_iota(jnp.int32, (size * len(block_refs), tokens_ref.shape[0]), 0)
+    line = lax.broadcasted_iota(jnp.int32, (lines_ref.shape[0], tokens_ref.shape[0]), 0)
     picked = functools.reduce(jnp.logical_or, [line == target for target in found])
     selector = jnp.where(picked, 1.0, 0.0).astype(jnp.bfloat16)
     copies[-1].wait()
-    buffer = jnp.dot(selector, tokens_ref[...], preferred_element_type=jnp.float32)
-    for b, block_ref in enumerate(block_refs):
-        block_ref[...] = buffer[size * b : size * (b + 1)].astype(jnp.bfloat16)
+    lines = jnp.dot(selector, tokens_ref[...], preferred_element_type=jnp.float32)
+    lines_ref[...] = lines.astype(jnp.bfloat16)
 
 
 def prepare_kernel(
@@ -110,22 +95,16 @@
         copy.wait()
 
 
-def stack(refs):
-    return jnp.concatenate([ref[...].astype(jnp.float32) for ref in refs], axis=0)
-
-
-def expert_kernel(split, in_ref, down_ref, twin_in_ref, twin_down_ref, *refs):
+def expert_kernel(size, in_ref, down_ref, twin_in_ref, twin_down_ref, rows_ref, out_ref):
     odd = lax.axis_index("expert") & 1
-    count = len(refs) // 2
-    rows = stack(refs[:count]).astype(jnp.bfloat16)
-    size = refs[0].shape[0]
+    rows = rows_ref[...]
     hidden = []
     for half, ref in enumerate((in_ref, twin_in_ref)):
         gate = jnp.dot(rows, ref[0], preferred_element_type=jnp.float32)
         up = jnp.dot(rows, ref[1], preferred_element_type=jnp.float32)
         value = jax.nn.silu(gate) * up
-        if split:
-            place = lax.broadcasted_iota(jnp.int32, value.shape, 0) // (size // 2)
+        if size:
+            place = lax.broadcasted_iota(jnp.int32, value.shape, 0) // size
             value = jnp.where((place & 1) == (odd ^ half), value, 0.0)
         hidden.append(value.astype(jnp.bfloat16))
     piece = jnp.dot(
@@ -133,23 +112,22 @@
         jnp.concatenate([down_ref[...], twin_down_ref[...]], axis=0),
         preferred_element_type=jnp.float32,
     )
-    for b, out_ref in enumerate(refs[count:]):
-        out_ref[...] = piece[size * b : size * (b + 1)].astype(jnp.bfloat16)
-
-
-def mix_kernel(repeats, weight_ref, *refs):
-    out_hbm, out_ref, sems = refs[-3:]
-    refs = refs[:-3]
+    out_ref[...] = piece.astype(jnp.bfloat16)
+
+
+def mix_kernel(weight_ref, pieces_ref, out_hbm, out_ref, sems):
     rows, width = out_ref.shape
+    lines = weight_ref.shape[1]
+    repeats = pieces_ref.shape[0] // lines
     parts = sems.shape[0]
     step = width // parts
     copies = []
     for part in range(parts):
         columns = slice(part * step, (part + 1) * step)
-        total = functools.reduce(
-            jnp.add,
-            [stack([ref.at[:, columns] for ref in refs[j::repeats]]) for j in range(repeats)],
-        )
+        total = pieces_ref[:, columns]
+        if repeats > 1:
+            total = total.astype(jnp.float32).reshape(lines // CAP, repeats, CAP, step)
+            total = jnp.sum(total, axis=1).reshape(lines, step)
         high = total.astype(jnp.bfloat16)
         mixed = jnp.dot(weight_ref[...], high, preferred_element_type=jnp.float32)
         if repeats > 1:
@@ -186,18 +164,12 @@
     return [pltpu.VMEM(x.shape, x.dtype) for x in arrays] + [pltpu.SemaphoreType.DMA((len(arrays),))]
 
 
-def exchange(blocks, split, back=False):
+def exchange(lines):
     devices = lax.axis_size("expert")
-    result = list(blocks)
-    for k in range(1, len(blocks)):
-        if split:
-            pairs = [(i, i ^ 1 ^ 2 * CHIP_STEPS[i & 1][k]) for i in range(devices)]
-        else:
-            pairs = [(i, i ^ 2 * k) for i in range(devices)]
-        if back:
-            pairs = [(target, source) for source, target in pairs]
-        result[k] = lax.ppermute(blocks[k], "expert", pairs)
-    return result
+    groups = [list(range(core, devices, 2)) for core in range(2)]
+    return lax.all_to_all(
+        lines, "expert", split_axis=0, concat_axis=0, axis_index_groups=groups, tiled=True
+    )
 
 
 def from_twin(array):
@@ -208,24 +180,24 @@
 def body(tokens, w_in, w_down, old_place, new_place, expert_ids, replica, combine):
     devices = lax.axis_size("expert")
     shards = devices // SLOTS
-    split = shards == 1
-    repeats = max(shards // 2, 1)
     chips = devices // 2
     rows, width = tokens.shape
     hidden = w_down.shape[0]
     twin_in, twin_down = from_twin(w_in), from_twin(w_down)
     operands = (new_place[None], old_place[None], expert_ids.T, replica.T, tokens)
     combine = combine.T
-    block = jax.ShapeDtypeStruct((CAP * (2 if split else 1), width), jnp.bfloat16)
-    found, *blocks = call(
-        functools.partial(dispatch_kernel, shards),
-        [shape_of(operands[2])] + [block] * (chips // repeats),
+    found, lines = call(
+        dispatch_kernel,
+        [shape_of(operands[2]), jax.ShapeDtypeStruct((SLOTS * CAP, width), jnp.bfloat16)],
         operands,
         2 * SLOTS * CAP * rows * width,
         [HBM] * len(operands),
         scratch=scratch_for(*operands),
     )
-    received = exchange([blocks[c // repeats] for c in range(chips)], split)
+    if shards > 1:
+        lines = jnp.repeat(lines.reshape(SLOTS, CAP, width), shards // 2, axis=0)
+        lines = lines.reshape(chips * CAP, width)
+    received = exchange(lines)
     own_in, own_down, weight = call(
         prepare_kernel,
         [
@@ -239,17 +211,17 @@
         scratch=[pltpu.VMEM(combine.shape, combine.dtype), pltpu.SemaphoreType.DMA((3,))],
     )
     pieces = call(
-        functools.partial(expert_kernel, split),
-        [block] * chips,
-        (own_in, own_down, twin_in, twin_down, *received),
-        12 * chips * block.shape[0] * hidden * width,
-    )
-    returned = exchange(pieces, split, back=True)
+        functools.partial(expert_kernel, CAP if shards == 1 else 0),
+        shape_of(received),
+        (own_in, own_down, twin_in, twin_down, received),
+        12 * received.shape[0] * hidden * width,
+    )
+    returned = exchange(pieces)
     parts = 4 if width % 512 == 0 else 1
     return call(
-        functools.partial(mix_kernel, repeats),
+        mix_kernel,
         shape_of(tokens),
-        (weight, *returned),
+        (weight, returned),
         4 * SLOTS * CAP * rows * width,
         out_specs=HBM,
         scratch=[pltpu.VMEM(tokens.shape, tokens.dtype), pltpu.SemaphoreType.DMA((parts,))],

time: 18.6 us -> 26.2 us (1.41)
  blocking collectives: 0 us -> 8.34 us
  local copies, waits for them, and re-layouts: 0 us -> 4.88 us
  waiting for transfers between devices: 5.14 us -> 1.3 us
  starting transfers between devices: 8.36 us -> 5.69 us
  Pallas kernels: 4.87 us -> 5.59 us
    all_to_all x0 -> x1, blocking collectives: none -> 8.34 us  [exchange(): lax.all_to_all(lines, 'expert', split_axis=0, concat_axis=0, axis_index_g...]
    ppermute x6 -> x0, starting transfers between devices: 7.85 us -> none  [exchange(): result[k] = lax.ppermute(blocks[k], 'expert', pairs)]
    all_to_all x0 -> x1, starting transfers between devices: none -> 5.18 us  [exchange(): lax.all_to_all(lines, 'expert', split_axis=0, concat_axis=0, axis_index_g...]
    ppermute x6 -> x0, waiting for transfers between devices: 5.14 us -> none  [exchange(): result[k] = lax.ppermute(blocks[k], 'expert', pairs)]
    unnamed x0 -> x8, local copies, waits for them, and re-layouts: none -> 4.88 us
    all_to_all x0 -> x1, waiting for transfers between devices: none -> 1.3 us  [exchange(): lax.all_to_all(lines, 'expert', split_axis=0, concat_axis=0, axis_index_g...]
    pallas_call x4, Pallas kernels: 4.87 us -> 5.59 us  [call(): pl.pallas_call(kernel, out_shape=outs, in_specs=arg_specs, out_specs=out_...]
  transfers between devices with their start and end apart: 8 -> 3, of which waited for: 4 -> 1; matrix products, arithmetic and copies ran while one was open for 0% -> 0% of each run, Pallas kernels for 16% -> 14%
where the time goes in v5:
time: 26.2 us; the launch traced here: 25.8 us
  blocking collectives  8.34 us (32%)
  starting transfers between devices  5.69 us (22%)
  Pallas kernels  5.59 us (21%)
  local copies, waits for them, and re-layouts  4.88 us (19%)
  waiting for transfers between devices  1.3 us (5%)
    all_to_all x1, blocking collectives, exchange(): lax.all_to_all(lines, 'expert', split_axis=0, concat_axis=0, axis_index_g...  8.34 us
    pallas_call x4, Pallas kernels, call(): pl.pallas_call(kernel, out_shape=outs, in_specs=arg_specs, out_specs=out_...  5.59 us
    all_to_all x1, starting transfers between devices, exchange(): lax.all_to_all(lines, 'expert', split_axis=0, concat_axis=0, axis_index_g...  5.18 us
    unnamed x8, local copies, waits for them, and re-layouts  4.88 us
    all_to_all x1, waiting for transfers between devices, exchange(): lax.all_to_all(lines, 'expert', split_axis=0, concat_axis=0, axis_index_g...  1.3 us
  transfers between devices with their start and end apart: 3, of which 1 were waited for; matrix products, arithmetic and copies ran while one was open for 0% of the time, Pallas kernels for 14%

profile of v5, /device:TPU:0, one launch (start us, length us, event | category | flops | bytes accessed | tf_op | source)
XLA Modules:
  0.0 25.8 jit_solution(14865678085332065562)
XLA Ops:
  0.0 0.5 %collective-permute-start = (bf16[2,3584,128]{2,1,0:T(8,128)(2,1)}, bf16[2,3584,128]{2,1,0:T(8,128)(2,1)S(1)}, u32[]{:S(2)}, u32[]{:S(2)}) collective-permute-start(bf16[2,3584,128]{2,1,0:T(8,128)(2,1)} %in_hbm.1), channel_id=1, source_target_pairs={{0,1},{1,0},{2,3},{3,2},{4,5},{5,4},{6,7},{7,6},{8,9},{9,8},{10,11... | collective-permute-start | bytes 5505032 | tf_op jit(solution)/shard_map/ppermute | solution.py:177
  0.5 0.1 collective-permute-start.1
  0.5 2.0 %shard_map.82 = (s32[2,16]{1,0:T(2,128)S(1)}, bf16[32,3584]{1,0:T(8,128)(2,1)}) custom-call(s32[1,8]{1,0:T(1,128)} %bitcast.15, s32[1,8]{1,0:T(1,128)} %bitcast.16, s32[2,16]{1,0:T(2,128)} %bitcast.12, s32[2,16]{1,0:T(2,128)} %bitcast.13, bf16[16,3584]{1,0:T(8,128)(2,1)} %refs_4_.1), custom_call_target="tpu_custom_call" | custom-call | flops 3670016 | bytes 344512 | tf_op jit(solution)/shard_map/pallas_call | solution.py:148
  2.5 5.2 %all-to-all-start = ((bf16[4,8,3584]{2,1,0:T(8,128)(2,1)}), bf16[4,8,3584]{2,1,0:T(8,128)(2,1)S(1)}, u32[]{:S(2)}, u32[]{:S(2)}) async-start(bf16[4,8,3584]{2,1,0:T(8,128)(2,1)} %bitcast.5), calls=%async_computation | async-start | bytes 458752 | tf_op jit(solution)/shard_map/all_to_all | solution.py:170
  7.7 1.8 %shard_map.83 = (bf16[2,3584,128]{2,1,0:T(8,128)(2,1)S(1)}, bf16[128,3584]{1,0:T(8,128)(2,1)S(1)}, bf16[32,32]{1,0:T(8,128)(2,1)S(1)}) custom-call(s32[2,16]{1,0:T(2,128)S(1)} %get-tuple-element.10.found_ref, f32[2,16]{1,0:T(2,128)} %bitcast.14, bf16[2,3584,128]{2,1,0:T(8,128)(2,1)} %in_hbm.1, bf16[128,3584]{1,0:T(8,128)(2,1)} %down_hbm.1), custom_call_target="tpu_custom_call" | custom-call | bytes 5507328 | tf_op jit(solution)/shard_map/pallas_call | solution.py:148
  9.4 0.0 copy-start
  9.4 1.2 %copy-done = bf16[2,3584,128]{2,1,0:T(8,128)(2,1)} copy-done((bf16[2,3584,128]{2,1,0:T(8,128)(2,1)}, bf16[2,3584,128]{2,1,0:T(8,128)(2,1)S(1)}, u32[]{:S(2)}) %copy-start) | copy-done | bytes 1835032
  10.7 0.0 copy-start.2
  10.7 1.0 %copy-done.2 = bf16[128,3584]{1,0:T(8,128)(2,1)} copy-done((bf16[128,3584]{1,0:T(8,128)(2,1)}, bf16[128,3584]{1,0:T(8,128)(2,1)S(1)}, u32[]{:S(2)}) %copy-start.2) | copy-done | bytes 917528
  11.6 1.3 %all-to-all-done = bf16[4,8,3584]{2,1,0:T(8,128)(2,1)S(1)} async-done(((bf16[4,8,3584]{2,1,0:T(8,128)(2,1)}), bf16[4,8,3584]{2,1,0:T(8,128)(2,1)S(1)}, u32[]{:S(2)}, u32[]{:S(2)}) %all-to-all-start) | async-done | bytes 229408 | tf_op jit(solution)/shard_map/all_to_all | solution.py:170
  12.9 0.0 collective-permute-done.1.twin_down_ref
  12.9 0.0 collective-permute-done.twin_in_ref
  12.9 0.0 copy-start.1
  13.0 1.5 %copy-done.1 = bf16[2,3584,128]{2,1,0:T(8,128)(2,1)S(1)} copy-done((bf16[2,3584,128]{2,1,0:T(8,128)(2,1)S(1)}, bf16[2,3584,128]{2,1,0:T(8,128)(2,1)}, u32[]{:S(2)}) %copy-start.1) | copy-done | bytes 1835032
  14.4 0.0 copy-start.3
  14.5 1.2 %copy-done.3 = bf16[128,3584]{1,0:T(8,128)(2,1)S(1)} copy-done((bf16[128,3584]{1,0:T(8,128)(2,1)S(1)}, bf16[128,3584]{1,0:T(8,128)(2,1)}, u32[]{:S(2)}) %copy-start.3) | copy-done | bytes 917528
  15.6 1.0 %shard_map.84 = bf16[32,3584]{1,0:T(8,128)(2,1)S(1)} custom-call(bf16[2,3584,128]{2,1,0:T(8,128)(2,1)S(1)} %copy-done.1, bf16[128,3584]{1,0:T(8,128)(2,1)S(1)} %copy-done.3, bf16[2,3584,128]{2,1,0:T(8,128)(2,1)S(1)} %collective-permute-done.twin_in_ref, bf16[128,3584]{1,0:T(8,128)(2,1)S(1)} %collective-permute-done.1.twin_down_ref, bf16[32,3584]{1,0:T(8,128)(2,1)S(1)} %bitcast.10), custom_call_target="tpu_custom_call" | custom-call | flops 176160768 | bytes 5963776 | tf_op jit(solution)/shard_map/pallas_call | solution.py:148
  16.6 8.3 %all_to_all.22 = bf16[4,8,3584]{2,1,0:T(8,128)(2,1)S(1)} all-to-all(bf16[4,8,3584]{2,1,0:T(8,128)(2,1)S(1)} %bitcast.11), channel_id=1, replica_groups={{0,2,4,6},{1,3,5,7},{8,10,12,14},{9,11,13,15},{16,18,20,22},{17,19,21,2..., dimensions={0} | all-to-all | bytes 458752 | tf_op jit(solution)/shard_map/all_to_all | solution.py:170
  25.0 0.9 %shard_map.85 = bf16[16,3584]{1,0:T(8,128)(2,1)} custom-call(bf16[32,32]{1,0:T(8,128)(2,1)S(1)} %get-tuple-element.11.weight_ref, bf16[32,3584]{1,0:T(8,128)(2,1)S(1)} %bitcast.9), custom_call_target="tpu_custom_call" | custom-call | flops 7340032 | bytes 346112 | tf_op jit(solution)/shard_map/pallas_call | solution.py:148
Async XLA Ops:
  0.0 12.9 %collective-permute-start = (bf16[2,3584,128]{2,1,0:T(8,128)(2,1)}, bf16[2,3584,128]{2,1,0:T(8,128)(2,1)S(1)}, u32[]{:S(2)}, u32[]{:S(2)}) collective-permute-start(bf16[2,3584,128]{2,1,0:T(8,128)(2,1)} %in_hbm.1), channel_id=1, source_target_pairs={{0,1},{1,0},{2,3},{3,2},{4,5},{5,4},{6,7},{7,6},{8,9},{9,8},{10,11... | collective-permute-start | bytes 5505032 | tf_op jit(solution)/shard_map/ppermute | solution.py:177
  0.5 12.5 %collective-permute-start.1 = (bf16[128,3584]{1,0:T(8,128)(2,1)}, bf16[128,3584]{1,0:T(8,128)(2,1)S(1)}, u32[]{:S(2)}, u32[]{:S(2)}) collective-permute-start(bf16[128,3584]{1,0:T(8,128)(2,1)} %down_hbm.1), channel_id=1, source_target_pairs={{0,1},{1,0},{2,3},{3,2},{4,5},{5,4},{6,7},{7,6},{8,9},{9,8},{10,11... | collective-permute-start | bytes 2752520 | tf_op jit(solution)/shard_map/ppermute | solution.py:177
  2.5 10.5 %all-to-all-start = ((bf16[4,8,3584]{2,1,0:T(8,128)(2,1)}), bf16[4,8,3584]{2,1,0:T(8,128)(2,1)S(1)}, u32[]{:S(2)}, u32[]{:S(2)}) async-start(bf16[4,8,3584]{2,1,0:T(8,128)(2,1)} %bitcast.5), calls=%async_computation | async-start | bytes 458752 | tf_op jit(solution)/shard_map/all_to_all | solution.py:170
  9.4 1.2 %copy-start = (bf16[2,3584,128]{2,1,0:T(8,128)(2,1)}, bf16[2,3584,128]{2,1,0:T(8,128)(2,1)S(1)}, u32[]{:S(2)}) copy-start(bf16[2,3584,128]{2,1,0:T(8,128)(2,1)S(1)} %get-tuple-element.12.in_ref) | copy-start | bytes 5505028
  10.7 1.0 %copy-start.2 = (bf16[128,3584]{1,0:T(8,128)(2,1)}, bf16[128,3584]{1,0:T(8,128)(2,1)S(1)}, u32[]{:S(2)}) copy-start(bf16[128,3584]{1,0:T(8,128)(2,1)S(1)} %get-tuple-element.13.down_ref) | copy-start | bytes 2752516
  12.9 1.5 %copy-start.1 = (bf16[2,3584,128]{2,1,0:T(8,128)(2,1)S(1)}, bf16[2,3584,128]{2,1,0:T(8,128)(2,1)}, u32[]{:S(2)}) copy-start(bf16[2,3584,128]{2,1,0:T(8,128)(2,1)} %copy-done) | copy-start | bytes 5505028
  14.4 1.2 %copy-start.3 = (bf16[128,3584]{1,0:T(8,128)(2,1)S(1)}, bf16[128,3584]{1,0:T(8,128)(2,1)}, u32[]{:S(2)}) copy-start(bf16[128,3584]{1,0:T(8,128)(2,1)} %copy-done.2) | copy-start | bytes 2752516

commit v6 on v4

--- a/solution.py
+++ b/solution.py
@@ -9,7 +9,6 @@
 
 SLOTS = 8
 CAP = 4
-CHIP_STEPS = ((0, 3, 1, 2), (0, 3, 2, 1))
 
 VMEM = pl.BlockSpec(memory_space=pltpu.VMEM)
 HBM = pl.BlockSpec(memory_space=pltpu.HBM)
@@ -24,13 +23,7 @@
     source = jnp.where(new == old, across, across ^ 1)
     away = source ^ (device // shards)
     if shards == 1:
-        odd = device & 1
-        chip = away >> 1
-        step = sum(
-            jnp.where(chip == jnp.where(odd == 1, c_odd, c_even), k, 0)
-            for k, (c_even, c_odd) in enumerate(zip(*CHIP_STEPS))
-        )
-        away = (source & 1) | (step << 1)
+        away = (away & -2) | (source & 1)
     base = (CAP * away).astype(jnp.float32)
     diagonal = down == across
     mine = jnp.sum(jnp.where(diagonal, new_full, 0.0), axis=1, keepdims=True)
@@ -110,15 +103,21 @@
         copy.wait()
 
 
-def stack(refs):
-    return jnp.concatenate([ref[...].astype(jnp.float32) for ref in refs], axis=0)
-
-
-def expert_kernel(split, in_ref, down_ref, twin_in_ref, twin_down_ref, *refs):
+def arrived(split, refs, columns=slice(None)):
+    blocks = [ref[:, columns].astype(jnp.float32) for ref in refs]
+    if split:
+        near = len(blocks) // 2 - 1
+        own, to_odd, far, to_even = blocks[0], blocks[1:-near - 1], blocks[-near - 1], blocks[-near:]
+        odd = (lax.axis_index("expert") & 1) == 1
+        blocks = [own, *[jnp.where(odd, *pair) for pair in zip(to_odd, to_even)], far]
+    return blocks
+
+
+def expert_kernel(split, count, in_ref, down_ref, twin_in_ref, twin_down_ref, *refs):
     odd = lax.axis_index("expert") & 1
-    count = len(refs) // 2
-    rows = stack(refs[:count]).astype(jnp.bfloat16)
-    size = refs[0].shape[0]
+    outs = refs[count:]
+    rows = jnp.concatenate(arrived(split, refs[:count]), axis=0).astype(jnp.bfloat16)
+    size = outs[0].shape[0]
     hidden = []
     for half, ref in enumerate((in_ref, twin_in_ref)):
         gate = jnp.dot(rows, ref[0], preferred_element_type=jnp.float32)
@@ -133,11 +132,11 @@
         jnp.concatenate([down_ref[...], twin_down_ref[...]], axis=0),
         preferred_element_type=jnp.float32,
     )
-    for b, out_ref in enumerate(refs[count:]):
+    for b, out_ref in enumerate(outs):
         out_ref[...] = piece[size * b : size * (b + 1)].astype(jnp.bfloat16)
 
 
-def mix_kernel(repeats, weight_ref, *refs):
+def mix_kernel(split, repeats, weight_ref, *refs):
     out_hbm, out_ref, sems = refs[-3:]
     refs = refs[:-3]
     rows, width = out_ref.shape
@@ -148,7 +147,10 @@
         columns = slice(part * step, (part + 1) * step)
         total = functools.reduce(
             jnp.add,
-            [stack([ref.at[:, columns] for ref in refs[j::repeats]]) for j in range(repeats)],
+            [
+                jnp.concatenate(arrived(split, refs[j::repeats], columns), axis=0)
+                for j in range(repeats)
+            ],
         )
         high = total.astype(jnp.bfloat16)
         mixed = jnp.dot(weight_ref[...], high, preferred_element_type=jnp.float32)
@@ -186,18 +188,24 @@
     return [pltpu.VMEM(x.shape, x.dtype) for x in arrays] + [pltpu.SemaphoreType.DMA((len(arrays),))]
 
 
-def exchange(blocks, split, back=False):
+def exchange(blocks, split, ready=(0, 0)):
     devices = lax.axis_size("expert")
-    result = list(blocks)
-    for k in range(1, len(blocks)):
-        if split:
-            pairs = [(i, i ^ 1 ^ 2 * CHIP_STEPS[i & 1][k]) for i in range(devices)]
-        else:
-            pairs = [(i, i ^ 2 * k) for i in range(devices)]
-        if back:
-            pairs = [(target, source) for source, target in pairs]
-        result[k] = lax.ppermute(blocks[k], "expert", pairs)
-    return result
+
+    def move(block, distance, cores=(0, 1)):
+        pairs = [(i, i ^ distance) for i in range(devices) if i & 1 in cores]
+        return lax.ppermute(block, "expert", pairs)
+
+    if not split:
+        return [blocks[0]] + [move(block, 2 * c) for c, block in enumerate(blocks) if c > 0]
+    far = len(blocks) - 1
+    near = [c for c in range(1, far)]
+    from_even = [move(blocks[c], 2 * c + 1, (0,)) for c in near]
+    from_far = move(blocks[far], 2 * far + 1)
+    from_odd = [
+        move(lax.optimization_barrier((blocks[c], first))[0], 2 * c + 1, (1,))
+        for c, first in zip(near, ready)
+    ]
+    return [blocks[0], *from_even, from_far, *from_odd]
 
 
 def from_twin(array):
@@ -225,7 +233,7 @@
         [HBM] * len(operands),
         scratch=scratch_for(*operands),
     )
-    received = exchange([blocks[c // repeats] for c in range(chips)], split)
+    received = exchange([blocks[c // repeats] for c in range(chips)], split, (twin_in, twin_down))
     own_in, own_down, weight = call(
         prepare_kernel,
         [
@@ -239,15 +247,15 @@
         scratch=[pltpu.VMEM(combine.shape, combine.dtype), pltpu.SemaphoreType.DMA((3,))],
     )
     pieces = call(
-        functools.partial(expert_kernel, split),
+        functools.partial(expert_kernel, split, len(received)),
         [block] * chips,
         (own_in, own_down, twin_in, twin_down, *received),
         12 * chips * block.shape[0] * hidden * width,
     )
-    returned = exchange(pieces, split, back=True)
+    returned = exchange(pieces, split)
     parts = 4 if width % 512 == 0 else 1
     return call(
-        functools.partial(mix_kernel, repeats),
+        functools.partial(mix_kernel, split, repeats),
         shape_of(tokens),
         (weight, *returned),
         4 * SLOTS * CAP * rows * width,

time: 18.6 us -> 27 us (1.45)
  starting transfers between devices: 8.36 us -> 15.1 us
  waiting for transfers between devices: 5.14 us -> 6.58 us
    ppermute x6 -> x10, starting transfers between devices: 7.85 us -> 14.6 us  [move(): return lax.ppermute(block, 'expert', pairs)]
    ppermute x6 -> x10, waiting for transfers between devices: 5.14 us -> 6.57 us  [move(): return lax.ppermute(block, 'expert', pairs)]
  transfers between devices with their start and end apart: 8 -> 12, of which waited for: 4 -> 5; matrix products, arithmetic and copies ran while one was open for 0% -> 0% of each run, Pallas kernels for 16% -> 11%
where the time goes in v6:
time: 27 us; the launch traced here: 26.7 us
  starting transfers between devices  15.1 us (56%)
  waiting for transfers between devices  6.58 us (24%)
  Pallas kernels  4.88 us (18%)
    ppermute x10, starting transfers between devices, move(): return lax.ppermute(block, 'expert', pairs)  14.6 us
    ppermute x10, waiting for transfers between devices, move(): return lax.ppermute(block, 'expert', pairs)  6.57 us
    pallas_call x4, Pallas kernels, call(): pl.pallas_call(kernel, out_shape=outs, in_specs=arg_specs, out_specs=out_...  4.88 us
  transfers between devices with their start and end apart: 12, of which 5 were waited for; matrix products, arithmetic and copies ran while one was open for 0% of the time, Pallas kernels for 11%

profile of v6, /device:TPU:0, one launch (start us, length us, event | category | flops | bytes accessed | tf_op | source)
XLA Modules:
  0.0 26.7 jit_solution(18128716088788265192)
XLA Ops:
  0.0 0.5 %collective-permute-start = (bf16[2,3584,128]{2,1,0:T(8,128)(2,1)}, bf16[2,3584,128]{2,1,0:T(8,128)(2,1)S(1)}, u32[]{:S(2)}, u32[]{:S(2)}) collective-permute-start(bf16[2,3584,128]{2,1,0:T(8,128)(2,1)} %in_hbm.1), channel_id=1, source_target_pairs={{0,1},{1,0},{2,3},{3,2},{4,5},{5,4},{6,7},{7,6},{8,9},{9,8},{10,11... | collective-permute-start | bytes 5505032 | tf_op jit(solution)/shard_map/ppermute | solution.py:213
  0.5 0.1 collective-permute-start.1
  0.5 1.2 %shard_map.82 = (s32[2,16]{1,0:T(2,128)S(1)}, bf16[8,3584]{1,0:T(8,128)(2,1)S(1)}, bf16[8,3584]{1,0:T(8,128)(2,1)S(1)}, bf16[8,3584]{1,0:T(8,128)(2,1)S(1)}, bf16[8,3584]{1,0:T(8,128)(2,1)S(1)}) custom-call(s32[1,8]{1,0:T(1,128)} %bitcast.8, s32[1,8]{1,0:T(1,128)} %bitcast.9, s32[2,16]{1,0:T(2,128)} %bitcast.5, s32[2,16]{1,0:T(2,128)} %bitcast.6, ...), custom_call_target="tpu_custom_call" | custom-call | flops 3670016 | bytes 344512 | tf_op jit(solution)/shard_map/pallas_call | solution.py:172
  1.8 4.5 %collective-permute-start.2 = (bf16[8,3584]{1,0:T(8,128)(2,1)S(1)}, bf16[8,3584]{1,0:T(8,128)(2,1)S(1)}, u32[]{:S(2)}, u32[]{:S(2)}) collective-permute-start(bf16[8,3584]{1,0:T(8,128)(2,1)S(1)} %get-tuple-element.29), channel_id=1, source_target_pairs={{0,3},{2,1},{4,7},{6,5},{8,11},{10,9},{12,15},{14,13},{16,19},{18,... | collective-permute-start | bytes 172040 | tf_op jit(solution)/shard_map/ppermute | solution.py:196
  6.2 1.3 %collective-permute-start.3 = (bf16[8,3584]{1,0:T(8,128)(2,1)S(1)}, bf16[8,3584]{1,0:T(8,128)(2,1)S(1)}, u32[]{:S(2)}, u32[]{:S(2)}) collective-permute-start(bf16[8,3584]{1,0:T(8,128)(2,1)S(1)} %get-tuple-element.30), channel_id=1, source_target_pairs={{0,5},{2,7},{4,1},{6,3},{8,13},{10,15},{12,9},{14,11},{16,21},{18,... | collective-permute-start | bytes 172040 | tf_op jit(solution)/shard_map/ppermute | solution.py:196
  7.6 0.4 %collective-permute-start.4 = (bf16[8,3584]{1,0:T(8,128)(2,1)S(1)}, bf16[8,3584]{1,0:T(8,128)(2,1)S(1)}, u32[]{:S(2)}, u32[]{:S(2)}) collective-permute-start(bf16[8,3584]{1,0:T(8,128)(2,1)S(1)} %get-tuple-element.28), channel_id=1, source_target_pairs={{0,7},{1,6},{2,5},{3,4},{4,3},{5,2},{6,1},{7,0},{8,15},{9,14},{10,... | collective-permute-start | bytes 172040 | tf_op jit(solution)/shard_map/ppermute | solution.py:196
  7.9 0.0 collective-permute-done.1.twin_down_ref
  7.9 1.3 %collective-permute-start.6 = (bf16[8,3584]{1,0:T(8,128)(2,1)S(1)}, bf16[8,3584]{1,0:T(8,128)(2,1)S(1)}, u32[]{:S(2)}, u32[]{:S(2)}) collective-permute-start(bf16[8,3584]{1,0:T(8,128)(2,1)S(1)} %get-tuple-element.30), channel_id=1, source_target_pairs={{1,4},{3,6},{5,0},{7,2},{9,12},{11,14},{13,8},{15,10},{17,20},{19,... | collective-permute-start | bytes 172040 | tf_op jit(solution)/shard_map/ppermute | solution.py:196
  9.2 0.0 collective-permute-done.twin_in_ref
  9.2 1.3 %collective-permute-start.5 = (bf16[8,3584]{1,0:T(8,128)(2,1)S(1)}, bf16[8,3584]{1,0:T(8,128)(2,1)S(1)}, u32[]{:S(2)}, u32[]{:S(2)}) collective-permute-start(bf16[8,3584]{1,0:T(8,128)(2,1)S(1)} %get-tuple-element.29), channel_id=1, source_target_pairs={{1,2},{3,0},{5,6},{7,4},{9,10},{11,8},{13,14},{15,12},{17,18},{19,... | collective-permute-start | bytes 172040 | tf_op jit(solution)/shard_map/ppermute | solution.py:196
  10.5 1.8 %shard_map.83 = (bf16[2,3584,128]{2,1,0:T(8,128)(2,1)S(1)}, bf16[128,3584]{1,0:T(8,128)(2,1)S(1)}, bf16[32,32]{1,0:T(8,128)(2,1)S(1)}) custom-call(s32[2,16]{1,0:T(2,128)S(1)} %get-tuple-element.21.found_ref, f32[2,16]{1,0:T(2,128)} %bitcast.7, bf16[2,3584,128]{2,1,0:T(8,128)(2,1)} %in_hbm.1, bf16[128,3584]{1,0:T(8,128)(2,1)} %down_hbm.1), custom_call_target="tpu_custom_call" | custom-call | bytes 5507328 | tf_op jit(solution)/shard_map/pallas_call | solution.py:172
  12.3 0.0 collective-permute-done.2.refs_1_
  12.3 0.0 collective-permute-done.3.refs_2_
  12.3 0.0 collective-permute-done.4.refs_3_
  12.4 1.1 %collective-permute-done.6.refs_5_ = bf16[8,3584]{1,0:T(8,128)(2,1)S(1)} collective-permute-done((bf16[8,3584]{1,0:T(8,128)(2,1)S(1)}, bf16[8,3584]{1,0:T(8,128)(2,1)S(1)}, u32[]{:S(2)}, u32[]{:S(2)}) %collective-permute-start.6) | collective-permute-done | bytes 57376 | tf_op jit(solution)/shard_map/ppermute | solution.py:196
  13.4 1.3 %collective-permute-done.5.refs_4_ = bf16[8,3584]{1,0:T(8,128)(2,1)S(1)} collective-permute-done((bf16[8,3584]{1,0:T(8,128)(2,1)S(1)}, bf16[8,3584]{1,0:T(8,128)(2,1)S(1)}, u32[]{:S(2)}, u32[]{:S(2)}) %collective-permute-start.5) | collective-permute-done | bytes 57376 | tf_op jit(solution)/shard_map/ppermute | solution.py:196
  14.7 1.0 %shard_map.84 = (bf16[8,3584]{1,0:T(8,128)(2,1)S(1)}, bf16[8,3584]{1,0:T(8,128)(2,1)S(1)}, bf16[8,3584]{1,0:T(8,128)(2,1)S(1)}, bf16[8,3584]{1,0:T(8,128)(2,1)S(1)}) custom-call(bf16[2,3584,128]{2,1,0:T(8,128)(2,1)S(1)} %get-tuple-element.23.in_ref, bf16[128,3584]{1,0:T(8,128)(2,1)S(1)} %get-tuple-element.24.down_ref, ...), custom_call_target="tpu_custom_call" | custom-call | flops 176160768 | bytes 6078464 | tf_op jit(solution)/shard_map/pallas_call | solution.py:172
  15.7 1.9 %collective-permute-start.7 = (bf16[8,3584]{1,0:T(8,128)(2,1)S(1)}, bf16[8,3584]{1,0:T(8,128)(2,1)S(1)}, u32[]{:S(2)}, u32[]{:S(2)}) collective-permute-start(bf16[8,3584]{1,0:T(8,128)(2,1)S(1)} %get-tuple-element.35), channel_id=1, source_target_pairs={{0,3},{2,1},{4,7},{6,5},{8,11},{10,9},{12,15},{14,13},{16,19},{18,... | collective-permute-start | bytes 172040 | tf_op jit(solution)/shard_map/ppermute | solution.py:196
  17.7 1.3 %collective-permute-start.8 = (bf16[8,3584]{1,0:T(8,128)(2,1)S(1)}, bf16[8,3584]{1,0:T(8,128)(2,1)S(1)}, u32[]{:S(2)}, u32[]{:S(2)}) collective-permute-start(bf16[8,3584]{1,0:T(8,128)(2,1)S(1)} %get-tuple-element.36), channel_id=1, source_target_pairs={{0,5},{2,7},{4,1},{6,3},{8,13},{10,15},{12,9},{14,11},{16,21},{18,... | collective-permute-start | bytes 172040 | tf_op jit(solution)/shard_map/ppermute | solution.py:196
  19.0 0.1 collective-permute-start.9
  19.1 1.3 %collective-permute-start.10 = (bf16[8,3584]{1,0:T(8,128)(2,1)S(1)}, bf16[8,3584]{1,0:T(8,128)(2,1)S(1)}, u32[]{:S(2)}, u32[]{:S(2)}) collective-permute-start(bf16[8,3584]{1,0:T(8,128)(2,1)S(1)} %get-tuple-element.35), channel_id=1, source_target_pairs={{1,2},{3,0},{5,6},{7,4},{9,10},{11,8},{13,14},{15,12},{17,18},{19,... | collective-permute-start | bytes 172040 | tf_op jit(solution)/shard_map/ppermute | solution.py:196
  20.4 1.3 %collective-permute-start.11 = (bf16[8,3584]{1,0:T(8,128)(2,1)S(1)}, bf16[8,3584]{1,0:T(8,128)(2,1)S(1)}, u32[]{:S(2)}, u32[]{:S(2)}) collective-permute-start(bf16[8,3584]{1,0:T(8,128)(2,1)S(1)} %get-tuple-element.36), channel_id=1, source_target_pairs={{1,4},{3,6},{5,0},{7,2},{9,12},{11,14},{13,8},{15,10},{17,20},{19,... | collective-permute-start | bytes 172040 | tf_op jit(solution)/shard_map/ppermute | solution.py:196
  21.7 0.0 collective-permute-done.7.refs_1_
  21.7 0.0 collective-permute-done.8.refs_2_
  21.7 1.9 %collective-permute-done.9.refs_3_ = bf16[8,3584]{1,0:T(8,128)(2,1)S(1)} collective-permute-done((bf16[8,3584]{1,0:T(8,128)(2,1)S(1)}, bf16[8,3584]{1,0:T(8,128)(2,1)S(1)}, u32[]{:S(2)}, u32[]{:S(2)}) %collective-permute-start.9) | collective-permute-done | bytes 57376 | tf_op jit(solution)/shard_map/ppermute | solution.py:196
  23.5 1.0 %collective-permute-done.10.refs_4_ = bf16[8,3584]{1,0:T(8,128)(2,1)S(1)} collective-permute-done((bf16[8,3584]{1,0:T(8,128)(2,1)S(1)}, bf16[8,3584]{1,0:T(8,128)(2,1)S(1)}, u32[]{:S(2)}, u32[]{:S(2)}) %collective-permute-start.10) | collective-permute-done | bytes 57376 | tf_op jit(solution)/shard_map/ppermute | solution.py:196
  24.6 1.3 %collective-permute-done.11.refs_5_ = bf16[8,3584]{1,0:T(8,128)(2,1)S(1)} collective-permute-done((bf16[8,3584]{1,0:T(8,128)(2,1)S(1)}, bf16[8,3584]{1,0:T(8,128)(2,1)S(1)}, u32[]{:S(2)}, u32[]{:S(2)}) %collective-permute-start.11) | collective-permute-done | bytes 57376 | tf_op jit(solution)/shard_map/ppermute | solution.py:196
  25.9 0.9 %shard_map.85 = bf16[16,3584]{1,0:T(8,128)(2,1)} custom-call(bf16[32,32]{1,0:T(8,128)(2,1)S(1)} %get-tuple-element.22.weight_ref, bf16[8,3584]{1,0:T(8,128)(2,1)S(1)} %get-tuple-element.31.refs_0_, bf16[8,3584]{1,0:T(8,128)(2,1)S(1)} %collective-permute-done.7.refs_1_, bf16[8,3584]{1,0:T(8,128)(2,1)S(1)} %collective-permute-done.8.refs_2_, ...), custom_call_target="tpu_custom_call" | custom-call | flops 7340032 | bytes 460800 | tf_op jit(solution)/shard_map/pallas_call | solution.py:172
Async XLA Ops:
  0.0 9.2 %collective-permute-start = (bf16[2,3584,128]{2,1,0:T(8,128)(2,1)}, bf16[2,3584,128]{2,1,0:T(8,128)(2,1)S(1)}, u32[]{:S(2)}, u32[]{:S(2)}) collective-permute-start(bf16[2,3584,128]{2,1,0:T(8,128)(2,1)} %in_hbm.1), channel_id=1, source_target_pairs={{0,1},{1,0},{2,3},{3,2},{4,5},{5,4},{6,7},{7,6},{8,9},{9,8},{10,11... | collective-permute-start | bytes 5505032 | tf_op jit(solution)/shard_map/ppermute | solution.py:213
  0.5 7.5 %collective-permute-start.1 = (bf16[128,3584]{1,0:T(8,128)(2,1)}, bf16[128,3584]{1,0:T(8,128)(2,1)S(1)}, u32[]{:S(2)}, u32[]{:S(2)}) collective-permute-start(bf16[128,3584]{1,0:T(8,128)(2,1)} %down_hbm.1), channel_id=1, source_target_pairs={{0,1},{1,0},{2,3},{3,2},{4,5},{5,4},{6,7},{7,6},{8,9},{9,8},{10,11... | collective-permute-start | bytes 2752520 | tf_op jit(solution)/shard_map/ppermute | solution.py:213
  1.8 10.6 %collective-permute-start.2 = (bf16[8,3584]{1,0:T(8,128)(2,1)S(1)}, bf16[8,3584]{1,0:T(8,128)(2,1)S(1)}, u32[]{:S(2)}, u32[]{:S(2)}) collective-permute-start(bf16[8,3584]{1,0:T(8,128)(2,1)S(1)} %get-tuple-element.29), channel_id=1, source_target_pairs={{0,3},{2,1},{4,7},{6,5},{8,11},{10,9},{12,15},{14,13},{16,19},{18,... | collective-permute-start | bytes 172040 | tf_op jit(solution)/shard_map/ppermute | solution.py:196
  6.2 6.1 %collective-permute-start.3 = (bf16[8,3584]{1,0:T(8,128)(2,1)S(1)}, bf16[8,3584]{1,0:T(8,128)(2,1)S(1)}, u32[]{:S(2)}, u32[]{:S(2)}) collective-permute-start(bf16[8,3584]{1,0:T(8,128)(2,1)S(1)} %get-tuple-element.30), channel_id=1, source_target_pairs={{0,5},{2,7},{4,1},{6,3},{8,13},{10,15},{12,9},{14,11},{16,21},{18,... | collective-permute-start | bytes 172040 | tf_op jit(solution)/shard_map/ppermute | solution.py:196
  7.6 4.8 %collective-permute-start.4 = (bf16[8,3584]{1,0:T(8,128)(2,1)S(1)}, bf16[8,3584]{1,0:T(8,128)(2,1)S(1)}, u32[]{:S(2)}, u32[]{:S(2)}) collective-permute-start(bf16[8,3584]{1,0:T(8,128)(2,1)S(1)} %get-tuple-element.28), channel_id=1, source_target_pairs={{0,7},{1,6},{2,5},{3,4},{4,3},{5,2},{6,1},{7,0},{8,15},{9,14},{10,... | collective-permute-start | bytes 172040 | tf_op jit(solution)/shard_map/ppermute | solution.py:196
  7.9 5.5 %collective-permute-start.6 = (bf16[8,3584]{1,0:T(8,128)(2,1)S(1)}, bf16[8,3584]{1,0:T(8,128)(2,1)S(1)}, u32[]{:S(2)}, u32[]{:S(2)}) collective-permute-start(bf16[8,3584]{1,0:T(8,128)(2,1)S(1)} %get-tuple-element.30), channel_id=1, source_target_pairs={{1,4},{3,6},{5,0},{7,2},{9,12},{11,14},{13,8},{15,10},{17,20},{19,... | collective-permute-start | bytes 172040 | tf_op jit(solution)/shard_map/ppermute | solution.py:196
  9.2 5.5 %collective-permute-start.5 = (bf16[8,3584]{1,0:T(8,128)(2,1)S(1)}, bf16[8,3584]{1,0:T(8,128)(2,1)S(1)}, u32[]{:S(2)}, u32[]{:S(2)}) collective-permute-start(bf16[8,3584]{1,0:T(8,128)(2,1)S(1)} %get-tuple-element.29), channel_id=1, source_target_pairs={{1,2},{3,0},{5,6},{7,4},{9,10},{11,8},{13,14},{15,12},{17,18},{19,... | collective-permute-start | bytes 172040 | tf_op jit(solution)/shard_map/ppermute | solution.py:196
  15.7 5.9 %collective-permute-start.7 = (bf16[8,3584]{1,0:T(8,128)(2,1)S(1)}, bf16[8,3584]{1,0:T(8,128)(2,1)S(1)}, u32[]{:S(2)}, u32[]{:S(2)}) collective-permute-start(bf16[8,3584]{1,0:T(8,128)(2,1)S(1)} %get-tuple-element.35), channel_id=1, source_target_pairs={{0,3},{2,1},{4,7},{6,5},{8,11},{10,9},{12,15},{14,13},{16,19},{18,... | collective-permute-start | bytes 172040 | tf_op jit(solution)/shard_map/ppermute | solution.py:196
  17.7 4.0 %collective-permute-start.8 = (bf16[8,3584]{1,0:T(8,128)(2,1)S(1)}, bf16[8,3584]{1,0:T(8,128)(2,1)S(1)}, u32[]{:S(2)}, u32[]{:S(2)}) collective-permute-start(bf16[8,3584]{1,0:T(8,128)(2,1)S(1)} %get-tuple-element.36), channel_id=1, source_target_pairs={{0,5},{2,7},{4,1},{6,3},{8,13},{10,15},{12,9},{14,11},{16,21},{18,... | collective-permute-start | bytes 172040 | tf_op jit(solution)/shard_map/ppermute | solution.py:196
  19.0 4.6 %collective-permute-start.9 = (bf16[8,3584]{1,0:T(8,128)(2,1)S(1)}, bf16[8,3584]{1,0:T(8,128)(2,1)S(1)}, u32[]{:S(2)}, u32[]{:S(2)}) collective-permute-start(bf16[8,3584]{1,0:T(8,128)(2,1)S(1)} %get-tuple-element.34), channel_id=1, source_target_pairs={{0,7},{1,6},{2,5},{3,4},{4,3},{5,2},{6,1},{7,0},{8,15},{9,14},{10,... | collective-permute-start | bytes 172040 | tf_op jit(solution)/shard_map/ppermute | solution.py:196
  19.1 5.5 %collective-permute-start.10 = (bf16[8,3584]{1,0:T(8,128)(2,1)S(1)}, bf16[8,3584]{1,0:T(8,128)(2,1)S(1)}, u32[]{:S(2)}, u32[]{:S(2)}) collective-permute-start(bf16[8,3584]{1,0:T(8,128)(2,1)S(1)} %get-tuple-element.35), channel_id=1, source_target_pairs={{1,2},{3,0},{5,6},{7,4},{9,10},{11,8},{13,14},{15,12},{17,18},{19,... | collective-permute-start | bytes 172040 | tf_op jit(solution)/shard_map/ppermute | solution.py:196
  20.4 5.5 %collective-permute-start.11 = (bf16[8,3584]{1,0:T(8,128)(2,1)S(1)}, bf16[8,3584]{1,0:T(8,128)(2,1)S(1)}, u32[]{:S(2)}, u32[]{:S(2)}) collective-permute-start(bf16[8,3584]{1,0:T(8,128)(2,1)S(1)} %get-tuple-element.36), channel_id=1, source_target_pairs={{1,4},{3,6},{5,0},{7,2},{9,12},{11,14},{13,8},{15,10},{17,20},{19,... | collective-permute-start | bytes 172040 | tf_op jit(solution)/shard_map/ppermute | solution.py:196

commit v7 on v4

--- a/solution.py
+++ b/solution.py
@@ -15,34 +15,32 @@
 HBM = pl.BlockSpec(memory_space=pltpu.HBM)
 
 
-def targets(shards, new, old, ids, replica):
-    slots, rows = new.shape[1], ids.shape[1]
+def targets(shards, new_ref, old_ref, ids, replica):
+    slots, rows = new_ref.shape[0], ids.shape[1]
     device = lax.axis_index("expert")
-    down = lax.broadcasted_iota(jnp.int32, (slots, slots), 0)
-    across = lax.broadcasted_iota(jnp.int32, (slots, slots), 1)
-    new_full = jnp.broadcast_to(new, (slots, slots)).astype(jnp.float32)
-    source = jnp.where(new == old, across, across ^ 1)
-    away = source ^ (device // shards)
-    if shards == 1:
-        odd = device & 1
-        chip = away >> 1
-        step = sum(
-            jnp.where(chip == jnp.where(odd == 1, c_odd, c_even), k, 0)
-            for k, (c_even, c_odd) in enumerate(zip(*CHIP_STEPS))
-        )
-        away = (source & 1) | (step << 1)
-    base = (CAP * away).astype(jnp.float32)
-    diagonal = down == across
-    mine = jnp.sum(jnp.where(diagonal, new_full, 0.0), axis=1, keepdims=True)
-    line = jnp.sum(jnp.where(diagonal, base, 0.0), axis=1, keepdims=True)
-    same = jnp.where(mine == new_full, 1.0, 0.0)
-    count = jnp.sum(same, axis=1, keepdims=True).astype(jnp.int32)
-    rank = jnp.sum(jnp.where(across < down, same, 0.0), axis=1, keepdims=True).astype(jnp.int32)
-    expert = mine.astype(jnp.int32)
+    down = lax.broadcasted_iota(jnp.int32, (slots, rows), 0)
+    expert = jnp.zeros((slots, rows), jnp.int32)
+    line = jnp.zeros((slots, rows), jnp.int32)
+    for slot in range(slots):
+        source = jnp.where(new_ref[slot] == old_ref[slot], slot, slot ^ 1)
+        away = source ^ (device // shards)
+        if shards == 1:
+            chip = away >> 1
+            even, odd = [
+                sum(jnp.where(chip == c, k, 0) for k, c in enumerate(steps)) for steps in CHIP_STEPS
+            ]
+            away = (source & 1) | (jnp.where((device & 1) == 1, odd, even) << 1)
+        expert = jnp.where(down == slot, new_ref[slot], expert)
+        line = jnp.where(down == slot, CAP * away, line)
+    count = jnp.zeros((slots, rows), jnp.int32)
+    rank = jnp.zeros((slots, rows), jnp.int32)
+    for slot in range(slots):
+        same = expert == new_ref[slot]
+        count += jnp.where(same, 1, 0)
+        rank += jnp.where(same & (down > slot), 1, 0)
     chosen = []
     for k in range(ids.shape[0]):
-        wanted = replica[k : k + 1] & (count - 1)
-        hit = (ids[k : k + 1] == expert) & (rank == wanted)
+        hit = (ids[k : k + 1] == expert) & (rank == (replica[k : k + 1] & (count - 1)))
         chosen.append(jnp.where(hit, 1.0, 0.0))
     earlier = lax.broadcasted_iota(jnp.int32, (rows, rows), 0) < lax.broadcasted_iota(
         jnp.int32, (rows, rows), 1
@@ -53,6 +51,7 @@
         jnp.where(earlier, 1.0, 0.0).astype(jnp.bfloat16),
         preferred_element_type=jnp.float32,
     )
+    line = line.astype(jnp.float32)
     found = []
     for hit in chosen:
         place = jnp.where(position < CAP, line + position + 1.0, 0.0)
@@ -75,7 +74,7 @@
     copies = start_copies(sources, buffers, sems)
     for copy in copies[:-1]:
         copy.wait()
-    found = targets(shards, *[ref[...] for ref in buffers[:-1]])
+    found = targets(shards, *buffers[:2], *[ref[...] for ref in buffers[2:-1]])
     found_ref[...] = jnp.concatenate(found, axis=0)
     tokens_ref = buffers[-1]
     size = block_refs[0].shape[0]
@@ -121,8 +120,9 @@
     size = refs[0].shape[0]
     hidden = []
     for half, ref in enumerate((in_ref, twin_in_ref)):
-        gate = jnp.dot(rows, ref[0], preferred_element_type=jnp.float32)
-        up = jnp.dot(rows, ref[1], preferred_element_type=jnp.float32)
+        both = jnp.concatenate([ref[0], ref[1]], axis=1)
+        both = jnp.dot(rows, both, preferred_element_type=jnp.float32)
+        gate, up = both[:, : ref.shape[2]], both[:, ref.shape[2] :]
         value = jax.nn.silu(gate) * up
         if split:
             place = lax.broadcasted_iota(jnp.int32, value.shape, 0) // (size // 2)
@@ -182,8 +182,12 @@
     return jax.ShapeDtypeStruct(array.shape, array.dtype)
 
 
-def scratch_for(*arrays):
-    return [pltpu.VMEM(x.shape, x.dtype) for x in arrays] + [pltpu.SemaphoreType.DMA((len(arrays),))]
+def scratch_for(scalars, arrays):
+    return [
+        *[pltpu.SMEM(x.shape, x.dtype) for x in scalars],
+        *[pltpu.VMEM(x.shape, x.dtype) for x in arrays],
+        pltpu.SemaphoreType.DMA((len(scalars) + len(arrays),)),
+    ]
 
 
 def exchange(blocks, split, back=False):
@@ -214,7 +218,7 @@
     rows, width = tokens.shape
     hidden = w_down.shape[0]
     twin_in, twin_down = from_twin(w_in), from_twin(w_down)
-    operands = (new_place[None], old_place[None], expert_ids.T, replica.T, tokens)
+    operands = (new_place, old_place, expert_ids.T, replica.T, tokens)
     combine = combine.T
     block = jax.ShapeDtypeStruct((CAP * (2 if split else 1), width), jnp.bfloat16)
     found, *blocks = call(
@@ -223,7 +227,7 @@
         operands,
         2 * SLOTS * CAP * rows * width,
         [HBM] * len(operands),
-        scratch=scratch_for(*operands),
+        scratch=scratch_for(operands[:2], operands[2:]),
     )
     received = exchange([blocks[c // repeats] for c in range(chips)], split)
     own_in, own_down, weight = call(

time: 18.6 us -> 18.6 us (level)
  no operation moved by 1% of the time
where the time goes in v7:
time: 18.6 us; the launch traced here: 18.4 us
  starting transfers between devices  8.35 us (45%)
  waiting for transfers between devices  5.16 us (28%)
  Pallas kernels  4.91 us (26%)
    ppermute x6, starting transfers between devices, exchange(): result[k] = lax.ppermute(blocks[k], 'expert', pairs)  7.84 us
    ppermute x6, waiting for transfers between devices, exchange(): result[k] = lax.ppermute(blocks[k], 'expert', pairs)  5.15 us
    pallas_call x4, Pallas kernels, call(): pl.pallas_call(kernel, out_shape=outs, in_specs=arg_specs, out_specs=out_...  4.91 us
    ppermute x2, starting transfers between devices, from_twin(): return lax.ppermute(array, 'expert', pairs)  0.51 us
  transfers between devices with their start and end apart: 8, of which 4 were waited for; matrix products, arithmetic and copies ran while one was open for 0% of the time, Pallas kernels for 16%

profile of v7, /device:TPU:0, one launch (start us, length us, event | category | flops | bytes accessed | tf_op | source)
XLA Modules:
  0.0 18.4 jit_solution(5419960357779729816)
XLA Ops:
  0.0 0.5 %collective-permute-start = (bf16[2,3584,128]{2,1,0:T(8,128)(2,1)}, bf16[2,3584,128]{2,1,0:T(8,128)(2,1)S(1)}, u32[]{:S(2)}, u32[]{:S(2)}) collective-permute-start(bf16[2,3584,128]{2,1,0:T(8,128)(2,1)} %in_hbm.1), channel_id=1, source_target_pairs={{0,1},{1,0},{2,3},{3,2},{4,5},{5,4},{6,7},{7,6},{8,9},{9,8},{10,11... | collective-permute-start | bytes 5505032 | tf_op jit(solution)/shard_map/ppermute | solution.py:209
  0.5 0.1 collective-permute-start.1
  0.5 1.2 %shard_map.82 = (s32[2,16]{1,0:T(2,128)S(1)}, bf16[8,3584]{1,0:T(8,128)(2,1)S(1)}, bf16[8,3584]{1,0:T(8,128)(2,1)S(1)}, bf16[8,3584]{1,0:T(8,128)(2,1)S(1)}, bf16[8,3584]{1,0:T(8,128)(2,1)S(1)}) custom-call(s32[8]{0:T(128)} %refs_0_.1, s32[8]{0:T(128)} %refs_1_.1, s32[2,16]{1,0:T(2,128)} %bitcast.3, s32[2,16]{1,0:T(2,128)} %bitcast.4, bf16[16,3584]{1,0:T(8,128)(2,1)} %refs_4_.1), custom_call_target="tpu_custom_call" | custom-call | flops 3670016 | bytes 344512 | tf_op jit(solution)/shard_map/pallas_call | solution.py:170
  1.7 3.6 %collective-permute-start.2 = (bf16[8,3584]{1,0:T(8,128)(2,1)S(1)}, bf16[8,3584]{1,0:T(8,128)(2,1)S(1)}, u32[]{:S(2)}, u32[]{:S(2)}) collective-permute-start(bf16[8,3584]{1,0:T(8,128)(2,1)S(1)} %get-tuple-element.22), channel_id=1, source_target_pairs={{0,7},{1,6},{2,5},{3,4},{4,3},{5,2},{6,1},{7,0},{8,15},{9,14},{10,... | collective-permute-start | bytes 172040 | tf_op jit(solution)/shard_map/ppermute | solution.py:203
  5.3 0.6 %collective-permute-start.3 = (bf16[8,3584]{1,0:T(8,128)(2,1)S(1)}, bf16[8,3584]{1,0:T(8,128)(2,1)S(1)}, u32[]{:S(2)}, u32[]{:S(2)}) collective-permute-start(bf16[8,3584]{1,0:T(8,128)(2,1)S(1)} %get-tuple-element.23), channel_id=1, source_target_pairs={{0,3},{1,4},{2,1},{3,6},{4,7},{5,0},{6,5},{7,2},{8,11},{9,12},{10,... | collective-permute-start | bytes 172040 | tf_op jit(solution)/shard_map/ppermute | solution.py:203
  5.9 1.1 %collective-permute-start.4 = (bf16[8,3584]{1,0:T(8,128)(2,1)S(1)}, bf16[8,3584]{1,0:T(8,128)(2,1)S(1)}, u32[]{:S(2)}, u32[]{:S(2)}) collective-permute-start(bf16[8,3584]{1,0:T(8,128)(2,1)S(1)} %get-tuple-element.24), channel_id=1, source_target_pairs={{0,5},{1,2},{2,7},{3,0},{4,1},{5,6},{6,3},{7,4},{8,13},{9,10},{10,... | collective-permute-start | bytes 172040 | tf_op jit(solution)/shard_map/ppermute | solution.py:203
  7.0 1.8 %shard_map.83 = (bf16[2,3584,128]{2,1,0:T(8,128)(2,1)S(1)}, bf16[128,3584]{1,0:T(8,128)(2,1)S(1)}, bf16[32,32]{1,0:T(8,128)(2,1)S(1)}) custom-call(s32[2,16]{1,0:T(2,128)S(1)} %get-tuple-element.17.found_ref, f32[2,16]{1,0:T(2,128)} %bitcast.5, bf16[2,3584,128]{2,1,0:T(8,128)(2,1)} %in_hbm.1, bf16[128,3584]{1,0:T(8,128)(2,1)} %down_hbm.1), custom_call_target="tpu_custom_call" | custom-call | bytes 5507328 | tf_op jit(solution)/shard_map/pallas_call | solution.py:170
  8.8 0.0 collective-permute-done.2.refs_1_
  8.8 0.1 collective-permute-done.3.refs_2_
  8.9 1.2 %collective-permute-done.4.refs_3_ = bf16[8,3584]{1,0:T(8,128)(2,1)S(1)} collective-permute-done((bf16[8,3584]{1,0:T(8,128)(2,1)S(1)}, bf16[8,3584]{1,0:T(8,128)(2,1)S(1)}, u32[]{:S(2)}, u32[]{:S(2)}) %collective-permute-start.4) | collective-permute-done | bytes 57376 | tf_op jit(solution)/shard_map/ppermute | solution.py:203
  10.1 0.0 collective-permute-done.1.twin_down_ref
  10.1 0.0 collective-permute-done.twin_in_ref
  10.1 1.1 %shard_map.84 = (bf16[8,3584]{1,0:T(8,128)(2,1)S(1)}, bf16[8,3584]{1,0:T(8,128)(2,1)S(1)}, bf16[8,3584]{1,0:T(8,128)(2,1)S(1)}, bf16[8,3584]{1,0:T(8,128)(2,1)S(1)}) custom-call(bf16[2,3584,128]{2,1,0:T(8,128)(2,1)S(1)} %get-tuple-element.19.in_ref, bf16[128,3584]{1,0:T(8,128)(2,1)S(1)} %get-tuple-element.20.down_ref, ...), custom_call_target="tpu_custom_call" | custom-call | flops 176160768 | bytes 5963776 | tf_op jit(solution)/shard_map/pallas_call | solution.py:170
  11.2 0.8 %collective-permute-start.5 = (bf16[8,3584]{1,0:T(8,128)(2,1)S(1)}, bf16[8,3584]{1,0:T(8,128)(2,1)S(1)}, u32[]{:S(2)}, u32[]{:S(2)}) collective-permute-start(bf16[8,3584]{1,0:T(8,128)(2,1)S(1)} %get-tuple-element.26), channel_id=1, source_target_pairs={{7,0},{6,1},{5,2},{4,3},{3,4},{2,5},{1,6},{0,7},{15,8},{14,9},{13,... | collective-permute-start | bytes 172040 | tf_op jit(solution)/shard_map/ppermute | solution.py:203
  12.0 1.5 %collective-permute-start.6 = (bf16[8,3584]{1,0:T(8,128)(2,1)S(1)}, bf16[8,3584]{1,0:T(8,128)(2,1)S(1)}, u32[]{:S(2)}, u32[]{:S(2)}) collective-permute-start(bf16[8,3584]{1,0:T(8,128)(2,1)S(1)} %get-tuple-element.27), channel_id=1, source_target_pairs={{3,0},{4,1},{1,2},{6,3},{7,4},{0,5},{5,6},{2,7},{11,8},{12,9},{9,1... | collective-permute-start | bytes 172040 | tf_op jit(solution)/shard_map/ppermute | solution.py:203
  13.5 0.3 %collective-permute-start.7 = (bf16[8,3584]{1,0:T(8,128)(2,1)S(1)}, bf16[8,3584]{1,0:T(8,128)(2,1)S(1)}, u32[]{:S(2)}, u32[]{:S(2)}) collective-permute-start(bf16[8,3584]{1,0:T(8,128)(2,1)S(1)} %get-tuple-element.28), channel_id=1, source_target_pairs={{5,0},{2,1},{7,2},{0,3},{1,4},{6,5},{3,6},{4,7},{13,8},{10,9},{15,... | collective-permute-start | bytes 172040 | tf_op jit(solution)/shard_map/ppermute | solution.py:203
  13.7 2.4 %collective-permute-done.5.refs_1_ = bf16[8,3584]{1,0:T(8,128)(2,1)S(1)} collective-permute-done((bf16[8,3584]{1,0:T(8,128)(2,1)S(1)}, bf16[8,3584]{1,0:T(8,128)(2,1)S(1)}, u32[]{:S(2)}, u32[]{:S(2)}) %collective-permute-start.5) | collective-permute-done | bytes 57376 | tf_op jit(solution)/shard_map/ppermute | solution.py:203
  16.1 0.0 collective-permute-done.6.refs_2_
  16.1 1.5 %collective-permute-done.7.refs_3_ = bf16[8,3584]{1,0:T(8,128)(2,1)S(1)} collective-permute-done((bf16[8,3584]{1,0:T(8,128)(2,1)S(1)}, bf16[8,3584]{1,0:T(8,128)(2,1)S(1)}, u32[]{:S(2)}, u32[]{:S(2)}) %collective-permute-start.7) | collective-permute-done | bytes 57376 | tf_op jit(solution)/shard_map/ppermute | solution.py:203
  17.6 0.8 %shard_map.85 = bf16[16,3584]{1,0:T(8,128)(2,1)} custom-call(bf16[32,32]{1,0:T(8,128)(2,1)S(1)} %get-tuple-element.18.weight_ref, bf16[8,3584]{1,0:T(8,128)(2,1)S(1)} %get-tuple-element.25.refs_0_, bf16[8,3584]{1,0:T(8,128)(2,1)S(1)} %collective-permute-done.5.refs_1_, bf16[8,3584]{1,0:T(8,128)(2,1)S(1)} %collective-permute-done.6.refs_2_, ...), custom_call_target="tpu_custom_call" | custom-call | flops 7340032 | bytes 346112 | tf_op jit(solution)/shard_map/pallas_call | solution.py:170
Async XLA Ops:
  0.0 10.1 %collective-permute-start = (bf16[2,3584,128]{2,1,0:T(8,128)(2,1)}, bf16[2,3584,128]{2,1,0:T(8,128)(2,1)S(1)}, u32[]{:S(2)}, u32[]{:S(2)}) collective-permute-start(bf16[2,3584,128]{2,1,0:T(8,128)(2,1)} %in_hbm.1), channel_id=1, source_target_pairs={{0,1},{1,0},{2,3},{3,2},{4,5},{5,4},{6,7},{7,6},{8,9},{9,8},{10,11... | collective-permute-start | bytes 5505032 | tf_op jit(solution)/shard_map/ppermute | solution.py:209
  0.5 9.6 %collective-permute-start.1 = (bf16[128,3584]{1,0:T(8,128)(2,1)}, bf16[128,3584]{1,0:T(8,128)(2,1)S(1)}, u32[]{:S(2)}, u32[]{:S(2)}) collective-permute-start(bf16[128,3584]{1,0:T(8,128)(2,1)} %down_hbm.1), channel_id=1, source_target_pairs={{0,1},{1,0},{2,3},{3,2},{4,5},{5,4},{6,7},{7,6},{8,9},{9,8},{10,11... | collective-permute-start | bytes 2752520 | tf_op jit(solution)/shard_map/ppermute | solution.py:209
  1.7 7.1 %collective-permute-start.2 = (bf16[8,3584]{1,0:T(8,128)(2,1)S(1)}, bf16[8,3584]{1,0:T(8,128)(2,1)S(1)}, u32[]{:S(2)}, u32[]{:S(2)}) collective-permute-start(bf16[8,3584]{1,0:T(8,128)(2,1)S(1)} %get-tuple-element.22), channel_id=1, source_target_pairs={{0,7},{1,6},{2,5},{3,4},{4,3},{5,2},{6,1},{7,0},{8,15},{9,14},{10,... | collective-permute-start | bytes 172040 | tf_op jit(solution)/shard_map/ppermute | solution.py:203
  5.3 3.6 %collective-permute-start.3 = (bf16[8,3584]{1,0:T(8,128)(2,1)S(1)}, bf16[8,3584]{1,0:T(8,128)(2,1)S(1)}, u32[]{:S(2)}, u32[]{:S(2)}) collective-permute-start(bf16[8,3584]{1,0:T(8,128)(2,1)S(1)} %get-tuple-element.23), channel_id=1, source_target_pairs={{0,3},{1,4},{2,1},{3,6},{4,7},{5,0},{6,5},{7,2},{8,11},{9,12},{10,... | collective-permute-start | bytes 172040 | tf_op jit(solution)/shard_map/ppermute | solution.py:203
  5.9 4.2 %collective-permute-start.4 = (bf16[8,3584]{1,0:T(8,128)(2,1)S(1)}, bf16[8,3584]{1,0:T(8,128)(2,1)S(1)}, u32[]{:S(2)}, u32[]{:S(2)}) collective-permute-start(bf16[8,3584]{1,0:T(8,128)(2,1)S(1)} %get-tuple-element.24), channel_id=1, source_target_pairs={{0,5},{1,2},{2,7},{3,0},{4,1},{5,6},{6,3},{7,4},{8,13},{9,10},{10,... | collective-permute-start | bytes 172040 | tf_op jit(solution)/shard_map/ppermute | solution.py:203
  11.2 4.9 %collective-permute-start.5 = (bf16[8,3584]{1,0:T(8,128)(2,1)S(1)}, bf16[8,3584]{1,0:T(8,128)(2,1)S(1)}, u32[]{:S(2)}, u32[]{:S(2)}) collective-permute-start(bf16[8,3584]{1,0:T(8,128)(2,1)S(1)} %get-tuple-element.26), channel_id=1, source_target_pairs={{7,0},{6,1},{5,2},{4,3},{3,4},{2,5},{1,6},{0,7},{15,8},{14,9},{13,... | collective-permute-start | bytes 172040 | tf_op jit(solution)/shard_map/ppermute | solution.py:203
  12.0 4.1 %collective-permute-start.6 = (bf16[8,3584]{1,0:T(8,128)(2,1)S(1)}, bf16[8,3584]{1,0:T(8,128)(2,1)S(1)}, u32[]{:S(2)}, u32[]{:S(2)}) collective-permute-start(bf16[8,3584]{1,0:T(8,128)(2,1)S(1)} %get-tuple-element.27), channel_id=1, source_target_pairs={{3,0},{4,1},{1,2},{6,3},{7,4},{0,5},{5,6},{2,7},{11,8},{12,9},{9,1... | collective-permute-start | bytes 172040 | tf_op jit(solution)/shard_map/ppermute | solution.py:203
  13.5 4.1 %collective-permute-start.7 = (bf16[8,3584]{1,0:T(8,128)(2,1)S(1)}, bf16[8,3584]{1,0:T(8,128)(2,1)S(1)}, u32[]{:S(2)}, u32[]{:S(2)}) collective-permute-start(bf16[8,3584]{1,0:T(8,128)(2,1)S(1)} %get-tuple-element.28), channel_id=1, source_target_pairs={{5,0},{2,1},{7,2},{0,3},{1,4},{6,5},{3,6},{4,7},{13,8},{10,9},{15,... | collective-permute-start | bytes 172040 | tf_op jit(solution)/shard_map/ppermute | solution.py:203

commit v8 on v7

--- a/solution.py
+++ b/solution.py
@@ -113,24 +113,22 @@
     return jnp.concatenate([ref[...].astype(jnp.float32) for ref in refs], axis=0)
 
 
-def expert_kernel(split, in_ref, down_ref, twin_in_ref, twin_down_ref, *refs):
-    odd = lax.axis_index("expert") & 1
+def expert_kernel(split, in_ref, down_ref, *refs):
     count = len(refs) // 2
     rows = stack(refs[:count]).astype(jnp.bfloat16)
     size = refs[0].shape[0]
     hidden = []
-    for half, ref in enumerate((in_ref, twin_in_ref)):
-        both = jnp.concatenate([ref[0], ref[1]], axis=1)
-        both = jnp.dot(rows, both, preferred_element_type=jnp.float32)
-        gate, up = both[:, : ref.shape[2]], both[:, ref.shape[2] :]
+    for half in range(2):
+        gate = jnp.dot(rows, in_ref[half, 0], preferred_element_type=jnp.float32)
+        up = jnp.dot(rows, in_ref[half, 1], preferred_element_type=jnp.float32)
         value = jax.nn.silu(gate) * up
         if split:
             place = lax.broadcasted_iota(jnp.int32, value.shape, 0) // (size // 2)
-            value = jnp.where((place & 1) == (odd ^ half), value, 0.0)
+            value = jnp.where((place & 1) == half, value, 0.0)
         hidden.append(value.astype(jnp.bfloat16))
     piece = jnp.dot(
         jnp.concatenate(hidden, axis=1),
-        jnp.concatenate([down_ref[...], twin_down_ref[...]], axis=0),
+        down_ref[...].reshape(-1, down_ref.shape[2]),
         preferred_element_type=jnp.float32,
     )
     for b, out_ref in enumerate(refs[count:]):
@@ -204,9 +202,9 @@
     return result
 
 
-def from_twin(array):
-    pairs = [(i, i ^ 1) for i in range(lax.axis_size("expert"))]
-    return lax.ppermute(array, "expert", pairs)
+def of_chip(array):
+    pairs = [[i, i + 1] for i in range(0, lax.axis_size("expert"), 2)]
+    return lax.all_gather(array, "expert", axis_index_groups=pairs)
 
 
 def body(tokens, w_in, w_down, old_place, new_place, expert_ids, replica, combine):
@@ -217,7 +215,7 @@
     chips = devices // 2
     rows, width = tokens.shape
     hidden = w_down.shape[0]
-    twin_in, twin_down = from_twin(w_in), from_twin(w_down)
+    chip_in, chip_down = of_chip(w_in), of_chip(w_down)
     operands = (new_place, old_place, expert_ids.T, replica.T, tokens)
     combine = combine.T
     block = jax.ShapeDtypeStruct((CAP * (2 if split else 1), width), jnp.bfloat16)
@@ -230,14 +228,14 @@
         scratch=scratch_for(operands[:2], operands[2:]),
     )
     received = exchange([blocks[c // repeats] for c in range(chips)], split)
-    own_in, own_down, weight = call(
+    both_in, both_down, weight = call(
         prepare_kernel,
         [
-            shape_of(w_in),
-            shape_of(w_down),
+            shape_of(chip_in),
+            shape_of(chip_down),
             jax.ShapeDtypeStruct((2 * rows, SLOTS * CAP), jnp.bfloat16),
         ],
-        (found, combine, w_in, w_down),
+        (found, combine, chip_in, chip_down),
         0,
         [VMEM, HBM, HBM, HBM],
         scratch=[pltpu.VMEM(combine.shape, combine.dtype), pltpu.SemaphoreType.DMA((3,))],
@@ -245,7 +243,7 @@
     pieces = call(
         functools.partial(expert_kernel, split),
         [block] * chips,
-        (own_in, own_down, twin_in, twin_down, *received),
+        (both_in, both_down, *received),
         12 * chips * block.shape[0] * hidden * width,
     )
     returned = exchange(pieces, split, back=True)

time: 18.6 us -> 56.2 us (3.02)
  waiting for transfers between devices: 5.16 us -> 27.4 us
  between operations: 0.03 us -> 13.5 us
  starting transfers between devices: 8.35 us -> 9.52 us
  Pallas kernels: 4.91 us -> 5.67 us
    all_gather x0 -> x2, waiting for transfers between devices: none -> 23.1 us  [of_chip(): return lax.all_gather(array, 'expert', axis_index_groups=pairs)]
    ppermute x6, waiting for transfers between devices: 5.15 us -> 2.82 us  [exchange(): result[k] = lax.ppermute(blocks[k], 'expert', pairs)]
    ppermute x6, starting transfers between devices: 7.84 us -> 9.48 us  [exchange(): result[k] = lax.ppermute(blocks[k], 'expert', pairs)]
    unnamed x0 -> x2, waiting for transfers between devices: none -> 1.41 us
    pallas_call x4, Pallas kernels: 4.91 us -> 5.67 us  [call(): pl.pallas_call(kernel, out_shape=outs, in_specs=arg_specs, out_specs=out_...]
  transfers between devices with their start and end apart: 8 -> 8, of which waited for: 4 -> 5; matrix products, arithmetic and copies ran while one was open for 0% -> 0% of each run, Pallas kernels for 16% -> 7%
where the time goes in v8:
time: 56.2 us; the launch traced here: 56 us
  waiting for transfers between devices  27.4 us (49%)
  between operations  13.5 us (24%)
  starting transfers between devices  9.52 us (17%)
  Pallas kernels  5.67 us (10%)
    all_gather x2, waiting for transfers between devices, of_chip(): return lax.all_gather(array, 'expert', axis_index_groups=pairs)  23.1 us
    ppermute x6, starting transfers between devices, exchange(): result[k] = lax.ppermute(blocks[k], 'expert', pairs)  9.48 us
    pallas_call x4, Pallas kernels, call(): pl.pallas_call(kernel, out_shape=outs, in_specs=arg_specs, out_specs=out_...  5.67 us
    ppermute x6, waiting for transfers between devices, exchange(): result[k] = lax.ppermute(blocks[k], 'expert', pairs)  2.82 us
    unnamed x2, waiting for transfers between devices  1.41 us
  transfers between devices with their start and end apart: 8, of which 5 were waited for; matrix products, arithmetic and copies ran while one was open for 0% of the time, Pallas kernels for 7%

profile of v8, /device:TPU:0, one launch (start us, length us, event | category | flops | bytes accessed | tf_op | source)
XLA Modules:
  0.0 56.0 jit_solution(7815857516985233223)
XLA Ops:
  6.5 0.0 all-gather.7.cloned.1.call-start
  6.5 0.7 %all-gather.7.cloned.1.call-update = ((bf16[128,3584]{1,0:T(8,128)(2,1)}), bf16[256,3584]{1,0:T(8,128)(2,1)}) async-update(((), (), s32[]{:S(2)}) %all-gather.7.cloned.1.call-start, bf16[128,3584]{1,0:T(8,128)(2,1)} %param.10) | async-update | bytes 3670040
  7.3 0.0 all-gather.5.cloned.1.call-start
  7.3 0.7 %all-gather.5.cloned.1.call-update = ((bf16[2,3584,128]{2,1,0:T(8,128)(2,1)}), bf16[4,3584,128]{2,1,0:T(8,128)(2,1)}) async-update(((), (), s32[]{:S(2)}) %all-gather.5.cloned.1.call-start, bf16[2,3584,128]{2,1,0:T(8,128)(2,1)} %param.9) | async-update | bytes 7340056
  8.0 1.2 %shard_map.82 = (s32[2,16]{1,0:T(2,128)S(1)}, bf16[8,3584]{1,0:T(8,128)(2,1)S(1)}, bf16[8,3584]{1,0:T(8,128)(2,1)S(1)}, bf16[8,3584]{1,0:T(8,128)(2,1)S(1)}, bf16[8,3584]{1,0:T(8,128)(2,1)S(1)}) custom-call(s32[8]{0:T(128)} %refs_0_.1, s32[8]{0:T(128)} %refs_1_.1, s32[2,16]{1,0:T(2,128)} %bitcast.7, s32[2,16]{1,0:T(2,128)} %bitcast.8, bf16[16,3584]{1,0:T(8,128)(2,1)} %refs_4_.1), custom_call_target="tpu_custom_call" | custom-call | flops 3670016 | bytes 344512 | tf_op jit(solution)/shard_map/pallas_call | solution.py:168
  9.2 3.4 %collective-permute-start = (bf16[8,3584]{1,0:T(8,128)(2,1)S(1)}, bf16[8,3584]{1,0:T(8,128)(2,1)S(1)}, u32[]{:S(2)}, u32[]{:S(2)}) collective-permute-start(bf16[8,3584]{1,0:T(8,128)(2,1)S(1)} %get-tuple-element.22), channel_id=1, source_target_pairs={{0,7},{1,6},{2,5},{3,4},{4,3},{5,2},{6,1},{7,0},{8,15},{9,14},{10,... | collective-permute-start | bytes 172040 | tf_op jit(solution)/shard_map/ppermute | solution.py:201
  12.6 0.8 %collective-permute-start.1 = (bf16[8,3584]{1,0:T(8,128)(2,1)S(1)}, bf16[8,3584]{1,0:T(8,128)(2,1)S(1)}, u32[]{:S(2)}, u32[]{:S(2)}) collective-permute-start(bf16[8,3584]{1,0:T(8,128)(2,1)S(1)} %get-tuple-element.23), channel_id=1, source_target_pairs={{0,3},{1,4},{2,1},{3,6},{4,7},{5,0},{6,5},{7,2},{8,11},{9,12},{10,... | collective-permute-start | bytes 172040 | tf_op jit(solution)/shard_map/ppermute | solution.py:201
  13.4 0.9 %collective-permute-start.2 = (bf16[8,3584]{1,0:T(8,128)(2,1)S(1)}, bf16[8,3584]{1,0:T(8,128)(2,1)S(1)}, u32[]{:S(2)}, u32[]{:S(2)}) collective-permute-start(bf16[8,3584]{1,0:T(8,128)(2,1)S(1)} %get-tuple-element.24), channel_id=1, source_target_pairs={{0,5},{1,2},{2,7},{3,0},{4,1},{5,6},{6,3},{7,4},{8,13},{9,10},{10,... | collective-permute-start | bytes 172040 | tf_op jit(solution)/shard_map/ppermute | solution.py:201
  14.3 7.5 %all-gather.7.cloned.1.call-done = bf16[256,3584]{1,0:T(8,128)(2,1)} async-done(((bf16[128,3584]{1,0:T(8,128)(2,1)}), bf16[256,3584]{1,0:T(8,128)(2,1)}) %all-gather.7.cloned.1.call-update) | async-done | bytes 1835024 | tf_op jit(solution)/shard_map/all_gather | solution.py:207
  21.8 15.6 %all-gather.5.cloned.1.call-done = bf16[4,3584,128]{2,1,0:T(8,128)(2,1)} async-done(((bf16[2,3584,128]{2,1,0:T(8,128)(2,1)}), bf16[4,3584,128]{2,1,0:T(8,128)(2,1)}) %all-gather.5.cloned.1.call-update) | async-done | bytes 3670032 | tf_op jit(solution)/shard_map/all_gather | solution.py:207
  37.5 2.6 %shard_map.83 = (bf16[2,2,3584,128]{3,2,1,0:T(8,128)(2,1)S(1)}, bf16[2,128,3584]{2,1,0:T(8,128)(2,1)S(1)}, bf16[32,32]{1,0:T(8,128)(2,1)S(1)}) custom-call(s32[2,16]{1,0:T(2,128)S(1)} %get-tuple-element.17.found_ref, f32[2,16]{1,0:T(2,128)} %bitcast.9, bf16[2,2,3584,128]{3,2,1,0:T(8,128)(2,1)} %bitcast.5, bf16[2,128,3584]{2,1,0:T(8,128)(2,1)} %bitcast.6), custom_call_target="tpu_custom_call" | custom-call | bytes 11012352 | tf_op jit(solution)/shard_map/pallas_call | solution.py:168
  40.1 0.0 collective-permute-done.refs_1_
  40.1 0.0 collective-permute-done.1.refs_2_
  40.1 0.0 collective-permute-done.2.refs_3_
  40.2 1.0 %shard_map.84 = (bf16[8,3584]{1,0:T(8,128)(2,1)S(1)}, bf16[8,3584]{1,0:T(8,128)(2,1)S(1)}, bf16[8,3584]{1,0:T(8,128)(2,1)S(1)}, bf16[8,3584]{1,0:T(8,128)(2,1)S(1)}) custom-call(bf16[2,2,3584,128]{3,2,1,0:T(8,128)(2,1)S(1)} %get-tuple-element.19.in_ref, bf16[2,128,3584]{2,1,0:T(8,128)(2,1)S(1)} %get-tuple-element.20.down_ref, ...), custom_call_target="tpu_custom_call" | custom-call | flops 176160768 | bytes 5963776 | tf_op jit(solution)/shard_map/pallas_call | solution.py:168
  41.2 2.6 %collective-permute-start.3 = (bf16[8,3584]{1,0:T(8,128)(2,1)S(1)}, bf16[8,3584]{1,0:T(8,128)(2,1)S(1)}, u32[]{:S(2)}, u32[]{:S(2)}) collective-permute-start(bf16[8,3584]{1,0:T(8,128)(2,1)S(1)} %get-tuple-element.26), channel_id=1, source_target_pairs={{7,0},{6,1},{5,2},{4,3},{3,4},{2,5},{1,6},{0,7},{15,8},{14,9},{13,... | collective-permute-start | bytes 172040 | tf_op jit(solution)/shard_map/ppermute | solution.py:201
  43.7 0.4 collective-permute-start.4
  44.1 1.4 %collective-permute-start.5 = (bf16[8,3584]{1,0:T(8,128)(2,1)S(1)}, bf16[8,3584]{1,0:T(8,128)(2,1)S(1)}, u32[]{:S(2)}, u32[]{:S(2)}) collective-permute-start(bf16[8,3584]{1,0:T(8,128)(2,1)S(1)} %get-tuple-element.28), channel_id=1, source_target_pairs={{5,0},{2,1},{7,2},{0,3},{1,4},{6,5},{3,6},{4,7},{13,8},{10,9},{15,... | collective-permute-start | bytes 172040 | tf_op jit(solution)/shard_map/ppermute | solution.py:201
  45.5 0.5 collective-permute-done.3.refs_1_
  46.0 1.3 %collective-permute-done.4.refs_2_ = bf16[8,3584]{1,0:T(8,128)(2,1)S(1)} collective-permute-done((bf16[8,3584]{1,0:T(8,128)(2,1)S(1)}, bf16[8,3584]{1,0:T(8,128)(2,1)S(1)}, u32[]{:S(2)}, u32[]{:S(2)}) %collective-permute-start.4) | collective-permute-done | bytes 57376 | tf_op jit(solution)/shard_map/ppermute | solution.py:201
  47.4 1.0 %collective-permute-done.5.refs_3_ = bf16[8,3584]{1,0:T(8,128)(2,1)S(1)} collective-permute-done((bf16[8,3584]{1,0:T(8,128)(2,1)S(1)}, bf16[8,3584]{1,0:T(8,128)(2,1)S(1)}, u32[]{:S(2)}, u32[]{:S(2)}) %collective-permute-start.5) | collective-permute-done | bytes 57376 | tf_op jit(solution)/shard_map/ppermute | solution.py:201
  48.3 0.8 %shard_map.85 = bf16[16,3584]{1,0:T(8,128)(2,1)} custom-call(bf16[32,32]{1,0:T(8,128)(2,1)S(1)} %get-tuple-element.18.weight_ref, bf16[8,3584]{1,0:T(8,128)(2,1)S(1)} %get-tuple-element.25.refs_0_, bf16[8,3584]{1,0:T(8,128)(2,1)S(1)} %collective-permute-done.3.refs_1_, bf16[8,3584]{1,0:T(8,128)(2,1)S(1)} %collective-permute-done.4.refs_2_, ...), custom_call_target="tpu_custom_call" | custom-call | flops 7340032 | bytes 346112 | tf_op jit(solution)/shard_map/pallas_call | solution.py:168
Async XLA Ops:
  6.5 15.3 %all-gather.7.cloned.1.call-start = ((), (), s32[]{:S(2)}) async-start(), calls=%async_computation.1 | async-start | bytes 2752512 | tf_op jit(solution)/shard_map/all_gather | solution.py:207
  7.3 30.2 %all-gather.5.cloned.1.call-start = ((), (), s32[]{:S(2)}) async-start(), calls=%async_computation | async-start | bytes 5505024 | tf_op jit(solution)/shard_map/all_gather | solution.py:207
  9.2 30.9 %collective-permute-start = (bf16[8,3584]{1,0:T(8,128)(2,1)S(1)}, bf16[8,3584]{1,0:T(8,128)(2,1)S(1)}, u32[]{:S(2)}, u32[]{:S(2)}) collective-permute-start(bf16[8,3584]{1,0:T(8,128)(2,1)S(1)} %get-tuple-element.22), channel_id=1, source_target_pairs={{0,7},{1,6},{2,5},{3,4},{4,3},{5,2},{6,1},{7,0},{8,15},{9,14},{10,... | collective-permute-start | bytes 172040 | tf_op jit(solution)/shard_map/ppermute | solution.py:201
  12.6 27.6 %collective-permute-start.1 = (bf16[8,3584]{1,0:T(8,128)(2,1)S(1)}, bf16[8,3584]{1,0:T(8,128)(2,1)S(1)}, u32[]{:S(2)}, u32[]{:S(2)}) collective-permute-start(bf16[8,3584]{1,0:T(8,128)(2,1)S(1)} %get-tuple-element.23), channel_id=1, source_target_pairs={{0,3},{1,4},{2,1},{3,6},{4,7},{5,0},{6,5},{7,2},{8,11},{9,12},{10,... | collective-permute-start | bytes 172040 | tf_op jit(solution)/shard_map/ppermute | solution.py:201
  13.4 26.8 %collective-permute-start.2 = (bf16[8,3584]{1,0:T(8,128)(2,1)S(1)}, bf16[8,3584]{1,0:T(8,128)(2,1)S(1)}, u32[]{:S(2)}, u32[]{:S(2)}) collective-permute-start(bf16[8,3584]{1,0:T(8,128)(2,1)S(1)} %get-tuple-element.24), channel_id=1, source_target_pairs={{0,5},{1,2},{2,7},{3,0},{4,1},{5,6},{6,3},{7,4},{8,13},{9,10},{10,... | collective-permute-start | bytes 172040 | tf_op jit(solution)/shard_map/ppermute | solution.py:201
  41.2 4.9 %collective-permute-start.3 = (bf16[8,3584]{1,0:T(8,128)(2,1)S(1)}, bf16[8,3584]{1,0:T(8,128)(2,1)S(1)}, u32[]{:S(2)}, u32[]{:S(2)}) collective-permute-start(bf16[8,3584]{1,0:T(8,128)(2,1)S(1)} %get-tuple-element.26), channel_id=1, source_target_pairs={{7,0},{6,1},{5,2},{4,3},{3,4},{2,5},{1,6},{0,7},{15,8},{14,9},{13,... | collective-permute-start | bytes 172040 | tf_op jit(solution)/shard_map/ppermute | solution.py:201
  43.7 3.6 %collective-permute-start.4 = (bf16[8,3584]{1,0:T(8,128)(2,1)S(1)}, bf16[8,3584]{1,0:T(8,128)(2,1)S(1)}, u32[]{:S(2)}, u32[]{:S(2)}) collective-permute-start(bf16[8,3584]{1,0:T(8,128)(2,1)S(1)} %get-tuple-element.27), channel_id=1, source_target_pairs={{3,0},{4,1},{1,2},{6,3},{7,4},{0,5},{5,6},{2,7},{11,8},{12,9},{9,1... | collective-permute-start | bytes 172040 | tf_op jit(solution)/shard_map/ppermute | solution.py:201
  44.1 4.2 %collective-permute-start.5 = (bf16[8,3584]{1,0:T(8,128)(2,1)S(1)}, bf16[8,3584]{1,0:T(8,128)(2,1)S(1)}, u32[]{:S(2)}, u32[]{:S(2)}) collective-permute-start(bf16[8,3584]{1,0:T(8,128)(2,1)S(1)} %get-tuple-element.28), channel_id=1, source_target_pairs={{5,0},{2,1},{7,2},{0,3},{1,4},{6,5},{3,6},{4,7},{13,8},{10,9},{15,... | collective-permute-start | bytes 172040 | tf_op jit(solution)/shard_map/ppermute | solution.py:201
Sparse Core Ops, SparseCore 0:
  8.9 12.8 all-gather.6
  23.4 14.0 all-gather.4

commit v9 on v7

--- a/solution.py
+++ b/solution.py
@@ -113,28 +113,34 @@
     return jnp.concatenate([ref[...].astype(jnp.float32) for ref in refs], axis=0)
 
 
+def chunks(width, size=256):
+    step = size if width % size == 0 else width
+    return [slice(start, start + step) for start in range(0, width, step)]
+
+
 def expert_kernel(split, in_ref, down_ref, twin_in_ref, twin_down_ref, *refs):
     odd = lax.axis_index("expert") & 1
     count = len(refs) // 2
     rows = stack(refs[:count]).astype(jnp.bfloat16)
     size = refs[0].shape[0]
+    width, units = in_ref.shape[1:]
     hidden = []
     for half, ref in enumerate((in_ref, twin_in_ref)):
-        both = jnp.concatenate([ref[0], ref[1]], axis=1)
-        both = jnp.dot(rows, both, preferred_element_type=jnp.float32)
-        gate, up = both[:, : ref.shape[2]], both[:, ref.shape[2] :]
-        value = jax.nn.silu(gate) * up
+        both = jnp.zeros((rows.shape[0], 2 * units), jnp.float32)
+        for chunk in chunks(width):
+            part = jnp.concatenate([ref[0, chunk], ref[1, chunk]], axis=1)
+            both += jnp.dot(rows[:, chunk], part, preferred_element_type=jnp.float32)
+        value = jax.nn.silu(both[:, :units]) * both[:, units:]
         if split:
             place = lax.broadcasted_iota(jnp.int32, value.shape, 0) // (size // 2)
             value = jnp.where((place & 1) == (odd ^ half), value, 0.0)
         hidden.append(value.astype(jnp.bfloat16))
-    piece = jnp.dot(
-        jnp.concatenate(hidden, axis=1),
-        jnp.concatenate([down_ref[...], twin_down_ref[...]], axis=0),
-        preferred_element_type=jnp.float32,
-    )
-    for b, out_ref in enumerate(refs[count:]):
-        out_ref[...] = piece[size * b : size * (b + 1)].astype(jnp.bfloat16)
+    hidden = jnp.concatenate(hidden, axis=1)
+    for chunk in chunks(width):
+        part = jnp.concatenate([down_ref[:, chunk], twin_down_ref[:, chunk]], axis=0)
+        piece = jnp.dot(hidden, part, preferred_element_type=jnp.float32)
+        for b, out_ref in enumerate(refs[count:]):
+            out_ref[:, chunk] = piece[size * b : size * (b + 1)].astype(jnp.bfloat16)
 
 
 def mix_kernel(repeats, weight_ref, *refs):

time: 18.6 us -> 18.6 us (level)
  no operation moved by 1% of the time
where the time goes in v9:
time: 18.6 us; the launch traced here: 18.4 us
  starting transfers between devices  8.35 us (45%)
  waiting for transfers between devices  5.16 us (28%)
  Pallas kernels  4.91 us (26%)
    ppermute x6, starting transfers between devices, exchange(): result[k] = lax.ppermute(blocks[k], 'expert', pairs)  7.84 us
    ppermute x6, waiting for transfers between devices, exchange(): result[k] = lax.ppermute(blocks[k], 'expert', pairs)  5.15 us
    pallas_call x4, Pallas kernels, call(): pl.pallas_call(kernel, out_shape=outs, in_specs=arg_specs, out_specs=out_...  4.91 us
    ppermute x2, starting transfers between devices, from_twin(): return lax.ppermute(array, 'expert', pairs)  0.51 us
  transfers between devices with their start and end apart: 8, of which 4 were waited for; matrix products, arithmetic and copies ran while one was open for 0% of the time, Pallas kernels for 16%

profile of v9, /device:TPU:0, one launch (start us, length us, event | category | flops | bytes accessed | tf_op | source)
XLA Modules:
  0.0 18.4 jit_solution(16295927017563622251)
XLA Ops:
  0.0 0.5 %collective-permute-start = (bf16[2,3584,128]{2,1,0:T(8,128)(2,1)}, bf16[2,3584,128]{2,1,0:T(8,128)(2,1)S(1)}, u32[]{:S(2)}, u32[]{:S(2)}) collective-permute-start(bf16[2,3584,128]{2,1,0:T(8,128)(2,1)} %in_hbm.1), channel_id=1, source_target_pairs={{0,1},{1,0},{2,3},{3,2},{4,5},{5,4},{6,7},{7,6},{8,9},{9,8},{10,11... | collective-permute-start | bytes 5505032 | tf_op jit(solution)/shard_map/ppermute | solution.py:215
  0.5 0.1 collective-permute-start.1
  0.5 1.2 %shard_map.82 = (s32[2,16]{1,0:T(2,128)S(1)}, bf16[8,3584]{1,0:T(8,128)(2,1)S(1)}, bf16[8,3584]{1,0:T(8,128)(2,1)S(1)}, bf16[8,3584]{1,0:T(8,128)(2,1)S(1)}, bf16[8,3584]{1,0:T(8,128)(2,1)S(1)}) custom-call(s32[8]{0:T(128)} %refs_0_.1, s32[8]{0:T(128)} %refs_1_.1, s32[2,16]{1,0:T(2,128)} %bitcast.3, s32[2,16]{1,0:T(2,128)} %bitcast.4, bf16[16,3584]{1,0:T(8,128)(2,1)} %refs_4_.1), custom_call_target="tpu_custom_call" | custom-call | flops 3670016 | bytes 344512 | tf_op jit(solution)/shard_map/pallas_call | solution.py:176
  1.7 3.6 %collective-permute-start.2 = (bf16[8,3584]{1,0:T(8,128)(2,1)S(1)}, bf16[8,3584]{1,0:T(8,128)(2,1)S(1)}, u32[]{:S(2)}, u32[]{:S(2)}) collective-permute-start(bf16[8,3584]{1,0:T(8,128)(2,1)S(1)} %get-tuple-element.22), channel_id=1, source_target_pairs={{0,7},{1,6},{2,5},{3,4},{4,3},{5,2},{6,1},{7,0},{8,15},{9,14},{10,... | collective-permute-start | bytes 172040 | tf_op jit(solution)/shard_map/ppermute | solution.py:209
  5.3 0.6 %collective-permute-start.3 = (bf16[8,3584]{1,0:T(8,128)(2,1)S(1)}, bf16[8,3584]{1,0:T(8,128)(2,1)S(1)}, u32[]{:S(2)}, u32[]{:S(2)}) collective-permute-start(bf16[8,3584]{1,0:T(8,128)(2,1)S(1)} %get-tuple-element.23), channel_id=1, source_target_pairs={{0,3},{1,4},{2,1},{3,6},{4,7},{5,0},{6,5},{7,2},{8,11},{9,12},{10,... | collective-permute-start | bytes 172040 | tf_op jit(solution)/shard_map/ppermute | solution.py:209
  5.9 1.1 %collective-permute-start.4 = (bf16[8,3584]{1,0:T(8,128)(2,1)S(1)}, bf16[8,3584]{1,0:T(8,128)(2,1)S(1)}, u32[]{:S(2)}, u32[]{:S(2)}) collective-permute-start(bf16[8,3584]{1,0:T(8,128)(2,1)S(1)} %get-tuple-element.24), channel_id=1, source_target_pairs={{0,5},{1,2},{2,7},{3,0},{4,1},{5,6},{6,3},{7,4},{8,13},{9,10},{10,... | collective-permute-start | bytes 172040 | tf_op jit(solution)/shard_map/ppermute | solution.py:209
  7.0 1.8 %shard_map.83 = (bf16[2,3584,128]{2,1,0:T(8,128)(2,1)S(1)}, bf16[128,3584]{1,0:T(8,128)(2,1)S(1)}, bf16[32,32]{1,0:T(8,128)(2,1)S(1)}) custom-call(s32[2,16]{1,0:T(2,128)S(1)} %get-tuple-element.17.found_ref, f32[2,16]{1,0:T(2,128)} %bitcast.5, bf16[2,3584,128]{2,1,0:T(8,128)(2,1)} %in_hbm.1, bf16[128,3584]{1,0:T(8,128)(2,1)} %down_hbm.1), custom_call_target="tpu_custom_call" | custom-call | bytes 5507328 | tf_op jit(solution)/shard_map/pallas_call | solution.py:176
  8.8 0.0 collective-permute-done.2.refs_1_
  8.8 0.1 collective-permute-done.3.refs_2_
  8.9 1.2 %collective-permute-done.4.refs_3_ = bf16[8,3584]{1,0:T(8,128)(2,1)S(1)} collective-permute-done((bf16[8,3584]{1,0:T(8,128)(2,1)S(1)}, bf16[8,3584]{1,0:T(8,128)(2,1)S(1)}, u32[]{:S(2)}, u32[]{:S(2)}) %collective-permute-start.4) | collective-permute-done | bytes 57376 | tf_op jit(solution)/shard_map/ppermute | solution.py:209
  10.1 0.0 collective-permute-done.1.twin_down_ref
  10.1 0.0 collective-permute-done.twin_in_ref
  10.1 1.1 %shard_map.84 = (bf16[8,3584]{1,0:T(8,128)(2,1)S(1)}, bf16[8,3584]{1,0:T(8,128)(2,1)S(1)}, bf16[8,3584]{1,0:T(8,128)(2,1)S(1)}, bf16[8,3584]{1,0:T(8,128)(2,1)S(1)}) custom-call(bf16[2,3584,128]{2,1,0:T(8,128)(2,1)S(1)} %get-tuple-element.19.in_ref, bf16[128,3584]{1,0:T(8,128)(2,1)S(1)} %get-tuple-element.20.down_ref, ...), custom_call_target="tpu_custom_call" | custom-call | flops 176160768 | bytes 5963776 | tf_op jit(solution)/shard_map/pallas_call | solution.py:176
  11.2 0.8 %collective-permute-start.5 = (bf16[8,3584]{1,0:T(8,128)(2,1)S(1)}, bf16[8,3584]{1,0:T(8,128)(2,1)S(1)}, u32[]{:S(2)}, u32[]{:S(2)}) collective-permute-start(bf16[8,3584]{1,0:T(8,128)(2,1)S(1)} %get-tuple-element.26), channel_id=1, source_target_pairs={{7,0},{6,1},{5,2},{4,3},{3,4},{2,5},{1,6},{0,7},{15,8},{14,9},{13,... | collective-permute-start | bytes 172040 | tf_op jit(solution)/shard_map/ppermute | solution.py:209
  12.0 1.5 %collective-permute-start.6 = (bf16[8,3584]{1,0:T(8,128)(2,1)S(1)}, bf16[8,3584]{1,0:T(8,128)(2,1)S(1)}, u32[]{:S(2)}, u32[]{:S(2)}) collective-permute-start(bf16[8,3584]{1,0:T(8,128)(2,1)S(1)} %get-tuple-element.27), channel_id=1, source_target_pairs={{3,0},{4,1},{1,2},{6,3},{7,4},{0,5},{5,6},{2,7},{11,8},{12,9},{9,1... | collective-permute-start | bytes 172040 | tf_op jit(solution)/shard_map/ppermute | solution.py:209
  13.5 0.3 %collective-permute-start.7 = (bf16[8,3584]{1,0:T(8,128)(2,1)S(1)}, bf16[8,3584]{1,0:T(8,128)(2,1)S(1)}, u32[]{:S(2)}, u32[]{:S(2)}) collective-permute-start(bf16[8,3584]{1,0:T(8,128)(2,1)S(1)} %get-tuple-element.28), channel_id=1, source_target_pairs={{5,0},{2,1},{7,2},{0,3},{1,4},{6,5},{3,6},{4,7},{13,8},{10,9},{15,... | collective-permute-start | bytes 172040 | tf_op jit(solution)/shard_map/ppermute | solution.py:209
  13.7 2.4 %collective-permute-done.5.refs_1_ = bf16[8,3584]{1,0:T(8,128)(2,1)S(1)} collective-permute-done((bf16[8,3584]{1,0:T(8,128)(2,1)S(1)}, bf16[8,3584]{1,0:T(8,128)(2,1)S(1)}, u32[]{:S(2)}, u32[]{:S(2)}) %collective-permute-start.5) | collective-permute-done | bytes 57376 | tf_op jit(solution)/shard_map/ppermute | solution.py:209
  16.1 0.0 collective-permute-done.6.refs_2_
  16.1 1.5 %collective-permute-done.7.refs_3_ = bf16[8,3584]{1,0:T(8,128)(2,1)S(1)} collective-permute-done((bf16[8,3584]{1,0:T(8,128)(2,1)S(1)}, bf16[8,3584]{1,0:T(8,128)(2,1)S(1)}, u32[]{:S(2)}, u32[]{:S(2)}) %collective-permute-start.7) | collective-permute-done | bytes 57376 | tf_op jit(solution)/shard_map/ppermute | solution.py:209
  17.6 0.8 %shard_map.85 = bf16[16,3584]{1,0:T(8,128)(2,1)} custom-call(bf16[32,32]{1,0:T(8,128)(2,1)S(1)} %get-tuple-element.18.weight_ref, bf16[8,3584]{1,0:T(8,128)(2,1)S(1)} %get-tuple-element.25.refs_0_, bf16[8,3584]{1,0:T(8,128)(2,1)S(1)} %collective-permute-done.5.refs_1_, bf16[8,3584]{1,0:T(8,128)(2,1)S(1)} %collective-permute-done.6.refs_2_, ...), custom_call_target="tpu_custom_call" | custom-call | flops 7340032 | bytes 346112 | tf_op jit(solution)/shard_map/pallas_call | solution.py:176
Async XLA Ops:
  0.0 10.1 %collective-permute-start = (bf16[2,3584,128]{2,1,0:T(8,128)(2,1)}, bf16[2,3584,128]{2,1,0:T(8,128)(2,1)S(1)}, u32[]{:S(2)}, u32[]{:S(2)}) collective-permute-start(bf16[2,3584,128]{2,1,0:T(8,128)(2,1)} %in_hbm.1), channel_id=1, source_target_pairs={{0,1},{1,0},{2,3},{3,2},{4,5},{5,4},{6,7},{7,6},{8,9},{9,8},{10,11... | collective-permute-start | bytes 5505032 | tf_op jit(solution)/shard_map/ppermute | solution.py:215
  0.5 9.6 %collective-permute-start.1 = (bf16[128,3584]{1,0:T(8,128)(2,1)}, bf16[128,3584]{1,0:T(8,128)(2,1)S(1)}, u32[]{:S(2)}, u32[]{:S(2)}) collective-permute-start(bf16[128,3584]{1,0:T(8,128)(2,1)} %down_hbm.1), channel_id=1, source_target_pairs={{0,1},{1,0},{2,3},{3,2},{4,5},{5,4},{6,7},{7,6},{8,9},{9,8},{10,11... | collective-permute-start | bytes 2752520 | tf_op jit(solution)/shard_map/ppermute | solution.py:215
  1.7 7.1 %collective-permute-start.2 = (bf16[8,3584]{1,0:T(8,128)(2,1)S(1)}, bf16[8,3584]{1,0:T(8,128)(2,1)S(1)}, u32[]{:S(2)}, u32[]{:S(2)}) collective-permute-start(bf16[8,3584]{1,0:T(8,128)(2,1)S(1)} %get-tuple-element.22), channel_id=1, source_target_pairs={{0,7},{1,6},{2,5},{3,4},{4,3},{5,2},{6,1},{7,0},{8,15},{9,14},{10,... | collective-permute-start | bytes 172040 | tf_op jit(solution)/shard_map/ppermute | solution.py:209
  5.3 3.6 %collective-permute-start.3 = (bf16[8,3584]{1,0:T(8,128)(2,1)S(1)}, bf16[8,3584]{1,0:T(8,128)(2,1)S(1)}, u32[]{:S(2)}, u32[]{:S(2)}) collective-permute-start(bf16[8,3584]{1,0:T(8,128)(2,1)S(1)} %get-tuple-element.23), channel_id=1, source_target_pairs={{0,3},{1,4},{2,1},{3,6},{4,7},{5,0},{6,5},{7,2},{8,11},{9,12},{10,... | collective-permute-start | bytes 172040 | tf_op jit(solution)/shard_map/ppermute | solution.py:209
  5.9 4.2 %collective-permute-start.4 = (bf16[8,3584]{1,0:T(8,128)(2,1)S(1)}, bf16[8,3584]{1,0:T(8,128)(2,1)S(1)}, u32[]{:S(2)}, u32[]{:S(2)}) collective-permute-start(bf16[8,3584]{1,0:T(8,128)(2,1)S(1)} %get-tuple-element.24), channel_id=1, source_target_pairs={{0,5},{1,2},{2,7},{3,0},{4,1},{5,6},{6,3},{7,4},{8,13},{9,10},{10,... | collective-permute-start | bytes 172040 | tf_op jit(solution)/shard_map/ppermute | solution.py:209
  11.2 4.9 %collective-permute-start.5 = (bf16[8,3584]{1,0:T(8,128)(2,1)S(1)}, bf16[8,3584]{1,0:T(8,128)(2,1)S(1)}, u32[]{:S(2)}, u32[]{:S(2)}) collective-permute-start(bf16[8,3584]{1,0:T(8,128)(2,1)S(1)} %get-tuple-element.26), channel_id=1, source_target_pairs={{7,0},{6,1},{5,2},{4,3},{3,4},{2,5},{1,6},{0,7},{15,8},{14,9},{13,... | collective-permute-start | bytes 172040 | tf_op jit(solution)/shard_map/ppermute | solution.py:209
  12.0 4.1 %collective-permute-start.6 = (bf16[8,3584]{1,0:T(8,128)(2,1)S(1)}, bf16[8,3584]{1,0:T(8,128)(2,1)S(1)}, u32[]{:S(2)}, u32[]{:S(2)}) collective-permute-start(bf16[8,3584]{1,0:T(8,128)(2,1)S(1)} %get-tuple-element.27), channel_id=1, source_target_pairs={{3,0},{4,1},{1,2},{6,3},{7,4},{0,5},{5,6},{2,7},{11,8},{12,9},{9,1... | collective-permute-start | bytes 172040 | tf_op jit(solution)/shard_map/ppermute | solution.py:209
  13.5 4.1 %collective-permute-start.7 = (bf16[8,3584]{1,0:T(8,128)(2,1)S(1)}, bf16[8,3584]{1,0:T(8,128)(2,1)S(1)}, u32[]{:S(2)}, u32[]{:S(2)}) collective-permute-start(bf16[8,3584]{1,0:T(8,128)(2,1)S(1)} %get-tuple-element.28), channel_id=1, source_target_pairs={{5,0},{2,1},{7,2},{0,3},{1,4},{6,5},{3,6},{4,7},{13,8},{10,9},{15,... | collective-permute-start | bytes 172040 | tf_op jit(solution)/shard_map/ppermute | solution.py:209

commit v10 on v7

--- a/solution.py
+++ b/solution.py
@@ -113,27 +113,31 @@
     return jnp.concatenate([ref[...].astype(jnp.float32) for ref in refs], axis=0)
 
 
-def expert_kernel(split, in_ref, down_ref, twin_in_ref, twin_down_ref, *refs):
+def hidden_kernel(split, in_ref, twin_in_ref, *refs):
+    *refs, out_ref = refs
     odd = lax.axis_index("expert") & 1
-    count = len(refs) // 2
-    rows = stack(refs[:count]).astype(jnp.bfloat16)
-    size = refs[0].shape[0]
+    rows = stack(refs).astype(jnp.bfloat16)
+    half_size = refs[0].shape[0] // 2
     hidden = []
     for half, ref in enumerate((in_ref, twin_in_ref)):
-        both = jnp.concatenate([ref[0], ref[1]], axis=1)
-        both = jnp.dot(rows, both, preferred_element_type=jnp.float32)
-        gate, up = both[:, : ref.shape[2]], both[:, ref.shape[2] :]
+        gate = jnp.dot(rows, ref[0], preferred_element_type=jnp.float32)
+        up = jnp.dot(rows, ref[1], preferred_element_type=jnp.float32)
         value = jax.nn.silu(gate) * up
         if split:
-            place = lax.broadcasted_iota(jnp.int32, value.shape, 0) // (size // 2)
+            place = lax.broadcasted_iota(jnp.int32, value.shape, 0) // half_size
             value = jnp.where((place & 1) == (odd ^ half), value, 0.0)
         hidden.append(value.astype(jnp.bfloat16))
+    out_ref[...] = jnp.concatenate(hidden, axis=1)
+
+
+def down_kernel(hidden_ref, down_ref, twin_down_ref, *refs):
     piece = jnp.dot(
-        jnp.concatenate(hidden, axis=1),
+        hidden_ref[...],
         jnp.concatenate([down_ref[...], twin_down_ref[...]], axis=0),
         preferred_element_type=jnp.float32,
     )
-    for b, out_ref in enumerate(refs[count:]):
+    size = refs[0].shape[0]
+    for b, out_ref in enumerate(refs):
         out_ref[...] = piece[size * b : size * (b + 1)].astype(jnp.bfloat16)
 
 
@@ -217,7 +221,7 @@
     chips = devices // 2
     rows, width = tokens.shape
     hidden = w_down.shape[0]
-    twin_in, twin_down = from_twin(w_in), from_twin(w_down)
+    twin_in = from_twin(w_in)
     operands = (new_place, old_place, expert_ids.T, replica.T, tokens)
     combine = combine.T
     block = jax.ShapeDtypeStruct((CAP * (2 if split else 1), width), jnp.bfloat16)
@@ -230,6 +234,7 @@
         scratch=scratch_for(operands[:2], operands[2:]),
     )
     received = exchange([blocks[c // repeats] for c in range(chips)], split)
+    twin_down = from_twin(lax.optimization_barrier((w_down, found))[0])
     own_in, own_down, weight = call(
         prepare_kernel,
         [
@@ -242,11 +247,17 @@
         [VMEM, HBM, HBM, HBM],
         scratch=[pltpu.VMEM(combine.shape, combine.dtype), pltpu.SemaphoreType.DMA((3,))],
     )
+    units = call(
+        functools.partial(hidden_kernel, split),
+        jax.ShapeDtypeStruct((chips * block.shape[0], 2 * hidden), jnp.bfloat16),
+        (own_in, twin_in, *received),
+        800 * chips * block.shape[0] * hidden * width,
+    )
     pieces = call(
-        functools.partial(expert_kernel, split),
+        down_kernel,
         [block] * chips,
-        (own_in, own_down, twin_in, twin_down, *received),
-        12 * chips * block.shape[0] * hidden * width,
+        (units, own_down, twin_down),
+        4 * chips * block.shape[0] * hidden * width,
     )
     returned = exchange(pieces, split, back=True)
     parts = 4 if width % 512 == 0 else 1

time: 18.6 us -> 18 us (0.968)
  waiting for transfers between devices: 5.16 us -> 4.36 us
  starting transfers between devices: 8.35 us -> 8.63 us
    ppermute x6, waiting for transfers between devices: 5.15 us -> 4.35 us  [exchange(): result[k] = lax.ppermute(blocks[k], 'expert', pairs)]
    ppermute x6, starting transfers between devices: 7.84 us -> 8.17 us  [exchange(): result[k] = lax.ppermute(blocks[k], 'expert', pairs)]
    pallas_call x4 -> x5, Pallas kernels: 4.91 us -> 4.82 us  [call(): pl.pallas_call(kernel, out_shape=outs, in_specs=arg_specs, out_specs=out_...]
  transfers between devices with their start and end apart: 8 -> 8, of which waited for: 4 -> 5; matrix products, arithmetic and copies ran while one was open for 0% -> 0% of each run, Pallas kernels for 16% -> 20%
where the time goes in v10:
time: 18 us; the launch traced here: 17.9 us
  starting transfers between devices  8.63 us (48%)
  Pallas kernels  4.82 us (27%)
  waiting for transfers between devices  4.36 us (24%)
    ppermute x6, starting transfers between devices, exchange(): result[k] = lax.ppermute(blocks[k], 'expert', pairs)  8.17 us
    pallas_call x5, Pallas kernels, call(): pl.pallas_call(kernel, out_shape=outs, in_specs=arg_specs, out_specs=out_...  4.82 us
    ppermute x6, waiting for transfers between devices, exchange(): result[k] = lax.ppermute(blocks[k], 'expert', pairs)  4.35 us
    ppermute x2, starting transfers between devices, from_twin(): return lax.ppermute(array, 'expert', pairs)  0.46 us
  transfers between devices with their start and end apart: 8, of which 5 were waited for; matrix products, arithmetic and copies ran while one was open for 0% of the time, Pallas kernels for 20%

profile of v10, /device:TPU:0, one launch (start us, length us, event | category | flops | bytes accessed | tf_op | source)
XLA Modules:
  0.0 17.9 jit_solution(6948569938484071599)
XLA Ops:
  0.0 0.5 %collective-permute-start = (bf16[2,3584,128]{2,1,0:T(8,128)(2,1)}, bf16[2,3584,128]{2,1,0:T(8,128)(2,1)S(1)}, u32[]{:S(2)}, u32[]{:S(2)}) collective-permute-start(bf16[2,3584,128]{2,1,0:T(8,128)(2,1)} %in_hbm.1), channel_id=1, source_target_pairs={{0,1},{1,0},{2,3},{3,2},{4,5},{5,4},{6,7},{7,6},{8,9},{9,8},{10,11... | collective-permute-start | bytes 5505032 | tf_op jit(solution)/shard_map/ppermute | solution.py:213
  0.5 1.2 %shard_map.82 = (s32[2,16]{1,0:T(2,128)S(1)}, bf16[8,3584]{1,0:T(8,128)(2,1)S(1)}, bf16[8,3584]{1,0:T(8,128)(2,1)S(1)}, bf16[8,3584]{1,0:T(8,128)(2,1)S(1)}, bf16[8,3584]{1,0:T(8,128)(2,1)S(1)}) custom-call(s32[8]{0:T(128)} %refs_0_.1, s32[8]{0:T(128)} %refs_1_.1, s32[2,16]{1,0:T(2,128)} %bitcast.3, s32[2,16]{1,0:T(2,128)} %bitcast.4, bf16[16,3584]{1,0:T(8,128)(2,1)} %refs_4_.1), custom_call_target="tpu_custom_call" | custom-call | flops 3670016 | bytes 344512 | tf_op jit(solution)/shard_map/pallas_call | solution.py:174
  1.6 3.6 %collective-permute-start.1 = (bf16[8,3584]{1,0:T(8,128)(2,1)S(1)}, bf16[8,3584]{1,0:T(8,128)(2,1)S(1)}, u32[]{:S(2)}, u32[]{:S(2)}) collective-permute-start(bf16[8,3584]{1,0:T(8,128)(2,1)S(1)} %get-tuple-element.22), channel_id=1, source_target_pairs={{0,7},{1,6},{2,5},{3,4},{4,3},{5,2},{6,1},{7,0},{8,15},{9,14},{10,... | collective-permute-start | bytes 172040 | tf_op jit(solution)/shard_map/ppermute | solution.py:207
  5.2 0.1 collective-permute-start.2
  5.4 1.6 %collective-permute-start.3 = (bf16[8,3584]{1,0:T(8,128)(2,1)S(1)}, bf16[8,3584]{1,0:T(8,128)(2,1)S(1)}, u32[]{:S(2)}, u32[]{:S(2)}) collective-permute-start(bf16[8,3584]{1,0:T(8,128)(2,1)S(1)} %get-tuple-element.24), channel_id=1, source_target_pairs={{0,5},{1,2},{2,7},{3,0},{4,1},{5,6},{6,3},{7,4},{8,13},{9,10},{10,... | collective-permute-start | bytes 172040 | tf_op jit(solution)/shard_map/ppermute | solution.py:207
  7.0 0.0 collective-permute-start.4
  7.0 1.8 %shard_map.83 = (bf16[2,3584,128]{2,1,0:T(8,128)(2,1)S(1)}, bf16[128,3584]{1,0:T(8,128)(2,1)S(1)}, bf16[32,32]{1,0:T(8,128)(2,1)S(1)}) custom-call(s32[2,16]{1,0:T(2,128)S(1)} %get-tuple-element.18.found_ref, f32[2,16]{1,0:T(2,128)} %bitcast.5, bf16[2,3584,128]{2,1,0:T(8,128)(2,1)} %in_hbm.1, bf16[128,3584]{1,0:T(8,128)(2,1)} %down_hbm.1), custom_call_target="tpu_custom_call" | custom-call | bytes 5507328 | tf_op jit(solution)/shard_map/pallas_call | solution.py:174
  8.8 0.0 collective-permute-done.1.refs_1_
  8.8 0.1 collective-permute-done.2.refs_2_
  8.8 0.7 %collective-permute-done.3.refs_3_ = bf16[8,3584]{1,0:T(8,128)(2,1)S(1)} collective-permute-done((bf16[8,3584]{1,0:T(8,128)(2,1)S(1)}, bf16[8,3584]{1,0:T(8,128)(2,1)S(1)}, u32[]{:S(2)}, u32[]{:S(2)}) %collective-permute-start.3) | collective-permute-done | bytes 57376 | tf_op jit(solution)/shard_map/ppermute | solution.py:207
  9.6 0.0 collective-permute-done.twin_in_ref
  9.6 0.6 %shard_map.84.hidden_ref = bf16[32,256]{1,0:T(8,128)(2,1)S(1)} custom-call(bf16[2,3584,128]{2,1,0:T(8,128)(2,1)S(1)} %get-tuple-element.20.in_ref, bf16[2,3584,128]{2,1,0:T(8,128)(2,1)S(1)} %collective-permute-done.twin_in_ref, bf16[8,3584]{1,0:T(8,128)(2,1)S(1)} %get-tuple-element.21.refs_0_, bf16[8,3584]{1,0:T(8,128)(2,1)S(1)} %collective-permute-done.1.refs_1_, ...), custom_call_target="tpu_custom_call" | custom-call | flops 11744051200 | bytes 3915776 | tf_op jit(solution)/shard_map/pallas_call | solution.py:174
  10.2 0.0 collective-permute-done.4.twin_down_ref
  10.2 0.4 %shard_map.85 = (bf16[8,3584]{1,0:T(8,128)(2,1)S(1)}, bf16[8,3584]{1,0:T(8,128)(2,1)S(1)}, bf16[8,3584]{1,0:T(8,128)(2,1)S(1)}, bf16[8,3584]{1,0:T(8,128)(2,1)S(1)}) custom-call(bf16[32,256]{1,0:T(8,128)(2,1)S(1)} %shard_map.84.hidden_ref, bf16[128,3584]{1,0:T(8,128)(2,1)S(1)} %get-tuple-element.25.down_ref, ...), custom_call_target="tpu_custom_call" | custom-call | flops 58720256 | bytes 2080768 | tf_op jit(solution)/shard_map/pallas_call | solution.py:174
  10.6 1.1 %collective-permute-start.5 = (bf16[8,3584]{1,0:T(8,128)(2,1)S(1)}, bf16[8,3584]{1,0:T(8,128)(2,1)S(1)}, u32[]{:S(2)}, u32[]{:S(2)}) collective-permute-start(bf16[8,3584]{1,0:T(8,128)(2,1)S(1)} %get-tuple-element.28), channel_id=1, source_target_pairs={{7,0},{6,1},{5,2},{4,3},{3,4},{2,5},{1,6},{0,7},{15,8},{14,9},{13,... | collective-permute-start | bytes 172040 | tf_op jit(solution)/shard_map/ppermute | solution.py:207
  11.7 1.3 %collective-permute-start.6 = (bf16[8,3584]{1,0:T(8,128)(2,1)S(1)}, bf16[8,3584]{1,0:T(8,128)(2,1)S(1)}, u32[]{:S(2)}, u32[]{:S(2)}) collective-permute-start(bf16[8,3584]{1,0:T(8,128)(2,1)S(1)} %get-tuple-element.29), channel_id=1, source_target_pairs={{3,0},{4,1},{1,2},{6,3},{7,4},{0,5},{5,6},{2,7},{11,8},{12,9},{9,1... | collective-permute-start | bytes 172040 | tf_op jit(solution)/shard_map/ppermute | solution.py:207
  12.9 0.5 %collective-permute-start.7 = (bf16[8,3584]{1,0:T(8,128)(2,1)S(1)}, bf16[8,3584]{1,0:T(8,128)(2,1)S(1)}, u32[]{:S(2)}, u32[]{:S(2)}) collective-permute-start(bf16[8,3584]{1,0:T(8,128)(2,1)S(1)} %get-tuple-element.30), channel_id=1, source_target_pairs={{5,0},{2,1},{7,2},{0,3},{1,4},{6,5},{3,6},{4,7},{13,8},{10,9},{15,... | collective-permute-start | bytes 172040 | tf_op jit(solution)/shard_map/ppermute | solution.py:207
  13.4 2.1 %collective-permute-done.5.refs_1_ = bf16[8,3584]{1,0:T(8,128)(2,1)S(1)} collective-permute-done((bf16[8,3584]{1,0:T(8,128)(2,1)S(1)}, bf16[8,3584]{1,0:T(8,128)(2,1)S(1)}, u32[]{:S(2)}, u32[]{:S(2)}) %collective-permute-start.5) | collective-permute-done | bytes 57376 | tf_op jit(solution)/shard_map/ppermute | solution.py:207
  15.5 0.3 %collective-permute-done.6.refs_2_ = bf16[8,3584]{1,0:T(8,128)(2,1)S(1)} collective-permute-done((bf16[8,3584]{1,0:T(8,128)(2,1)S(1)}, bf16[8,3584]{1,0:T(8,128)(2,1)S(1)}, u32[]{:S(2)}, u32[]{:S(2)}) %collective-permute-start.6) | collective-permute-done | bytes 57376 | tf_op jit(solution)/shard_map/ppermute | solution.py:207
  15.9 1.1 %collective-permute-done.7.refs_3_ = bf16[8,3584]{1,0:T(8,128)(2,1)S(1)} collective-permute-done((bf16[8,3584]{1,0:T(8,128)(2,1)S(1)}, bf16[8,3584]{1,0:T(8,128)(2,1)S(1)}, u32[]{:S(2)}, u32[]{:S(2)}) %collective-permute-start.7) | collective-permute-done | bytes 57376 | tf_op jit(solution)/shard_map/ppermute | solution.py:207
  17.0 0.8 %shard_map.86 = bf16[16,3584]{1,0:T(8,128)(2,1)} custom-call(bf16[32,32]{1,0:T(8,128)(2,1)S(1)} %get-tuple-element.19.weight_ref, bf16[8,3584]{1,0:T(8,128)(2,1)S(1)} %get-tuple-element.27.refs_0_, bf16[8,3584]{1,0:T(8,128)(2,1)S(1)} %collective-permute-done.5.refs_1_, bf16[8,3584]{1,0:T(8,128)(2,1)S(1)} %collective-permute-done.6.refs_2_, ...), custom_call_target="tpu_custom_call" | custom-call | flops 7340032 | bytes 346112 | tf_op jit(solution)/shard_map/pallas_call | solution.py:174
Async XLA Ops:
  0.0 9.6 %collective-permute-start = (bf16[2,3584,128]{2,1,0:T(8,128)(2,1)}, bf16[2,3584,128]{2,1,0:T(8,128)(2,1)S(1)}, u32[]{:S(2)}, u32[]{:S(2)}) collective-permute-start(bf16[2,3584,128]{2,1,0:T(8,128)(2,1)} %in_hbm.1), channel_id=1, source_target_pairs={{0,1},{1,0},{2,3},{3,2},{4,5},{5,4},{6,7},{7,6},{8,9},{9,8},{10,11... | collective-permute-start | bytes 5505032 | tf_op jit(solution)/shard_map/ppermute | solution.py:213
  1.6 7.2 %collective-permute-start.1 = (bf16[8,3584]{1,0:T(8,128)(2,1)S(1)}, bf16[8,3584]{1,0:T(8,128)(2,1)S(1)}, u32[]{:S(2)}, u32[]{:S(2)}) collective-permute-start(bf16[8,3584]{1,0:T(8,128)(2,1)S(1)} %get-tuple-element.22), channel_id=1, source_target_pairs={{0,7},{1,6},{2,5},{3,4},{4,3},{5,2},{6,1},{7,0},{8,15},{9,14},{10,... | collective-permute-start | bytes 172040 | tf_op jit(solution)/shard_map/ppermute | solution.py:207
  5.2 3.6 %collective-permute-start.2 = (bf16[8,3584]{1,0:T(8,128)(2,1)S(1)}, bf16[8,3584]{1,0:T(8,128)(2,1)S(1)}, u32[]{:S(2)}, u32[]{:S(2)}) collective-permute-start(bf16[8,3584]{1,0:T(8,128)(2,1)S(1)} %get-tuple-element.23), channel_id=1, source_target_pairs={{0,3},{1,4},{2,1},{3,6},{4,7},{5,0},{6,5},{7,2},{8,11},{9,12},{10,... | collective-permute-start | bytes 172040 | tf_op jit(solution)/shard_map/ppermute | solution.py:207
  5.4 4.2 %collective-permute-start.3 = (bf16[8,3584]{1,0:T(8,128)(2,1)S(1)}, bf16[8,3584]{1,0:T(8,128)(2,1)S(1)}, u32[]{:S(2)}, u32[]{:S(2)}) collective-permute-start(bf16[8,3584]{1,0:T(8,128)(2,1)S(1)} %get-tuple-element.24), channel_id=1, source_target_pairs={{0,5},{1,2},{2,7},{3,0},{4,1},{5,6},{6,3},{7,4},{8,13},{9,10},{10,... | collective-permute-start | bytes 172040 | tf_op jit(solution)/shard_map/ppermute | solution.py:207
  7.0 3.2 %collective-permute-start.4 = (bf16[128,3584]{1,0:T(8,128)(2,1)}, bf16[128,3584]{1,0:T(8,128)(2,1)S(1)}, u32[]{:S(2)}, u32[]{:S(2)}) collective-permute-start(bf16[128,3584]{1,0:T(8,128)(2,1)} %down_hbm.1), channel_id=1, source_target_pairs={{0,1},{1,0},{2,3},{3,2},{4,5},{5,4},{6,7},{7,6},{8,9},{9,8},{10,11... | collective-permute-start | bytes 2752520 | tf_op jit(solution)/shard_map/ppermute | solution.py:213
  10.6 4.9 %collective-permute-start.5 = (bf16[8,3584]{1,0:T(8,128)(2,1)S(1)}, bf16[8,3584]{1,0:T(8,128)(2,1)S(1)}, u32[]{:S(2)}, u32[]{:S(2)}) collective-permute-start(bf16[8,3584]{1,0:T(8,128)(2,1)S(1)} %get-tuple-element.28), channel_id=1, source_target_pairs={{7,0},{6,1},{5,2},{4,3},{3,4},{2,5},{1,6},{0,7},{15,8},{14,9},{13,... | collective-permute-start | bytes 172040 | tf_op jit(solution)/shard_map/ppermute | solution.py:207
  11.7 4.2 %collective-permute-start.6 = (bf16[8,3584]{1,0:T(8,128)(2,1)S(1)}, bf16[8,3584]{1,0:T(8,128)(2,1)S(1)}, u32[]{:S(2)}, u32[]{:S(2)}) collective-permute-start(bf16[8,3584]{1,0:T(8,128)(2,1)S(1)} %get-tuple-element.29), channel_id=1, source_target_pairs={{3,0},{4,1},{1,2},{6,3},{7,4},{0,5},{5,6},{2,7},{11,8},{12,9},{9,1... | collective-permute-start | bytes 172040 | tf_op jit(solution)/shard_map/ppermute | solution.py:207
  12.9 4.1 %collective-permute-start.7 = (bf16[8,3584]{1,0:T(8,128)(2,1)S(1)}, bf16[8,3584]{1,0:T(8,128)(2,1)S(1)}, u32[]{:S(2)}, u32[]{:S(2)}) collective-permute-start(bf16[8,3584]{1,0:T(8,128)(2,1)S(1)} %get-tuple-element.30), channel_id=1, source_target_pairs={{5,0},{2,1},{7,2},{0,3},{1,4},{6,5},{3,6},{4,7},{13,8},{10,9},{15,... | collective-permute-start | bytes 172040 | tf_op jit(solution)/shard_map/ppermute | solution.py:207

commit v11 on v10

--- a/solution.py
+++ b/solution.py
@@ -110,13 +110,13 @@
 
 
 def stack(refs):
-    return jnp.concatenate([ref[...].astype(jnp.float32) for ref in refs], axis=0)
+    return jnp.concatenate([ref[...] for ref in refs], axis=0)
 
 
 def hidden_kernel(split, in_ref, twin_in_ref, *refs):
     *refs, out_ref = refs
     odd = lax.axis_index("expert") & 1
-    rows = stack(refs).astype(jnp.bfloat16)
+    rows = stack(refs)
     half_size = refs[0].shape[0] // 2
     hidden = []
     for half, ref in enumerate((in_ref, twin_in_ref)):
@@ -131,11 +131,11 @@
 
 
 def down_kernel(hidden_ref, down_ref, twin_down_ref, *refs):
-    piece = jnp.dot(
-        hidden_ref[...],
-        jnp.concatenate([down_ref[...], twin_down_ref[...]], axis=0),
-        preferred_element_type=jnp.float32,
-    )
+    units = down_ref.shape[0]
+    own = hidden_ref[:, :units], down_ref[...]
+    twin = hidden_ref[:, units:], twin_down_ref[...]
+    piece = jnp.dot(*own, preferred_element_type=jnp.float32)
+    piece += jnp.dot(*twin, preferred_element_type=jnp.float32)
     size = refs[0].shape[0]
     for b, out_ref in enumerate(refs):
         out_ref[...] = piece[size * b : size * (b + 1)].astype(jnp.bfloat16)
@@ -150,14 +150,14 @@
     copies = []
     for part in range(parts):
         columns = slice(part * step, (part + 1) * step)
-        total = functools.reduce(
-            jnp.add,
-            [stack([ref.at[:, columns] for ref in refs[j::repeats]]) for j in range(repeats)],
-        )
-        high = total.astype(jnp.bfloat16)
-        mixed = jnp.dot(weight_ref[...], high, preferred_element_type=jnp.float32)
-        if repeats > 1:
+        pieces = [stack([ref.at[:, columns] for ref in refs[j::repeats]]) for j in range(repeats)]
+        if repeats == 1:
+            mixed = jnp.dot(weight_ref[...], pieces[0], preferred_element_type=jnp.float32)
+        else:
+            total = sum(piece.astype(jnp.float32) for piece in pieces)
+            high = total.astype(jnp.bfloat16)
             low = (total - high.astype(jnp.float32)).astype(jnp.bfloat16)
+            mixed = jnp.dot(weight_ref[...], high, preferred_element_type=jnp.float32)
             mixed += jnp.dot(weight_ref[...], low, preferred_element_type=jnp.float32)
         out_ref[:, columns] = (mixed[:rows] + mixed[rows:]).astype(jnp.bfloat16)
         copies.append(

time: 18 us -> 18 us (level)
  no operation moved by 1% of the time
where the time goes in v11:
time: 18 us; the launch traced here: 17.8 us
  starting transfers between devices  8.65 us (48%)
  Pallas kernels  4.78 us (27%)
  waiting for transfers between devices  4.35 us (24%)
    ppermute x6, starting transfers between devices, exchange(): result[k] = lax.ppermute(blocks[k], 'expert', pairs)  8.19 us
    pallas_call x5, Pallas kernels, call(): pl.pallas_call(kernel, out_shape=outs, in_specs=arg_specs, out_specs=out_...  4.78 us
    ppermute x6, waiting for transfers between devices, exchange(): result[k] = lax.ppermute(blocks[k], 'expert', pairs)  4.35 us
    ppermute x2, starting transfers between devices, from_twin(): return lax.ppermute(array, 'expert', pairs)  0.46 us
  transfers between devices with their start and end apart: 8, of which 5 were waited for; matrix products, arithmetic and copies ran while one was open for 0% of the time, Pallas kernels for 20%

profile of v11, /device:TPU:0, one launch (start us, length us, event | category | flops | bytes accessed | tf_op | source)
XLA Modules:
  0.0 17.8 jit_solution(4574901152313979666)
XLA Ops:
  0.0 0.5 %collective-permute-start = (bf16[2,3584,128]{2,1,0:T(8,128)(2,1)}, bf16[2,3584,128]{2,1,0:T(8,128)(2,1)S(1)}, u32[]{:S(2)}, u32[]{:S(2)}) collective-permute-start(bf16[2,3584,128]{2,1,0:T(8,128)(2,1)} %in_hbm.1), channel_id=1, source_target_pairs={{0,1},{1,0},{2,3},{3,2},{4,5},{5,4},{6,7},{7,6},{8,9},{9,8},{10,11... | collective-permute-start | bytes 5505032 | tf_op jit(solution)/shard_map/ppermute | solution.py:213
  0.5 1.2 %shard_map.82 = (s32[2,16]{1,0:T(2,128)S(1)}, bf16[8,3584]{1,0:T(8,128)(2,1)S(1)}, bf16[8,3584]{1,0:T(8,128)(2,1)S(1)}, bf16[8,3584]{1,0:T(8,128)(2,1)S(1)}, bf16[8,3584]{1,0:T(8,128)(2,1)S(1)}) custom-call(s32[8]{0:T(128)} %refs_0_.1, s32[8]{0:T(128)} %refs_1_.1, s32[2,16]{1,0:T(2,128)} %bitcast.3, s32[2,16]{1,0:T(2,128)} %bitcast.4, bf16[16,3584]{1,0:T(8,128)(2,1)} %refs_4_.1), custom_call_target="tpu_custom_call" | custom-call | flops 3670016 | bytes 344512 | tf_op jit(solution)/shard_map/pallas_call | solution.py:174
  1.6 3.6 %collective-permute-start.1 = (bf16[8,3584]{1,0:T(8,128)(2,1)S(1)}, bf16[8,3584]{1,0:T(8,128)(2,1)S(1)}, u32[]{:S(2)}, u32[]{:S(2)}) collective-permute-start(bf16[8,3584]{1,0:T(8,128)(2,1)S(1)} %get-tuple-element.22), channel_id=1, source_target_pairs={{0,7},{1,6},{2,5},{3,4},{4,3},{5,2},{6,1},{7,0},{8,15},{9,14},{10,... | collective-permute-start | bytes 172040 | tf_op jit(solution)/shard_map/ppermute | solution.py:207
  5.2 0.1 collective-permute-start.2
  5.4 1.6 %collective-permute-start.3 = (bf16[8,3584]{1,0:T(8,128)(2,1)S(1)}, bf16[8,3584]{1,0:T(8,128)(2,1)S(1)}, u32[]{:S(2)}, u32[]{:S(2)}) collective-permute-start(bf16[8,3584]{1,0:T(8,128)(2,1)S(1)} %get-tuple-element.24), channel_id=1, source_target_pairs={{0,5},{1,2},{2,7},{3,0},{4,1},{5,6},{6,3},{7,4},{8,13},{9,10},{10,... | collective-permute-start | bytes 172040 | tf_op jit(solution)/shard_map/ppermute | solution.py:207
  7.0 0.0 collective-permute-start.4
  7.0 1.8 %shard_map.83 = (bf16[2,3584,128]{2,1,0:T(8,128)(2,1)S(1)}, bf16[128,3584]{1,0:T(8,128)(2,1)S(1)}, bf16[32,32]{1,0:T(8,128)(2,1)S(1)}) custom-call(s32[2,16]{1,0:T(2,128)S(1)} %get-tuple-element.18.found_ref, f32[2,16]{1,0:T(2,128)} %bitcast.5, bf16[2,3584,128]{2,1,0:T(8,128)(2,1)} %in_hbm.1, bf16[128,3584]{1,0:T(8,128)(2,1)} %down_hbm.1), custom_call_target="tpu_custom_call" | custom-call | bytes 5507328 | tf_op jit(solution)/shard_map/pallas_call | solution.py:174
  8.8 0.0 collective-permute-done.1.refs_1_
  8.8 0.1 collective-permute-done.2.refs_2_
  8.8 0.7 %collective-permute-done.3.refs_3_ = bf16[8,3584]{1,0:T(8,128)(2,1)S(1)} collective-permute-done((bf16[8,3584]{1,0:T(8,128)(2,1)S(1)}, bf16[8,3584]{1,0:T(8,128)(2,1)S(1)}, u32[]{:S(2)}, u32[]{:S(2)}) %collective-permute-start.3) | collective-permute-done | bytes 57376 | tf_op jit(solution)/shard_map/ppermute | solution.py:207
  9.6 0.0 collective-permute-done.twin_in_ref
  9.6 0.6 %shard_map.84.hidden_ref = bf16[32,256]{1,0:T(8,128)(2,1)S(1)} custom-call(bf16[2,3584,128]{2,1,0:T(8,128)(2,1)S(1)} %get-tuple-element.20.in_ref, bf16[2,3584,128]{2,1,0:T(8,128)(2,1)S(1)} %collective-permute-done.twin_in_ref, bf16[8,3584]{1,0:T(8,128)(2,1)S(1)} %get-tuple-element.21.refs_0_, bf16[8,3584]{1,0:T(8,128)(2,1)S(1)} %collective-permute-done.1.refs_1_, ...), custom_call_target="tpu_custom_call" | custom-call | flops 11744051200 | bytes 3915776 | tf_op jit(solution)/shard_map/pallas_call | solution.py:174
  10.2 0.0 collective-permute-done.4.twin_down_ref
  10.2 0.4 %shard_map.85 = (bf16[8,3584]{1,0:T(8,128)(2,1)S(1)}, bf16[8,3584]{1,0:T(8,128)(2,1)S(1)}, bf16[8,3584]{1,0:T(8,128)(2,1)S(1)}, bf16[8,3584]{1,0:T(8,128)(2,1)S(1)}) custom-call(bf16[32,256]{1,0:T(8,128)(2,1)S(1)} %shard_map.84.hidden_ref, bf16[128,3584]{1,0:T(8,128)(2,1)S(1)} %get-tuple-element.25.down_ref, ...), custom_call_target="tpu_custom_call" | custom-call | flops 58720256 | bytes 2080768 | tf_op jit(solution)/shard_map/pallas_call | solution.py:174
  10.6 1.1 %collective-permute-start.5 = (bf16[8,3584]{1,0:T(8,128)(2,1)S(1)}, bf16[8,3584]{1,0:T(8,128)(2,1)S(1)}, u32[]{:S(2)}, u32[]{:S(2)}) collective-permute-start(bf16[8,3584]{1,0:T(8,128)(2,1)S(1)} %get-tuple-element.28), channel_id=1, source_target_pairs={{7,0},{6,1},{5,2},{4,3},{3,4},{2,5},{1,6},{0,7},{15,8},{14,9},{13,... | collective-permute-start | bytes 172040 | tf_op jit(solution)/shard_map/ppermute | solution.py:207
  11.7 1.3 %collective-permute-start.6 = (bf16[8,3584]{1,0:T(8,128)(2,1)S(1)}, bf16[8,3584]{1,0:T(8,128)(2,1)S(1)}, u32[]{:S(2)}, u32[]{:S(2)}) collective-permute-start(bf16[8,3584]{1,0:T(8,128)(2,1)S(1)} %get-tuple-element.29), channel_id=1, source_target_pairs={{3,0},{4,1},{1,2},{6,3},{7,4},{0,5},{5,6},{2,7},{11,8},{12,9},{9,1... | collective-permute-start | bytes 172040 | tf_op jit(solution)/shard_map/ppermute | solution.py:207
  12.9 0.5 %collective-permute-start.7 = (bf16[8,3584]{1,0:T(8,128)(2,1)S(1)}, bf16[8,3584]{1,0:T(8,128)(2,1)S(1)}, u32[]{:S(2)}, u32[]{:S(2)}) collective-permute-start(bf16[8,3584]{1,0:T(8,128)(2,1)S(1)} %get-tuple-element.30), channel_id=1, source_target_pairs={{5,0},{2,1},{7,2},{0,3},{1,4},{6,5},{3,6},{4,7},{13,8},{10,9},{15,... | collective-permute-start | bytes 172040 | tf_op jit(solution)/shard_map/ppermute | solution.py:207
  13.4 2.1 %collective-permute-done.5.refs_1_ = bf16[8,3584]{1,0:T(8,128)(2,1)S(1)} collective-permute-done((bf16[8,3584]{1,0:T(8,128)(2,1)S(1)}, bf16[8,3584]{1,0:T(8,128)(2,1)S(1)}, u32[]{:S(2)}, u32[]{:S(2)}) %collective-permute-start.5) | collective-permute-done | bytes 57376 | tf_op jit(solution)/shard_map/ppermute | solution.py:207
  15.5 0.3 %collective-permute-done.6.refs_2_ = bf16[8,3584]{1,0:T(8,128)(2,1)S(1)} collective-permute-done((bf16[8,3584]{1,0:T(8,128)(2,1)S(1)}, bf16[8,3584]{1,0:T(8,128)(2,1)S(1)}, u32[]{:S(2)}, u32[]{:S(2)}) %collective-permute-start.6) | collective-permute-done | bytes 57376 | tf_op jit(solution)/shard_map/ppermute | solution.py:207
  15.8 1.1 %collective-permute-done.7.refs_3_ = bf16[8,3584]{1,0:T(8,128)(2,1)S(1)} collective-permute-done((bf16[8,3584]{1,0:T(8,128)(2,1)S(1)}, bf16[8,3584]{1,0:T(8,128)(2,1)S(1)}, u32[]{:S(2)}, u32[]{:S(2)}) %collective-permute-start.7) | collective-permute-done | bytes 57376 | tf_op jit(solution)/shard_map/ppermute | solution.py:207
  17.0 0.9 %shard_map.86 = bf16[16,3584]{1,0:T(8,128)(2,1)} custom-call(bf16[32,32]{1,0:T(8,128)(2,1)S(1)} %get-tuple-element.19.weight_ref, bf16[8,3584]{1,0:T(8,128)(2,1)S(1)} %get-tuple-element.27.refs_0_, bf16[8,3584]{1,0:T(8,128)(2,1)S(1)} %collective-permute-done.5.refs_1_, bf16[8,3584]{1,0:T(8,128)(2,1)S(1)} %collective-permute-done.6.refs_2_, ...), custom_call_target="tpu_custom_call" | custom-call | flops 7340032 | bytes 346112 | tf_op jit(solution)/shard_map/pallas_call | solution.py:174
Async XLA Ops:
  0.0 9.6 %collective-permute-start = (bf16[2,3584,128]{2,1,0:T(8,128)(2,1)}, bf16[2,3584,128]{2,1,0:T(8,128)(2,1)S(1)}, u32[]{:S(2)}, u32[]{:S(2)}) collective-permute-start(bf16[2,3584,128]{2,1,0:T(8,128)(2,1)} %in_hbm.1), channel_id=1, source_target_pairs={{0,1},{1,0},{2,3},{3,2},{4,5},{5,4},{6,7},{7,6},{8,9},{9,8},{10,11... | collective-permute-start | bytes 5505032 | tf_op jit(solution)/shard_map/ppermute | solution.py:213
  1.6 7.2 %collective-permute-start.1 = (bf16[8,3584]{1,0:T(8,128)(2,1)S(1)}, bf16[8,3584]{1,0:T(8,128)(2,1)S(1)}, u32[]{:S(2)}, u32[]{:S(2)}) collective-permute-start(bf16[8,3584]{1,0:T(8,128)(2,1)S(1)} %get-tuple-element.22), channel_id=1, source_target_pairs={{0,7},{1,6},{2,5},{3,4},{4,3},{5,2},{6,1},{7,0},{8,15},{9,14},{10,... | collective-permute-start | bytes 172040 | tf_op jit(solution)/shard_map/ppermute | solution.py:207
  5.2 3.6 %collective-permute-start.2 = (bf16[8,3584]{1,0:T(8,128)(2,1)S(1)}, bf16[8,3584]{1,0:T(8,128)(2,1)S(1)}, u32[]{:S(2)}, u32[]{:S(2)}) collective-permute-start(bf16[8,3584]{1,0:T(8,128)(2,1)S(1)} %get-tuple-element.23), channel_id=1, source_target_pairs={{0,3},{1,4},{2,1},{3,6},{4,7},{5,0},{6,5},{7,2},{8,11},{9,12},{10,... | collective-permute-start | bytes 172040 | tf_op jit(solution)/shard_map/ppermute | solution.py:207
  5.4 4.2 %collective-permute-start.3 = (bf16[8,3584]{1,0:T(8,128)(2,1)S(1)}, bf16[8,3584]{1,0:T(8,128)(2,1)S(1)}, u32[]{:S(2)}, u32[]{:S(2)}) collective-permute-start(bf16[8,3584]{1,0:T(8,128)(2,1)S(1)} %get-tuple-element.24), channel_id=1, source_target_pairs={{0,5},{1,2},{2,7},{3,0},{4,1},{5,6},{6,3},{7,4},{8,13},{9,10},{10,... | collective-permute-start | bytes 172040 | tf_op jit(solution)/shard_map/ppermute | solution.py:207
  7.0 3.2 %collective-permute-start.4 = (bf16[128,3584]{1,0:T(8,128)(2,1)}, bf16[128,3584]{1,0:T(8,128)(2,1)S(1)}, u32[]{:S(2)}, u32[]{:S(2)}) collective-permute-start(bf16[128,3584]{1,0:T(8,128)(2,1)} %down_hbm.1), channel_id=1, source_target_pairs={{0,1},{1,0},{2,3},{3,2},{4,5},{5,4},{6,7},{7,6},{8,9},{9,8},{10,11... | collective-permute-start | bytes 2752520 | tf_op jit(solution)/shard_map/ppermute | solution.py:213
  10.6 4.9 %collective-permute-start.5 = (bf16[8,3584]{1,0:T(8,128)(2,1)S(1)}, bf16[8,3584]{1,0:T(8,128)(2,1)S(1)}, u32[]{:S(2)}, u32[]{:S(2)}) collective-permute-start(bf16[8,3584]{1,0:T(8,128)(2,1)S(1)} %get-tuple-element.28), channel_id=1, source_target_pairs={{7,0},{6,1},{5,2},{4,3},{3,4},{2,5},{1,6},{0,7},{15,8},{14,9},{13,... | collective-permute-start | bytes 172040 | tf_op jit(solution)/shard_map/ppermute | solution.py:207
  11.7 4.2 %collective-permute-start.6 = (bf16[8,3584]{1,0:T(8,128)(2,1)S(1)}, bf16[8,3584]{1,0:T(8,128)(2,1)S(1)}, u32[]{:S(2)}, u32[]{:S(2)}) collective-permute-start(bf16[8,3584]{1,0:T(8,128)(2,1)S(1)} %get-tuple-element.29), channel_id=1, source_target_pairs={{3,0},{4,1},{1,2},{6,3},{7,4},{0,5},{5,6},{2,7},{11,8},{12,9},{9,1... | collective-permute-start | bytes 172040 | tf_op jit(solution)/shard_map/ppermute | solution.py:207
  12.9 4.1 %collective-permute-start.7 = (bf16[8,3584]{1,0:T(8,128)(2,1)S(1)}, bf16[8,3584]{1,0:T(8,128)(2,1)S(1)}, u32[]{:S(2)}, u32[]{:S(2)}) collective-permute-start(bf16[8,3584]{1,0:T(8,128)(2,1)S(1)} %get-tuple-element.30), channel_id=1, source_target_pairs={{5,0},{2,1},{7,2},{0,3},{1,4},{6,5},{3,6},{4,7},{13,8},{10,9},{15,... | collective-permute-start | bytes 172040 | tf_op jit(solution)/shard_map/ppermute | solution.py:207

commit v12 on v11

--- a/solution.py
+++ b/solution.py
@@ -9,7 +9,7 @@
 
 SLOTS = 8
 CAP = 4
-CHIP_STEPS = ((0, 3, 1, 2), (0, 3, 2, 1))
+CHIP_STEPS = ((0, 3, 1, 2), (0, 3, 1, 2))
 
 VMEM = pl.BlockSpec(memory_space=pltpu.VMEM)
 HBM = pl.BlockSpec(memory_space=pltpu.HBM)

time: 18 us -> 17.9 us (level)
  starting transfers between devices: 8.65 us -> 7.93 us
  waiting for transfers between devices: 4.35 us -> 4.95 us
    ppermute x6, starting transfers between devices: 8.19 us -> 6.98 us  [exchange(): result[k] = lax.ppermute(blocks[k], 'expert', pairs)]
    ppermute x6, waiting for transfers between devices: 4.35 us -> 4.95 us  [exchange(): result[k] = lax.ppermute(blocks[k], 'expert', pairs)]
    ppermute x2, starting transfers between devices: 0.46 us -> 0.95 us  [from_twin(): return lax.ppermute(array, 'expert', pairs)]
  transfers between devices with their start and end apart: 8 -> 8, of which waited for: 5 -> 4; matrix products, arithmetic and copies ran while one was open for 0% -> 0% of each run, Pallas kernels for 20% -> 20%
where the time goes in v12:
time: 17.9 us; the launch traced here: 17.7 us
  starting transfers between devices  7.93 us (44%)
  waiting for transfers between devices  4.95 us (28%)
  Pallas kernels  4.78 us (27%)
    ppermute x6, starting transfers between devices, exchange(): result[k] = lax.ppermute(blocks[k], 'expert', pairs)  6.98 us
    ppermute x6, waiting for transfers between devices, exchange(): result[k] = lax.ppermute(blocks[k], 'expert', pairs)  4.95 us
    pallas_call x5, Pallas kernels, call(): pl.pallas_call(kernel, out_shape=outs, in_specs=arg_specs, out_specs=out_...  4.78 us
    ppermute x2, starting transfers between devices, from_twin(): return lax.ppermute(array, 'expert', pairs)  0.95 us
  transfers between devices with their start and end apart: 8, of which 4 were waited for; matrix products, arithmetic and copies ran while one was open for 0% of the time, Pallas kernels for 20%

profile of v12, /device:TPU:0, one launch (start us, length us, event | category | flops | bytes accessed | tf_op | source)
XLA Modules:
  0.0 17.7 jit_solution(3299794566940145441)
XLA Ops:
  0.0 0.5 %collective-permute-start = (bf16[2,3584,128]{2,1,0:T(8,128)(2,1)}, bf16[2,3584,128]{2,1,0:T(8,128)(2,1)S(1)}, u32[]{:S(2)}, u32[]{:S(2)}) collective-permute-start(bf16[2,3584,128]{2,1,0:T(8,128)(2,1)} %in_hbm.1), channel_id=1, source_target_pairs={{0,1},{1,0},{2,3},{3,2},{4,5},{5,4},{6,7},{7,6},{8,9},{9,8},{10,11... | collective-permute-start | bytes 5505032 | tf_op jit(solution)/shard_map/ppermute | solution.py:213
  0.5 1.2 %shard_map.82 = (s32[2,16]{1,0:T(2,128)S(1)}, bf16[8,3584]{1,0:T(8,128)(2,1)S(1)}, bf16[8,3584]{1,0:T(8,128)(2,1)S(1)}, bf16[8,3584]{1,0:T(8,128)(2,1)S(1)}, bf16[8,3584]{1,0:T(8,128)(2,1)S(1)}) custom-call(s32[8]{0:T(128)} %refs_0_.1, s32[8]{0:T(128)} %refs_1_.1, s32[2,16]{1,0:T(2,128)} %bitcast.3, s32[2,16]{1,0:T(2,128)} %bitcast.4, bf16[16,3584]{1,0:T(8,128)(2,1)} %refs_4_.1), custom_call_target="tpu_custom_call" | custom-call | flops 3670016 | bytes 344512 | tf_op jit(solution)/shard_map/pallas_call | solution.py:174
  1.6 3.6 %collective-permute-start.1 = (bf16[8,3584]{1,0:T(8,128)(2,1)S(1)}, bf16[8,3584]{1,0:T(8,128)(2,1)S(1)}, u32[]{:S(2)}, u32[]{:S(2)}) collective-permute-start(bf16[8,3584]{1,0:T(8,128)(2,1)S(1)} %get-tuple-element.22), channel_id=1, source_target_pairs={{0,7},{1,6},{2,5},{3,4},{4,3},{5,2},{6,1},{7,0},{8,15},{9,14},{10,... | collective-permute-start | bytes 172040 | tf_op jit(solution)/shard_map/ppermute | solution.py:207
  5.2 0.1 collective-permute-start.2
  5.4 0.1 collective-permute-start.3
  5.5 0.5 %collective-permute-start.4 = (bf16[128,3584]{1,0:T(8,128)(2,1)}, bf16[128,3584]{1,0:T(8,128)(2,1)S(1)}, u32[]{:S(2)}, u32[]{:S(2)}) collective-permute-start(bf16[128,3584]{1,0:T(8,128)(2,1)} %down_hbm.1), channel_id=1, source_target_pairs={{0,1},{1,0},{2,3},{3,2},{4,5},{5,4},{6,7},{7,6},{8,9},{9,8},{10,11... | collective-permute-start | bytes 2752520 | tf_op jit(solution)/shard_map/ppermute | solution.py:213
  6.0 1.8 %shard_map.83 = (bf16[2,3584,128]{2,1,0:T(8,128)(2,1)S(1)}, bf16[128,3584]{1,0:T(8,128)(2,1)S(1)}, bf16[32,32]{1,0:T(8,128)(2,1)S(1)}) custom-call(s32[2,16]{1,0:T(2,128)S(1)} %get-tuple-element.18.found_ref, f32[2,16]{1,0:T(2,128)} %bitcast.5, bf16[2,3584,128]{2,1,0:T(8,128)(2,1)} %in_hbm.1, bf16[128,3584]{1,0:T(8,128)(2,1)} %down_hbm.1), custom_call_target="tpu_custom_call" | custom-call | bytes 5507328 | tf_op jit(solution)/shard_map/pallas_call | solution.py:174
  7.8 0.0 collective-permute-done.1.refs_1_
  7.8 1.5 %collective-permute-done.2.refs_2_ = bf16[8,3584]{1,0:T(8,128)(2,1)S(1)} collective-permute-done((bf16[8,3584]{1,0:T(8,128)(2,1)S(1)}, bf16[8,3584]{1,0:T(8,128)(2,1)S(1)}, u32[]{:S(2)}, u32[]{:S(2)}) %collective-permute-start.2) | collective-permute-done | bytes 57376 | tf_op jit(solution)/shard_map/ppermute | solution.py:207
  9.3 0.0 collective-permute-done.3.refs_3_
  9.3 0.0 collective-permute-done.twin_in_ref
  9.3 0.6 %shard_map.84.hidden_ref = bf16[32,256]{1,0:T(8,128)(2,1)S(1)} custom-call(bf16[2,3584,128]{2,1,0:T(8,128)(2,1)S(1)} %get-tuple-element.20.in_ref, bf16[2,3584,128]{2,1,0:T(8,128)(2,1)S(1)} %collective-permute-done.twin_in_ref, bf16[8,3584]{1,0:T(8,128)(2,1)S(1)} %get-tuple-element.21.refs_0_, bf16[8,3584]{1,0:T(8,128)(2,1)S(1)} %collective-permute-done.1.refs_1_, ...), custom_call_target="tpu_custom_call" | custom-call | flops 11744051200 | bytes 3915776 | tf_op jit(solution)/shard_map/pallas_call | solution.py:174
  9.9 0.0 collective-permute-done.4.twin_down_ref
  9.9 0.4 %shard_map.85 = (bf16[8,3584]{1,0:T(8,128)(2,1)S(1)}, bf16[8,3584]{1,0:T(8,128)(2,1)S(1)}, bf16[8,3584]{1,0:T(8,128)(2,1)S(1)}, bf16[8,3584]{1,0:T(8,128)(2,1)S(1)}) custom-call(bf16[32,256]{1,0:T(8,128)(2,1)S(1)} %shard_map.84.hidden_ref, bf16[128,3584]{1,0:T(8,128)(2,1)S(1)} %get-tuple-element.25.down_ref, ...), custom_call_target="tpu_custom_call" | custom-call | flops 58720256 | bytes 2080768 | tf_op jit(solution)/shard_map/pallas_call | solution.py:174
  10.3 1.8 %collective-permute-start.5 = (bf16[8,3584]{1,0:T(8,128)(2,1)S(1)}, bf16[8,3584]{1,0:T(8,128)(2,1)S(1)}, u32[]{:S(2)}, u32[]{:S(2)}) collective-permute-start(bf16[8,3584]{1,0:T(8,128)(2,1)S(1)} %get-tuple-element.28), channel_id=1, source_target_pairs={{7,0},{6,1},{5,2},{4,3},{3,4},{2,5},{1,6},{0,7},{15,8},{14,9},{13,... | collective-permute-start | bytes 172040 | tf_op jit(solution)/shard_map/ppermute | solution.py:207
  12.1 0.8 %collective-permute-start.6 = (bf16[8,3584]{1,0:T(8,128)(2,1)S(1)}, bf16[8,3584]{1,0:T(8,128)(2,1)S(1)}, u32[]{:S(2)}, u32[]{:S(2)}) collective-permute-start(bf16[8,3584]{1,0:T(8,128)(2,1)S(1)} %get-tuple-element.29), channel_id=1, source_target_pairs={{3,0},{2,1},{1,2},{0,3},{7,4},{6,5},{5,6},{4,7},{11,8},{10,9},{9,1... | collective-permute-start | bytes 172040 | tf_op jit(solution)/shard_map/ppermute | solution.py:207
  12.9 0.5 %collective-permute-start.7 = (bf16[8,3584]{1,0:T(8,128)(2,1)S(1)}, bf16[8,3584]{1,0:T(8,128)(2,1)S(1)}, u32[]{:S(2)}, u32[]{:S(2)}) collective-permute-start(bf16[8,3584]{1,0:T(8,128)(2,1)S(1)} %get-tuple-element.30), channel_id=1, source_target_pairs={{5,0},{4,1},{7,2},{6,3},{1,4},{0,5},{3,6},{2,7},{13,8},{12,9},{15,... | collective-permute-start | bytes 172040 | tf_op jit(solution)/shard_map/ppermute | solution.py:207
  13.4 1.7 %collective-permute-done.5.refs_1_ = bf16[8,3584]{1,0:T(8,128)(2,1)S(1)} collective-permute-done((bf16[8,3584]{1,0:T(8,128)(2,1)S(1)}, bf16[8,3584]{1,0:T(8,128)(2,1)S(1)}, u32[]{:S(2)}, u32[]{:S(2)}) %collective-permute-start.5) | collective-permute-done | bytes 57376 | tf_op jit(solution)/shard_map/ppermute | solution.py:207
  15.1 1.1 %collective-permute-done.6.refs_2_ = bf16[8,3584]{1,0:T(8,128)(2,1)S(1)} collective-permute-done((bf16[8,3584]{1,0:T(8,128)(2,1)S(1)}, bf16[8,3584]{1,0:T(8,128)(2,1)S(1)}, u32[]{:S(2)}, u32[]{:S(2)}) %collective-permute-start.6) | collective-permute-done | bytes 57376 | tf_op jit(solution)/shard_map/ppermute | solution.py:207
  16.3 0.6 %collective-permute-done.7.refs_3_ = bf16[8,3584]{1,0:T(8,128)(2,1)S(1)} collective-permute-done((bf16[8,3584]{1,0:T(8,128)(2,1)S(1)}, bf16[8,3584]{1,0:T(8,128)(2,1)S(1)}, u32[]{:S(2)}, u32[]{:S(2)}) %collective-permute-start.7) | collective-permute-done | bytes 57376 | tf_op jit(solution)/shard_map/ppermute | solution.py:207
  16.9 0.9 %shard_map.86 = bf16[16,3584]{1,0:T(8,128)(2,1)} custom-call(bf16[32,32]{1,0:T(8,128)(2,1)S(1)} %get-tuple-element.19.weight_ref, bf16[8,3584]{1,0:T(8,128)(2,1)S(1)} %get-tuple-element.27.refs_0_, bf16[8,3584]{1,0:T(8,128)(2,1)S(1)} %collective-permute-done.5.refs_1_, bf16[8,3584]{1,0:T(8,128)(2,1)S(1)} %collective-permute-done.6.refs_2_, ...), custom_call_target="tpu_custom_call" | custom-call | flops 7340032 | bytes 346112 | tf_op jit(solution)/shard_map/pallas_call | solution.py:174
Async XLA Ops:
  0.0 9.3 %collective-permute-start = (bf16[2,3584,128]{2,1,0:T(8,128)(2,1)}, bf16[2,3584,128]{2,1,0:T(8,128)(2,1)S(1)}, u32[]{:S(2)}, u32[]{:S(2)}) collective-permute-start(bf16[2,3584,128]{2,1,0:T(8,128)(2,1)} %in_hbm.1), channel_id=1, source_target_pairs={{0,1},{1,0},{2,3},{3,2},{4,5},{5,4},{6,7},{7,6},{8,9},{9,8},{10,11... | collective-permute-start | bytes 5505032 | tf_op jit(solution)/shard_map/ppermute | solution.py:213
  1.6 6.2 %collective-permute-start.1 = (bf16[8,3584]{1,0:T(8,128)(2,1)S(1)}, bf16[8,3584]{1,0:T(8,128)(2,1)S(1)}, u32[]{:S(2)}, u32[]{:S(2)}) collective-permute-start(bf16[8,3584]{1,0:T(8,128)(2,1)S(1)} %get-tuple-element.22), channel_id=1, source_target_pairs={{0,7},{1,6},{2,5},{3,4},{4,3},{5,2},{6,1},{7,0},{8,15},{9,14},{10,... | collective-permute-start | bytes 172040 | tf_op jit(solution)/shard_map/ppermute | solution.py:207
  5.2 4.0 %collective-permute-start.2 = (bf16[8,3584]{1,0:T(8,128)(2,1)S(1)}, bf16[8,3584]{1,0:T(8,128)(2,1)S(1)}, u32[]{:S(2)}, u32[]{:S(2)}) collective-permute-start(bf16[8,3584]{1,0:T(8,128)(2,1)S(1)} %get-tuple-element.23), channel_id=1, source_target_pairs={{0,3},{1,2},{2,1},{3,0},{4,7},{5,6},{6,5},{7,4},{8,11},{9,10},{10,... | collective-permute-start | bytes 172040 | tf_op jit(solution)/shard_map/ppermute | solution.py:207
  5.4 3.9 %collective-permute-start.3 = (bf16[8,3584]{1,0:T(8,128)(2,1)S(1)}, bf16[8,3584]{1,0:T(8,128)(2,1)S(1)}, u32[]{:S(2)}, u32[]{:S(2)}) collective-permute-start(bf16[8,3584]{1,0:T(8,128)(2,1)S(1)} %get-tuple-element.24), channel_id=1, source_target_pairs={{0,5},{1,4},{2,7},{3,6},{4,1},{5,0},{6,3},{7,2},{8,13},{9,12},{10,... | collective-permute-start | bytes 172040 | tf_op jit(solution)/shard_map/ppermute | solution.py:207
  5.5 4.4 %collective-permute-start.4 = (bf16[128,3584]{1,0:T(8,128)(2,1)}, bf16[128,3584]{1,0:T(8,128)(2,1)S(1)}, u32[]{:S(2)}, u32[]{:S(2)}) collective-permute-start(bf16[128,3584]{1,0:T(8,128)(2,1)} %down_hbm.1), channel_id=1, source_target_pairs={{0,1},{1,0},{2,3},{3,2},{4,5},{5,4},{6,7},{7,6},{8,9},{9,8},{10,11... | collective-permute-start | bytes 2752520 | tf_op jit(solution)/shard_map/ppermute | solution.py:213
  10.3 4.9 %collective-permute-start.5 = (bf16[8,3584]{1,0:T(8,128)(2,1)S(1)}, bf16[8,3584]{1,0:T(8,128)(2,1)S(1)}, u32[]{:S(2)}, u32[]{:S(2)}) collective-permute-start(bf16[8,3584]{1,0:T(8,128)(2,1)S(1)} %get-tuple-element.28), channel_id=1, source_target_pairs={{7,0},{6,1},{5,2},{4,3},{3,4},{2,5},{1,6},{0,7},{15,8},{14,9},{13,... | collective-permute-start | bytes 172040 | tf_op jit(solution)/shard_map/ppermute | solution.py:207
  12.1 4.2 %collective-permute-start.6 = (bf16[8,3584]{1,0:T(8,128)(2,1)S(1)}, bf16[8,3584]{1,0:T(8,128)(2,1)S(1)}, u32[]{:S(2)}, u32[]{:S(2)}) collective-permute-start(bf16[8,3584]{1,0:T(8,128)(2,1)S(1)} %get-tuple-element.29), channel_id=1, source_target_pairs={{3,0},{2,1},{1,2},{0,3},{7,4},{6,5},{5,6},{4,7},{11,8},{10,9},{9,1... | collective-permute-start | bytes 172040 | tf_op jit(solution)/shard_map/ppermute | solution.py:207
  12.9 4.0 %collective-permute-start.7 = (bf16[8,3584]{1,0:T(8,128)(2,1)S(1)}, bf16[8,3584]{1,0:T(8,128)(2,1)S(1)}, u32[]{:S(2)}, u32[]{:S(2)}) collective-permute-start(bf16[8,3584]{1,0:T(8,128)(2,1)S(1)} %get-tuple-element.30), channel_id=1, source_target_pairs={{5,0},{4,1},{7,2},{6,3},{1,4},{0,5},{3,6},{2,7},{13,8},{12,9},{15,... | collective-permute-start | bytes 172040 | tf_op jit(solution)/shard_map/ppermute | solution.py:207

commit v13 on v11

--- a/solution.py
+++ b/solution.py
@@ -141,9 +141,9 @@
         out_ref[...] = piece[size * b : size * (b + 1)].astype(jnp.bfloat16)
 
 
-def mix_kernel(repeats, weight_ref, *refs):
+def mix_kernel(repeats, order, weight_ref, *refs):
     out_hbm, out_ref, sems = refs[-3:]
-    refs = refs[:-3]
+    refs = [ref for _, ref in sorted(zip(order, refs[:-3]), key=lambda pair: pair[0])]
     rows, width = out_ref.shape
     parts = sems.shape[0]
     step = width // parts
@@ -196,15 +196,17 @@
 
 def exchange(blocks, split, back=False):
     devices = lax.axis_size("expert")
-    result = list(blocks)
+    steps = {}
     for k in range(1, len(blocks)):
         if split:
-            pairs = [(i, i ^ 1 ^ 2 * CHIP_STEPS[i & 1][k]) for i in range(devices)]
+            steps[k] = [(i, i ^ 1 ^ 2 * CHIP_STEPS[i & 1][k]) for i in range(devices)]
         else:
-            pairs = [(i, i ^ 2 * k) for i in range(devices)]
-        if back:
-            pairs = [(target, source) for source, target in pairs]
-        result[k] = lax.ppermute(blocks[k], "expert", pairs)
+            steps[k] = [(i, i ^ 2 * k) for i in range(devices)]
+    result = {0: blocks[0]}
+    for k, pairs in steps.items():
+        came = sorted((target, source) for source, target in pairs)
+        block = next(m for m in steps if steps[m] == came) if back else k
+        result[block] = lax.ppermute(blocks[block], "expert", pairs)
     return result
 
 
@@ -250,7 +252,7 @@
     units = call(
         functools.partial(hidden_kernel, split),
         jax.ShapeDtypeStruct((chips * block.shape[0], 2 * hidden), jnp.bfloat16),
-        (own_in, twin_in, *received),
+        (own_in, twin_in, *received.values()),
         800 * chips * block.shape[0] * hidden * width,
     )
     pieces = call(
@@ -262,9 +264,9 @@
     returned = exchange(pieces, split, back=True)
     parts = 4 if width % 512 == 0 else 1
     return call(
-        functools.partial(mix_kernel, repeats),
+        functools.partial(mix_kernel, repeats, tuple(returned)),
         shape_of(tokens),
-        (weight, *returned),
+        (weight, *returned.values()),
         4 * SLOTS * CAP * rows * width,
         out_specs=HBM,
         scratch=[pltpu.VMEM(tokens.shape, tokens.dtype), pltpu.SemaphoreType.DMA((parts,))],

time: 18 us -> 17.6 us (0.978)
  waiting for transfers between devices: 4.35 us -> 3.9 us
    ppermute x6, waiting for transfers between devices: 4.35 us -> 3.89 us  [exchange(): result[block] = lax.ppermute(blocks[block], 'expert', pairs)]
  transfers between devices with their start and end apart: 8 -> 8, of which waited for: 5 -> 4; matrix products, arithmetic and copies ran while one was open for 0% -> 0% of each run, Pallas kernels for 20% -> 20%
where the time goes in v13:
time: 17.6 us; the launch traced here: 17.4 us
  starting transfers between devices  8.65 us (49%)
  Pallas kernels  4.78 us (27%)
  waiting for transfers between devices  3.9 us (22%)
    ppermute x6, starting transfers between devices, exchange(): result[block] = lax.ppermute(blocks[block], 'expert', pairs)  8.19 us
    pallas_call x5, Pallas kernels, call(): pl.pallas_call(kernel, out_shape=outs, in_specs=arg_specs, out_specs=out_...  4.78 us
    ppermute x6, waiting for transfers between devices, exchange(): result[block] = lax.ppermute(blocks[block], 'expert', pairs)  3.89 us
    ppermute x2, starting transfers between devices, from_twin(): return lax.ppermute(array, 'expert', pairs)  0.46 us
  transfers between devices with their start and end apart: 8, of which 4 were waited for; matrix products, arithmetic and copies ran while one was open for 0% of the time, Pallas kernels for 20%

profile of v13, /device:TPU:0, one launch (start us, length us, event | category | flops | bytes accessed | tf_op | source)
XLA Modules:
  0.0 17.4 jit_solution(104287603865352076)
XLA Ops:
  0.0 0.5 %collective-permute-start = (bf16[2,3584,128]{2,1,0:T(8,128)(2,1)}, bf16[2,3584,128]{2,1,0:T(8,128)(2,1)S(1)}, u32[]{:S(2)}, u32[]{:S(2)}) collective-permute-start(bf16[2,3584,128]{2,1,0:T(8,128)(2,1)} %in_hbm.1), channel_id=1, source_target_pairs={{0,1},{1,0},{2,3},{3,2},{4,5},{5,4},{6,7},{7,6},{8,9},{9,8},{10,11... | collective-permute-start | bytes 5505032 | tf_op jit(solution)/shard_map/ppermute | solution.py:215
  0.5 1.2 %shard_map.82 = (s32[2,16]{1,0:T(2,128)S(1)}, bf16[8,3584]{1,0:T(8,128)(2,1)S(1)}, bf16[8,3584]{1,0:T(8,128)(2,1)S(1)}, bf16[8,3584]{1,0:T(8,128)(2,1)S(1)}, bf16[8,3584]{1,0:T(8,128)(2,1)S(1)}) custom-call(s32[8]{0:T(128)} %refs_0_.1, s32[8]{0:T(128)} %refs_1_.1, s32[2,16]{1,0:T(2,128)} %bitcast.3, s32[2,16]{1,0:T(2,128)} %bitcast.4, bf16[16,3584]{1,0:T(8,128)(2,1)} %refs_4_.1), custom_call_target="tpu_custom_call" | custom-call | flops 3670016 | bytes 344512 | tf_op jit(solution)/shard_map/pallas_call | solution.py:174
  1.6 3.6 %collective-permute-start.1 = (bf16[8,3584]{1,0:T(8,128)(2,1)S(1)}, bf16[8,3584]{1,0:T(8,128)(2,1)S(1)}, u32[]{:S(2)}, u32[]{:S(2)}) collective-permute-start(bf16[8,3584]{1,0:T(8,128)(2,1)S(1)} %get-tuple-element.22), channel_id=1, source_target_pairs={{0,7},{1,6},{2,5},{3,4},{4,3},{5,2},{6,1},{7,0},{8,15},{9,14},{10,... | collective-permute-start | bytes 172040 | tf_op jit(solution)/shard_map/ppermute | solution.py:209
  5.2 0.1 collective-permute-start.2
  5.4 1.6 %collective-permute-start.3 = (bf16[8,3584]{1,0:T(8,128)(2,1)S(1)}, bf16[8,3584]{1,0:T(8,128)(2,1)S(1)}, u32[]{:S(2)}, u32[]{:S(2)}) collective-permute-start(bf16[8,3584]{1,0:T(8,128)(2,1)S(1)} %get-tuple-element.24), channel_id=1, source_target_pairs={{0,5},{1,2},{2,7},{3,0},{4,1},{5,6},{6,3},{7,4},{8,13},{9,10},{10,... | collective-permute-start | bytes 172040 | tf_op jit(solution)/shard_map/ppermute | solution.py:209
  7.0 0.0 collective-permute-start.4
  7.0 1.8 %shard_map.83 = (bf16[2,3584,128]{2,1,0:T(8,128)(2,1)S(1)}, bf16[128,3584]{1,0:T(8,128)(2,1)S(1)}, bf16[32,32]{1,0:T(8,128)(2,1)S(1)}) custom-call(s32[2,16]{1,0:T(2,128)S(1)} %get-tuple-element.18.found_ref, f32[2,16]{1,0:T(2,128)} %bitcast.5, bf16[2,3584,128]{2,1,0:T(8,128)(2,1)} %in_hbm.1, bf16[128,3584]{1,0:T(8,128)(2,1)} %down_hbm.1), custom_call_target="tpu_custom_call" | custom-call | bytes 5507328 | tf_op jit(solution)/shard_map/pallas_call | solution.py:174
  8.8 0.0 collective-permute-done.1.refs_1_
  8.8 0.1 collective-permute-done.2.refs_2_
  8.8 0.7 %collective-permute-done.3.refs_3_ = bf16[8,3584]{1,0:T(8,128)(2,1)S(1)} collective-permute-done((bf16[8,3584]{1,0:T(8,128)(2,1)S(1)}, bf16[8,3584]{1,0:T(8,128)(2,1)S(1)}, u32[]{:S(2)}, u32[]{:S(2)}) %collective-permute-start.3) | collective-permute-done | bytes 57376 | tf_op jit(solution)/shard_map/ppermute | solution.py:209
  9.6 0.0 collective-permute-done.twin_in_ref
  9.6 0.6 %shard_map.84.hidden_ref = bf16[32,256]{1,0:T(8,128)(2,1)S(1)} custom-call(bf16[2,3584,128]{2,1,0:T(8,128)(2,1)S(1)} %get-tuple-element.20.in_ref, bf16[2,3584,128]{2,1,0:T(8,128)(2,1)S(1)} %collective-permute-done.twin_in_ref, bf16[8,3584]{1,0:T(8,128)(2,1)S(1)} %get-tuple-element.21.refs_0_, bf16[8,3584]{1,0:T(8,128)(2,1)S(1)} %collective-permute-done.1.refs_1_, ...), custom_call_target="tpu_custom_call" | custom-call | flops 11744051200 | bytes 3915776 | tf_op jit(solution)/shard_map/pallas_call | solution.py:174
  10.2 0.0 collective-permute-done.4.twin_down_ref
  10.2 0.4 %shard_map.85 = (bf16[8,3584]{1,0:T(8,128)(2,1)S(1)}, bf16[8,3584]{1,0:T(8,128)(2,1)S(1)}, bf16[8,3584]{1,0:T(8,128)(2,1)S(1)}, bf16[8,3584]{1,0:T(8,128)(2,1)S(1)}) custom-call(bf16[32,256]{1,0:T(8,128)(2,1)S(1)} %shard_map.84.hidden_ref, bf16[128,3584]{1,0:T(8,128)(2,1)S(1)} %get-tuple-element.25.down_ref, ...), custom_call_target="tpu_custom_call" | custom-call | flops 58720256 | bytes 2080768 | tf_op jit(solution)/shard_map/pallas_call | solution.py:174
  10.6 1.1 %collective-permute-start.5 = (bf16[8,3584]{1,0:T(8,128)(2,1)S(1)}, bf16[8,3584]{1,0:T(8,128)(2,1)S(1)}, u32[]{:S(2)}, u32[]{:S(2)}) collective-permute-start(bf16[8,3584]{1,0:T(8,128)(2,1)S(1)} %get-tuple-element.28), channel_id=1, source_target_pairs={{0,7},{1,6},{2,5},{3,4},{4,3},{5,2},{6,1},{7,0},{8,15},{9,14},{10,... | collective-permute-start | bytes 172040 | tf_op jit(solution)/shard_map/ppermute | solution.py:209
  11.7 0.6 %collective-permute-start.6 = (bf16[8,3584]{1,0:T(8,128)(2,1)S(1)}, bf16[8,3584]{1,0:T(8,128)(2,1)S(1)}, u32[]{:S(2)}, u32[]{:S(2)}) collective-permute-start(bf16[8,3584]{1,0:T(8,128)(2,1)S(1)} %get-tuple-element.29), channel_id=1, source_target_pairs={{0,3},{1,4},{2,1},{3,6},{4,7},{5,0},{6,5},{7,2},{8,11},{9,12},{10,... | collective-permute-start | bytes 172040 | tf_op jit(solution)/shard_map/ppermute | solution.py:209
  12.3 1.1 %collective-permute-start.7 = (bf16[8,3584]{1,0:T(8,128)(2,1)S(1)}, bf16[8,3584]{1,0:T(8,128)(2,1)S(1)}, u32[]{:S(2)}, u32[]{:S(2)}) collective-permute-start(bf16[8,3584]{1,0:T(8,128)(2,1)S(1)} %get-tuple-element.30), channel_id=1, source_target_pairs={{0,5},{1,2},{2,7},{3,0},{4,1},{5,6},{6,3},{7,4},{8,13},{9,10},{10,... | collective-permute-start | bytes 172040 | tf_op jit(solution)/shard_map/ppermute | solution.py:209
  13.4 2.1 %collective-permute-done.5.refs_1_ = bf16[8,3584]{1,0:T(8,128)(2,1)S(1)} collective-permute-done((bf16[8,3584]{1,0:T(8,128)(2,1)S(1)}, bf16[8,3584]{1,0:T(8,128)(2,1)S(1)}, u32[]{:S(2)}, u32[]{:S(2)}) %collective-permute-start.5) | collective-permute-done | bytes 57376 | tf_op jit(solution)/shard_map/ppermute | solution.py:209
  15.5 1.0 %collective-permute-done.6.refs_2_ = bf16[8,3584]{1,0:T(8,128)(2,1)S(1)} collective-permute-done((bf16[8,3584]{1,0:T(8,128)(2,1)S(1)}, bf16[8,3584]{1,0:T(8,128)(2,1)S(1)}, u32[]{:S(2)}, u32[]{:S(2)}) %collective-permute-start.6) | collective-permute-done | bytes 57376 | tf_op jit(solution)/shard_map/ppermute | solution.py:209
  16.5 0.0 collective-permute-done.7.refs_3_
  16.5 0.9 %shard_map.86 = bf16[16,3584]{1,0:T(8,128)(2,1)} custom-call(bf16[32,32]{1,0:T(8,128)(2,1)S(1)} %get-tuple-element.19.weight_ref, bf16[8,3584]{1,0:T(8,128)(2,1)S(1)} %get-tuple-element.27.refs_0_, bf16[8,3584]{1,0:T(8,128)(2,1)S(1)} %collective-permute-done.5.refs_1_, bf16[8,3584]{1,0:T(8,128)(2,1)S(1)} %collective-permute-done.6.refs_2_, ...), custom_call_target="tpu_custom_call" | custom-call | flops 7340032 | bytes 346112 | tf_op jit(solution)/shard_map/pallas_call | solution.py:174
Async XLA Ops:
  0.0 9.6 %collective-permute-start = (bf16[2,3584,128]{2,1,0:T(8,128)(2,1)}, bf16[2,3584,128]{2,1,0:T(8,128)(2,1)S(1)}, u32[]{:S(2)}, u32[]{:S(2)}) collective-permute-start(bf16[2,3584,128]{2,1,0:T(8,128)(2,1)} %in_hbm.1), channel_id=1, source_target_pairs={{0,1},{1,0},{2,3},{3,2},{4,5},{5,4},{6,7},{7,6},{8,9},{9,8},{10,11... | collective-permute-start | bytes 5505032 | tf_op jit(solution)/shard_map/ppermute | solution.py:215
  1.6 7.2 %collective-permute-start.1 = (bf16[8,3584]{1,0:T(8,128)(2,1)S(1)}, bf16[8,3584]{1,0:T(8,128)(2,1)S(1)}, u32[]{:S(2)}, u32[]{:S(2)}) collective-permute-start(bf16[8,3584]{1,0:T(8,128)(2,1)S(1)} %get-tuple-element.22), channel_id=1, source_target_pairs={{0,7},{1,6},{2,5},{3,4},{4,3},{5,2},{6,1},{7,0},{8,15},{9,14},{10,... | collective-permute-start | bytes 172040 | tf_op jit(solution)/shard_map/ppermute | solution.py:209
  5.2 3.6 %collective-permute-start.2 = (bf16[8,3584]{1,0:T(8,128)(2,1)S(1)}, bf16[8,3584]{1,0:T(8,128)(2,1)S(1)}, u32[]{:S(2)}, u32[]{:S(2)}) collective-permute-start(bf16[8,3584]{1,0:T(8,128)(2,1)S(1)} %get-tuple-element.23), channel_id=1, source_target_pairs={{0,3},{1,4},{2,1},{3,6},{4,7},{5,0},{6,5},{7,2},{8,11},{9,12},{10,... | collective-permute-start | bytes 172040 | tf_op jit(solution)/shard_map/ppermute | solution.py:209
  5.4 4.2 %collective-permute-start.3 = (bf16[8,3584]{1,0:T(8,128)(2,1)S(1)}, bf16[8,3584]{1,0:T(8,128)(2,1)S(1)}, u32[]{:S(2)}, u32[]{:S(2)}) collective-permute-start(bf16[8,3584]{1,0:T(8,128)(2,1)S(1)} %get-tuple-element.24), channel_id=1, source_target_pairs={{0,5},{1,2},{2,7},{3,0},{4,1},{5,6},{6,3},{7,4},{8,13},{9,10},{10,... | collective-permute-start | bytes 172040 | tf_op jit(solution)/shard_map/ppermute | solution.py:209
  7.0 3.2 %collective-permute-start.4 = (bf16[128,3584]{1,0:T(8,128)(2,1)}, bf16[128,3584]{1,0:T(8,128)(2,1)S(1)}, u32[]{:S(2)}, u32[]{:S(2)}) collective-permute-start(bf16[128,3584]{1,0:T(8,128)(2,1)} %down_hbm.1), channel_id=1, source_target_pairs={{0,1},{1,0},{2,3},{3,2},{4,5},{5,4},{6,7},{7,6},{8,9},{9,8},{10,11... | collective-permute-start | bytes 2752520 | tf_op jit(solution)/shard_map/ppermute | solution.py:215
  10.6 5.0 %collective-permute-start.5 = (bf16[8,3584]{1,0:T(8,128)(2,1)S(1)}, bf16[8,3584]{1,0:T(8,128)(2,1)S(1)}, u32[]{:S(2)}, u32[]{:S(2)}) collective-permute-start(bf16[8,3584]{1,0:T(8,128)(2,1)S(1)} %get-tuple-element.28), channel_id=1, source_target_pairs={{0,7},{1,6},{2,5},{3,4},{4,3},{5,2},{6,1},{7,0},{8,15},{9,14},{10,... | collective-permute-start | bytes 172040 | tf_op jit(solution)/shard_map/ppermute | solution.py:209
  11.7 4.9 %collective-permute-start.6 = (bf16[8,3584]{1,0:T(8,128)(2,1)S(1)}, bf16[8,3584]{1,0:T(8,128)(2,1)S(1)}, u32[]{:S(2)}, u32[]{:S(2)}) collective-permute-start(bf16[8,3584]{1,0:T(8,128)(2,1)S(1)} %get-tuple-element.29), channel_id=1, source_target_pairs={{0,3},{1,4},{2,1},{3,6},{4,7},{5,0},{6,5},{7,2},{8,11},{9,12},{10,... | collective-permute-start | bytes 172040 | tf_op jit(solution)/shard_map/ppermute | solution.py:209
  12.3 4.2 %collective-permute-start.7 = (bf16[8,3584]{1,0:T(8,128)(2,1)S(1)}, bf16[8,3584]{1,0:T(8,128)(2,1)S(1)}, u32[]{:S(2)}, u32[]{:S(2)}) collective-permute-start(bf16[8,3584]{1,0:T(8,128)(2,1)S(1)} %get-tuple-element.30), channel_id=1, source_target_pairs={{0,5},{1,2},{2,7},{3,0},{4,1},{5,6},{6,3},{7,4},{8,13},{9,10},{10,... | collective-permute-start | bytes 172040 | tf_op jit(solution)/shard_map/ppermute | solution.py:209

commit v14 on v13

--- a/solution.py
+++ b/solution.py
@@ -118,10 +118,16 @@
     odd = lax.axis_index("expert") & 1
     rows = stack(refs)
     half_size = refs[0].shape[0] // 2
+    middle = rows.shape[1] // 256 * 128
     hidden = []
     for half, ref in enumerate((in_ref, twin_in_ref)):
-        gate = jnp.dot(rows, ref[0], preferred_element_type=jnp.float32)
-        up = jnp.dot(rows, ref[1], preferred_element_type=jnp.float32)
+        gate, up = [
+            sum(
+                jnp.dot(rows[:, part], ref[g, part], preferred_element_type=jnp.float32)
+                for part in (slice(0, middle), slice(middle, None))
+            )
+            for g in range(2)
+        ]
         value = jax.nn.silu(gate) * up
         if split:
             place = lax.broadcasted_iota(jnp.int32, value.shape, 0) // half_size
@@ -262,7 +268,7 @@
         4 * chips * block.shape[0] * hidden * width,
     )
     returned = exchange(pieces, split, back=True)
-    parts = 4 if width % 512 == 0 else 1
+    parts = 2 if width % 256 == 0 else 1
     return call(
         functools.partial(mix_kernel, repeats, tuple(returned)),
         shape_of(tokens),

time: 17.6 us -> 17.5 us (level)
  transfers between devices with their start and end apart: 8 -> 8, of which waited for: 4 -> 4; matrix products, arithmetic and copies ran while one was open for 0% -> 0% of each run, Pallas kernels for 20% -> 21%
where the time goes in v14:
time: 17.5 us; the launch traced here: 17.4 us
  starting transfers between devices  8.65 us (49%)
  Pallas kernels  4.78 us (27%)
  waiting for transfers between devices  3.9 us (22%)
    ppermute x6, starting transfers between devices, exchange(): result[block] = lax.ppermute(blocks[block], 'expert', pairs)  8.19 us
    pallas_call x5, Pallas kernels, call(): pl.pallas_call(kernel, out_shape=outs, in_specs=arg_specs, out_specs=out_...  4.78 us
    ppermute x6, waiting for transfers between devices, exchange(): result[block] = lax.ppermute(blocks[block], 'expert', pairs)  3.89 us
    ppermute x2, starting transfers between devices, from_twin(): return lax.ppermute(array, 'expert', pairs)  0.46 us
  transfers between devices with their start and end apart: 8, of which 4 were waited for; matrix products, arithmetic and copies ran while one was open for 0% of the time, Pallas kernels for 21%

profile of v14, /device:TPU:0, one launch (start us, length us, event | category | flops | bytes accessed | tf_op | source)
XLA Modules:
  0.0 17.4 jit_solution(1544314467380512354)
XLA Ops:
  0.0 0.5 %collective-permute-start = (bf16[2,3584,128]{2,1,0:T(8,128)(2,1)}, bf16[2,3584,128]{2,1,0:T(8,128)(2,1)S(1)}, u32[]{:S(2)}, u32[]{:S(2)}) collective-permute-start(bf16[2,3584,128]{2,1,0:T(8,128)(2,1)} %in_hbm.1), channel_id=1, source_target_pairs={{0,1},{1,0},{2,3},{3,2},{4,5},{5,4},{6,7},{7,6},{8,9},{9,8},{10,11... | collective-permute-start | bytes 5505032 | tf_op jit(solution)/shard_map/ppermute | solution.py:221
  0.5 1.2 %shard_map.82 = (s32[2,16]{1,0:T(2,128)S(1)}, bf16[8,3584]{1,0:T(8,128)(2,1)S(1)}, bf16[8,3584]{1,0:T(8,128)(2,1)S(1)}, bf16[8,3584]{1,0:T(8,128)(2,1)S(1)}, bf16[8,3584]{1,0:T(8,128)(2,1)S(1)}) custom-call(s32[8]{0:T(128)} %refs_0_.1, s32[8]{0:T(128)} %refs_1_.1, s32[2,16]{1,0:T(2,128)} %bitcast.3, s32[2,16]{1,0:T(2,128)} %bitcast.4, bf16[16,3584]{1,0:T(8,128)(2,1)} %refs_4_.1), custom_call_target="tpu_custom_call" | custom-call | flops 3670016 | bytes 344512 | tf_op jit(solution)/shard_map/pallas_call | solution.py:180
  1.6 3.6 %collective-permute-start.1 = (bf16[8,3584]{1,0:T(8,128)(2,1)S(1)}, bf16[8,3584]{1,0:T(8,128)(2,1)S(1)}, u32[]{:S(2)}, u32[]{:S(2)}) collective-permute-start(bf16[8,3584]{1,0:T(8,128)(2,1)S(1)} %get-tuple-element.22), channel_id=1, source_target_pairs={{0,7},{1,6},{2,5},{3,4},{4,3},{5,2},{6,1},{7,0},{8,15},{9,14},{10,... | collective-permute-start | bytes 172040 | tf_op jit(solution)/shard_map/ppermute | solution.py:215
  5.2 0.1 collective-permute-start.2
  5.4 1.6 %collective-permute-start.3 = (bf16[8,3584]{1,0:T(8,128)(2,1)S(1)}, bf16[8,3584]{1,0:T(8,128)(2,1)S(1)}, u32[]{:S(2)}, u32[]{:S(2)}) collective-permute-start(bf16[8,3584]{1,0:T(8,128)(2,1)S(1)} %get-tuple-element.24), channel_id=1, source_target_pairs={{0,5},{1,2},{2,7},{3,0},{4,1},{5,6},{6,3},{7,4},{8,13},{9,10},{10,... | collective-permute-start | bytes 172040 | tf_op jit(solution)/shard_map/ppermute | solution.py:215
  7.0 0.0 collective-permute-start.4
  7.0 1.8 %shard_map.83 = (bf16[2,3584,128]{2,1,0:T(8,128)(2,1)S(1)}, bf16[128,3584]{1,0:T(8,128)(2,1)S(1)}, bf16[32,32]{1,0:T(8,128)(2,1)S(1)}) custom-call(s32[2,16]{1,0:T(2,128)S(1)} %get-tuple-element.18.found_ref, f32[2,16]{1,0:T(2,128)} %bitcast.5, bf16[2,3584,128]{2,1,0:T(8,128)(2,1)} %in_hbm.1, bf16[128,3584]{1,0:T(8,128)(2,1)} %down_hbm.1), custom_call_target="tpu_custom_call" | custom-call | bytes 5507328 | tf_op jit(solution)/shard_map/pallas_call | solution.py:180
  8.8 0.0 collective-permute-done.1.refs_1_
  8.8 0.1 collective-permute-done.2.refs_2_
  8.8 0.7 %collective-permute-done.3.refs_3_ = bf16[8,3584]{1,0:T(8,128)(2,1)S(1)} collective-permute-done((bf16[8,3584]{1,0:T(8,128)(2,1)S(1)}, bf16[8,3584]{1,0:T(8,128)(2,1)S(1)}, u32[]{:S(2)}, u32[]{:S(2)}) %collective-permute-start.3) | collective-permute-done | bytes 57376 | tf_op jit(solution)/shard_map/ppermute | solution.py:215
  9.6 0.0 collective-permute-done.twin_in_ref
  9.6 0.6 %shard_map.84.hidden_ref = bf16[32,256]{1,0:T(8,128)(2,1)S(1)} custom-call(bf16[2,3584,128]{2,1,0:T(8,128)(2,1)S(1)} %get-tuple-element.20.in_ref, bf16[2,3584,128]{2,1,0:T(8,128)(2,1)S(1)} %collective-permute-done.twin_in_ref, bf16[8,3584]{1,0:T(8,128)(2,1)S(1)} %get-tuple-element.21.refs_0_, bf16[8,3584]{1,0:T(8,128)(2,1)S(1)} %collective-permute-done.1.refs_1_, ...), custom_call_target="tpu_custom_call" | custom-call | flops 11744051200 | bytes 3915776 | tf_op jit(solution)/shard_map/pallas_call | solution.py:180
  10.2 0.0 collective-permute-done.4.twin_down_ref
  10.2 0.4 %shard_map.85 = (bf16[8,3584]{1,0:T(8,128)(2,1)S(1)}, bf16[8,3584]{1,0:T(8,128)(2,1)S(1)}, bf16[8,3584]{1,0:T(8,128)(2,1)S(1)}, bf16[8,3584]{1,0:T(8,128)(2,1)S(1)}) custom-call(bf16[32,256]{1,0:T(8,128)(2,1)S(1)} %shard_map.84.hidden_ref, bf16[128,3584]{1,0:T(8,128)(2,1)S(1)} %get-tuple-element.25.down_ref, ...), custom_call_target="tpu_custom_call" | custom-call | flops 58720256 | bytes 2080768 | tf_op jit(solution)/shard_map/pallas_call | solution.py:180
  10.6 1.1 %collective-permute-start.5 = (bf16[8,3584]{1,0:T(8,128)(2,1)S(1)}, bf16[8,3584]{1,0:T(8,128)(2,1)S(1)}, u32[]{:S(2)}, u32[]{:S(2)}) collective-permute-start(bf16[8,3584]{1,0:T(8,128)(2,1)S(1)} %get-tuple-element.28), channel_id=1, source_target_pairs={{0,7},{1,6},{2,5},{3,4},{4,3},{5,2},{6,1},{7,0},{8,15},{9,14},{10,... | collective-permute-start | bytes 172040 | tf_op jit(solution)/shard_map/ppermute | solution.py:215
  11.7 0.6 %collective-permute-start.6 = (bf16[8,3584]{1,0:T(8,128)(2,1)S(1)}, bf16[8,3584]{1,0:T(8,128)(2,1)S(1)}, u32[]{:S(2)}, u32[]{:S(2)}) collective-permute-start(bf16[8,3584]{1,0:T(8,128)(2,1)S(1)} %get-tuple-element.29), channel_id=1, source_target_pairs={{0,3},{1,4},{2,1},{3,6},{4,7},{5,0},{6,5},{7,2},{8,11},{9,12},{10,... | collective-permute-start | bytes 172040 | tf_op jit(solution)/shard_map/ppermute | solution.py:215
  12.3 1.1 %collective-permute-start.7 = (bf16[8,3584]{1,0:T(8,128)(2,1)S(1)}, bf16[8,3584]{1,0:T(8,128)(2,1)S(1)}, u32[]{:S(2)}, u32[]{:S(2)}) collective-permute-start(bf16[8,3584]{1,0:T(8,128)(2,1)S(1)} %get-tuple-element.30), channel_id=1, source_target_pairs={{0,5},{1,2},{2,7},{3,0},{4,1},{5,6},{6,3},{7,4},{8,13},{9,10},{10,... | collective-permute-start | bytes 172040 | tf_op jit(solution)/shard_map/ppermute | solution.py:215
  13.4 2.1 %collective-permute-done.5.refs_1_ = bf16[8,3584]{1,0:T(8,128)(2,1)S(1)} collective-permute-done((bf16[8,3584]{1,0:T(8,128)(2,1)S(1)}, bf16[8,3584]{1,0:T(8,128)(2,1)S(1)}, u32[]{:S(2)}, u32[]{:S(2)}) %collective-permute-start.5) | collective-permute-done | bytes 57376 | tf_op jit(solution)/shard_map/ppermute | solution.py:215
  15.5 1.0 %collective-permute-done.6.refs_2_ = bf16[8,3584]{1,0:T(8,128)(2,1)S(1)} collective-permute-done((bf16[8,3584]{1,0:T(8,128)(2,1)S(1)}, bf16[8,3584]{1,0:T(8,128)(2,1)S(1)}, u32[]{:S(2)}, u32[]{:S(2)}) %collective-permute-start.6) | collective-permute-done | bytes 57376 | tf_op jit(solution)/shard_map/ppermute | solution.py:215
  16.5 0.0 collective-permute-done.7.refs_3_
  16.5 0.8 %shard_map.86 = bf16[16,3584]{1,0:T(8,128)(2,1)} custom-call(bf16[32,32]{1,0:T(8,128)(2,1)S(1)} %get-tuple-element.19.weight_ref, bf16[8,3584]{1,0:T(8,128)(2,1)S(1)} %get-tuple-element.27.refs_0_, bf16[8,3584]{1,0:T(8,128)(2,1)S(1)} %collective-permute-done.5.refs_1_, bf16[8,3584]{1,0:T(8,128)(2,1)S(1)} %collective-permute-done.6.refs_2_, ...), custom_call_target="tpu_custom_call" | custom-call | flops 7340032 | bytes 346112 | tf_op jit(solution)/shard_map/pallas_call | solution.py:180
Async XLA Ops:
  0.0 9.6 %collective-permute-start = (bf16[2,3584,128]{2,1,0:T(8,128)(2,1)}, bf16[2,3584,128]{2,1,0:T(8,128)(2,1)S(1)}, u32[]{:S(2)}, u32[]{:S(2)}) collective-permute-start(bf16[2,3584,128]{2,1,0:T(8,128)(2,1)} %in_hbm.1), channel_id=1, source_target_pairs={{0,1},{1,0},{2,3},{3,2},{4,5},{5,4},{6,7},{7,6},{8,9},{9,8},{10,11... | collective-permute-start | bytes 5505032 | tf_op jit(solution)/shard_map/ppermute | solution.py:221
  1.6 7.2 %collective-permute-start.1 = (bf16[8,3584]{1,0:T(8,128)(2,1)S(1)}, bf16[8,3584]{1,0:T(8,128)(2,1)S(1)}, u32[]{:S(2)}, u32[]{:S(2)}) collective-permute-start(bf16[8,3584]{1,0:T(8,128)(2,1)S(1)} %get-tuple-element.22), channel_id=1, source_target_pairs={{0,7},{1,6},{2,5},{3,4},{4,3},{5,2},{6,1},{7,0},{8,15},{9,14},{10,... | collective-permute-start | bytes 172040 | tf_op jit(solution)/shard_map/ppermute | solution.py:215
  5.2 3.6 %collective-permute-start.2 = (bf16[8,3584]{1,0:T(8,128)(2,1)S(1)}, bf16[8,3584]{1,0:T(8,128)(2,1)S(1)}, u32[]{:S(2)}, u32[]{:S(2)}) collective-permute-start(bf16[8,3584]{1,0:T(8,128)(2,1)S(1)} %get-tuple-element.23), channel_id=1, source_target_pairs={{0,3},{1,4},{2,1},{3,6},{4,7},{5,0},{6,5},{7,2},{8,11},{9,12},{10,... | collective-permute-start | bytes 172040 | tf_op jit(solution)/shard_map/ppermute | solution.py:215
  5.4 4.2 %collective-permute-start.3 = (bf16[8,3584]{1,0:T(8,128)(2,1)S(1)}, bf16[8,3584]{1,0:T(8,128)(2,1)S(1)}, u32[]{:S(2)}, u32[]{:S(2)}) collective-permute-start(bf16[8,3584]{1,0:T(8,128)(2,1)S(1)} %get-tuple-element.24), channel_id=1, source_target_pairs={{0,5},{1,2},{2,7},{3,0},{4,1},{5,6},{6,3},{7,4},{8,13},{9,10},{10,... | collective-permute-start | bytes 172040 | tf_op jit(solution)/shard_map/ppermute | solution.py:215
  7.0 3.2 %collective-permute-start.4 = (bf16[128,3584]{1,0:T(8,128)(2,1)}, bf16[128,3584]{1,0:T(8,128)(2,1)S(1)}, u32[]{:S(2)}, u32[]{:S(2)}) collective-permute-start(bf16[128,3584]{1,0:T(8,128)(2,1)} %down_hbm.1), channel_id=1, source_target_pairs={{0,1},{1,0},{2,3},{3,2},{4,5},{5,4},{6,7},{7,6},{8,9},{9,8},{10,11... | collective-permute-start | bytes 2752520 | tf_op jit(solution)/shard_map/ppermute | solution.py:221
  10.6 5.0 %collective-permute-start.5 = (bf16[8,3584]{1,0:T(8,128)(2,1)S(1)}, bf16[8,3584]{1,0:T(8,128)(2,1)S(1)}, u32[]{:S(2)}, u32[]{:S(2)}) collective-permute-start(bf16[8,3584]{1,0:T(8,128)(2,1)S(1)} %get-tuple-element.28), channel_id=1, source_target_pairs={{0,7},{1,6},{2,5},{3,4},{4,3},{5,2},{6,1},{7,0},{8,15},{9,14},{10,... | collective-permute-start | bytes 172040 | tf_op jit(solution)/shard_map/ppermute | solution.py:215
  11.7 4.9 %collective-permute-start.6 = (bf16[8,3584]{1,0:T(8,128)(2,1)S(1)}, bf16[8,3584]{1,0:T(8,128)(2,1)S(1)}, u32[]{:S(2)}, u32[]{:S(2)}) collective-permute-start(bf16[8,3584]{1,0:T(8,128)(2,1)S(1)} %get-tuple-element.29), channel_id=1, source_target_pairs={{0,3},{1,4},{2,1},{3,6},{4,7},{5,0},{6,5},{7,2},{8,11},{9,12},{10,... | collective-permute-start | bytes 172040 | tf_op jit(solution)/shard_map/ppermute | solution.py:215
  12.3 4.2 %collective-permute-start.7 = (bf16[8,3584]{1,0:T(8,128)(2,1)S(1)}, bf16[8,3584]{1,0:T(8,128)(2,1)S(1)}, u32[]{:S(2)}, u32[]{:S(2)}) collective-permute-start(bf16[8,3584]{1,0:T(8,128)(2,1)S(1)} %get-tuple-element.30), channel_id=1, source_target_pairs={{0,5},{1,2},{2,7},{3,0},{4,1},{5,6},{6,3},{7,4},{8,13},{9,10},{10,... | collective-permute-start | bytes 172040 | tf_op jit(solution)/shard_map/ppermute | solution.py:215

commit v15 on v12

--- a/solution.py
+++ b/solution.py
@@ -9,13 +9,17 @@
 
 SLOTS = 8
 CAP = 4
-CHIP_STEPS = ((0, 3, 1, 2), (0, 3, 1, 2))
+SENDS = (
+    ((3, 2, 0, 1), (2, 3, 1, 0), (1, 0, 3, 2)),
+    ((1, 2, 3, 0), (2, 3, 0, 1), (3, 0, 1, 2)),
+)
+BACK = ((3, 2, 1), (2, 1, 3))
 
 VMEM = pl.BlockSpec(memory_space=pltpu.VMEM)
 HBM = pl.BlockSpec(memory_space=pltpu.HBM)
 
 
-def targets(shards, new_ref, old_ref, ids, replica):
+def targets(shards, goes, new_ref, old_ref, ids, replica):
     slots, rows = new_ref.shape[0], ids.shape[1]
     device = lax.axis_index("expert")
     down = lax.broadcasted_iota(jnp.int32, (slots, rows), 0)
@@ -25,11 +29,8 @@
         source = jnp.where(new_ref[slot] == old_ref[slot], slot, slot ^ 1)
         away = source ^ (device // shards)
         if shards == 1:
-            chip = away >> 1
-            even, odd = [
-                sum(jnp.where(chip == c, k, 0) for k, c in enumerate(steps)) for steps in CHIP_STEPS
-            ]
-            away = (source & 1) | (jnp.where((device & 1) == 1, odd, even) << 1)
+            step = sum(jnp.where(source >> 1 == chip, k, 0) for k, chip in enumerate(goes, 1))
+            away = (source & 1) | (step << 1)
         expert = jnp.where(down == slot, new_ref[slot], expert)
         line = jnp.where(down == slot, CAP * away, line)
     count = jnp.zeros((slots, rows), jnp.int32)
@@ -67,14 +68,20 @@
     return copies
 
 
+def by_device(table):
+    device = lax.axis_index("expert")
+    return sum(jnp.where(device == i, entry, 0) for i, entry in enumerate(table))
+
+
 def dispatch_kernel(shards, *refs):
     sources, refs = refs[:5], refs[5:]
     found_ref, *block_refs = refs[:-6]
     buffers, sems = refs[-6:-1], refs[-1]
     copies = start_copies(sources, buffers, sems)
+    goes = [by_device([SENDS[i & 1][k][i >> 1] for i in range(SLOTS)]) for k in range(3)]
     for copy in copies[:-1]:
         copy.wait()
-    found = targets(shards, *buffers[:2], *[ref[...] for ref in buffers[2:-1]])
+    found = targets(shards, goes, *buffers[:2], *[ref[...] for ref in buffers[2:-1]])
     found_ref[...] = jnp.concatenate(found, axis=0)
     tokens_ref = buffers[-1]
     size = block_refs[0].shape[0]
@@ -88,13 +95,19 @@
 
 
 def prepare_kernel(
-    found_ref, combine_hbm, in_hbm, down_hbm, in_ref, down_ref, weight_ref, combine_ref, sems
+    split, found_ref, combine_hbm, in_hbm, down_hbm, in_ref, down_ref, weight_ref, combine_ref, sems
 ):
     copies = start_copies(
         (combine_hbm, in_hbm, down_hbm), (combine_ref, in_ref, down_ref), sems
     )
     copies[0].wait()
     line = lax.broadcasted_iota(jnp.int32, (weight_ref.shape[1], combine_ref.shape[1]), 0)
+    if split:
+        even = (lax.axis_index("expert") & 1) == 0
+        block = line // (2 * CAP)
+        for at, steps in enumerate(zip(BACK[1], BACK[0]), 1):
+            came = jnp.where(even, *steps)
+            line = jnp.where(block == at, line + 2 * CAP * (came - at), line)
     weight = functools.reduce(
         jnp.add,
         [
@@ -130,15 +143,19 @@
     out_ref[...] = jnp.concatenate(hidden, axis=1)
 
 
-def down_kernel(hidden_ref, down_ref, twin_down_ref, *refs):
+def down_kernel(split, hidden_ref, down_ref, twin_down_ref, *refs):
     units = down_ref.shape[0]
     own = hidden_ref[:, :units], down_ref[...]
     twin = hidden_ref[:, units:], twin_down_ref[...]
     piece = jnp.dot(*own, preferred_element_type=jnp.float32)
     piece += jnp.dot(*twin, preferred_element_type=jnp.float32)
     size = refs[0].shape[0]
-    for b, out_ref in enumerate(refs):
-        out_ref[...] = piece[size * b : size * (b + 1)].astype(jnp.bfloat16)
+    blocks = [piece[size * b : size * (b + 1)] for b in range(len(refs))]
+    if split:
+        even = (lax.axis_index("expert") & 1) == 0
+        blocks[1:] = [jnp.where(even, blocks[e], blocks[o]) for e, o in zip(*BACK)]
+    for block, out_ref in zip(blocks, refs):
+        out_ref[...] = block.astype(jnp.bfloat16)
 
 
 def mix_kernel(repeats, weight_ref, *refs):
@@ -196,15 +213,20 @@
 
 def exchange(blocks, split, back=False):
     devices = lax.axis_size("expert")
-    result = list(blocks)
+
+    def sends(i, k):
+        return 2 * SENDS[i & 1][k - 1][i >> 1] + (1 - (i & 1)) if split else i ^ 2 * k
+
+    def sent_from(i, k):
+        return next(j for j in range(devices) if sends(j, k) == i)
+
+    result = [blocks[0]]
     for k in range(1, len(blocks)):
-        if split:
-            pairs = [(i, i ^ 1 ^ 2 * CHIP_STEPS[i & 1][k]) for i in range(devices)]
+        if back and split:
+            pairs = [(i, sent_from(i, BACK[i & 1][k - 1])) for i in range(devices)]
         else:
-            pairs = [(i, i ^ 2 * k) for i in range(devices)]
-        if back:
-            pairs = [(target, source) for source, target in pairs]
-        result[k] = lax.ppermute(blocks[k], "expert", pairs)
+            pairs = [(i, sends(i, k)) for i in range(devices)]
+        result.append(lax.ppermute(blocks[k], "expert", pairs))
     return result
 
 
@@ -236,7 +258,7 @@
     received = exchange([blocks[c // repeats] for c in range(chips)], split)
     twin_down = from_twin(lax.optimization_barrier((w_down, found))[0])
     own_in, own_down, weight = call(
-        prepare_kernel,
+        functools.partial(prepare_kernel, split),
         [
             shape_of(w_in),
             shape_of(w_down),
@@ -254,7 +276,7 @@
         800 * chips * block.shape[0] * hidden * width,
     )
     pieces = call(
-        down_kernel,
+        functools.partial(down_kernel, split),
         [block] * chips,
         (units, own_down, twin_down),
         4 * chips * block.shape[0] * hidden * width,

time: 17.9 us -> 17.2 us (0.961)
  waiting for transfers between devices: 4.95 us -> 2.6 us
  starting transfers between devices: 7.93 us -> 9.59 us
    ppermute x6, waiting for transfers between devices: 4.95 us -> 2.6 us  [exchange(): result.append(lax.ppermute(blocks[k], 'expert', pairs))]
    ppermute x6, starting transfers between devices: 6.98 us -> 8.24 us  [exchange(): result.append(lax.ppermute(blocks[k], 'expert', pairs))]
    ppermute x2, starting transfers between devices: 0.95 us -> 1.36 us  [from_twin(): return lax.ppermute(array, 'expert', pairs)]
  transfers between devices with their start and end apart: 8 -> 8, of which waited for: 4 -> 2; matrix products, arithmetic and copies ran while one was open for 0% -> 0% of each run, Pallas kernels for 20% -> 21%
where the time goes in v15:
time: 17.2 us; the launch traced here: 17 us
  starting transfers between devices  9.59 us (56%)
  Pallas kernels  4.79 us (28%)
  waiting for transfers between devices  2.6 us (15%)
    ppermute x6, starting transfers between devices, exchange(): result.append(lax.ppermute(blocks[k], 'expert', pairs))  8.24 us
    pallas_call x5, Pallas kernels, call(): pl.pallas_call(kernel, out_shape=outs, in_specs=arg_specs, out_specs=out_...  4.79 us
    ppermute x6, waiting for transfers between devices, exchange(): result.append(lax.ppermute(blocks[k], 'expert', pairs))  2.6 us
    ppermute x2, starting transfers between devices, from_twin(): return lax.ppermute(array, 'expert', pairs)  1.36 us
  transfers between devices with their start and end apart: 8, of which 2 were waited for; matrix products, arithmetic and copies ran while one was open for 0% of the time, Pallas kernels for 21%

profile of v15, /device:TPU:0, one launch (start us, length us, event | category | flops | bytes accessed | tf_op | source)
XLA Modules:
  0.0 17.0 jit_solution(17608454783621778669)
XLA Ops:
  0.0 0.5 %collective-permute-start = (bf16[2,3584,128]{2,1,0:T(8,128)(2,1)}, bf16[2,3584,128]{2,1,0:T(8,128)(2,1)S(1)}, u32[]{:S(2)}, u32[]{:S(2)}) collective-permute-start(bf16[2,3584,128]{2,1,0:T(8,128)(2,1)} %in_hbm.1), channel_id=1, source_target_pairs={{0,1},{1,0},{2,3},{3,2},{4,5},{5,4},{6,7},{7,6},{8,9},{9,8},{10,11... | collective-permute-start | bytes 5505032 | tf_op jit(solution)/shard_map/ppermute | solution.py:235
  0.5 1.2 %shard_map.82 = (s32[2,16]{1,0:T(2,128)S(1)}, bf16[8,3584]{1,0:T(8,128)(2,1)S(1)}, bf16[8,3584]{1,0:T(8,128)(2,1)S(1)}, bf16[8,3584]{1,0:T(8,128)(2,1)S(1)}, bf16[8,3584]{1,0:T(8,128)(2,1)S(1)}) custom-call(s32[8]{0:T(128)} %refs_0_.1, s32[8]{0:T(128)} %refs_1_.1, s32[2,16]{1,0:T(2,128)} %bitcast.3, s32[2,16]{1,0:T(2,128)} %bitcast.4, bf16[16,3584]{1,0:T(8,128)(2,1)} %refs_4_.1), custom_call_target="tpu_custom_call" | custom-call | flops 3670016 | bytes 344512 | tf_op jit(solution)/shard_map/pallas_call | solution.py:191
  1.6 3.6 %collective-permute-start.1 = (bf16[8,3584]{1,0:T(8,128)(2,1)S(1)}, bf16[8,3584]{1,0:T(8,128)(2,1)S(1)}, u32[]{:S(2)}, u32[]{:S(2)}) collective-permute-start(bf16[8,3584]{1,0:T(8,128)(2,1)S(1)} %get-tuple-element.22), channel_id=1, source_target_pairs={{0,7},{1,2},{2,5},{3,4},{4,1},{5,6},{6,3},{7,0},{8,15},{9,10},{10,... | collective-permute-start | bytes 172040 | tf_op jit(solution)/shard_map/ppermute | solution.py:229
  5.2 0.2 %collective-permute-start.2 = (bf16[8,3584]{1,0:T(8,128)(2,1)S(1)}, bf16[8,3584]{1,0:T(8,128)(2,1)S(1)}, u32[]{:S(2)}, u32[]{:S(2)}) collective-permute-start(bf16[8,3584]{1,0:T(8,128)(2,1)S(1)} %get-tuple-element.23), channel_id=1, source_target_pairs={{0,5},{1,4},{2,7},{3,6},{4,3},{5,0},{6,1},{7,2},{8,13},{9,12},{10,... | collective-permute-start | bytes 172040 | tf_op jit(solution)/shard_map/ppermute | solution.py:229
  5.4 0.6 %collective-permute-start.3 = (bf16[8,3584]{1,0:T(8,128)(2,1)S(1)}, bf16[8,3584]{1,0:T(8,128)(2,1)S(1)}, u32[]{:S(2)}, u32[]{:S(2)}) collective-permute-start(bf16[8,3584]{1,0:T(8,128)(2,1)S(1)} %get-tuple-element.24), channel_id=1, source_target_pairs={{0,3},{1,6},{2,1},{3,0},{4,7},{5,2},{6,5},{7,4},{8,11},{9,14},{10,... | collective-permute-start | bytes 172040 | tf_op jit(solution)/shard_map/ppermute | solution.py:229
  6.0 0.9 %collective-permute-start.4 = (bf16[128,3584]{1,0:T(8,128)(2,1)}, bf16[128,3584]{1,0:T(8,128)(2,1)S(1)}, u32[]{:S(2)}, u32[]{:S(2)}) collective-permute-start(bf16[128,3584]{1,0:T(8,128)(2,1)} %down_hbm.1), channel_id=1, source_target_pairs={{0,1},{1,0},{2,3},{3,2},{4,5},{5,4},{6,7},{7,6},{8,9},{9,8},{10,11... | collective-permute-start | bytes 2752520 | tf_op jit(solution)/shard_map/ppermute | solution.py:235
  6.9 1.8 %shard_map.83 = (bf16[2,3584,128]{2,1,0:T(8,128)(2,1)S(1)}, bf16[128,3584]{1,0:T(8,128)(2,1)S(1)}, bf16[32,32]{1,0:T(8,128)(2,1)S(1)}) custom-call(s32[2,16]{1,0:T(2,128)S(1)} %get-tuple-element.18.found_ref, f32[2,16]{1,0:T(2,128)} %bitcast.5, bf16[2,3584,128]{2,1,0:T(8,128)(2,1)} %in_hbm.1, bf16[128,3584]{1,0:T(8,128)(2,1)} %down_hbm.1), custom_call_target="tpu_custom_call" | custom-call | bytes 5507328 | tf_op jit(solution)/shard_map/pallas_call | solution.py:191
  8.7 0.0 collective-permute-done.1.refs_1_
  8.7 0.7 %collective-permute-done.2.refs_2_ = bf16[8,3584]{1,0:T(8,128)(2,1)S(1)} collective-permute-done((bf16[8,3584]{1,0:T(8,128)(2,1)S(1)}, bf16[8,3584]{1,0:T(8,128)(2,1)S(1)}, u32[]{:S(2)}, u32[]{:S(2)}) %collective-permute-start.2) | collective-permute-done | bytes 57376 | tf_op jit(solution)/shard_map/ppermute | solution.py:229
  9.4 0.0 collective-permute-done.3.refs_3_
  9.4 0.0 collective-permute-done.twin_in_ref
  9.5 0.6 %shard_map.84.hidden_ref = bf16[32,256]{1,0:T(8,128)(2,1)S(1)} custom-call(bf16[2,3584,128]{2,1,0:T(8,128)(2,1)S(1)} %get-tuple-element.20.in_ref, bf16[2,3584,128]{2,1,0:T(8,128)(2,1)S(1)} %collective-permute-done.twin_in_ref, bf16[8,3584]{1,0:T(8,128)(2,1)S(1)} %get-tuple-element.21.refs_0_, bf16[8,3584]{1,0:T(8,128)(2,1)S(1)} %collective-permute-done.1.refs_1_, ...), custom_call_target="tpu_custom_call" | custom-call | flops 11744051200 | bytes 3915776 | tf_op jit(solution)/shard_map/pallas_call | solution.py:191
  10.1 0.0 collective-permute-done.4.twin_down_ref
  10.1 0.4 %shard_map.85 = (bf16[8,3584]{1,0:T(8,128)(2,1)S(1)}, bf16[8,3584]{1,0:T(8,128)(2,1)S(1)}, bf16[8,3584]{1,0:T(8,128)(2,1)S(1)}, bf16[8,3584]{1,0:T(8,128)(2,1)S(1)}) custom-call(bf16[32,256]{1,0:T(8,128)(2,1)S(1)} %shard_map.84.hidden_ref, bf16[128,3584]{1,0:T(8,128)(2,1)S(1)} %get-tuple-element.25.down_ref, ...), custom_call_target="tpu_custom_call" | custom-call | flops 58720256 | bytes 2080768 | tf_op jit(solution)/shard_map/pallas_call | solution.py:191
  10.5 1.2 %collective-permute-start.5 = (bf16[8,3584]{1,0:T(8,128)(2,1)S(1)}, bf16[8,3584]{1,0:T(8,128)(2,1)S(1)}, u32[]{:S(2)}, u32[]{:S(2)}) collective-permute-start(bf16[8,3584]{1,0:T(8,128)(2,1)S(1)} %get-tuple-element.28), channel_id=1, source_target_pairs={{0,3},{1,6},{2,5},{3,4},{4,7},{5,0},{6,1},{7,2},{8,11},{9,14},{10,... | collective-permute-start | bytes 172040 | tf_op jit(solution)/shard_map/ppermute | solution.py:229
  11.7 0.6 %collective-permute-start.6 = (bf16[8,3584]{1,0:T(8,128)(2,1)S(1)}, bf16[8,3584]{1,0:T(8,128)(2,1)S(1)}, u32[]{:S(2)}, u32[]{:S(2)}) collective-permute-start(bf16[8,3584]{1,0:T(8,128)(2,1)S(1)} %get-tuple-element.29), channel_id=1, source_target_pairs={{0,5},{1,4},{2,7},{3,6},{4,1},{5,2},{6,3},{7,0},{8,13},{9,12},{10,... | collective-permute-start | bytes 172040 | tf_op jit(solution)/shard_map/ppermute | solution.py:229
  12.3 2.0 %collective-permute-start.7 = (bf16[8,3584]{1,0:T(8,128)(2,1)S(1)}, bf16[8,3584]{1,0:T(8,128)(2,1)S(1)}, u32[]{:S(2)}, u32[]{:S(2)}) collective-permute-start(bf16[8,3584]{1,0:T(8,128)(2,1)S(1)} %get-tuple-element.30), channel_id=1, source_target_pairs={{0,7},{1,2},{2,1},{3,0},{4,3},{5,6},{6,5},{7,4},{8,15},{9,10},{10,... | collective-permute-start | bytes 172040 | tf_op jit(solution)/shard_map/ppermute | solution.py:229
  14.3 0.0 collective-permute-done.5.refs_1_
  14.3 1.9 %collective-permute-done.6.refs_2_ = bf16[8,3584]{1,0:T(8,128)(2,1)S(1)} collective-permute-done((bf16[8,3584]{1,0:T(8,128)(2,1)S(1)}, bf16[8,3584]{1,0:T(8,128)(2,1)S(1)}, u32[]{:S(2)}, u32[]{:S(2)}) %collective-permute-start.6) | collective-permute-done | bytes 57376 | tf_op jit(solution)/shard_map/ppermute | solution.py:229
  16.2 0.0 collective-permute-done.7.refs_3_
  16.2 0.9 %shard_map.86 = bf16[16,3584]{1,0:T(8,128)(2,1)} custom-call(bf16[32,32]{1,0:T(8,128)(2,1)S(1)} %get-tuple-element.19.weight_ref, bf16[8,3584]{1,0:T(8,128)(2,1)S(1)} %get-tuple-element.27.refs_0_, bf16[8,3584]{1,0:T(8,128)(2,1)S(1)} %collective-permute-done.5.refs_1_, bf16[8,3584]{1,0:T(8,128)(2,1)S(1)} %collective-permute-done.6.refs_2_, ...), custom_call_target="tpu_custom_call" | custom-call | flops 7340032 | bytes 346112 | tf_op jit(solution)/shard_map/pallas_call | solution.py:191
Async XLA Ops:
  0.0 9.5 %collective-permute-start = (bf16[2,3584,128]{2,1,0:T(8,128)(2,1)}, bf16[2,3584,128]{2,1,0:T(8,128)(2,1)S(1)}, u32[]{:S(2)}, u32[]{:S(2)}) collective-permute-start(bf16[2,3584,128]{2,1,0:T(8,128)(2,1)} %in_hbm.1), channel_id=1, source_target_pairs={{0,1},{1,0},{2,3},{3,2},{4,5},{5,4},{6,7},{7,6},{8,9},{9,8},{10,11... | collective-permute-start | bytes 5505032 | tf_op jit(solution)/shard_map/ppermute | solution.py:235
  1.6 7.1 %collective-permute-start.1 = (bf16[8,3584]{1,0:T(8,128)(2,1)S(1)}, bf16[8,3584]{1,0:T(8,128)(2,1)S(1)}, u32[]{:S(2)}, u32[]{:S(2)}) collective-permute-start(bf16[8,3584]{1,0:T(8,128)(2,1)S(1)} %get-tuple-element.22), channel_id=1, source_target_pairs={{0,7},{1,2},{2,5},{3,4},{4,1},{5,6},{6,3},{7,0},{8,15},{9,10},{10,... | collective-permute-start | bytes 172040 | tf_op jit(solution)/shard_map/ppermute | solution.py:229
  5.2 4.2 %collective-permute-start.2 = (bf16[8,3584]{1,0:T(8,128)(2,1)S(1)}, bf16[8,3584]{1,0:T(8,128)(2,1)S(1)}, u32[]{:S(2)}, u32[]{:S(2)}) collective-permute-start(bf16[8,3584]{1,0:T(8,128)(2,1)S(1)} %get-tuple-element.23), channel_id=1, source_target_pairs={{0,5},{1,4},{2,7},{3,6},{4,3},{5,0},{6,1},{7,2},{8,13},{9,12},{10,... | collective-permute-start | bytes 172040 | tf_op jit(solution)/shard_map/ppermute | solution.py:229
  5.4 4.0 %collective-permute-start.3 = (bf16[8,3584]{1,0:T(8,128)(2,1)S(1)}, bf16[8,3584]{1,0:T(8,128)(2,1)S(1)}, u32[]{:S(2)}, u32[]{:S(2)}) collective-permute-start(bf16[8,3584]{1,0:T(8,128)(2,1)S(1)} %get-tuple-element.24), channel_id=1, source_target_pairs={{0,3},{1,6},{2,1},{3,0},{4,7},{5,2},{6,5},{7,4},{8,11},{9,14},{10,... | collective-permute-start | bytes 172040 | tf_op jit(solution)/shard_map/ppermute | solution.py:229
  6.0 4.1 %collective-permute-start.4 = (bf16[128,3584]{1,0:T(8,128)(2,1)}, bf16[128,3584]{1,0:T(8,128)(2,1)S(1)}, u32[]{:S(2)}, u32[]{:S(2)}) collective-permute-start(bf16[128,3584]{1,0:T(8,128)(2,1)} %down_hbm.1), channel_id=1, source_target_pairs={{0,1},{1,0},{2,3},{3,2},{4,5},{5,4},{6,7},{7,6},{8,9},{9,8},{10,11... | collective-permute-start | bytes 2752520 | tf_op jit(solution)/shard_map/ppermute | solution.py:235
  10.5 3.8 %collective-permute-start.5 = (bf16[8,3584]{1,0:T(8,128)(2,1)S(1)}, bf16[8,3584]{1,0:T(8,128)(2,1)S(1)}, u32[]{:S(2)}, u32[]{:S(2)}) collective-permute-start(bf16[8,3584]{1,0:T(8,128)(2,1)S(1)} %get-tuple-element.28), channel_id=1, source_target_pairs={{0,3},{1,6},{2,5},{3,4},{4,7},{5,0},{6,1},{7,2},{8,11},{9,14},{10,... | collective-permute-start | bytes 172040 | tf_op jit(solution)/shard_map/ppermute | solution.py:229
  11.7 4.5 %collective-permute-start.6 = (bf16[8,3584]{1,0:T(8,128)(2,1)S(1)}, bf16[8,3584]{1,0:T(8,128)(2,1)S(1)}, u32[]{:S(2)}, u32[]{:S(2)}) collective-permute-start(bf16[8,3584]{1,0:T(8,128)(2,1)S(1)} %get-tuple-element.29), channel_id=1, source_target_pairs={{0,5},{1,4},{2,7},{3,6},{4,1},{5,2},{6,3},{7,0},{8,13},{9,12},{10,... | collective-permute-start | bytes 172040 | tf_op jit(solution)/shard_map/ppermute | solution.py:229
  12.3 3.9 %collective-permute-start.7 = (bf16[8,3584]{1,0:T(8,128)(2,1)S(1)}, bf16[8,3584]{1,0:T(8,128)(2,1)S(1)}, u32[]{:S(2)}, u32[]{:S(2)}) collective-permute-start(bf16[8,3584]{1,0:T(8,128)(2,1)S(1)} %get-tuple-element.30), channel_id=1, source_target_pairs={{0,7},{1,2},{2,1},{3,0},{4,3},{5,6},{6,5},{7,4},{8,15},{9,10},{10,... | collective-permute-start | bytes 172040 | tf_op jit(solution)/shard_map/ppermute | solution.py:229

commit v16 on v15

--- a/solution.py
+++ b/solution.py
@@ -10,10 +10,10 @@
 SLOTS = 8
 CAP = 4
 SENDS = (
+    ((2, 3, 1, 0), (3, 2, 0, 1), (1, 0, 3, 2)),
     ((3, 2, 0, 1), (2, 3, 1, 0), (1, 0, 3, 2)),
-    ((1, 2, 3, 0), (2, 3, 0, 1), (3, 0, 1, 2)),
 )
-BACK = ((3, 2, 1), (2, 1, 3))
+BACK = ((1, 3, 2), (2, 3, 1))
 
 VMEM = pl.BlockSpec(memory_space=pltpu.VMEM)
 HBM = pl.BlockSpec(memory_space=pltpu.HBM)

time: 17.2 us -> 17.7 us (1.029)
  waiting for transfers between devices: 2.6 us -> 4.06 us
  starting transfers between devices: 9.59 us -> 8.67 us
    ppermute x6, waiting for transfers between devices: 2.6 us -> 4.05 us  [exchange(): result.append(lax.ppermute(blocks[k], 'expert', pairs))]
    ppermute x6, starting transfers between devices: 8.24 us -> 7.74 us  [exchange(): result.append(lax.ppermute(blocks[k], 'expert', pairs))]
    ppermute x2, starting transfers between devices: 1.36 us -> 0.93 us  [from_twin(): return lax.ppermute(array, 'expert', pairs)]
  transfers between devices with their start and end apart: 8 -> 8, of which waited for: 2 -> 5; matrix products, arithmetic and copies ran while one was open for 0% -> 0% of each run, Pallas kernels for 21% -> 20%
where the time goes in v16:
time: 17.7 us; the launch traced here: 17.6 us
  starting transfers between devices  8.67 us (49%)
  Pallas kernels  4.78 us (27%)
  waiting for transfers between devices  4.06 us (23%)
    ppermute x6, starting transfers between devices, exchange(): result.append(lax.ppermute(blocks[k], 'expert', pairs))  7.74 us
    pallas_call x5, Pallas kernels, call(): pl.pallas_call(kernel, out_shape=outs, in_specs=arg_specs, out_specs=out_...  4.78 us
    ppermute x6, waiting for transfers between devices, exchange(): result.append(lax.ppermute(blocks[k], 'expert', pairs))  4.05 us
    ppermute x2, starting transfers between devices, from_twin(): return lax.ppermute(array, 'expert', pairs)  0.93 us
  transfers between devices with their start and end apart: 8, of which 5 were waited for; matrix products, arithmetic and copies ran while one was open for 0% of the time, Pallas kernels for 20%

profile of v16, /device:TPU:0, one launch (start us, length us, event | category | flops | bytes accessed | tf_op | source)
XLA Modules:
  0.0 17.6 jit_solution(7293084718851244896)
XLA Ops:
  0.0 0.5 %collective-permute-start = (bf16[2,3584,128]{2,1,0:T(8,128)(2,1)}, bf16[2,3584,128]{2,1,0:T(8,128)(2,1)S(1)}, u32[]{:S(2)}, u32[]{:S(2)}) collective-permute-start(bf16[2,3584,128]{2,1,0:T(8,128)(2,1)} %in_hbm.1), channel_id=1, source_target_pairs={{0,1},{1,0},{2,3},{3,2},{4,5},{5,4},{6,7},{7,6},{8,9},{9,8},{10,11... | collective-permute-start | bytes 5505032 | tf_op jit(solution)/shard_map/ppermute | solution.py:235
  0.5 1.2 %shard_map.82 = (s32[2,16]{1,0:T(2,128)S(1)}, bf16[8,3584]{1,0:T(8,128)(2,1)S(1)}, bf16[8,3584]{1,0:T(8,128)(2,1)S(1)}, bf16[8,3584]{1,0:T(8,128)(2,1)S(1)}, bf16[8,3584]{1,0:T(8,128)(2,1)S(1)}) custom-call(s32[8]{0:T(128)} %refs_0_.1, s32[8]{0:T(128)} %refs_1_.1, s32[2,16]{1,0:T(2,128)} %bitcast.3, s32[2,16]{1,0:T(2,128)} %bitcast.4, bf16[16,3584]{1,0:T(8,128)(2,1)} %refs_4_.1), custom_call_target="tpu_custom_call" | custom-call | flops 3670016 | bytes 344512 | tf_op jit(solution)/shard_map/pallas_call | solution.py:191
  1.6 2.7 %collective-permute-start.1 = (bf16[8,3584]{1,0:T(8,128)(2,1)S(1)}, bf16[8,3584]{1,0:T(8,128)(2,1)S(1)}, u32[]{:S(2)}, u32[]{:S(2)}) collective-permute-start(bf16[8,3584]{1,0:T(8,128)(2,1)S(1)} %get-tuple-element.22), channel_id=1, source_target_pairs={{0,5},{1,6},{2,7},{3,4},{4,3},{5,0},{6,1},{7,2},{8,13},{9,14},{10,... | collective-permute-start | bytes 172040 | tf_op jit(solution)/shard_map/ppermute | solution.py:229
  4.3 1.0 %collective-permute-start.2 = (bf16[8,3584]{1,0:T(8,128)(2,1)S(1)}, bf16[8,3584]{1,0:T(8,128)(2,1)S(1)}, u32[]{:S(2)}, u32[]{:S(2)}) collective-permute-start(bf16[8,3584]{1,0:T(8,128)(2,1)S(1)} %get-tuple-element.23), channel_id=1, source_target_pairs={{0,7},{1,4},{2,5},{3,6},{4,1},{5,2},{6,3},{7,0},{8,15},{9,12},{10,... | collective-permute-start | bytes 172040 | tf_op jit(solution)/shard_map/ppermute | solution.py:229
  5.4 0.1 collective-permute-start.3
  5.5 0.5 %collective-permute-start.4 = (bf16[128,3584]{1,0:T(8,128)(2,1)}, bf16[128,3584]{1,0:T(8,128)(2,1)S(1)}, u32[]{:S(2)}, u32[]{:S(2)}) collective-permute-start(bf16[128,3584]{1,0:T(8,128)(2,1)} %down_hbm.1), channel_id=1, source_target_pairs={{0,1},{1,0},{2,3},{3,2},{4,5},{5,4},{6,7},{7,6},{8,9},{9,8},{10,11... | collective-permute-start | bytes 2752520 | tf_op jit(solution)/shard_map/ppermute | solution.py:235
  6.0 1.8 %shard_map.83 = (bf16[2,3584,128]{2,1,0:T(8,128)(2,1)S(1)}, bf16[128,3584]{1,0:T(8,128)(2,1)S(1)}, bf16[32,32]{1,0:T(8,128)(2,1)S(1)}) custom-call(s32[2,16]{1,0:T(2,128)S(1)} %get-tuple-element.18.found_ref, f32[2,16]{1,0:T(2,128)} %bitcast.5, bf16[2,3584,128]{2,1,0:T(8,128)(2,1)} %in_hbm.1, bf16[128,3584]{1,0:T(8,128)(2,1)} %down_hbm.1), custom_call_target="tpu_custom_call" | custom-call | bytes 5507328 | tf_op jit(solution)/shard_map/pallas_call | solution.py:191
  7.8 0.0 collective-permute-done.1.refs_1_
  7.8 1.1 %collective-permute-done.2.refs_2_ = bf16[8,3584]{1,0:T(8,128)(2,1)S(1)} collective-permute-done((bf16[8,3584]{1,0:T(8,128)(2,1)S(1)}, bf16[8,3584]{1,0:T(8,128)(2,1)S(1)}, u32[]{:S(2)}, u32[]{:S(2)}) %collective-permute-start.2) | collective-permute-done | bytes 57376 | tf_op jit(solution)/shard_map/ppermute | solution.py:229
  8.9 0.1 collective-permute-done.3.refs_3_
  9.0 0.0 collective-permute-done.twin_in_ref
  9.0 0.6 %shard_map.84.hidden_ref = bf16[32,256]{1,0:T(8,128)(2,1)S(1)} custom-call(bf16[2,3584,128]{2,1,0:T(8,128)(2,1)S(1)} %get-tuple-element.20.in_ref, bf16[2,3584,128]{2,1,0:T(8,128)(2,1)S(1)} %collective-permute-done.twin_in_ref, bf16[8,3584]{1,0:T(8,128)(2,1)S(1)} %get-tuple-element.21.refs_0_, bf16[8,3584]{1,0:T(8,128)(2,1)S(1)} %collective-permute-done.1.refs_1_, ...), custom_call_target="tpu_custom_call" | custom-call | flops 11744051200 | bytes 3915776 | tf_op jit(solution)/shard_map/pallas_call | solution.py:191
  9.6 0.0 collective-permute-done.4.twin_down_ref
  9.6 0.4 %shard_map.85 = (bf16[8,3584]{1,0:T(8,128)(2,1)S(1)}, bf16[8,3584]{1,0:T(8,128)(2,1)S(1)}, bf16[8,3584]{1,0:T(8,128)(2,1)S(1)}, bf16[8,3584]{1,0:T(8,128)(2,1)S(1)}) custom-call(bf16[32,256]{1,0:T(8,128)(2,1)S(1)} %shard_map.84.hidden_ref, bf16[128,3584]{1,0:T(8,128)(2,1)S(1)} %get-tuple-element.25.down_ref, ...), custom_call_target="tpu_custom_call" | custom-call | flops 58720256 | bytes 2080768 | tf_op jit(solution)/shard_map/pallas_call | solution.py:191
  10.0 1.7 %collective-permute-start.5 = (bf16[8,3584]{1,0:T(8,128)(2,1)S(1)}, bf16[8,3584]{1,0:T(8,128)(2,1)S(1)}, u32[]{:S(2)}, u32[]{:S(2)}) collective-permute-start(bf16[8,3584]{1,0:T(8,128)(2,1)S(1)} %get-tuple-element.28), channel_id=1, source_target_pairs={{0,5},{1,4},{2,7},{3,6},{4,3},{5,2},{6,1},{7,0},{8,13},{9,12},{10,... | collective-permute-start | bytes 172040 | tf_op jit(solution)/shard_map/ppermute | solution.py:229
  11.7 1.1 %collective-permute-start.6 = (bf16[8,3584]{1,0:T(8,128)(2,1)S(1)}, bf16[8,3584]{1,0:T(8,128)(2,1)S(1)}, u32[]{:S(2)}, u32[]{:S(2)}) collective-permute-start(bf16[8,3584]{1,0:T(8,128)(2,1)S(1)} %get-tuple-element.29), channel_id=1, source_target_pairs={{0,3},{1,2},{2,1},{3,0},{4,7},{5,6},{6,5},{7,4},{8,11},{9,10},{10,... | collective-permute-start | bytes 172040 | tf_op jit(solution)/shard_map/ppermute | solution.py:229
  12.8 1.1 %collective-permute-start.7 = (bf16[8,3584]{1,0:T(8,128)(2,1)S(1)}, bf16[8,3584]{1,0:T(8,128)(2,1)S(1)}, u32[]{:S(2)}, u32[]{:S(2)}) collective-permute-start(bf16[8,3584]{1,0:T(8,128)(2,1)S(1)} %get-tuple-element.30), channel_id=1, source_target_pairs={{0,7},{1,6},{2,5},{3,4},{4,1},{5,0},{6,3},{7,2},{8,15},{9,14},{10,... | collective-permute-start | bytes 172040 | tf_op jit(solution)/shard_map/ppermute | solution.py:229
  13.9 0.7 %collective-permute-done.5.refs_1_ = bf16[8,3584]{1,0:T(8,128)(2,1)S(1)} collective-permute-done((bf16[8,3584]{1,0:T(8,128)(2,1)S(1)}, bf16[8,3584]{1,0:T(8,128)(2,1)S(1)}, u32[]{:S(2)}, u32[]{:S(2)}) %collective-permute-start.5) | collective-permute-done | bytes 57376 | tf_op jit(solution)/shard_map/ppermute | solution.py:229
  14.5 1.2 %collective-permute-done.6.refs_2_ = bf16[8,3584]{1,0:T(8,128)(2,1)S(1)} collective-permute-done((bf16[8,3584]{1,0:T(8,128)(2,1)S(1)}, bf16[8,3584]{1,0:T(8,128)(2,1)S(1)}, u32[]{:S(2)}, u32[]{:S(2)}) %collective-permute-start.6) | collective-permute-done | bytes 57376 | tf_op jit(solution)/shard_map/ppermute | solution.py:229
  15.7 1.0 %collective-permute-done.7.refs_3_ = bf16[8,3584]{1,0:T(8,128)(2,1)S(1)} collective-permute-done((bf16[8,3584]{1,0:T(8,128)(2,1)S(1)}, bf16[8,3584]{1,0:T(8,128)(2,1)S(1)}, u32[]{:S(2)}, u32[]{:S(2)}) %collective-permute-start.7) | collective-permute-done | bytes 57376 | tf_op jit(solution)/shard_map/ppermute | solution.py:229
  16.7 0.9 %shard_map.86 = bf16[16,3584]{1,0:T(8,128)(2,1)} custom-call(bf16[32,32]{1,0:T(8,128)(2,1)S(1)} %get-tuple-element.19.weight_ref, bf16[8,3584]{1,0:T(8,128)(2,1)S(1)} %get-tuple-element.27.refs_0_, bf16[8,3584]{1,0:T(8,128)(2,1)S(1)} %collective-permute-done.5.refs_1_, bf16[8,3584]{1,0:T(8,128)(2,1)S(1)} %collective-permute-done.6.refs_2_, ...), custom_call_target="tpu_custom_call" | custom-call | flops 7340032 | bytes 346112 | tf_op jit(solution)/shard_map/pallas_call | solution.py:191
Async XLA Ops:
  0.0 9.0 %collective-permute-start = (bf16[2,3584,128]{2,1,0:T(8,128)(2,1)}, bf16[2,3584,128]{2,1,0:T(8,128)(2,1)S(1)}, u32[]{:S(2)}, u32[]{:S(2)}) collective-permute-start(bf16[2,3584,128]{2,1,0:T(8,128)(2,1)} %in_hbm.1), channel_id=1, source_target_pairs={{0,1},{1,0},{2,3},{3,2},{4,5},{5,4},{6,7},{7,6},{8,9},{9,8},{10,11... | collective-permute-start | bytes 5505032 | tf_op jit(solution)/shard_map/ppermute | solution.py:235
  1.6 6.1 %collective-permute-start.1 = (bf16[8,3584]{1,0:T(8,128)(2,1)S(1)}, bf16[8,3584]{1,0:T(8,128)(2,1)S(1)}, u32[]{:S(2)}, u32[]{:S(2)}) collective-permute-start(bf16[8,3584]{1,0:T(8,128)(2,1)S(1)} %get-tuple-element.22), channel_id=1, source_target_pairs={{0,5},{1,6},{2,7},{3,4},{4,3},{5,0},{6,1},{7,2},{8,13},{9,14},{10,... | collective-permute-start | bytes 172040 | tf_op jit(solution)/shard_map/ppermute | solution.py:229
  4.3 4.5 %collective-permute-start.2 = (bf16[8,3584]{1,0:T(8,128)(2,1)S(1)}, bf16[8,3584]{1,0:T(8,128)(2,1)S(1)}, u32[]{:S(2)}, u32[]{:S(2)}) collective-permute-start(bf16[8,3584]{1,0:T(8,128)(2,1)S(1)} %get-tuple-element.23), channel_id=1, source_target_pairs={{0,7},{1,4},{2,5},{3,6},{4,1},{5,2},{6,3},{7,0},{8,15},{9,12},{10,... | collective-permute-start | bytes 172040 | tf_op jit(solution)/shard_map/ppermute | solution.py:229
  5.4 3.6 %collective-permute-start.3 = (bf16[8,3584]{1,0:T(8,128)(2,1)S(1)}, bf16[8,3584]{1,0:T(8,128)(2,1)S(1)}, u32[]{:S(2)}, u32[]{:S(2)}) collective-permute-start(bf16[8,3584]{1,0:T(8,128)(2,1)S(1)} %get-tuple-element.24), channel_id=1, source_target_pairs={{0,3},{1,2},{2,1},{3,0},{4,7},{5,6},{6,5},{7,4},{8,11},{9,10},{10,... | collective-permute-start | bytes 172040 | tf_op jit(solution)/shard_map/ppermute | solution.py:229
  5.5 4.1 %collective-permute-start.4 = (bf16[128,3584]{1,0:T(8,128)(2,1)}, bf16[128,3584]{1,0:T(8,128)(2,1)S(1)}, u32[]{:S(2)}, u32[]{:S(2)}) collective-permute-start(bf16[128,3584]{1,0:T(8,128)(2,1)} %down_hbm.1), channel_id=1, source_target_pairs={{0,1},{1,0},{2,3},{3,2},{4,5},{5,4},{6,7},{7,6},{8,9},{9,8},{10,11... | collective-permute-start | bytes 2752520 | tf_op jit(solution)/shard_map/ppermute | solution.py:235
  10.0 4.6 %collective-permute-start.5 = (bf16[8,3584]{1,0:T(8,128)(2,1)S(1)}, bf16[8,3584]{1,0:T(8,128)(2,1)S(1)}, u32[]{:S(2)}, u32[]{:S(2)}) collective-permute-start(bf16[8,3584]{1,0:T(8,128)(2,1)S(1)} %get-tuple-element.28), channel_id=1, source_target_pairs={{0,5},{1,4},{2,7},{3,6},{4,3},{5,2},{6,1},{7,0},{8,13},{9,12},{10,... | collective-permute-start | bytes 172040 | tf_op jit(solution)/shard_map/ppermute | solution.py:229
  11.7 4.0 %collective-permute-start.6 = (bf16[8,3584]{1,0:T(8,128)(2,1)S(1)}, bf16[8,3584]{1,0:T(8,128)(2,1)S(1)}, u32[]{:S(2)}, u32[]{:S(2)}) collective-permute-start(bf16[8,3584]{1,0:T(8,128)(2,1)S(1)} %get-tuple-element.29), channel_id=1, source_target_pairs={{0,3},{1,2},{2,1},{3,0},{4,7},{5,6},{6,5},{7,4},{8,11},{9,10},{10,... | collective-permute-start | bytes 172040 | tf_op jit(solution)/shard_map/ppermute | solution.py:229
  12.8 4.0 %collective-permute-start.7 = (bf16[8,3584]{1,0:T(8,128)(2,1)S(1)}, bf16[8,3584]{1,0:T(8,128)(2,1)S(1)}, u32[]{:S(2)}, u32[]{:S(2)}) collective-permute-start(bf16[8,3584]{1,0:T(8,128)(2,1)S(1)} %get-tuple-element.30), channel_id=1, source_target_pairs={{0,7},{1,6},{2,5},{3,4},{4,1},{5,0},{6,3},{7,2},{8,15},{9,14},{10,... | collective-permute-start | bytes 172040 | tf_op jit(solution)/shard_map/ppermute | solution.py:229

commit v17 on v15

--- a/solution.py
+++ b/solution.py
@@ -19,40 +19,34 @@
 HBM = pl.BlockSpec(memory_space=pltpu.HBM)
 
 
-def targets(shards, goes, new_ref, old_ref, ids, replica):
-    slots, rows = new_ref.shape[0], ids.shape[1]
-    device = lax.axis_index("expert")
+def slot_lines(shards, goes, new_ref, old_ref, rows):
+    slots = new_ref.shape[0]
+    mine = lax.axis_index("expert") // shards
     down = lax.broadcasted_iota(jnp.int32, (slots, rows), 0)
-    expert = jnp.zeros((slots, rows), jnp.int32)
-    line = jnp.zeros((slots, rows), jnp.int32)
+    expert, line, count, rank = [jnp.zeros((slots, rows), jnp.int32)] * 4
     for slot in range(slots):
         source = jnp.where(new_ref[slot] == old_ref[slot], slot, slot ^ 1)
-        away = source ^ (device // shards)
+        away = source ^ mine
         if shards == 1:
             step = sum(jnp.where(source >> 1 == chip, k, 0) for k, chip in enumerate(goes, 1))
             away = (source & 1) | (step << 1)
         expert = jnp.where(down == slot, new_ref[slot], expert)
         line = jnp.where(down == slot, CAP * away, line)
-    count = jnp.zeros((slots, rows), jnp.int32)
-    rank = jnp.zeros((slots, rows), jnp.int32)
     for slot in range(slots):
         same = expert == new_ref[slot]
         count += jnp.where(same, 1, 0)
         rank += jnp.where(same & (down > slot), 1, 0)
+    return expert, line.astype(jnp.float32), count, rank
+
+
+def targets(slot_values, earlier, ids, replica):
+    expert, line, count, rank = slot_values
     chosen = []
     for k in range(ids.shape[0]):
         hit = (ids[k : k + 1] == expert) & (rank == (replica[k : k + 1] & (count - 1)))
         chosen.append(jnp.where(hit, 1.0, 0.0))
-    earlier = lax.broadcasted_iota(jnp.int32, (rows, rows), 0) < lax.broadcasted_iota(
-        jnp.int32, (rows, rows), 1
-    )
-    any_choice = functools.reduce(jnp.add, chosen)
-    position = jnp.dot(
-        any_choice.astype(jnp.bfloat16),
-        jnp.where(earlier, 1.0, 0.0).astype(jnp.bfloat16),
-        preferred_element_type=jnp.float32,
-    )
-    line = line.astype(jnp.float32)
+    any_choice = functools.reduce(jnp.add, chosen).astype(jnp.bfloat16)
+    position = jnp.dot(any_choice, earlier, preferred_element_type=jnp.float32)
     found = []
     for hit in chosen:
         place = jnp.where(position < CAP, line + position + 1.0, 0.0)
@@ -78,18 +72,26 @@
     found_ref, *block_refs = refs[:-6]
     buffers, sems = refs[-6:-1], refs[-1]
     copies = start_copies(sources, buffers, sems)
+    tokens_ref = buffers[-1]
+    rows = tokens_ref.shape[0]
+    size = block_refs[0].shape[0]
     goes = [by_device([SENDS[i & 1][k][i >> 1] for i in range(SLOTS)]) for k in range(3)]
-    for copy in copies[:-1]:
+    earlier = lax.broadcasted_iota(jnp.int32, (rows, rows), 0) < lax.broadcasted_iota(
+        jnp.int32, (rows, rows), 1
+    )
+    earlier = jnp.where(earlier, 1.0, 0.0).astype(jnp.bfloat16)
+    line = lax.broadcasted_iota(jnp.int32, (size * len(block_refs), rows), 0)
+    for copy in copies[:2]:
         copy.wait()
-    found = targets(shards, goes, *buffers[:2], *[ref[...] for ref in buffers[2:-1]])
-    found_ref[...] = jnp.concatenate(found, axis=0)
-    tokens_ref = buffers[-1]
-    size = block_refs[0].shape[0]
-    line = lax.broadcasted_iota(jnp.int32, (size * len(block_refs), tokens_ref.shape[0]), 0)
+    slot_values = slot_lines(shards, goes, *buffers[:2], rows)
+    for copy in copies[2:-1]:
+        copy.wait()
+    found = targets(slot_values, earlier, *[ref[...] for ref in buffers[2:-1]])
     picked = functools.reduce(jnp.logical_or, [line == target for target in found])
     selector = jnp.where(picked, 1.0, 0.0).astype(jnp.bfloat16)
     copies[-1].wait()
     buffer = jnp.dot(selector, tokens_ref[...], preferred_element_type=jnp.float32)
+    found_ref[...] = jnp.concatenate(found, axis=0)
     for b, block_ref in enumerate(block_refs):
         block_ref[...] = buffer[size * b : size * (b + 1)].astype(jnp.bfloat16)
 

time: 17.2 us -> 17.2 us (level)
  no operation moved by 1% of the time
where the time goes in v17:
time: 17.2 us; the launch traced here: 17.1 us
  starting transfers between devices  9.61 us (56%)
  Pallas kernels  4.78 us (28%)
  waiting for transfers between devices  2.61 us (15%)
    ppermute x6, starting transfers between devices, exchange(): result.append(lax.ppermute(blocks[k], 'expert', pairs))  8.25 us
    pallas_call x5, Pallas kernels, call(): pl.pallas_call(kernel, out_shape=outs, in_specs=arg_specs, out_specs=out_...  4.78 us
    ppermute x6, waiting for transfers between devices, exchange(): result.append(lax.ppermute(blocks[k], 'expert', pairs))  2.6 us
    ppermute x2, starting transfers between devices, from_twin(): return lax.ppermute(array, 'expert', pairs)  1.36 us
  transfers between devices with their start and end apart: 8, of which 2 were waited for; matrix products, arithmetic and copies ran while one was open for 0% of the time, Pallas kernels for 21%

profile of v17, /device:TPU:0, one launch (start us, length us, event | category | flops | bytes accessed | tf_op | source)
XLA Modules:
  0.0 17.1 jit_solution(5524594440461366908)
XLA Ops:
  0.0 0.5 %collective-permute-start = (bf16[2,3584,128]{2,1,0:T(8,128)(2,1)}, bf16[2,3584,128]{2,1,0:T(8,128)(2,1)S(1)}, u32[]{:S(2)}, u32[]{:S(2)}) collective-permute-start(bf16[2,3584,128]{2,1,0:T(8,128)(2,1)} %in_hbm.1), channel_id=1, source_target_pairs={{0,1},{1,0},{2,3},{3,2},{4,5},{5,4},{6,7},{7,6},{8,9},{9,8},{10,11... | collective-permute-start | bytes 5505032 | tf_op jit(solution)/shard_map/ppermute | solution.py:237
  0.5 1.2 %shard_map.82 = (s32[2,16]{1,0:T(2,128)S(1)}, bf16[8,3584]{1,0:T(8,128)(2,1)S(1)}, bf16[8,3584]{1,0:T(8,128)(2,1)S(1)}, bf16[8,3584]{1,0:T(8,128)(2,1)S(1)}, bf16[8,3584]{1,0:T(8,128)(2,1)S(1)}) custom-call(s32[8]{0:T(128)} %refs_0_.1, s32[8]{0:T(128)} %refs_1_.1, s32[2,16]{1,0:T(2,128)} %bitcast.3, s32[2,16]{1,0:T(2,128)} %bitcast.4, bf16[16,3584]{1,0:T(8,128)(2,1)} %refs_4_.1), custom_call_target="tpu_custom_call" | custom-call | flops 3670016 | bytes 344512 | tf_op jit(solution)/shard_map/pallas_call | solution.py:193
  1.6 3.6 %collective-permute-start.1 = (bf16[8,3584]{1,0:T(8,128)(2,1)S(1)}, bf16[8,3584]{1,0:T(8,128)(2,1)S(1)}, u32[]{:S(2)}, u32[]{:S(2)}) collective-permute-start(bf16[8,3584]{1,0:T(8,128)(2,1)S(1)} %get-tuple-element.22), channel_id=1, source_target_pairs={{0,7},{1,2},{2,5},{3,4},{4,1},{5,6},{6,3},{7,0},{8,15},{9,10},{10,... | collective-permute-start | bytes 172040 | tf_op jit(solution)/shard_map/ppermute | solution.py:231
  5.2 0.2 %collective-permute-start.2 = (bf16[8,3584]{1,0:T(8,128)(2,1)S(1)}, bf16[8,3584]{1,0:T(8,128)(2,1)S(1)}, u32[]{:S(2)}, u32[]{:S(2)}) collective-permute-start(bf16[8,3584]{1,0:T(8,128)(2,1)S(1)} %get-tuple-element.23), channel_id=1, source_target_pairs={{0,5},{1,4},{2,7},{3,6},{4,3},{5,0},{6,1},{7,2},{8,13},{9,12},{10,... | collective-permute-start | bytes 172040 | tf_op jit(solution)/shard_map/ppermute | solution.py:231
  5.4 0.6 %collective-permute-start.3 = (bf16[8,3584]{1,0:T(8,128)(2,1)S(1)}, bf16[8,3584]{1,0:T(8,128)(2,1)S(1)}, u32[]{:S(2)}, u32[]{:S(2)}) collective-permute-start(bf16[8,3584]{1,0:T(8,128)(2,1)S(1)} %get-tuple-element.24), channel_id=1, source_target_pairs={{0,3},{1,6},{2,1},{3,0},{4,7},{5,2},{6,5},{7,4},{8,11},{9,14},{10,... | collective-permute-start | bytes 172040 | tf_op jit(solution)/shard_map/ppermute | solution.py:231
  6.0 0.9 %collective-permute-start.4 = (bf16[128,3584]{1,0:T(8,128)(2,1)}, bf16[128,3584]{1,0:T(8,128)(2,1)S(1)}, u32[]{:S(2)}, u32[]{:S(2)}) collective-permute-start(bf16[128,3584]{1,0:T(8,128)(2,1)} %down_hbm.1), channel_id=1, source_target_pairs={{0,1},{1,0},{2,3},{3,2},{4,5},{5,4},{6,7},{7,6},{8,9},{9,8},{10,11... | collective-permute-start | bytes 2752520 | tf_op jit(solution)/shard_map/ppermute | solution.py:237
  6.9 1.8 %shard_map.83 = (bf16[2,3584,128]{2,1,0:T(8,128)(2,1)S(1)}, bf16[128,3584]{1,0:T(8,128)(2,1)S(1)}, bf16[32,32]{1,0:T(8,128)(2,1)S(1)}) custom-call(s32[2,16]{1,0:T(2,128)S(1)} %get-tuple-element.18.found_ref, f32[2,16]{1,0:T(2,128)} %bitcast.5, bf16[2,3584,128]{2,1,0:T(8,128)(2,1)} %in_hbm.1, bf16[128,3584]{1,0:T(8,128)(2,1)} %down_hbm.1), custom_call_target="tpu_custom_call" | custom-call | bytes 5507328 | tf_op jit(solution)/shard_map/pallas_call | solution.py:193
  8.7 0.0 collective-permute-done.1.refs_1_
  8.7 0.7 %collective-permute-done.2.refs_2_ = bf16[8,3584]{1,0:T(8,128)(2,1)S(1)} collective-permute-done((bf16[8,3584]{1,0:T(8,128)(2,1)S(1)}, bf16[8,3584]{1,0:T(8,128)(2,1)S(1)}, u32[]{:S(2)}, u32[]{:S(2)}) %collective-permute-start.2) | collective-permute-done | bytes 57376 | tf_op jit(solution)/shard_map/ppermute | solution.py:231
  9.5 0.0 collective-permute-done.3.refs_3_
  9.5 0.0 collective-permute-done.twin_in_ref
  9.5 0.6 %shard_map.84.hidden_ref = bf16[32,256]{1,0:T(8,128)(2,1)S(1)} custom-call(bf16[2,3584,128]{2,1,0:T(8,128)(2,1)S(1)} %get-tuple-element.20.in_ref, bf16[2,3584,128]{2,1,0:T(8,128)(2,1)S(1)} %collective-permute-done.twin_in_ref, bf16[8,3584]{1,0:T(8,128)(2,1)S(1)} %get-tuple-element.21.refs_0_, bf16[8,3584]{1,0:T(8,128)(2,1)S(1)} %collective-permute-done.1.refs_1_, ...), custom_call_target="tpu_custom_call" | custom-call | flops 11744051200 | bytes 3915776 | tf_op jit(solution)/shard_map/pallas_call | solution.py:193
  10.1 0.0 collective-permute-done.4.twin_down_ref
  10.1 0.4 %shard_map.85 = (bf16[8,3584]{1,0:T(8,128)(2,1)S(1)}, bf16[8,3584]{1,0:T(8,128)(2,1)S(1)}, bf16[8,3584]{1,0:T(8,128)(2,1)S(1)}, bf16[8,3584]{1,0:T(8,128)(2,1)S(1)}) custom-call(bf16[32,256]{1,0:T(8,128)(2,1)S(1)} %shard_map.84.hidden_ref, bf16[128,3584]{1,0:T(8,128)(2,1)S(1)} %get-tuple-element.25.down_ref, ...), custom_call_target="tpu_custom_call" | custom-call | flops 58720256 | bytes 2080768 | tf_op jit(solution)/shard_map/pallas_call | solution.py:193
  10.5 1.2 %collective-permute-start.5 = (bf16[8,3584]{1,0:T(8,128)(2,1)S(1)}, bf16[8,3584]{1,0:T(8,128)(2,1)S(1)}, u32[]{:S(2)}, u32[]{:S(2)}) collective-permute-start(bf16[8,3584]{1,0:T(8,128)(2,1)S(1)} %get-tuple-element.28), channel_id=1, source_target_pairs={{0,3},{1,6},{2,5},{3,4},{4,7},{5,0},{6,1},{7,2},{8,11},{9,14},{10,... | collective-permute-start | bytes 172040 | tf_op jit(solution)/shard_map/ppermute | solution.py:231
  11.7 0.6 %collective-permute-start.6 = (bf16[8,3584]{1,0:T(8,128)(2,1)S(1)}, bf16[8,3584]{1,0:T(8,128)(2,1)S(1)}, u32[]{:S(2)}, u32[]{:S(2)}) collective-permute-start(bf16[8,3584]{1,0:T(8,128)(2,1)S(1)} %get-tuple-element.29), channel_id=1, source_target_pairs={{0,5},{1,4},{2,7},{3,6},{4,1},{5,2},{6,3},{7,0},{8,13},{9,12},{10,... | collective-permute-start | bytes 172040 | tf_op jit(solution)/shard_map/ppermute | solution.py:231
  12.3 2.1 %collective-permute-start.7 = (bf16[8,3584]{1,0:T(8,128)(2,1)S(1)}, bf16[8,3584]{1,0:T(8,128)(2,1)S(1)}, u32[]{:S(2)}, u32[]{:S(2)}) collective-permute-start(bf16[8,3584]{1,0:T(8,128)(2,1)S(1)} %get-tuple-element.30), channel_id=1, source_target_pairs={{0,7},{1,2},{2,1},{3,0},{4,3},{5,6},{6,5},{7,4},{8,15},{9,10},{10,... | collective-permute-start | bytes 172040 | tf_op jit(solution)/shard_map/ppermute | solution.py:231
  14.3 0.0 collective-permute-done.5.refs_1_
  14.3 1.9 %collective-permute-done.6.refs_2_ = bf16[8,3584]{1,0:T(8,128)(2,1)S(1)} collective-permute-done((bf16[8,3584]{1,0:T(8,128)(2,1)S(1)}, bf16[8,3584]{1,0:T(8,128)(2,1)S(1)}, u32[]{:S(2)}, u32[]{:S(2)}) %collective-permute-start.6) | collective-permute-done | bytes 57376 | tf_op jit(solution)/shard_map/ppermute | solution.py:231
  16.2 0.0 collective-permute-done.7.refs_3_
  16.2 0.9 %shard_map.86 = bf16[16,3584]{1,0:T(8,128)(2,1)} custom-call(bf16[32,32]{1,0:T(8,128)(2,1)S(1)} %get-tuple-element.19.weight_ref, bf16[8,3584]{1,0:T(8,128)(2,1)S(1)} %get-tuple-element.27.refs_0_, bf16[8,3584]{1,0:T(8,128)(2,1)S(1)} %collective-permute-done.5.refs_1_, bf16[8,3584]{1,0:T(8,128)(2,1)S(1)} %collective-permute-done.6.refs_2_, ...), custom_call_target="tpu_custom_call" | custom-call | flops 7340032 | bytes 346112 | tf_op jit(solution)/shard_map/pallas_call | solution.py:193
Async XLA Ops:
  0.0 9.5 %collective-permute-start = (bf16[2,3584,128]{2,1,0:T(8,128)(2,1)}, bf16[2,3584,128]{2,1,0:T(8,128)(2,1)S(1)}, u32[]{:S(2)}, u32[]{:S(2)}) collective-permute-start(bf16[2,3584,128]{2,1,0:T(8,128)(2,1)} %in_hbm.1), channel_id=1, source_target_pairs={{0,1},{1,0},{2,3},{3,2},{4,5},{5,4},{6,7},{7,6},{8,9},{9,8},{10,11... | collective-permute-start | bytes 5505032 | tf_op jit(solution)/shard_map/ppermute | solution.py:237
  1.6 7.1 %collective-permute-start.1 = (bf16[8,3584]{1,0:T(8,128)(2,1)S(1)}, bf16[8,3584]{1,0:T(8,128)(2,1)S(1)}, u32[]{:S(2)}, u32[]{:S(2)}) collective-permute-start(bf16[8,3584]{1,0:T(8,128)(2,1)S(1)} %get-tuple-element.22), channel_id=1, source_target_pairs={{0,7},{1,2},{2,5},{3,4},{4,1},{5,6},{6,3},{7,0},{8,15},{9,10},{10,... | collective-permute-start | bytes 172040 | tf_op jit(solution)/shard_map/ppermute | solution.py:231
  5.2 4.2 %collective-permute-start.2 = (bf16[8,3584]{1,0:T(8,128)(2,1)S(1)}, bf16[8,3584]{1,0:T(8,128)(2,1)S(1)}, u32[]{:S(2)}, u32[]{:S(2)}) collective-permute-start(bf16[8,3584]{1,0:T(8,128)(2,1)S(1)} %get-tuple-element.23), channel_id=1, source_target_pairs={{0,5},{1,4},{2,7},{3,6},{4,3},{5,0},{6,1},{7,2},{8,13},{9,12},{10,... | collective-permute-start | bytes 172040 | tf_op jit(solution)/shard_map/ppermute | solution.py:231
  5.4 4.0 %collective-permute-start.3 = (bf16[8,3584]{1,0:T(8,128)(2,1)S(1)}, bf16[8,3584]{1,0:T(8,128)(2,1)S(1)}, u32[]{:S(2)}, u32[]{:S(2)}) collective-permute-start(bf16[8,3584]{1,0:T(8,128)(2,1)S(1)} %get-tuple-element.24), channel_id=1, source_target_pairs={{0,3},{1,6},{2,1},{3,0},{4,7},{5,2},{6,5},{7,4},{8,11},{9,14},{10,... | collective-permute-start | bytes 172040 | tf_op jit(solution)/shard_map/ppermute | solution.py:231
  6.0 4.1 %collective-permute-start.4 = (bf16[128,3584]{1,0:T(8,128)(2,1)}, bf16[128,3584]{1,0:T(8,128)(2,1)S(1)}, u32[]{:S(2)}, u32[]{:S(2)}) collective-permute-start(bf16[128,3584]{1,0:T(8,128)(2,1)} %down_hbm.1), channel_id=1, source_target_pairs={{0,1},{1,0},{2,3},{3,2},{4,5},{5,4},{6,7},{7,6},{8,9},{9,8},{10,11... | collective-permute-start | bytes 2752520 | tf_op jit(solution)/shard_map/ppermute | solution.py:237
  10.5 3.9 %collective-permute-start.5 = (bf16[8,3584]{1,0:T(8,128)(2,1)S(1)}, bf16[8,3584]{1,0:T(8,128)(2,1)S(1)}, u32[]{:S(2)}, u32[]{:S(2)}) collective-permute-start(bf16[8,3584]{1,0:T(8,128)(2,1)S(1)} %get-tuple-element.28), channel_id=1, source_target_pairs={{0,3},{1,6},{2,5},{3,4},{4,7},{5,0},{6,1},{7,2},{8,11},{9,14},{10,... | collective-permute-start | bytes 172040 | tf_op jit(solution)/shard_map/ppermute | solution.py:231
  11.7 4.5 %collective-permute-start.6 = (bf16[8,3584]{1,0:T(8,128)(2,1)S(1)}, bf16[8,3584]{1,0:T(8,128)(2,1)S(1)}, u32[]{:S(2)}, u32[]{:S(2)}) collective-permute-start(bf16[8,3584]{1,0:T(8,128)(2,1)S(1)} %get-tuple-element.29), channel_id=1, source_target_pairs={{0,5},{1,4},{2,7},{3,6},{4,1},{5,2},{6,3},{7,0},{8,13},{9,12},{10,... | collective-permute-start | bytes 172040 | tf_op jit(solution)/shard_map/ppermute | solution.py:231
  12.3 3.9 %collective-permute-start.7 = (bf16[8,3584]{1,0:T(8,128)(2,1)S(1)}, bf16[8,3584]{1,0:T(8,128)(2,1)S(1)}, u32[]{:S(2)}, u32[]{:S(2)}) collective-permute-start(bf16[8,3584]{1,0:T(8,128)(2,1)S(1)} %get-tuple-element.30), channel_id=1, source_target_pairs={{0,7},{1,2},{2,1},{3,0},{4,3},{5,6},{6,5},{7,4},{8,15},{9,10},{10,... | collective-permute-start | bytes 172040 | tf_op jit(solution)/shard_map/ppermute | solution.py:231

commit v18 on v15

--- a/solution.py
+++ b/solution.py
@@ -158,9 +158,18 @@
         out_ref[...] = block.astype(jnp.bfloat16)
 
 
-def mix_kernel(repeats, weight_ref, *refs):
+def early_kernel(weight_ref, *refs):
+    *refs, late_ref, total_ref = refs
+    rows = total_ref.shape[0]
+    lines = weight_ref.shape[1] - late_ref.shape[1]
+    late_ref[...] = weight_ref[:, lines:]
+    mixed = jnp.dot(weight_ref[:, :lines], stack(refs), preferred_element_type=jnp.float32)
+    total_ref[...] = mixed[:rows] + mixed[rows:]
+
+
+def mix_kernel(repeats, early, weight_ref, *refs):
     out_hbm, out_ref, sems = refs[-3:]
-    refs = refs[:-3]
+    early_refs, refs = refs[:early], refs[early:-3]
     rows, width = out_ref.shape
     parts = sems.shape[0]
     step = width // parts
@@ -176,7 +185,10 @@
             low = (total - high.astype(jnp.float32)).astype(jnp.bfloat16)
             mixed = jnp.dot(weight_ref[...], high, preferred_element_type=jnp.float32)
             mixed += jnp.dot(weight_ref[...], low, preferred_element_type=jnp.float32)
-        out_ref[:, columns] = (mixed[:rows] + mixed[rows:]).astype(jnp.bfloat16)
+        mixed = mixed[:rows] + mixed[rows:]
+        for ref in early_refs:
+            mixed += ref[:, columns]
+        out_ref[:, columns] = mixed.astype(jnp.bfloat16)
         copies.append(
             pltpu.make_async_copy(out_ref.at[:, columns], out_hbm.at[:, columns], sems.at[part])
         )
@@ -282,11 +294,25 @@
         4 * chips * block.shape[0] * hidden * width,
     )
     returned = exchange(pieces, split, back=True)
+    early = []
+    if split:
+        first, returned = returned[:2], returned[2:]
+        late_lines = len(returned) * block.shape[0]
+        weight, total = call(
+            early_kernel,
+            [
+                jax.ShapeDtypeStruct((2 * rows, late_lines), jnp.bfloat16),
+                jax.ShapeDtypeStruct((rows, width), jnp.float32),
+            ],
+            (weight, *first),
+            4 * len(first) * block.shape[0] * rows * width,
+        )
+        early = [total]
     parts = 4 if width % 512 == 0 else 1
     return call(
-        functools.partial(mix_kernel, repeats),
+        functools.partial(mix_kernel, repeats, len(early)),
         shape_of(tokens),
-        (weight, *returned),
+        (weight, *early, *returned),
         4 * SLOTS * CAP * rows * width,
         out_specs=HBM,
         scratch=[pltpu.VMEM(tokens.shape, tokens.dtype), pltpu.SemaphoreType.DMA((parts,))],

time: 17.2 us -> 17.2 us (level)
  waiting for transfers between devices: 2.6 us -> 2.42 us
    ppermute x6, waiting for transfers between devices: 2.6 us -> 2.42 us  [exchange(): result.append(lax.ppermute(blocks[k], 'expert', pairs))]
    pallas_call x5 -> x6, Pallas kernels: 4.79 us -> 4.96 us  [call(): pl.pallas_call(kernel, out_shape=outs, in_specs=arg_specs, out_specs=out_...]
  transfers between devices with their start and end apart: 8 -> 8, of which waited for: 2 -> 2; matrix products, arithmetic and copies ran while one was open for 0% -> 0% of each run, Pallas kernels for 21% -> 22%
where the time goes in v18:
time: 17.2 us; the launch traced here: 17 us
  starting transfers between devices  9.59 us (56%)
  Pallas kernels  4.96 us (29%)
  waiting for transfers between devices  2.42 us (14%)
    ppermute x6, starting transfers between devices, exchange(): result.append(lax.ppermute(blocks[k], 'expert', pairs))  8.24 us
    pallas_call x6, Pallas kernels, call(): pl.pallas_call(kernel, out_shape=outs, in_specs=arg_specs, out_specs=out_...  4.96 us
    ppermute x6, waiting for transfers between devices, exchange(): result.append(lax.ppermute(blocks[k], 'expert', pairs))  2.42 us
    ppermute x2, starting transfers between devices, from_twin(): return lax.ppermute(array, 'expert', pairs)  1.36 us
  transfers between devices with their start and end apart: 8, of which 2 were waited for; matrix products, arithmetic and copies ran while one was open for 0% of the time, Pallas kernels for 22%

profile of v18, /device:TPU:0, one launch (start us, length us, event | category | flops | bytes accessed | tf_op | source)
XLA Modules:
  0.0 17.0 jit_solution(17212249539700023365)
XLA Ops:
  0.0 0.5 %collective-permute-start = (bf16[2,3584,128]{2,1,0:T(8,128)(2,1)}, bf16[2,3584,128]{2,1,0:T(8,128)(2,1)S(1)}, u32[]{:S(2)}, u32[]{:S(2)}) collective-permute-start(bf16[2,3584,128]{2,1,0:T(8,128)(2,1)} %in_hbm.1), channel_id=1, source_target_pairs={{0,1},{1,0},{2,3},{3,2},{4,5},{5,4},{6,7},{7,6},{8,9},{9,8},{10,11... | collective-permute-start | bytes 5505032 | tf_op jit(solution)/shard_map/ppermute | solution.py:247
  0.5 1.2 %shard_map.82 = (s32[2,16]{1,0:T(2,128)S(1)}, bf16[8,3584]{1,0:T(8,128)(2,1)S(1)}, bf16[8,3584]{1,0:T(8,128)(2,1)S(1)}, bf16[8,3584]{1,0:T(8,128)(2,1)S(1)}, bf16[8,3584]{1,0:T(8,128)(2,1)S(1)}) custom-call(s32[8]{0:T(128)} %refs_0_.1, s32[8]{0:T(128)} %refs_1_.1, s32[2,16]{1,0:T(2,128)} %bitcast.3, s32[2,16]{1,0:T(2,128)} %bitcast.4, bf16[16,3584]{1,0:T(8,128)(2,1)} %refs_4_.1), custom_call_target="tpu_custom_call" | custom-call | flops 3670016 | bytes 344512 | tf_op jit(solution)/shard_map/pallas_call | solution.py:203
  1.6 3.6 %collective-permute-start.1 = (bf16[8,3584]{1,0:T(8,128)(2,1)S(1)}, bf16[8,3584]{1,0:T(8,128)(2,1)S(1)}, u32[]{:S(2)}, u32[]{:S(2)}) collective-permute-start(bf16[8,3584]{1,0:T(8,128)(2,1)S(1)} %get-tuple-element.24), channel_id=1, source_target_pairs={{0,7},{1,2},{2,5},{3,4},{4,1},{5,6},{6,3},{7,0},{8,15},{9,10},{10,... | collective-permute-start | bytes 172040 | tf_op jit(solution)/shard_map/ppermute | solution.py:241
  5.2 0.2 %collective-permute-start.2 = (bf16[8,3584]{1,0:T(8,128)(2,1)S(1)}, bf16[8,3584]{1,0:T(8,128)(2,1)S(1)}, u32[]{:S(2)}, u32[]{:S(2)}) collective-permute-start(bf16[8,3584]{1,0:T(8,128)(2,1)S(1)} %get-tuple-element.25), channel_id=1, source_target_pairs={{0,5},{1,4},{2,7},{3,6},{4,3},{5,0},{6,1},{7,2},{8,13},{9,12},{10,... | collective-permute-start | bytes 172040 | tf_op jit(solution)/shard_map/ppermute | solution.py:241
  5.4 0.6 %collective-permute-start.3 = (bf16[8,3584]{1,0:T(8,128)(2,1)S(1)}, bf16[8,3584]{1,0:T(8,128)(2,1)S(1)}, u32[]{:S(2)}, u32[]{:S(2)}) collective-permute-start(bf16[8,3584]{1,0:T(8,128)(2,1)S(1)} %get-tuple-element.26), channel_id=1, source_target_pairs={{0,3},{1,6},{2,1},{3,0},{4,7},{5,2},{6,5},{7,4},{8,11},{9,14},{10,... | collective-permute-start | bytes 172040 | tf_op jit(solution)/shard_map/ppermute | solution.py:241
  6.0 0.9 %collective-permute-start.4 = (bf16[128,3584]{1,0:T(8,128)(2,1)}, bf16[128,3584]{1,0:T(8,128)(2,1)S(1)}, u32[]{:S(2)}, u32[]{:S(2)}) collective-permute-start(bf16[128,3584]{1,0:T(8,128)(2,1)} %down_hbm.1), channel_id=1, source_target_pairs={{0,1},{1,0},{2,3},{3,2},{4,5},{5,4},{6,7},{7,6},{8,9},{9,8},{10,11... | collective-permute-start | bytes 2752520 | tf_op jit(solution)/shard_map/ppermute | solution.py:247
  6.9 1.8 %shard_map.83 = (bf16[2,3584,128]{2,1,0:T(8,128)(2,1)S(1)}, bf16[128,3584]{1,0:T(8,128)(2,1)S(1)}, bf16[32,32]{1,0:T(8,128)(2,1)S(1)}) custom-call(s32[2,16]{1,0:T(2,128)S(1)} %get-tuple-element.20.found_ref, f32[2,16]{1,0:T(2,128)} %bitcast.5, bf16[2,3584,128]{2,1,0:T(8,128)(2,1)} %in_hbm.1, bf16[128,3584]{1,0:T(8,128)(2,1)} %down_hbm.1), custom_call_target="tpu_custom_call" | custom-call | bytes 5507328 | tf_op jit(solution)/shard_map/pallas_call | solution.py:203
  8.7 0.0 collective-permute-done.1.refs_1_
  8.7 0.7 %collective-permute-done.2.refs_2_ = bf16[8,3584]{1,0:T(8,128)(2,1)S(1)} collective-permute-done((bf16[8,3584]{1,0:T(8,128)(2,1)S(1)}, bf16[8,3584]{1,0:T(8,128)(2,1)S(1)}, u32[]{:S(2)}, u32[]{:S(2)}) %collective-permute-start.2) | collective-permute-done | bytes 57376 | tf_op jit(solution)/shard_map/ppermute | solution.py:241
  9.4 0.0 collective-permute-done.3.refs_3_
  9.4 0.0 collective-permute-done.twin_in_ref
  9.5 0.6 %shard_map.84.hidden_ref = bf16[32,256]{1,0:T(8,128)(2,1)S(1)} custom-call(bf16[2,3584,128]{2,1,0:T(8,128)(2,1)S(1)} %get-tuple-element.22.in_ref, bf16[2,3584,128]{2,1,0:T(8,128)(2,1)S(1)} %collective-permute-done.twin_in_ref, bf16[8,3584]{1,0:T(8,128)(2,1)S(1)} %get-tuple-element.23.refs_0_, bf16[8,3584]{1,0:T(8,128)(2,1)S(1)} %collective-permute-done.1.refs_1_, ...), custom_call_target="tpu_custom_call" | custom-call | flops 11744051200 | bytes 3915776 | tf_op jit(solution)/shard_map/pallas_call | solution.py:203
  10.1 0.0 collective-permute-done.4.twin_down_ref
  10.1 0.4 %shard_map.85 = (bf16[8,3584]{1,0:T(8,128)(2,1)S(1)}, bf16[8,3584]{1,0:T(8,128)(2,1)S(1)}, bf16[8,3584]{1,0:T(8,128)(2,1)S(1)}, bf16[8,3584]{1,0:T(8,128)(2,1)S(1)}) custom-call(bf16[32,256]{1,0:T(8,128)(2,1)S(1)} %shard_map.84.hidden_ref, bf16[128,3584]{1,0:T(8,128)(2,1)S(1)} %get-tuple-element.27.down_ref, ...), custom_call_target="tpu_custom_call" | custom-call | flops 58720256 | bytes 2080768 | tf_op jit(solution)/shard_map/pallas_call | solution.py:203
  10.5 1.2 %collective-permute-start.5 = (bf16[8,3584]{1,0:T(8,128)(2,1)S(1)}, bf16[8,3584]{1,0:T(8,128)(2,1)S(1)}, u32[]{:S(2)}, u32[]{:S(2)}) collective-permute-start(bf16[8,3584]{1,0:T(8,128)(2,1)S(1)} %get-tuple-element.30), channel_id=1, source_target_pairs={{0,3},{1,6},{2,5},{3,4},{4,7},{5,0},{6,1},{7,2},{8,11},{9,14},{10,... | collective-permute-start | bytes 172040 | tf_op jit(solution)/shard_map/ppermute | solution.py:241
  11.7 0.6 %collective-permute-start.6 = (bf16[8,3584]{1,0:T(8,128)(2,1)S(1)}, bf16[8,3584]{1,0:T(8,128)(2,1)S(1)}, u32[]{:S(2)}, u32[]{:S(2)}) collective-permute-start(bf16[8,3584]{1,0:T(8,128)(2,1)S(1)} %get-tuple-element.33), channel_id=1, source_target_pairs={{0,5},{1,4},{2,7},{3,6},{4,1},{5,2},{6,3},{7,0},{8,13},{9,12},{10,... | collective-permute-start | bytes 172040 | tf_op jit(solution)/shard_map/ppermute | solution.py:241
  12.3 2.0 %collective-permute-start.7 = (bf16[8,3584]{1,0:T(8,128)(2,1)S(1)}, bf16[8,3584]{1,0:T(8,128)(2,1)S(1)}, u32[]{:S(2)}, u32[]{:S(2)}) collective-permute-start(bf16[8,3584]{1,0:T(8,128)(2,1)S(1)} %get-tuple-element.34), channel_id=1, source_target_pairs={{0,7},{1,2},{2,1},{3,0},{4,3},{5,6},{6,5},{7,4},{8,15},{9,10},{10,... | collective-permute-start | bytes 172040 | tf_op jit(solution)/shard_map/ppermute | solution.py:241
  14.3 0.0 collective-permute-done.5.refs_1_
  14.3 0.2 %shard_map.86 = (bf16[32,16]{1,0:T(8,128)(2,1)S(1)}, f32[16,3584]{1,0:T(8,128)S(1)}) custom-call(bf16[32,32]{1,0:T(8,128)(2,1)S(1)} %get-tuple-element.21.weight_ref, bf16[8,3584]{1,0:T(8,128)(2,1)S(1)} %get-tuple-element.29.refs_0_, bf16[8,3584]{1,0:T(8,128)(2,1)S(1)} %collective-permute-done.5.refs_1_), custom_call_target="tpu_custom_call" | custom-call | flops 3670016 | bytes 347136 | tf_op jit(solution)/shard_map/pallas_call | solution.py:203
  14.5 1.7 %collective-permute-done.6.refs_1_ = bf16[8,3584]{1,0:T(8,128)(2,1)S(1)} collective-permute-done((bf16[8,3584]{1,0:T(8,128)(2,1)S(1)}, bf16[8,3584]{1,0:T(8,128)(2,1)S(1)}, u32[]{:S(2)}, u32[]{:S(2)}) %collective-permute-start.6) | collective-permute-done | bytes 57376 | tf_op jit(solution)/shard_map/ppermute | solution.py:241
  16.2 0.0 collective-permute-done.7.refs_2_
  16.2 0.8 %shard_map.87 = bf16[16,3584]{1,0:T(8,128)(2,1)} custom-call(bf16[32,16]{1,0:T(8,128)(2,1)S(1)} %get-tuple-element.31.weight_ref, f32[16,3584]{1,0:T(8,128)S(1)} %get-tuple-element.32.refs_0_, bf16[8,3584]{1,0:T(8,128)(2,1)S(1)} %collective-permute-done.6.refs_1_, bf16[8,3584]{1,0:T(8,128)(2,1)S(1)} %collective-permute-done.7.refs_2_), custom_call_target="tpu_custom_call" | custom-call | flops 7340032 | bytes 459776 | tf_op jit(solution)/shard_map/pallas_call | solution.py:203
Async XLA Ops:
  0.0 9.5 %collective-permute-start = (bf16[2,3584,128]{2,1,0:T(8,128)(2,1)}, bf16[2,3584,128]{2,1,0:T(8,128)(2,1)S(1)}, u32[]{:S(2)}, u32[]{:S(2)}) collective-permute-start(bf16[2,3584,128]{2,1,0:T(8,128)(2,1)} %in_hbm.1), channel_id=1, source_target_pairs={{0,1},{1,0},{2,3},{3,2},{4,5},{5,4},{6,7},{7,6},{8,9},{9,8},{10,11... | collective-permute-start | bytes 5505032 | tf_op jit(solution)/shard_map/ppermute | solution.py:247
  1.6 7.1 %collective-permute-start.1 = (bf16[8,3584]{1,0:T(8,128)(2,1)S(1)}, bf16[8,3584]{1,0:T(8,128)(2,1)S(1)}, u32[]{:S(2)}, u32[]{:S(2)}) collective-permute-start(bf16[8,3584]{1,0:T(8,128)(2,1)S(1)} %get-tuple-element.24), channel_id=1, source_target_pairs={{0,7},{1,2},{2,5},{3,4},{4,1},{5,6},{6,3},{7,0},{8,15},{9,10},{10,... | collective-permute-start | bytes 172040 | tf_op jit(solution)/shard_map/ppermute | solution.py:241
  5.2 4.2 %collective-permute-start.2 = (bf16[8,3584]{1,0:T(8,128)(2,1)S(1)}, bf16[8,3584]{1,0:T(8,128)(2,1)S(1)}, u32[]{:S(2)}, u32[]{:S(2)}) collective-permute-start(bf16[8,3584]{1,0:T(8,128)(2,1)S(1)} %get-tuple-element.25), channel_id=1, source_target_pairs={{0,5},{1,4},{2,7},{3,6},{4,3},{5,0},{6,1},{7,2},{8,13},{9,12},{10,... | collective-permute-start | bytes 172040 | tf_op jit(solution)/shard_map/ppermute | solution.py:241
  5.4 4.0 %collective-permute-start.3 = (bf16[8,3584]{1,0:T(8,128)(2,1)S(1)}, bf16[8,3584]{1,0:T(8,128)(2,1)S(1)}, u32[]{:S(2)}, u32[]{:S(2)}) collective-permute-start(bf16[8,3584]{1,0:T(8,128)(2,1)S(1)} %get-tuple-element.26), channel_id=1, source_target_pairs={{0,3},{1,6},{2,1},{3,0},{4,7},{5,2},{6,5},{7,4},{8,11},{9,14},{10,... | collective-permute-start | bytes 172040 | tf_op jit(solution)/shard_map/ppermute | solution.py:241
  6.0 4.1 %collective-permute-start.4 = (bf16[128,3584]{1,0:T(8,128)(2,1)}, bf16[128,3584]{1,0:T(8,128)(2,1)S(1)}, u32[]{:S(2)}, u32[]{:S(2)}) collective-permute-start(bf16[128,3584]{1,0:T(8,128)(2,1)} %down_hbm.1), channel_id=1, source_target_pairs={{0,1},{1,0},{2,3},{3,2},{4,5},{5,4},{6,7},{7,6},{8,9},{9,8},{10,11... | collective-permute-start | bytes 2752520 | tf_op jit(solution)/shard_map/ppermute | solution.py:247
  10.5 3.8 %collective-permute-start.5 = (bf16[8,3584]{1,0:T(8,128)(2,1)S(1)}, bf16[8,3584]{1,0:T(8,128)(2,1)S(1)}, u32[]{:S(2)}, u32[]{:S(2)}) collective-permute-start(bf16[8,3584]{1,0:T(8,128)(2,1)S(1)} %get-tuple-element.30), channel_id=1, source_target_pairs={{0,3},{1,6},{2,5},{3,4},{4,7},{5,0},{6,1},{7,2},{8,11},{9,14},{10,... | collective-permute-start | bytes 172040 | tf_op jit(solution)/shard_map/ppermute | solution.py:241
  11.7 4.5 %collective-permute-start.6 = (bf16[8,3584]{1,0:T(8,128)(2,1)S(1)}, bf16[8,3584]{1,0:T(8,128)(2,1)S(1)}, u32[]{:S(2)}, u32[]{:S(2)}) collective-permute-start(bf16[8,3584]{1,0:T(8,128)(2,1)S(1)} %get-tuple-element.33), channel_id=1, source_target_pairs={{0,5},{1,4},{2,7},{3,6},{4,1},{5,2},{6,3},{7,0},{8,13},{9,12},{10,... | collective-permute-start | bytes 172040 | tf_op jit(solution)/shard_map/ppermute | solution.py:241
  12.3 3.9 %collective-permute-start.7 = (bf16[8,3584]{1,0:T(8,128)(2,1)S(1)}, bf16[8,3584]{1,0:T(8,128)(2,1)S(1)}, u32[]{:S(2)}, u32[]{:S(2)}) collective-permute-start(bf16[8,3584]{1,0:T(8,128)(2,1)S(1)} %get-tuple-element.34), channel_id=1, source_target_pairs={{0,7},{1,2},{2,1},{3,0},{4,3},{5,6},{6,5},{7,4},{8,15},{9,10},{10,... | collective-permute-start | bytes 172040 | tf_op jit(solution)/shard_map/ppermute | solution.py:241

commit v19 on v18

--- a/solution.py
+++ b/solution.py
@@ -308,7 +308,7 @@
             4 * len(first) * block.shape[0] * rows * width,
         )
         early = [total]
-    parts = 4 if width % 512 == 0 else 1
+    parts = 1 if split or width % 512 else 4
     return call(
         functools.partial(mix_kernel, repeats, len(early)),
         shape_of(tokens),

time: 17.2 us -> 17.2 us (level)
  no operation moved by 1% of the time
where the time goes in v19:
time: 17.2 us; the launch traced here: 17 us
  starting transfers between devices  9.59 us (56%)
  Pallas kernels  4.97 us (29%)
  waiting for transfers between devices  2.42 us (14%)
    ppermute x6, starting transfers between devices, exchange(): result.append(lax.ppermute(blocks[k], 'expert', pairs))  8.24 us
    pallas_call x6, Pallas kernels, call(): pl.pallas_call(kernel, out_shape=outs, in_specs=arg_specs, out_specs=out_...  4.97 us
    ppermute x6, waiting for transfers between devices, exchange(): result.append(lax.ppermute(blocks[k], 'expert', pairs))  2.42 us
    ppermute x2, starting transfers between devices, from_twin(): return lax.ppermute(array, 'expert', pairs)  1.36 us
  transfers between devices with their start and end apart: 8, of which 2 were waited for; matrix products, arithmetic and copies ran while one was open for 0% of the time, Pallas kernels for 22%

profile of v19, /device:TPU:0, one launch (start us, length us, event | category | flops | bytes accessed | tf_op | source)
XLA Modules:
  0.0 17.0 jit_solution(9047302701630650466)
XLA Ops:
  0.0 0.5 %collective-permute-start = (bf16[2,3584,128]{2,1,0:T(8,128)(2,1)}, bf16[2,3584,128]{2,1,0:T(8,128)(2,1)S(1)}, u32[]{:S(2)}, u32[]{:S(2)}) collective-permute-start(bf16[2,3584,128]{2,1,0:T(8,128)(2,1)} %in_hbm.1), channel_id=1, source_target_pairs={{0,1},{1,0},{2,3},{3,2},{4,5},{5,4},{6,7},{7,6},{8,9},{9,8},{10,11... | collective-permute-start | bytes 5505032 | tf_op jit(solution)/shard_map/ppermute | solution.py:247
  0.5 1.2 %shard_map.82 = (s32[2,16]{1,0:T(2,128)S(1)}, bf16[8,3584]{1,0:T(8,128)(2,1)S(1)}, bf16[8,3584]{1,0:T(8,128)(2,1)S(1)}, bf16[8,3584]{1,0:T(8,128)(2,1)S(1)}, bf16[8,3584]{1,0:T(8,128)(2,1)S(1)}) custom-call(s32[8]{0:T(128)} %refs_0_.1, s32[8]{0:T(128)} %refs_1_.1, s32[2,16]{1,0:T(2,128)} %bitcast.3, s32[2,16]{1,0:T(2,128)} %bitcast.4, bf16[16,3584]{1,0:T(8,128)(2,1)} %refs_4_.1), custom_call_target="tpu_custom_call" | custom-call | flops 3670016 | bytes 344512 | tf_op jit(solution)/shard_map/pallas_call | solution.py:203
  1.6 3.6 %collective-permute-start.1 = (bf16[8,3584]{1,0:T(8,128)(2,1)S(1)}, bf16[8,3584]{1,0:T(8,128)(2,1)S(1)}, u32[]{:S(2)}, u32[]{:S(2)}) collective-permute-start(bf16[8,3584]{1,0:T(8,128)(2,1)S(1)} %get-tuple-element.24), channel_id=1, source_target_pairs={{0,7},{1,2},{2,5},{3,4},{4,1},{5,6},{6,3},{7,0},{8,15},{9,10},{10,... | collective-permute-start | bytes 172040 | tf_op jit(solution)/shard_map/ppermute | solution.py:241
  5.2 0.2 %collective-permute-start.2 = (bf16[8,3584]{1,0:T(8,128)(2,1)S(1)}, bf16[8,3584]{1,0:T(8,128)(2,1)S(1)}, u32[]{:S(2)}, u32[]{:S(2)}) collective-permute-start(bf16[8,3584]{1,0:T(8,128)(2,1)S(1)} %get-tuple-element.25), channel_id=1, source_target_pairs={{0,5},{1,4},{2,7},{3,6},{4,3},{5,0},{6,1},{7,2},{8,13},{9,12},{10,... | collective-permute-start | bytes 172040 | tf_op jit(solution)/shard_map/ppermute | solution.py:241
  5.4 0.6 %collective-permute-start.3 = (bf16[8,3584]{1,0:T(8,128)(2,1)S(1)}, bf16[8,3584]{1,0:T(8,128)(2,1)S(1)}, u32[]{:S(2)}, u32[]{:S(2)}) collective-permute-start(bf16[8,3584]{1,0:T(8,128)(2,1)S(1)} %get-tuple-element.26), channel_id=1, source_target_pairs={{0,3},{1,6},{2,1},{3,0},{4,7},{5,2},{6,5},{7,4},{8,11},{9,14},{10,... | collective-permute-start | bytes 172040 | tf_op jit(solution)/shard_map/ppermute | solution.py:241
  6.0 0.9 %collective-permute-start.4 = (bf16[128,3584]{1,0:T(8,128)(2,1)}, bf16[128,3584]{1,0:T(8,128)(2,1)S(1)}, u32[]{:S(2)}, u32[]{:S(2)}) collective-permute-start(bf16[128,3584]{1,0:T(8,128)(2,1)} %down_hbm.1), channel_id=1, source_target_pairs={{0,1},{1,0},{2,3},{3,2},{4,5},{5,4},{6,7},{7,6},{8,9},{9,8},{10,11... | collective-permute-start | bytes 2752520 | tf_op jit(solution)/shard_map/ppermute | solution.py:247
  6.9 1.8 %shard_map.83 = (bf16[2,3584,128]{2,1,0:T(8,128)(2,1)S(1)}, bf16[128,3584]{1,0:T(8,128)(2,1)S(1)}, bf16[32,32]{1,0:T(8,128)(2,1)S(1)}) custom-call(s32[2,16]{1,0:T(2,128)S(1)} %get-tuple-element.20.found_ref, f32[2,16]{1,0:T(2,128)} %bitcast.5, bf16[2,3584,128]{2,1,0:T(8,128)(2,1)} %in_hbm.1, bf16[128,3584]{1,0:T(8,128)(2,1)} %down_hbm.1), custom_call_target="tpu_custom_call" | custom-call | bytes 5507328 | tf_op jit(solution)/shard_map/pallas_call | solution.py:203
  8.7 0.0 collective-permute-done.1.refs_1_
  8.7 0.7 %collective-permute-done.2.refs_2_ = bf16[8,3584]{1,0:T(8,128)(2,1)S(1)} collective-permute-done((bf16[8,3584]{1,0:T(8,128)(2,1)S(1)}, bf16[8,3584]{1,0:T(8,128)(2,1)S(1)}, u32[]{:S(2)}, u32[]{:S(2)}) %collective-permute-start.2) | collective-permute-done | bytes 57376 | tf_op jit(solution)/shard_map/ppermute | solution.py:241
  9.4 0.0 collective-permute-done.3.refs_3_
  9.4 0.0 collective-permute-done.twin_in_ref
  9.5 0.6 %shard_map.84.hidden_ref = bf16[32,256]{1,0:T(8,128)(2,1)S(1)} custom-call(bf16[2,3584,128]{2,1,0:T(8,128)(2,1)S(1)} %get-tuple-element.22.in_ref, bf16[2,3584,128]{2,1,0:T(8,128)(2,1)S(1)} %collective-permute-done.twin_in_ref, bf16[8,3584]{1,0:T(8,128)(2,1)S(1)} %get-tuple-element.23.refs_0_, bf16[8,3584]{1,0:T(8,128)(2,1)S(1)} %collective-permute-done.1.refs_1_, ...), custom_call_target="tpu_custom_call" | custom-call | flops 11744051200 | bytes 3915776 | tf_op jit(solution)/shard_map/pallas_call | solution.py:203
  10.1 0.0 collective-permute-done.4.twin_down_ref
  10.1 0.4 %shard_map.85 = (bf16[8,3584]{1,0:T(8,128)(2,1)S(1)}, bf16[8,3584]{1,0:T(8,128)(2,1)S(1)}, bf16[8,3584]{1,0:T(8,128)(2,1)S(1)}, bf16[8,3584]{1,0:T(8,128)(2,1)S(1)}) custom-call(bf16[32,256]{1,0:T(8,128)(2,1)S(1)} %shard_map.84.hidden_ref, bf16[128,3584]{1,0:T(8,128)(2,1)S(1)} %get-tuple-element.27.down_ref, ...), custom_call_target="tpu_custom_call" | custom-call | flops 58720256 | bytes 2080768 | tf_op jit(solution)/shard_map/pallas_call | solution.py:203
  10.5 1.2 %collective-permute-start.5 = (bf16[8,3584]{1,0:T(8,128)(2,1)S(1)}, bf16[8,3584]{1,0:T(8,128)(2,1)S(1)}, u32[]{:S(2)}, u32[]{:S(2)}) collective-permute-start(bf16[8,3584]{1,0:T(8,128)(2,1)S(1)} %get-tuple-element.30), channel_id=1, source_target_pairs={{0,3},{1,6},{2,5},{3,4},{4,7},{5,0},{6,1},{7,2},{8,11},{9,14},{10,... | collective-permute-start | bytes 172040 | tf_op jit(solution)/shard_map/ppermute | solution.py:241
  11.7 0.6 %collective-permute-start.6 = (bf16[8,3584]{1,0:T(8,128)(2,1)S(1)}, bf16[8,3584]{1,0:T(8,128)(2,1)S(1)}, u32[]{:S(2)}, u32[]{:S(2)}) collective-permute-start(bf16[8,3584]{1,0:T(8,128)(2,1)S(1)} %get-tuple-element.33), channel_id=1, source_target_pairs={{0,5},{1,4},{2,7},{3,6},{4,1},{5,2},{6,3},{7,0},{8,13},{9,12},{10,... | collective-permute-start | bytes 172040 | tf_op jit(solution)/shard_map/ppermute | solution.py:241
  12.3 2.0 %collective-permute-start.7 = (bf16[8,3584]{1,0:T(8,128)(2,1)S(1)}, bf16[8,3584]{1,0:T(8,128)(2,1)S(1)}, u32[]{:S(2)}, u32[]{:S(2)}) collective-permute-start(bf16[8,3584]{1,0:T(8,128)(2,1)S(1)} %get-tuple-element.34), channel_id=1, source_target_pairs={{0,7},{1,2},{2,1},{3,0},{4,3},{5,6},{6,5},{7,4},{8,15},{9,10},{10,... | collective-permute-start | bytes 172040 | tf_op jit(solution)/shard_map/ppermute | solution.py:241
  14.3 0.0 collective-permute-done.5.refs_1_
  14.3 0.2 %shard_map.86 = (bf16[32,16]{1,0:T(8,128)(2,1)S(1)}, f32[16,3584]{1,0:T(8,128)S(1)}) custom-call(bf16[32,32]{1,0:T(8,128)(2,1)S(1)} %get-tuple-element.21.weight_ref, bf16[8,3584]{1,0:T(8,128)(2,1)S(1)} %get-tuple-element.29.refs_0_, bf16[8,3584]{1,0:T(8,128)(2,1)S(1)} %collective-permute-done.5.refs_1_), custom_call_target="tpu_custom_call" | custom-call | flops 3670016 | bytes 347136 | tf_op jit(solution)/shard_map/pallas_call | solution.py:203
  14.5 1.7 %collective-permute-done.6.refs_1_ = bf16[8,3584]{1,0:T(8,128)(2,1)S(1)} collective-permute-done((bf16[8,3584]{1,0:T(8,128)(2,1)S(1)}, bf16[8,3584]{1,0:T(8,128)(2,1)S(1)}, u32[]{:S(2)}, u32[]{:S(2)}) %collective-permute-start.6) | collective-permute-done | bytes 57376 | tf_op jit(solution)/shard_map/ppermute | solution.py:241
  16.2 0.0 collective-permute-done.7.refs_2_
  16.2 0.9 %shard_map.87 = bf16[16,3584]{1,0:T(8,128)(2,1)} custom-call(bf16[32,16]{1,0:T(8,128)(2,1)S(1)} %get-tuple-element.31.weight_ref, f32[16,3584]{1,0:T(8,128)S(1)} %get-tuple-element.32.refs_0_, bf16[8,3584]{1,0:T(8,128)(2,1)S(1)} %collective-permute-done.6.refs_1_, bf16[8,3584]{1,0:T(8,128)(2,1)S(1)} %collective-permute-done.7.refs_2_), custom_call_target="tpu_custom_call" | custom-call | flops 7340032 | bytes 459776 | tf_op jit(solution)/shard_map/pallas_call | solution.py:203
Async XLA Ops:
  0.0 9.5 %collective-permute-start = (bf16[2,3584,128]{2,1,0:T(8,128)(2,1)}, bf16[2,3584,128]{2,1,0:T(8,128)(2,1)S(1)}, u32[]{:S(2)}, u32[]{:S(2)}) collective-permute-start(bf16[2,3584,128]{2,1,0:T(8,128)(2,1)} %in_hbm.1), channel_id=1, source_target_pairs={{0,1},{1,0},{2,3},{3,2},{4,5},{5,4},{6,7},{7,6},{8,9},{9,8},{10,11... | collective-permute-start | bytes 5505032 | tf_op jit(solution)/shard_map/ppermute | solution.py:247
  1.6 7.1 %collective-permute-start.1 = (bf16[8,3584]{1,0:T(8,128)(2,1)S(1)}, bf16[8,3584]{1,0:T(8,128)(2,1)S(1)}, u32[]{:S(2)}, u32[]{:S(2)}) collective-permute-start(bf16[8,3584]{1,0:T(8,128)(2,1)S(1)} %get-tuple-element.24), channel_id=1, source_target_pairs={{0,7},{1,2},{2,5},{3,4},{4,1},{5,6},{6,3},{7,0},{8,15},{9,10},{10,... | collective-permute-start | bytes 172040 | tf_op jit(solution)/shard_map/ppermute | solution.py:241
  5.2 4.2 %collective-permute-start.2 = (bf16[8,3584]{1,0:T(8,128)(2,1)S(1)}, bf16[8,3584]{1,0:T(8,128)(2,1)S(1)}, u32[]{:S(2)}, u32[]{:S(2)}) collective-permute-start(bf16[8,3584]{1,0:T(8,128)(2,1)S(1)} %get-tuple-element.25), channel_id=1, source_target_pairs={{0,5},{1,4},{2,7},{3,6},{4,3},{5,0},{6,1},{7,2},{8,13},{9,12},{10,... | collective-permute-start | bytes 172040 | tf_op jit(solution)/shard_map/ppermute | solution.py:241
  5.4 4.0 %collective-permute-start.3 = (bf16[8,3584]{1,0:T(8,128)(2,1)S(1)}, bf16[8,3584]{1,0:T(8,128)(2,1)S(1)}, u32[]{:S(2)}, u32[]{:S(2)}) collective-permute-start(bf16[8,3584]{1,0:T(8,128)(2,1)S(1)} %get-tuple-element.26), channel_id=1, source_target_pairs={{0,3},{1,6},{2,1},{3,0},{4,7},{5,2},{6,5},{7,4},{8,11},{9,14},{10,... | collective-permute-start | bytes 172040 | tf_op jit(solution)/shard_map/ppermute | solution.py:241
  6.0 4.1 %collective-permute-start.4 = (bf16[128,3584]{1,0:T(8,128)(2,1)}, bf16[128,3584]{1,0:T(8,128)(2,1)S(1)}, u32[]{:S(2)}, u32[]{:S(2)}) collective-permute-start(bf16[128,3584]{1,0:T(8,128)(2,1)} %down_hbm.1), channel_id=1, source_target_pairs={{0,1},{1,0},{2,3},{3,2},{4,5},{5,4},{6,7},{7,6},{8,9},{9,8},{10,11... | collective-permute-start | bytes 2752520 | tf_op jit(solution)/shard_map/ppermute | solution.py:247
  10.5 3.8 %collective-permute-start.5 = (bf16[8,3584]{1,0:T(8,128)(2,1)S(1)}, bf16[8,3584]{1,0:T(8,128)(2,1)S(1)}, u32[]{:S(2)}, u32[]{:S(2)}) collective-permute-start(bf16[8,3584]{1,0:T(8,128)(2,1)S(1)} %get-tuple-element.30), channel_id=1, source_target_pairs={{0,3},{1,6},{2,5},{3,4},{4,7},{5,0},{6,1},{7,2},{8,11},{9,14},{10,... | collective-permute-start | bytes 172040 | tf_op jit(solution)/shard_map/ppermute | solution.py:241
  11.7 4.5 %collective-permute-start.6 = (bf16[8,3584]{1,0:T(8,128)(2,1)S(1)}, bf16[8,3584]{1,0:T(8,128)(2,1)S(1)}, u32[]{:S(2)}, u32[]{:S(2)}) collective-permute-start(bf16[8,3584]{1,0:T(8,128)(2,1)S(1)} %get-tuple-element.33), channel_id=1, source_target_pairs={{0,5},{1,4},{2,7},{3,6},{4,1},{5,2},{6,3},{7,0},{8,13},{9,12},{10,... | collective-permute-start | bytes 172040 | tf_op jit(solution)/shard_map/ppermute | solution.py:241
  12.3 3.9 %collective-permute-start.7 = (bf16[8,3584]{1,0:T(8,128)(2,1)S(1)}, bf16[8,3584]{1,0:T(8,128)(2,1)S(1)}, u32[]{:S(2)}, u32[]{:S(2)}) collective-permute-start(bf16[8,3584]{1,0:T(8,128)(2,1)S(1)} %get-tuple-element.34), channel_id=1, source_target_pairs={{0,7},{1,2},{2,1},{3,0},{4,3},{5,6},{6,5},{7,4},{8,15},{9,10},{10,... | collective-permute-start | bytes 172040 | tf_op jit(solution)/shard_map/ppermute | solution.py:241

commit v20 on v15

--- a/solution.py
+++ b/solution.py
@@ -243,7 +243,6 @@
     chips = devices // 2
     rows, width = tokens.shape
     hidden = w_down.shape[0]
-    twin_in = from_twin(w_in)
     operands = (new_place, old_place, expert_ids.T, replica.T, tokens)
     combine = combine.T
     block = jax.ShapeDtypeStruct((CAP * (2 if split else 1), width), jnp.bfloat16)
@@ -256,7 +255,8 @@
         scratch=scratch_for(operands[:2], operands[2:]),
     )
     received = exchange([blocks[c // repeats] for c in range(chips)], split)
-    twin_down = from_twin(lax.optimization_barrier((w_down, found))[0])
+    after_in, after_down, _ = lax.optimization_barrier((w_in, w_down, found))
+    twin_in, twin_down = from_twin(after_in), from_twin(after_down)
     own_in, own_down, weight = call(
         functools.partial(prepare_kernel, split),
         [

time: 17.2 us -> 17.2 us (level); the launches traced: 17 us -> 16.9 us
    ppermute x6, starting transfers between devices: 8.24 us -> 8.01 us  [exchange(): result.append(lax.ppermute(blocks[k], 'expert', pairs))]
  transfers between devices with their start and end apart: 8 -> 8, of which waited for: 2 -> 2; matrix products, arithmetic and copies ran while one was open for 0% -> 0% of each run, Pallas kernels for 21% -> 14%
where the time goes in v20:
time: 17.2 us; the launch traced here: 16.9 us
  starting transfers between devices  9.48 us (55%)
  Pallas kernels  4.78 us (28%)
  waiting for transfers between devices  2.54 us (15%)
    ppermute x6, starting transfers between devices, exchange(): result.append(lax.ppermute(blocks[k], 'expert', pairs))  8.01 us
    pallas_call x5, Pallas kernels, call(): pl.pallas_call(kernel, out_shape=outs, in_specs=arg_specs, out_specs=out_...  4.78 us
    ppermute x6, waiting for transfers between devices, exchange(): result.append(lax.ppermute(blocks[k], 'expert', pairs))  2.53 us
    ppermute x2, starting transfers between devices, from_twin(): return lax.ppermute(array, 'expert', pairs)  1.48 us
  transfers between devices with their start and end apart: 8, of which 2 were waited for; matrix products, arithmetic and copies ran while one was open for 0% of the time, Pallas kernels for 14%

profile of v20, /device:TPU:0, one launch (start us, length us, event | category | flops | bytes accessed | tf_op | source)
XLA Modules:
  0.0 16.9 jit_solution(9971217360230986218)
XLA Ops:
  0.0 1.2 %shard_map.82 = (s32[2,16]{1,0:T(2,128)S(1)}, bf16[8,3584]{1,0:T(8,128)(2,1)S(1)}, bf16[8,3584]{1,0:T(8,128)(2,1)S(1)}, bf16[8,3584]{1,0:T(8,128)(2,1)S(1)}, bf16[8,3584]{1,0:T(8,128)(2,1)S(1)}) custom-call(s32[8]{0:T(128)} %refs_0_.1, s32[8]{0:T(128)} %refs_1_.1, s32[2,16]{1,0:T(2,128)} %bitcast.3, s32[2,16]{1,0:T(2,128)} %bitcast.4, bf16[16,3584]{1,0:T(8,128)(2,1)} %refs_4_.1), custom_call_target="tpu_custom_call" | custom-call | flops 3670016 | bytes 344512 | tf_op jit(solution)/shard_map/pallas_call | solution.py:191
  1.2 0.5 %collective-permute-start = (bf16[2,3584,128]{2,1,0:T(8,128)(2,1)}, bf16[2,3584,128]{2,1,0:T(8,128)(2,1)S(1)}, u32[]{:S(2)}, u32[]{:S(2)}) collective-permute-start(bf16[2,3584,128]{2,1,0:T(8,128)(2,1)} %in_hbm.1), channel_id=1, source_target_pairs={{0,1},{1,0},{2,3},{3,2},{4,5},{5,4},{6,7},{7,6},{8,9},{9,8},{10,11... | collective-permute-start | bytes 5505032 | tf_op jit(solution)/shard_map/ppermute | solution.py:235
  1.7 3.6 %collective-permute-start.1 = (bf16[8,3584]{1,0:T(8,128)(2,1)S(1)}, bf16[8,3584]{1,0:T(8,128)(2,1)S(1)}, u32[]{:S(2)}, u32[]{:S(2)}) collective-permute-start(bf16[8,3584]{1,0:T(8,128)(2,1)S(1)} %get-tuple-element.24), channel_id=1, source_target_pairs={{0,7},{1,2},{2,5},{3,4},{4,1},{5,6},{6,3},{7,0},{8,15},{9,10},{10,... | collective-permute-start | bytes 172040 | tf_op jit(solution)/shard_map/ppermute | solution.py:229
  5.2 0.2 %collective-permute-start.2 = (bf16[8,3584]{1,0:T(8,128)(2,1)S(1)}, bf16[8,3584]{1,0:T(8,128)(2,1)S(1)}, u32[]{:S(2)}, u32[]{:S(2)}) collective-permute-start(bf16[8,3584]{1,0:T(8,128)(2,1)S(1)} %get-tuple-element.25), channel_id=1, source_target_pairs={{0,5},{1,4},{2,7},{3,6},{4,3},{5,0},{6,1},{7,2},{8,13},{9,12},{10,... | collective-permute-start | bytes 172040 | tf_op jit(solution)/shard_map/ppermute | solution.py:229
  5.5 0.6 %collective-permute-start.3 = (bf16[8,3584]{1,0:T(8,128)(2,1)S(1)}, bf16[8,3584]{1,0:T(8,128)(2,1)S(1)}, u32[]{:S(2)}, u32[]{:S(2)}) collective-permute-start(bf16[8,3584]{1,0:T(8,128)(2,1)S(1)} %get-tuple-element.26), channel_id=1, source_target_pairs={{0,3},{1,6},{2,1},{3,0},{4,7},{5,2},{6,5},{7,4},{8,11},{9,14},{10,... | collective-permute-start | bytes 172040 | tf_op jit(solution)/shard_map/ppermute | solution.py:229
  6.0 1.0 %collective-permute-start.4 = (bf16[128,3584]{1,0:T(8,128)(2,1)}, bf16[128,3584]{1,0:T(8,128)(2,1)S(1)}, u32[]{:S(2)}, u32[]{:S(2)}) collective-permute-start(bf16[128,3584]{1,0:T(8,128)(2,1)} %down_hbm.1), channel_id=1, source_target_pairs={{0,1},{1,0},{2,3},{3,2},{4,5},{5,4},{6,7},{7,6},{8,9},{9,8},{10,11... | collective-permute-start | bytes 2752520 | tf_op jit(solution)/shard_map/ppermute | solution.py:235
  7.0 1.8 %shard_map.83 = (bf16[2,3584,128]{2,1,0:T(8,128)(2,1)S(1)}, bf16[128,3584]{1,0:T(8,128)(2,1)S(1)}, bf16[32,32]{1,0:T(8,128)(2,1)S(1)}) custom-call(s32[2,16]{1,0:T(2,128)S(1)} %get-tuple-element.19.found_ref, f32[2,16]{1,0:T(2,128)} %bitcast.5, bf16[2,3584,128]{2,1,0:T(8,128)(2,1)} %in_hbm.1, bf16[128,3584]{1,0:T(8,128)(2,1)} %down_hbm.1), custom_call_target="tpu_custom_call" | custom-call | bytes 5507328 | tf_op jit(solution)/shard_map/pallas_call | solution.py:191
  8.8 0.0 collective-permute-done.1.refs_1_
  8.8 0.7 %collective-permute-done.2.refs_2_ = bf16[8,3584]{1,0:T(8,128)(2,1)S(1)} collective-permute-done((bf16[8,3584]{1,0:T(8,128)(2,1)S(1)}, bf16[8,3584]{1,0:T(8,128)(2,1)S(1)}, u32[]{:S(2)}, u32[]{:S(2)}) %collective-permute-start.2) | collective-permute-done | bytes 57376 | tf_op jit(solution)/shard_map/ppermute | solution.py:229
  9.5 0.0 collective-permute-done.3.refs_3_
  9.5 0.0 collective-permute-done.twin_in_ref
  9.5 0.6 %shard_map.84.hidden_ref = bf16[32,256]{1,0:T(8,128)(2,1)S(1)} custom-call(bf16[2,3584,128]{2,1,0:T(8,128)(2,1)S(1)} %get-tuple-element.21.in_ref, bf16[2,3584,128]{2,1,0:T(8,128)(2,1)S(1)} %collective-permute-done.twin_in_ref, bf16[8,3584]{1,0:T(8,128)(2,1)S(1)} %get-tuple-element.23.refs_0_, bf16[8,3584]{1,0:T(8,128)(2,1)S(1)} %collective-permute-done.1.refs_1_, ...), custom_call_target="tpu_custom_call" | custom-call | flops 11744051200 | bytes 3915776 | tf_op jit(solution)/shard_map/pallas_call | solution.py:191
  10.1 0.0 collective-permute-done.4.twin_down_ref
  10.1 0.4 %shard_map.85 = (bf16[8,3584]{1,0:T(8,128)(2,1)S(1)}, bf16[8,3584]{1,0:T(8,128)(2,1)S(1)}, bf16[8,3584]{1,0:T(8,128)(2,1)S(1)}, bf16[8,3584]{1,0:T(8,128)(2,1)S(1)}) custom-call(bf16[32,256]{1,0:T(8,128)(2,1)S(1)} %shard_map.84.hidden_ref, bf16[128,3584]{1,0:T(8,128)(2,1)S(1)} %get-tuple-element.27.down_ref, ...), custom_call_target="tpu_custom_call" | custom-call | flops 58720256 | bytes 2080768 | tf_op jit(solution)/shard_map/pallas_call | solution.py:191
  10.5 1.0 %collective-permute-start.5 = (bf16[8,3584]{1,0:T(8,128)(2,1)S(1)}, bf16[8,3584]{1,0:T(8,128)(2,1)S(1)}, u32[]{:S(2)}, u32[]{:S(2)}) collective-permute-start(bf16[8,3584]{1,0:T(8,128)(2,1)S(1)} %get-tuple-element.30), channel_id=1, source_target_pairs={{0,3},{1,6},{2,5},{3,4},{4,7},{5,0},{6,1},{7,2},{8,11},{9,14},{10,... | collective-permute-start | bytes 172040 | tf_op jit(solution)/shard_map/ppermute | solution.py:229
  11.5 0.8 %collective-permute-start.6 = (bf16[8,3584]{1,0:T(8,128)(2,1)S(1)}, bf16[8,3584]{1,0:T(8,128)(2,1)S(1)}, u32[]{:S(2)}, u32[]{:S(2)}) collective-permute-start(bf16[8,3584]{1,0:T(8,128)(2,1)S(1)} %get-tuple-element.31), channel_id=1, source_target_pairs={{0,5},{1,4},{2,7},{3,6},{4,1},{5,2},{6,3},{7,0},{8,13},{9,12},{10,... | collective-permute-start | bytes 172040 | tf_op jit(solution)/shard_map/ppermute | solution.py:229
  12.3 1.9 %collective-permute-start.7 = (bf16[8,3584]{1,0:T(8,128)(2,1)S(1)}, bf16[8,3584]{1,0:T(8,128)(2,1)S(1)}, u32[]{:S(2)}, u32[]{:S(2)}) collective-permute-start(bf16[8,3584]{1,0:T(8,128)(2,1)S(1)} %get-tuple-element.32), channel_id=1, source_target_pairs={{0,7},{1,2},{2,1},{3,0},{4,3},{5,6},{6,5},{7,4},{8,15},{9,10},{10,... | collective-permute-start | bytes 172040 | tf_op jit(solution)/shard_map/ppermute | solution.py:229
  14.1 0.0 collective-permute-done.5.refs_1_
  14.2 1.9 %collective-permute-done.6.refs_2_ = bf16[8,3584]{1,0:T(8,128)(2,1)S(1)} collective-permute-done((bf16[8,3584]{1,0:T(8,128)(2,1)S(1)}, bf16[8,3584]{1,0:T(8,128)(2,1)S(1)}, u32[]{:S(2)}, u32[]{:S(2)}) %collective-permute-start.6) | collective-permute-done | bytes 57376 | tf_op jit(solution)/shard_map/ppermute | solution.py:229
  16.0 0.0 collective-permute-done.7.refs_3_
  16.0 0.9 %shard_map.86 = bf16[16,3584]{1,0:T(8,128)(2,1)} custom-call(bf16[32,32]{1,0:T(8,128)(2,1)S(1)} %get-tuple-element.20.weight_ref, bf16[8,3584]{1,0:T(8,128)(2,1)S(1)} %get-tuple-element.29.refs_0_, bf16[8,3584]{1,0:T(8,128)(2,1)S(1)} %collective-permute-done.5.refs_1_, bf16[8,3584]{1,0:T(8,128)(2,1)S(1)} %collective-permute-done.6.refs_2_, ...), custom_call_target="tpu_custom_call" | custom-call | flops 7340032 | bytes 346112 | tf_op jit(solution)/shard_map/pallas_call | solution.py:191
Async XLA Ops:
  1.2 8.3 %collective-permute-start = (bf16[2,3584,128]{2,1,0:T(8,128)(2,1)}, bf16[2,3584,128]{2,1,0:T(8,128)(2,1)S(1)}, u32[]{:S(2)}, u32[]{:S(2)}) collective-permute-start(bf16[2,3584,128]{2,1,0:T(8,128)(2,1)} %in_hbm.1), channel_id=1, source_target_pairs={{0,1},{1,0},{2,3},{3,2},{4,5},{5,4},{6,7},{7,6},{8,9},{9,8},{10,11... | collective-permute-start | bytes 5505032 | tf_op jit(solution)/shard_map/ppermute | solution.py:235
  1.7 7.1 %collective-permute-start.1 = (bf16[8,3584]{1,0:T(8,128)(2,1)S(1)}, bf16[8,3584]{1,0:T(8,128)(2,1)S(1)}, u32[]{:S(2)}, u32[]{:S(2)}) collective-permute-start(bf16[8,3584]{1,0:T(8,128)(2,1)S(1)} %get-tuple-element.24), channel_id=1, source_target_pairs={{0,7},{1,2},{2,5},{3,4},{4,1},{5,6},{6,3},{7,0},{8,15},{9,10},{10,... | collective-permute-start | bytes 172040 | tf_op jit(solution)/shard_map/ppermute | solution.py:229
  5.2 4.2 %collective-permute-start.2 = (bf16[8,3584]{1,0:T(8,128)(2,1)S(1)}, bf16[8,3584]{1,0:T(8,128)(2,1)S(1)}, u32[]{:S(2)}, u32[]{:S(2)}) collective-permute-start(bf16[8,3584]{1,0:T(8,128)(2,1)S(1)} %get-tuple-element.25), channel_id=1, source_target_pairs={{0,5},{1,4},{2,7},{3,6},{4,3},{5,0},{6,1},{7,2},{8,13},{9,12},{10,... | collective-permute-start | bytes 172040 | tf_op jit(solution)/shard_map/ppermute | solution.py:229
  5.5 4.0 %collective-permute-start.3 = (bf16[8,3584]{1,0:T(8,128)(2,1)S(1)}, bf16[8,3584]{1,0:T(8,128)(2,1)S(1)}, u32[]{:S(2)}, u32[]{:S(2)}) collective-permute-start(bf16[8,3584]{1,0:T(8,128)(2,1)S(1)} %get-tuple-element.26), channel_id=1, source_target_pairs={{0,3},{1,6},{2,1},{3,0},{4,7},{5,2},{6,5},{7,4},{8,11},{9,14},{10,... | collective-permute-start | bytes 172040 | tf_op jit(solution)/shard_map/ppermute | solution.py:229
  6.0 4.1 %collective-permute-start.4 = (bf16[128,3584]{1,0:T(8,128)(2,1)}, bf16[128,3584]{1,0:T(8,128)(2,1)S(1)}, u32[]{:S(2)}, u32[]{:S(2)}) collective-permute-start(bf16[128,3584]{1,0:T(8,128)(2,1)} %down_hbm.1), channel_id=1, source_target_pairs={{0,1},{1,0},{2,3},{3,2},{4,5},{5,4},{6,7},{7,6},{8,9},{9,8},{10,11... | collective-permute-start | bytes 2752520 | tf_op jit(solution)/shard_map/ppermute | solution.py:235
  10.5 3.7 %collective-permute-start.5 = (bf16[8,3584]{1,0:T(8,128)(2,1)S(1)}, bf16[8,3584]{1,0:T(8,128)(2,1)S(1)}, u32[]{:S(2)}, u32[]{:S(2)}) collective-permute-start(bf16[8,3584]{1,0:T(8,128)(2,1)S(1)} %get-tuple-element.30), channel_id=1, source_target_pairs={{0,3},{1,6},{2,5},{3,4},{4,7},{5,0},{6,1},{7,2},{8,11},{9,14},{10,... | collective-permute-start | bytes 172040 | tf_op jit(solution)/shard_map/ppermute | solution.py:229
  11.5 4.5 %collective-permute-start.6 = (bf16[8,3584]{1,0:T(8,128)(2,1)S(1)}, bf16[8,3584]{1,0:T(8,128)(2,1)S(1)}, u32[]{:S(2)}, u32[]{:S(2)}) collective-permute-start(bf16[8,3584]{1,0:T(8,128)(2,1)S(1)} %get-tuple-element.31), channel_id=1, source_target_pairs={{0,5},{1,4},{2,7},{3,6},{4,1},{5,2},{6,3},{7,0},{8,13},{9,12},{10,... | collective-permute-start | bytes 172040 | tf_op jit(solution)/shard_map/ppermute | solution.py:229
  12.3 3.7 %collective-permute-start.7 = (bf16[8,3584]{1,0:T(8,128)(2,1)S(1)}, bf16[8,3584]{1,0:T(8,128)(2,1)S(1)}, u32[]{:S(2)}, u32[]{:S(2)}) collective-permute-start(bf16[8,3584]{1,0:T(8,128)(2,1)S(1)} %get-tuple-element.32), channel_id=1, source_target_pairs={{0,7},{1,2},{2,1},{3,0},{4,3},{5,6},{6,5},{7,4},{8,15},{9,10},{10,... | collective-permute-start | bytes 172040 | tf_op jit(solution)/shard_map/ppermute | solution.py:229

commit v21 on v20

--- a/solution.py
+++ b/solution.py
@@ -20,23 +20,26 @@
 
 
 def targets(shards, goes, new_ref, old_ref, ids, replica):
-    slots, rows = new_ref.shape[0], ids.shape[1]
-    device = lax.axis_index("expert")
+    new, old = new_ref[...], old_ref[...]
+    slots, rows = new.shape[1], ids.shape[1]
+    across = lax.broadcasted_iota(jnp.int32, new.shape, 1)
+    source = jnp.where(new == old, across, across ^ 1)
+    away = source ^ (lax.axis_index("expert") // shards)
+    if shards == 1:
+        step = sum(jnp.where(source >> 1 == chip, k, 0) for k, chip in enumerate(goes, 1))
+        away = (source & 1) | (step << 1)
+    holds = [jnp.broadcast_to(new[:, slot : slot + 1], (slots, rows)) for slot in range(slots)]
+    first = [jnp.broadcast_to(away[:, slot : slot + 1], (slots, rows)) for slot in range(slots)]
     down = lax.broadcasted_iota(jnp.int32, (slots, rows), 0)
     expert = jnp.zeros((slots, rows), jnp.int32)
     line = jnp.zeros((slots, rows), jnp.int32)
     for slot in range(slots):
-        source = jnp.where(new_ref[slot] == old_ref[slot], slot, slot ^ 1)
-        away = source ^ (device // shards)
-        if shards == 1:
-            step = sum(jnp.where(source >> 1 == chip, k, 0) for k, chip in enumerate(goes, 1))
-            away = (source & 1) | (step << 1)
-        expert = jnp.where(down == slot, new_ref[slot], expert)
-        line = jnp.where(down == slot, CAP * away, line)
+        expert = jnp.where(down == slot, holds[slot], expert)
+        line = jnp.where(down == slot, CAP * first[slot], line)
     count = jnp.zeros((slots, rows), jnp.int32)
     rank = jnp.zeros((slots, rows), jnp.int32)
     for slot in range(slots):
-        same = expert == new_ref[slot]
+        same = expert == holds[slot]
         count += jnp.where(same, 1, 0)
         rank += jnp.where(same & (down > slot), 1, 0)
     chosen = []
@@ -203,11 +206,10 @@
     return jax.ShapeDtypeStruct(array.shape, array.dtype)
 
 
-def scratch_for(scalars, arrays):
+def scratch_for(arrays):
     return [
-        *[pltpu.SMEM(x.shape, x.dtype) for x in scalars],
         *[pltpu.VMEM(x.shape, x.dtype) for x in arrays],
-        pltpu.SemaphoreType.DMA((len(scalars) + len(arrays),)),
+        pltpu.SemaphoreType.DMA((len(arrays),)),
     ]
 
 
@@ -243,7 +245,7 @@
     chips = devices // 2
     rows, width = tokens.shape
     hidden = w_down.shape[0]
-    operands = (new_place, old_place, expert_ids.T, replica.T, tokens)
+    operands = (new_place[None], old_place[None], expert_ids.T, replica.T, tokens)
     combine = combine.T
     block = jax.ShapeDtypeStruct((CAP * (2 if split else 1), width), jnp.bfloat16)
     found, *blocks = call(
@@ -252,7 +254,7 @@
         operands,
         2 * SLOTS * CAP * rows * width,
         [HBM] * len(operands),
-        scratch=scratch_for(operands[:2], operands[2:]),
+        scratch=scratch_for(operands),
     )
     received = exchange([blocks[c // repeats] for c in range(chips)], split)
     after_in, after_down, _ = lax.optimization_barrier((w_in, w_down, found))

time: 17.2 us -> 17.2 us (level)
  no operation moved by 1% of the time
where the time goes in v21:
time: 17.2 us; the launch traced here: 16.9 us
  starting transfers between devices  9.5 us (55%)
  Pallas kernels  4.82 us (28%)
  waiting for transfers between devices  2.54 us (15%)
    ppermute x6, starting transfers between devices, exchange(): result.append(lax.ppermute(blocks[k], 'expert', pairs))  8.01 us
    pallas_call x5, Pallas kernels, call(): pl.pallas_call(kernel, out_shape=outs, in_specs=arg_specs, out_specs=out_...  4.82 us
    ppermute x6, waiting for transfers between devices, exchange(): result.append(lax.ppermute(blocks[k], 'expert', pairs))  2.53 us
    ppermute x2, starting transfers between devices, from_twin(): return lax.ppermute(array, 'expert', pairs)  1.49 us
  transfers between devices with their start and end apart: 8, of which 2 were waited for; matrix products, arithmetic and copies ran while one was open for 0% of the time, Pallas kernels for 14%

profile of v21, /device:TPU:0, one launch (start us, length us, event | category | flops | bytes accessed | tf_op | source)
XLA Modules:
  0.0 16.9 jit_solution(15692979022144307358)
XLA Ops:
  0.0 1.2 %shard_map.82 = (s32[2,16]{1,0:T(2,128)S(1)}, bf16[8,3584]{1,0:T(8,128)(2,1)S(1)}, bf16[8,3584]{1,0:T(8,128)(2,1)S(1)}, bf16[8,3584]{1,0:T(8,128)(2,1)S(1)}, bf16[8,3584]{1,0:T(8,128)(2,1)S(1)}) custom-call(s32[1,8]{1,0:T(1,128)} %bitcast.8, s32[1,8]{1,0:T(1,128)} %bitcast.9, s32[2,16]{1,0:T(2,128)} %bitcast.5, s32[2,16]{1,0:T(2,128)} %bitcast.6, ...), custom_call_target="tpu_custom_call" | custom-call | flops 3670016 | bytes 344512 | tf_op jit(solution)/shard_map/pallas_call | solution.py:194
  1.2 0.5 %collective-permute-start = (bf16[2,3584,128]{2,1,0:T(8,128)(2,1)}, bf16[2,3584,128]{2,1,0:T(8,128)(2,1)S(1)}, u32[]{:S(2)}, u32[]{:S(2)}) collective-permute-start(bf16[2,3584,128]{2,1,0:T(8,128)(2,1)} %in_hbm.1), channel_id=1, source_target_pairs={{0,1},{1,0},{2,3},{3,2},{4,5},{5,4},{6,7},{7,6},{8,9},{9,8},{10,11... | collective-permute-start | bytes 5505032 | tf_op jit(solution)/shard_map/ppermute | solution.py:237
  1.7 3.6 %collective-permute-start.1 = (bf16[8,3584]{1,0:T(8,128)(2,1)S(1)}, bf16[8,3584]{1,0:T(8,128)(2,1)S(1)}, u32[]{:S(2)}, u32[]{:S(2)}) collective-permute-start(bf16[8,3584]{1,0:T(8,128)(2,1)S(1)} %get-tuple-element.24), channel_id=1, source_target_pairs={{0,7},{1,2},{2,5},{3,4},{4,1},{5,6},{6,3},{7,0},{8,15},{9,10},{10,... | collective-permute-start | bytes 172040 | tf_op jit(solution)/shard_map/ppermute | solution.py:231
  5.3 0.2 %collective-permute-start.2 = (bf16[8,3584]{1,0:T(8,128)(2,1)S(1)}, bf16[8,3584]{1,0:T(8,128)(2,1)S(1)}, u32[]{:S(2)}, u32[]{:S(2)}) collective-permute-start(bf16[8,3584]{1,0:T(8,128)(2,1)S(1)} %get-tuple-element.25), channel_id=1, source_target_pairs={{0,5},{1,4},{2,7},{3,6},{4,3},{5,0},{6,1},{7,2},{8,13},{9,12},{10,... | collective-permute-start | bytes 172040 | tf_op jit(solution)/shard_map/ppermute | solution.py:231
  5.5 0.6 %collective-permute-start.3 = (bf16[8,3584]{1,0:T(8,128)(2,1)S(1)}, bf16[8,3584]{1,0:T(8,128)(2,1)S(1)}, u32[]{:S(2)}, u32[]{:S(2)}) collective-permute-start(bf16[8,3584]{1,0:T(8,128)(2,1)S(1)} %get-tuple-element.26), channel_id=1, source_target_pairs={{0,3},{1,6},{2,1},{3,0},{4,7},{5,2},{6,5},{7,4},{8,11},{9,14},{10,... | collective-permute-start | bytes 172040 | tf_op jit(solution)/shard_map/ppermute | solution.py:231
  6.1 1.0 %collective-permute-start.4 = (bf16[128,3584]{1,0:T(8,128)(2,1)}, bf16[128,3584]{1,0:T(8,128)(2,1)S(1)}, u32[]{:S(2)}, u32[]{:S(2)}) collective-permute-start(bf16[128,3584]{1,0:T(8,128)(2,1)} %down_hbm.1), channel_id=1, source_target_pairs={{0,1},{1,0},{2,3},{3,2},{4,5},{5,4},{6,7},{7,6},{8,9},{9,8},{10,11... | collective-permute-start | bytes 2752520 | tf_op jit(solution)/shard_map/ppermute | solution.py:237
  7.0 1.8 %shard_map.83 = (bf16[2,3584,128]{2,1,0:T(8,128)(2,1)S(1)}, bf16[128,3584]{1,0:T(8,128)(2,1)S(1)}, bf16[32,32]{1,0:T(8,128)(2,1)S(1)}) custom-call(s32[2,16]{1,0:T(2,128)S(1)} %get-tuple-element.19.found_ref, f32[2,16]{1,0:T(2,128)} %bitcast.7, bf16[2,3584,128]{2,1,0:T(8,128)(2,1)} %in_hbm.1, bf16[128,3584]{1,0:T(8,128)(2,1)} %down_hbm.1), custom_call_target="tpu_custom_call" | custom-call | bytes 5507328 | tf_op jit(solution)/shard_map/pallas_call | solution.py:194
  8.8 0.0 collective-permute-done.1.refs_1_
  8.8 0.7 %collective-permute-done.2.refs_2_ = bf16[8,3584]{1,0:T(8,128)(2,1)S(1)} collective-permute-done((bf16[8,3584]{1,0:T(8,128)(2,1)S(1)}, bf16[8,3584]{1,0:T(8,128)(2,1)S(1)}, u32[]{:S(2)}, u32[]{:S(2)}) %collective-permute-start.2) | collective-permute-done | bytes 57376 | tf_op jit(solution)/shard_map/ppermute | solution.py:231
  9.5 0.0 collective-permute-done.3.refs_3_
  9.5 0.0 collective-permute-done.twin_in_ref
  9.5 0.6 %shard_map.84.hidden_ref = bf16[32,256]{1,0:T(8,128)(2,1)S(1)} custom-call(bf16[2,3584,128]{2,1,0:T(8,128)(2,1)S(1)} %get-tuple-element.21.in_ref, bf16[2,3584,128]{2,1,0:T(8,128)(2,1)S(1)} %collective-permute-done.twin_in_ref, bf16[8,3584]{1,0:T(8,128)(2,1)S(1)} %get-tuple-element.23.refs_0_, bf16[8,3584]{1,0:T(8,128)(2,1)S(1)} %collective-permute-done.1.refs_1_, ...), custom_call_target="tpu_custom_call" | custom-call | flops 11744051200 | bytes 3915776 | tf_op jit(solution)/shard_map/pallas_call | solution.py:194
  10.1 0.0 collective-permute-done.4.twin_down_ref
  10.2 0.4 %shard_map.85 = (bf16[8,3584]{1,0:T(8,128)(2,1)S(1)}, bf16[8,3584]{1,0:T(8,128)(2,1)S(1)}, bf16[8,3584]{1,0:T(8,128)(2,1)S(1)}, bf16[8,3584]{1,0:T(8,128)(2,1)S(1)}) custom-call(bf16[32,256]{1,0:T(8,128)(2,1)S(1)} %shard_map.84.hidden_ref, bf16[128,3584]{1,0:T(8,128)(2,1)S(1)} %get-tuple-element.27.down_ref, ...), custom_call_target="tpu_custom_call" | custom-call | flops 58720256 | bytes 2080768 | tf_op jit(solution)/shard_map/pallas_call | solution.py:194
  10.5 1.0 %collective-permute-start.5 = (bf16[8,3584]{1,0:T(8,128)(2,1)S(1)}, bf16[8,3584]{1,0:T(8,128)(2,1)S(1)}, u32[]{:S(2)}, u32[]{:S(2)}) collective-permute-start(bf16[8,3584]{1,0:T(8,128)(2,1)S(1)} %get-tuple-element.30), channel_id=1, source_target_pairs={{0,3},{1,6},{2,5},{3,4},{4,7},{5,0},{6,1},{7,2},{8,11},{9,14},{10,... | collective-permute-start | bytes 172040 | tf_op jit(solution)/shard_map/ppermute | solution.py:231
  11.6 0.8 %collective-permute-start.6 = (bf16[8,3584]{1,0:T(8,128)(2,1)S(1)}, bf16[8,3584]{1,0:T(8,128)(2,1)S(1)}, u32[]{:S(2)}, u32[]{:S(2)}) collective-permute-start(bf16[8,3584]{1,0:T(8,128)(2,1)S(1)} %get-tuple-element.31), channel_id=1, source_target_pairs={{0,5},{1,4},{2,7},{3,6},{4,1},{5,2},{6,3},{7,0},{8,13},{9,12},{10,... | collective-permute-start | bytes 172040 | tf_op jit(solution)/shard_map/ppermute | solution.py:231
  12.3 1.9 %collective-permute-start.7 = (bf16[8,3584]{1,0:T(8,128)(2,1)S(1)}, bf16[8,3584]{1,0:T(8,128)(2,1)S(1)}, u32[]{:S(2)}, u32[]{:S(2)}) collective-permute-start(bf16[8,3584]{1,0:T(8,128)(2,1)S(1)} %get-tuple-element.32), channel_id=1, source_target_pairs={{0,7},{1,2},{2,1},{3,0},{4,3},{5,6},{6,5},{7,4},{8,15},{9,10},{10,... | collective-permute-start | bytes 172040 | tf_op jit(solution)/shard_map/ppermute | solution.py:231
  14.2 0.0 collective-permute-done.5.refs_1_
  14.2 1.9 %collective-permute-done.6.refs_2_ = bf16[8,3584]{1,0:T(8,128)(2,1)S(1)} collective-permute-done((bf16[8,3584]{1,0:T(8,128)(2,1)S(1)}, bf16[8,3584]{1,0:T(8,128)(2,1)S(1)}, u32[]{:S(2)}, u32[]{:S(2)}) %collective-permute-start.6) | collective-permute-done | bytes 57376 | tf_op jit(solution)/shard_map/ppermute | solution.py:231
  16.1 0.0 collective-permute-done.7.refs_3_
  16.1 0.9 %shard_map.86 = bf16[16,3584]{1,0:T(8,128)(2,1)} custom-call(bf16[32,32]{1,0:T(8,128)(2,1)S(1)} %get-tuple-element.20.weight_ref, bf16[8,3584]{1,0:T(8,128)(2,1)S(1)} %get-tuple-element.29.refs_0_, bf16[8,3584]{1,0:T(8,128)(2,1)S(1)} %collective-permute-done.5.refs_1_, bf16[8,3584]{1,0:T(8,128)(2,1)S(1)} %collective-permute-done.6.refs_2_, ...), custom_call_target="tpu_custom_call" | custom-call | flops 7340032 | bytes 346112 | tf_op jit(solution)/shard_map/pallas_call | solution.py:194
Async XLA Ops:
  1.2 8.3 %collective-permute-start = (bf16[2,3584,128]{2,1,0:T(8,128)(2,1)}, bf16[2,3584,128]{2,1,0:T(8,128)(2,1)S(1)}, u32[]{:S(2)}, u32[]{:S(2)}) collective-permute-start(bf16[2,3584,128]{2,1,0:T(8,128)(2,1)} %in_hbm.1), channel_id=1, source_target_pairs={{0,1},{1,0},{2,3},{3,2},{4,5},{5,4},{6,7},{7,6},{8,9},{9,8},{10,11... | collective-permute-start | bytes 5505032 | tf_op jit(solution)/shard_map/ppermute | solution.py:237
  1.7 7.1 %collective-permute-start.1 = (bf16[8,3584]{1,0:T(8,128)(2,1)S(1)}, bf16[8,3584]{1,0:T(8,128)(2,1)S(1)}, u32[]{:S(2)}, u32[]{:S(2)}) collective-permute-start(bf16[8,3584]{1,0:T(8,128)(2,1)S(1)} %get-tuple-element.24), channel_id=1, source_target_pairs={{0,7},{1,2},{2,5},{3,4},{4,1},{5,6},{6,3},{7,0},{8,15},{9,10},{10,... | collective-permute-start | bytes 172040 | tf_op jit(solution)/shard_map/ppermute | solution.py:231
  5.3 4.2 %collective-permute-start.2 = (bf16[8,3584]{1,0:T(8,128)(2,1)S(1)}, bf16[8,3584]{1,0:T(8,128)(2,1)S(1)}, u32[]{:S(2)}, u32[]{:S(2)}) collective-permute-start(bf16[8,3584]{1,0:T(8,128)(2,1)S(1)} %get-tuple-element.25), channel_id=1, source_target_pairs={{0,5},{1,4},{2,7},{3,6},{4,3},{5,0},{6,1},{7,2},{8,13},{9,12},{10,... | collective-permute-start | bytes 172040 | tf_op jit(solution)/shard_map/ppermute | solution.py:231
  5.5 4.0 %collective-permute-start.3 = (bf16[8,3584]{1,0:T(8,128)(2,1)S(1)}, bf16[8,3584]{1,0:T(8,128)(2,1)S(1)}, u32[]{:S(2)}, u32[]{:S(2)}) collective-permute-start(bf16[8,3584]{1,0:T(8,128)(2,1)S(1)} %get-tuple-element.26), channel_id=1, source_target_pairs={{0,3},{1,6},{2,1},{3,0},{4,7},{5,2},{6,5},{7,4},{8,11},{9,14},{10,... | collective-permute-start | bytes 172040 | tf_op jit(solution)/shard_map/ppermute | solution.py:231
  6.1 4.1 %collective-permute-start.4 = (bf16[128,3584]{1,0:T(8,128)(2,1)}, bf16[128,3584]{1,0:T(8,128)(2,1)S(1)}, u32[]{:S(2)}, u32[]{:S(2)}) collective-permute-start(bf16[128,3584]{1,0:T(8,128)(2,1)} %down_hbm.1), channel_id=1, source_target_pairs={{0,1},{1,0},{2,3},{3,2},{4,5},{5,4},{6,7},{7,6},{8,9},{9,8},{10,11... | collective-permute-start | bytes 2752520 | tf_op jit(solution)/shard_map/ppermute | solution.py:237
  10.5 3.7 %collective-permute-start.5 = (bf16[8,3584]{1,0:T(8,128)(2,1)S(1)}, bf16[8,3584]{1,0:T(8,128)(2,1)S(1)}, u32[]{:S(2)}, u32[]{:S(2)}) collective-permute-start(bf16[8,3584]{1,0:T(8,128)(2,1)S(1)} %get-tuple-element.30), channel_id=1, source_target_pairs={{0,3},{1,6},{2,5},{3,4},{4,7},{5,0},{6,1},{7,2},{8,11},{9,14},{10,... | collective-permute-start | bytes 172040 | tf_op jit(solution)/shard_map/ppermute | solution.py:231
  11.6 4.5 %collective-permute-start.6 = (bf16[8,3584]{1,0:T(8,128)(2,1)S(1)}, bf16[8,3584]{1,0:T(8,128)(2,1)S(1)}, u32[]{:S(2)}, u32[]{:S(2)}) collective-permute-start(bf16[8,3584]{1,0:T(8,128)(2,1)S(1)} %get-tuple-element.31), channel_id=1, source_target_pairs={{0,5},{1,4},{2,7},{3,6},{4,1},{5,2},{6,3},{7,0},{8,13},{9,12},{10,... | collective-permute-start | bytes 172040 | tf_op jit(solution)/shard_map/ppermute | solution.py:231
  12.3 3.7 %collective-permute-start.7 = (bf16[8,3584]{1,0:T(8,128)(2,1)S(1)}, bf16[8,3584]{1,0:T(8,128)(2,1)S(1)}, u32[]{:S(2)}, u32[]{:S(2)}) collective-permute-start(bf16[8,3584]{1,0:T(8,128)(2,1)S(1)} %get-tuple-element.32), channel_id=1, source_target_pairs={{0,7},{1,2},{2,1},{3,0},{4,3},{5,6},{6,5},{7,4},{8,15},{9,10},{10,... | collective-permute-start | bytes 172040 | tf_op jit(solution)/shard_map/ppermute | solution.py:231

commit v22 on v20

--- a/solution.py
+++ b/solution.py
@@ -145,17 +145,18 @@
 
 def down_kernel(split, hidden_ref, down_ref, twin_down_ref, *refs):
     units = down_ref.shape[0]
-    own = hidden_ref[:, :units], down_ref[...]
-    twin = hidden_ref[:, units:], twin_down_ref[...]
-    piece = jnp.dot(*own, preferred_element_type=jnp.float32)
-    piece += jnp.dot(*twin, preferred_element_type=jnp.float32)
     size = refs[0].shape[0]
-    blocks = [piece[size * b : size * (b + 1)] for b in range(len(refs))]
+    blocks = [
+        hidden_ref[size * b : size * (b + 1)].astype(jnp.float32) for b in range(len(refs))
+    ]
     if split:
         even = (lax.axis_index("expert") & 1) == 0
         blocks[1:] = [jnp.where(even, blocks[e], blocks[o]) for e, o in zip(*BACK)]
-    for block, out_ref in zip(blocks, refs):
-        out_ref[...] = block.astype(jnp.bfloat16)
+    hidden = jnp.concatenate(blocks, axis=0).astype(jnp.bfloat16)
+    piece = jnp.dot(hidden[:, :units], down_ref[...], preferred_element_type=jnp.float32)
+    piece += jnp.dot(hidden[:, units:], twin_down_ref[...], preferred_element_type=jnp.float32)
+    for b, out_ref in enumerate(refs):
+        out_ref[...] = piece[size * b : size * (b + 1)].astype(jnp.bfloat16)
 
 
 def mix_kernel(repeats, weight_ref, *refs):

time: 17.2 us -> 17.2 us (level)
  no operation moved by 1% of the time
where the time goes in v22:
time: 17.2 us; the launch traced here: 16.9 us
  starting transfers between devices  9.48 us (55%)
  Pallas kernels  4.78 us (28%)
  waiting for transfers between devices  2.54 us (15%)
    ppermute x6, starting transfers between devices, exchange(): result.append(lax.ppermute(blocks[k], 'expert', pairs))  8.01 us
    pallas_call x5, Pallas kernels, call(): pl.pallas_call(kernel, out_shape=outs, in_specs=arg_specs, out_specs=out_...  4.78 us
    ppermute x6, waiting for transfers between devices, exchange(): result.append(lax.ppermute(blocks[k], 'expert', pairs))  2.53 us
    ppermute x2, starting transfers between devices, from_twin(): return lax.ppermute(array, 'expert', pairs)  1.48 us
  transfers between devices with their start and end apart: 8, of which 2 were waited for; matrix products, arithmetic and copies ran while one was open for 0% of the time, Pallas kernels for 14%

profile of v22, /device:TPU:0, one launch (start us, length us, event | category | flops | bytes accessed | tf_op | source)
XLA Modules:
  0.0 16.9 jit_solution(3965490342302248565)
XLA Ops:
  0.0 1.2 %shard_map.82 = (s32[2,16]{1,0:T(2,128)S(1)}, bf16[8,3584]{1,0:T(8,128)(2,1)S(1)}, bf16[8,3584]{1,0:T(8,128)(2,1)S(1)}, bf16[8,3584]{1,0:T(8,128)(2,1)S(1)}, bf16[8,3584]{1,0:T(8,128)(2,1)S(1)}) custom-call(s32[8]{0:T(128)} %refs_0_.1, s32[8]{0:T(128)} %refs_1_.1, s32[2,16]{1,0:T(2,128)} %bitcast.3, s32[2,16]{1,0:T(2,128)} %bitcast.4, bf16[16,3584]{1,0:T(8,128)(2,1)} %refs_4_.1), custom_call_target="tpu_custom_call" | custom-call | flops 3670016 | bytes 344512 | tf_op jit(solution)/shard_map/pallas_call | solution.py:192
  1.2 0.5 %collective-permute-start = (bf16[2,3584,128]{2,1,0:T(8,128)(2,1)}, bf16[2,3584,128]{2,1,0:T(8,128)(2,1)S(1)}, u32[]{:S(2)}, u32[]{:S(2)}) collective-permute-start(bf16[2,3584,128]{2,1,0:T(8,128)(2,1)} %in_hbm.1), channel_id=1, source_target_pairs={{0,1},{1,0},{2,3},{3,2},{4,5},{5,4},{6,7},{7,6},{8,9},{9,8},{10,11... | collective-permute-start | bytes 5505032 | tf_op jit(solution)/shard_map/ppermute | solution.py:236
  1.7 3.6 %collective-permute-start.1 = (bf16[8,3584]{1,0:T(8,128)(2,1)S(1)}, bf16[8,3584]{1,0:T(8,128)(2,1)S(1)}, u32[]{:S(2)}, u32[]{:S(2)}) collective-permute-start(bf16[8,3584]{1,0:T(8,128)(2,1)S(1)} %get-tuple-element.24), channel_id=1, source_target_pairs={{0,7},{1,2},{2,5},{3,4},{4,1},{5,6},{6,3},{7,0},{8,15},{9,10},{10,... | collective-permute-start | bytes 172040 | tf_op jit(solution)/shard_map/ppermute | solution.py:230
  5.2 0.2 %collective-permute-start.2 = (bf16[8,3584]{1,0:T(8,128)(2,1)S(1)}, bf16[8,3584]{1,0:T(8,128)(2,1)S(1)}, u32[]{:S(2)}, u32[]{:S(2)}) collective-permute-start(bf16[8,3584]{1,0:T(8,128)(2,1)S(1)} %get-tuple-element.25), channel_id=1, source_target_pairs={{0,5},{1,4},{2,7},{3,6},{4,3},{5,0},{6,1},{7,2},{8,13},{9,12},{10,... | collective-permute-start | bytes 172040 | tf_op jit(solution)/shard_map/ppermute | solution.py:230
  5.5 0.6 %collective-permute-start.3 = (bf16[8,3584]{1,0:T(8,128)(2,1)S(1)}, bf16[8,3584]{1,0:T(8,128)(2,1)S(1)}, u32[]{:S(2)}, u32[]{:S(2)}) collective-permute-start(bf16[8,3584]{1,0:T(8,128)(2,1)S(1)} %get-tuple-element.26), channel_id=1, source_target_pairs={{0,3},{1,6},{2,1},{3,0},{4,7},{5,2},{6,5},{7,4},{8,11},{9,14},{10,... | collective-permute-start | bytes 172040 | tf_op jit(solution)/shard_map/ppermute | solution.py:230
  6.0 1.0 %collective-permute-start.4 = (bf16[128,3584]{1,0:T(8,128)(2,1)}, bf16[128,3584]{1,0:T(8,128)(2,1)S(1)}, u32[]{:S(2)}, u32[]{:S(2)}) collective-permute-start(bf16[128,3584]{1,0:T(8,128)(2,1)} %down_hbm.1), channel_id=1, source_target_pairs={{0,1},{1,0},{2,3},{3,2},{4,5},{5,4},{6,7},{7,6},{8,9},{9,8},{10,11... | collective-permute-start | bytes 2752520 | tf_op jit(solution)/shard_map/ppermute | solution.py:236
  7.0 1.8 %shard_map.83 = (bf16[2,3584,128]{2,1,0:T(8,128)(2,1)S(1)}, bf16[128,3584]{1,0:T(8,128)(2,1)S(1)}, bf16[32,32]{1,0:T(8,128)(2,1)S(1)}) custom-call(s32[2,16]{1,0:T(2,128)S(1)} %get-tuple-element.19.found_ref, f32[2,16]{1,0:T(2,128)} %bitcast.5, bf16[2,3584,128]{2,1,0:T(8,128)(2,1)} %in_hbm.1, bf16[128,3584]{1,0:T(8,128)(2,1)} %down_hbm.1), custom_call_target="tpu_custom_call" | custom-call | bytes 5507328 | tf_op jit(solution)/shard_map/pallas_call | solution.py:192
  8.8 0.0 collective-permute-done.1.refs_1_
  8.8 0.7 %collective-permute-done.2.refs_2_ = bf16[8,3584]{1,0:T(8,128)(2,1)S(1)} collective-permute-done((bf16[8,3584]{1,0:T(8,128)(2,1)S(1)}, bf16[8,3584]{1,0:T(8,128)(2,1)S(1)}, u32[]{:S(2)}, u32[]{:S(2)}) %collective-permute-start.2) | collective-permute-done | bytes 57376 | tf_op jit(solution)/shard_map/ppermute | solution.py:230
  9.5 0.0 collective-permute-done.3.refs_3_
  9.5 0.0 collective-permute-done.twin_in_ref
  9.5 0.6 %shard_map.84.hidden_ref = bf16[32,256]{1,0:T(8,128)(2,1)S(1)} custom-call(bf16[2,3584,128]{2,1,0:T(8,128)(2,1)S(1)} %get-tuple-element.21.in_ref, bf16[2,3584,128]{2,1,0:T(8,128)(2,1)S(1)} %collective-permute-done.twin_in_ref, bf16[8,3584]{1,0:T(8,128)(2,1)S(1)} %get-tuple-element.23.refs_0_, bf16[8,3584]{1,0:T(8,128)(2,1)S(1)} %collective-permute-done.1.refs_1_, ...), custom_call_target="tpu_custom_call" | custom-call | flops 11744051200 | bytes 3915776 | tf_op jit(solution)/shard_map/pallas_call | solution.py:192
  10.1 0.0 collective-permute-done.4.twin_down_ref
  10.1 0.4 %shard_map.85 = (bf16[8,3584]{1,0:T(8,128)(2,1)S(1)}, bf16[8,3584]{1,0:T(8,128)(2,1)S(1)}, bf16[8,3584]{1,0:T(8,128)(2,1)S(1)}, bf16[8,3584]{1,0:T(8,128)(2,1)S(1)}) custom-call(bf16[32,256]{1,0:T(8,128)(2,1)S(1)} %shard_map.84.hidden_ref, bf16[128,3584]{1,0:T(8,128)(2,1)S(1)} %get-tuple-element.27.down_ref, ...), custom_call_target="tpu_custom_call" | custom-call | flops 58720256 | bytes 2080768 | tf_op jit(solution)/shard_map/pallas_call | solution.py:192
  10.5 1.0 %collective-permute-start.5 = (bf16[8,3584]{1,0:T(8,128)(2,1)S(1)}, bf16[8,3584]{1,0:T(8,128)(2,1)S(1)}, u32[]{:S(2)}, u32[]{:S(2)}) collective-permute-start(bf16[8,3584]{1,0:T(8,128)(2,1)S(1)} %get-tuple-element.30), channel_id=1, source_target_pairs={{0,3},{1,6},{2,5},{3,4},{4,7},{5,0},{6,1},{7,2},{8,11},{9,14},{10,... | collective-permute-start | bytes 172040 | tf_op jit(solution)/shard_map/ppermute | solution.py:230
  11.5 0.8 %collective-permute-start.6 = (bf16[8,3584]{1,0:T(8,128)(2,1)S(1)}, bf16[8,3584]{1,0:T(8,128)(2,1)S(1)}, u32[]{:S(2)}, u32[]{:S(2)}) collective-permute-start(bf16[8,3584]{1,0:T(8,128)(2,1)S(1)} %get-tuple-element.31), channel_id=1, source_target_pairs={{0,5},{1,4},{2,7},{3,6},{4,1},{5,2},{6,3},{7,0},{8,13},{9,12},{10,... | collective-permute-start | bytes 172040 | tf_op jit(solution)/shard_map/ppermute | solution.py:230
  12.3 1.9 %collective-permute-start.7 = (bf16[8,3584]{1,0:T(8,128)(2,1)S(1)}, bf16[8,3584]{1,0:T(8,128)(2,1)S(1)}, u32[]{:S(2)}, u32[]{:S(2)}) collective-permute-start(bf16[8,3584]{1,0:T(8,128)(2,1)S(1)} %get-tuple-element.32), channel_id=1, source_target_pairs={{0,7},{1,2},{2,1},{3,0},{4,3},{5,6},{6,5},{7,4},{8,15},{9,10},{10,... | collective-permute-start | bytes 172040 | tf_op jit(solution)/shard_map/ppermute | solution.py:230
  14.1 0.0 collective-permute-done.5.refs_1_
  14.1 1.9 %collective-permute-done.6.refs_2_ = bf16[8,3584]{1,0:T(8,128)(2,1)S(1)} collective-permute-done((bf16[8,3584]{1,0:T(8,128)(2,1)S(1)}, bf16[8,3584]{1,0:T(8,128)(2,1)S(1)}, u32[]{:S(2)}, u32[]{:S(2)}) %collective-permute-start.6) | collective-permute-done | bytes 57376 | tf_op jit(solution)/shard_map/ppermute | solution.py:230
  16.0 0.0 collective-permute-done.7.refs_3_
  16.0 0.9 %shard_map.86 = bf16[16,3584]{1,0:T(8,128)(2,1)} custom-call(bf16[32,32]{1,0:T(8,128)(2,1)S(1)} %get-tuple-element.20.weight_ref, bf16[8,3584]{1,0:T(8,128)(2,1)S(1)} %get-tuple-element.29.refs_0_, bf16[8,3584]{1,0:T(8,128)(2,1)S(1)} %collective-permute-done.5.refs_1_, bf16[8,3584]{1,0:T(8,128)(2,1)S(1)} %collective-permute-done.6.refs_2_, ...), custom_call_target="tpu_custom_call" | custom-call | flops 7340032 | bytes 346112 | tf_op jit(solution)/shard_map/pallas_call | solution.py:192
Async XLA Ops:
  1.2 8.3 %collective-permute-start = (bf16[2,3584,128]{2,1,0:T(8,128)(2,1)}, bf16[2,3584,128]{2,1,0:T(8,128)(2,1)S(1)}, u32[]{:S(2)}, u32[]{:S(2)}) collective-permute-start(bf16[2,3584,128]{2,1,0:T(8,128)(2,1)} %in_hbm.1), channel_id=1, source_target_pairs={{0,1},{1,0},{2,3},{3,2},{4,5},{5,4},{6,7},{7,6},{8,9},{9,8},{10,11... | collective-permute-start | bytes 5505032 | tf_op jit(solution)/shard_map/ppermute | solution.py:236
  1.7 7.1 %collective-permute-start.1 = (bf16[8,3584]{1,0:T(8,128)(2,1)S(1)}, bf16[8,3584]{1,0:T(8,128)(2,1)S(1)}, u32[]{:S(2)}, u32[]{:S(2)}) collective-permute-start(bf16[8,3584]{1,0:T(8,128)(2,1)S(1)} %get-tuple-element.24), channel_id=1, source_target_pairs={{0,7},{1,2},{2,5},{3,4},{4,1},{5,6},{6,3},{7,0},{8,15},{9,10},{10,... | collective-permute-start | bytes 172040 | tf_op jit(solution)/shard_map/ppermute | solution.py:230
  5.2 4.2 %collective-permute-start.2 = (bf16[8,3584]{1,0:T(8,128)(2,1)S(1)}, bf16[8,3584]{1,0:T(8,128)(2,1)S(1)}, u32[]{:S(2)}, u32[]{:S(2)}) collective-permute-start(bf16[8,3584]{1,0:T(8,128)(2,1)S(1)} %get-tuple-element.25), channel_id=1, source_target_pairs={{0,5},{1,4},{2,7},{3,6},{4,3},{5,0},{6,1},{7,2},{8,13},{9,12},{10,... | collective-permute-start | bytes 172040 | tf_op jit(solution)/shard_map/ppermute | solution.py:230
  5.5 4.0 %collective-permute-start.3 = (bf16[8,3584]{1,0:T(8,128)(2,1)S(1)}, bf16[8,3584]{1,0:T(8,128)(2,1)S(1)}, u32[]{:S(2)}, u32[]{:S(2)}) collective-permute-start(bf16[8,3584]{1,0:T(8,128)(2,1)S(1)} %get-tuple-element.26), channel_id=1, source_target_pairs={{0,3},{1,6},{2,1},{3,0},{4,7},{5,2},{6,5},{7,4},{8,11},{9,14},{10,... | collective-permute-start | bytes 172040 | tf_op jit(solution)/shard_map/ppermute | solution.py:230
  6.0 4.1 %collective-permute-start.4 = (bf16[128,3584]{1,0:T(8,128)(2,1)}, bf16[128,3584]{1,0:T(8,128)(2,1)S(1)}, u32[]{:S(2)}, u32[]{:S(2)}) collective-permute-start(bf16[128,3584]{1,0:T(8,128)(2,1)} %down_hbm.1), channel_id=1, source_target_pairs={{0,1},{1,0},{2,3},{3,2},{4,5},{5,4},{6,7},{7,6},{8,9},{9,8},{10,11... | collective-permute-start | bytes 2752520 | tf_op jit(solution)/shard_map/ppermute | solution.py:236
  10.5 3.7 %collective-permute-start.5 = (bf16[8,3584]{1,0:T(8,128)(2,1)S(1)}, bf16[8,3584]{1,0:T(8,128)(2,1)S(1)}, u32[]{:S(2)}, u32[]{:S(2)}) collective-permute-start(bf16[8,3584]{1,0:T(8,128)(2,1)S(1)} %get-tuple-element.30), channel_id=1, source_target_pairs={{0,3},{1,6},{2,5},{3,4},{4,7},{5,0},{6,1},{7,2},{8,11},{9,14},{10,... | collective-permute-start | bytes 172040 | tf_op jit(solution)/shard_map/ppermute | solution.py:230
  11.5 4.5 %collective-permute-start.6 = (bf16[8,3584]{1,0:T(8,128)(2,1)S(1)}, bf16[8,3584]{1,0:T(8,128)(2,1)S(1)}, u32[]{:S(2)}, u32[]{:S(2)}) collective-permute-start(bf16[8,3584]{1,0:T(8,128)(2,1)S(1)} %get-tuple-element.31), channel_id=1, source_target_pairs={{0,5},{1,4},{2,7},{3,6},{4,1},{5,2},{6,3},{7,0},{8,13},{9,12},{10,... | collective-permute-start | bytes 172040 | tf_op jit(solution)/shard_map/ppermute | solution.py:230
  12.3 3.7 %collective-permute-start.7 = (bf16[8,3584]{1,0:T(8,128)(2,1)S(1)}, bf16[8,3584]{1,0:T(8,128)(2,1)S(1)}, u32[]{:S(2)}, u32[]{:S(2)}) collective-permute-start(bf16[8,3584]{1,0:T(8,128)(2,1)S(1)} %get-tuple-element.32), channel_id=1, source_target_pairs={{0,7},{1,2},{2,1},{3,0},{4,3},{5,6},{6,5},{7,4},{8,15},{9,10},{10,... | collective-permute-start | bytes 172040 | tf_op jit(solution)/shard_map/ppermute | solution.py:230

commit v23 on v18

--- a/solution.py
+++ b/solution.py
@@ -255,7 +255,6 @@
     chips = devices // 2
     rows, width = tokens.shape
     hidden = w_down.shape[0]
-    twin_in = from_twin(w_in)
     operands = (new_place, old_place, expert_ids.T, replica.T, tokens)
     combine = combine.T
     block = jax.ShapeDtypeStruct((CAP * (2 if split else 1), width), jnp.bfloat16)
@@ -268,7 +267,8 @@
         scratch=scratch_for(operands[:2], operands[2:]),
     )
     received = exchange([blocks[c // repeats] for c in range(chips)], split)
-    twin_down = from_twin(lax.optimization_barrier((w_down, found))[0])
+    after_in, after_down, _ = lax.optimization_barrier((w_in, w_down, found))
+    twin_in, twin_down = from_twin(after_in), from_twin(after_down)
     own_in, own_down, weight = call(
         functools.partial(prepare_kernel, split),
         [

time: 17.2 us -> 17.2 us (level); the launches traced: 17 us -> 16.9 us
    ppermute x6, starting transfers between devices: 8.24 us -> 8.01 us  [exchange(): result.append(lax.ppermute(blocks[k], 'expert', pairs))]
  transfers between devices with their start and end apart: 8 -> 8, of which waited for: 2 -> 2; matrix products, arithmetic and copies ran while one was open for 0% -> 0% of each run, Pallas kernels for 22% -> 15%
where the time goes in v23:
time: 17.2 us; the launch traced here: 16.9 us
  starting transfers between devices  9.48 us (55%)
  Pallas kernels  4.96 us (29%)
  waiting for transfers between devices  2.36 us (14%)
    ppermute x6, starting transfers between devices, exchange(): result.append(lax.ppermute(blocks[k], 'expert', pairs))  8.01 us
    pallas_call x6, Pallas kernels, call(): pl.pallas_call(kernel, out_shape=outs, in_specs=arg_specs, out_specs=out_...  4.96 us
    ppermute x6, waiting for transfers between devices, exchange(): result.append(lax.ppermute(blocks[k], 'expert', pairs))  2.35 us
    ppermute x2, starting transfers between devices, from_twin(): return lax.ppermute(array, 'expert', pairs)  1.48 us
  transfers between devices with their start and end apart: 8, of which 2 were waited for; matrix products, arithmetic and copies ran while one was open for 0% of the time, Pallas kernels for 15%

profile of v23, /device:TPU:0, one launch (start us, length us, event | category | flops | bytes accessed | tf_op | source)
XLA Modules:
  0.0 16.9 jit_solution(8080286135567150192)
XLA Ops:
  0.0 1.2 %shard_map.82 = (s32[2,16]{1,0:T(2,128)S(1)}, bf16[8,3584]{1,0:T(8,128)(2,1)S(1)}, bf16[8,3584]{1,0:T(8,128)(2,1)S(1)}, bf16[8,3584]{1,0:T(8,128)(2,1)S(1)}, bf16[8,3584]{1,0:T(8,128)(2,1)S(1)}) custom-call(s32[8]{0:T(128)} %refs_0_.1, s32[8]{0:T(128)} %refs_1_.1, s32[2,16]{1,0:T(2,128)} %bitcast.3, s32[2,16]{1,0:T(2,128)} %bitcast.4, bf16[16,3584]{1,0:T(8,128)(2,1)} %refs_4_.1), custom_call_target="tpu_custom_call" | custom-call | flops 3670016 | bytes 344512 | tf_op jit(solution)/shard_map/pallas_call | solution.py:203
  1.2 0.5 %collective-permute-start = (bf16[2,3584,128]{2,1,0:T(8,128)(2,1)}, bf16[2,3584,128]{2,1,0:T(8,128)(2,1)S(1)}, u32[]{:S(2)}, u32[]{:S(2)}) collective-permute-start(bf16[2,3584,128]{2,1,0:T(8,128)(2,1)} %in_hbm.1), channel_id=1, source_target_pairs={{0,1},{1,0},{2,3},{3,2},{4,5},{5,4},{6,7},{7,6},{8,9},{9,8},{10,11... | collective-permute-start | bytes 5505032 | tf_op jit(solution)/shard_map/ppermute | solution.py:247
  1.7 3.6 %collective-permute-start.1 = (bf16[8,3584]{1,0:T(8,128)(2,1)S(1)}, bf16[8,3584]{1,0:T(8,128)(2,1)S(1)}, u32[]{:S(2)}, u32[]{:S(2)}) collective-permute-start(bf16[8,3584]{1,0:T(8,128)(2,1)S(1)} %get-tuple-element.26), channel_id=1, source_target_pairs={{0,7},{1,2},{2,5},{3,4},{4,1},{5,6},{6,3},{7,0},{8,15},{9,10},{10,... | collective-permute-start | bytes 172040 | tf_op jit(solution)/shard_map/ppermute | solution.py:241
  5.2 0.2 %collective-permute-start.2 = (bf16[8,3584]{1,0:T(8,128)(2,1)S(1)}, bf16[8,3584]{1,0:T(8,128)(2,1)S(1)}, u32[]{:S(2)}, u32[]{:S(2)}) collective-permute-start(bf16[8,3584]{1,0:T(8,128)(2,1)S(1)} %get-tuple-element.27), channel_id=1, source_target_pairs={{0,5},{1,4},{2,7},{3,6},{4,3},{5,0},{6,1},{7,2},{8,13},{9,12},{10,... | collective-permute-start | bytes 172040 | tf_op jit(solution)/shard_map/ppermute | solution.py:241
  5.5 0.6 %collective-permute-start.3 = (bf16[8,3584]{1,0:T(8,128)(2,1)S(1)}, bf16[8,3584]{1,0:T(8,128)(2,1)S(1)}, u32[]{:S(2)}, u32[]{:S(2)}) collective-permute-start(bf16[8,3584]{1,0:T(8,128)(2,1)S(1)} %get-tuple-element.28), channel_id=1, source_target_pairs={{0,3},{1,6},{2,1},{3,0},{4,7},{5,2},{6,5},{7,4},{8,11},{9,14},{10,... | collective-permute-start | bytes 172040 | tf_op jit(solution)/shard_map/ppermute | solution.py:241
  6.0 1.0 %collective-permute-start.4 = (bf16[128,3584]{1,0:T(8,128)(2,1)}, bf16[128,3584]{1,0:T(8,128)(2,1)S(1)}, u32[]{:S(2)}, u32[]{:S(2)}) collective-permute-start(bf16[128,3584]{1,0:T(8,128)(2,1)} %down_hbm.1), channel_id=1, source_target_pairs={{0,1},{1,0},{2,3},{3,2},{4,5},{5,4},{6,7},{7,6},{8,9},{9,8},{10,11... | collective-permute-start | bytes 2752520 | tf_op jit(solution)/shard_map/ppermute | solution.py:247
  7.0 1.8 %shard_map.83 = (bf16[2,3584,128]{2,1,0:T(8,128)(2,1)S(1)}, bf16[128,3584]{1,0:T(8,128)(2,1)S(1)}, bf16[32,32]{1,0:T(8,128)(2,1)S(1)}) custom-call(s32[2,16]{1,0:T(2,128)S(1)} %get-tuple-element.21.found_ref, f32[2,16]{1,0:T(2,128)} %bitcast.5, bf16[2,3584,128]{2,1,0:T(8,128)(2,1)} %in_hbm.1, bf16[128,3584]{1,0:T(8,128)(2,1)} %down_hbm.1), custom_call_target="tpu_custom_call" | custom-call | bytes 5507328 | tf_op jit(solution)/shard_map/pallas_call | solution.py:203
  8.8 0.0 collective-permute-done.1.refs_1_
  8.8 0.7 %collective-permute-done.2.refs_2_ = bf16[8,3584]{1,0:T(8,128)(2,1)S(1)} collective-permute-done((bf16[8,3584]{1,0:T(8,128)(2,1)S(1)}, bf16[8,3584]{1,0:T(8,128)(2,1)S(1)}, u32[]{:S(2)}, u32[]{:S(2)}) %collective-permute-start.2) | collective-permute-done | bytes 57376 | tf_op jit(solution)/shard_map/ppermute | solution.py:241
  9.5 0.0 collective-permute-done.3.refs_3_
  9.5 0.0 collective-permute-done.twin_in_ref
  9.5 0.6 %shard_map.84.hidden_ref = bf16[32,256]{1,0:T(8,128)(2,1)S(1)} custom-call(bf16[2,3584,128]{2,1,0:T(8,128)(2,1)S(1)} %get-tuple-element.23.in_ref, bf16[2,3584,128]{2,1,0:T(8,128)(2,1)S(1)} %collective-permute-done.twin_in_ref, bf16[8,3584]{1,0:T(8,128)(2,1)S(1)} %get-tuple-element.25.refs_0_, bf16[8,3584]{1,0:T(8,128)(2,1)S(1)} %collective-permute-done.1.refs_1_, ...), custom_call_target="tpu_custom_call" | custom-call | flops 11744051200 | bytes 3915776 | tf_op jit(solution)/shard_map/pallas_call | solution.py:203
  10.1 0.0 collective-permute-done.4.twin_down_ref
  10.1 0.4 %shard_map.85 = (bf16[8,3584]{1,0:T(8,128)(2,1)S(1)}, bf16[8,3584]{1,0:T(8,128)(2,1)S(1)}, bf16[8,3584]{1,0:T(8,128)(2,1)S(1)}, bf16[8,3584]{1,0:T(8,128)(2,1)S(1)}) custom-call(bf16[32,256]{1,0:T(8,128)(2,1)S(1)} %shard_map.84.hidden_ref, bf16[128,3584]{1,0:T(8,128)(2,1)S(1)} %get-tuple-element.29.down_ref, ...), custom_call_target="tpu_custom_call" | custom-call | flops 58720256 | bytes 2080768 | tf_op jit(solution)/shard_map/pallas_call | solution.py:203
  10.5 1.0 %collective-permute-start.5 = (bf16[8,3584]{1,0:T(8,128)(2,1)S(1)}, bf16[8,3584]{1,0:T(8,128)(2,1)S(1)}, u32[]{:S(2)}, u32[]{:S(2)}) collective-permute-start(bf16[8,3584]{1,0:T(8,128)(2,1)S(1)} %get-tuple-element.32), channel_id=1, source_target_pairs={{0,3},{1,6},{2,5},{3,4},{4,7},{5,0},{6,1},{7,2},{8,11},{9,14},{10,... | collective-permute-start | bytes 172040 | tf_op jit(solution)/shard_map/ppermute | solution.py:241
  11.5 0.8 %collective-permute-start.6 = (bf16[8,3584]{1,0:T(8,128)(2,1)S(1)}, bf16[8,3584]{1,0:T(8,128)(2,1)S(1)}, u32[]{:S(2)}, u32[]{:S(2)}) collective-permute-start(bf16[8,3584]{1,0:T(8,128)(2,1)S(1)} %get-tuple-element.35), channel_id=1, source_target_pairs={{0,5},{1,4},{2,7},{3,6},{4,1},{5,2},{6,3},{7,0},{8,13},{9,12},{10,... | collective-permute-start | bytes 172040 | tf_op jit(solution)/shard_map/ppermute | solution.py:241
  12.3 1.9 %collective-permute-start.7 = (bf16[8,3584]{1,0:T(8,128)(2,1)S(1)}, bf16[8,3584]{1,0:T(8,128)(2,1)S(1)}, u32[]{:S(2)}, u32[]{:S(2)}) collective-permute-start(bf16[8,3584]{1,0:T(8,128)(2,1)S(1)} %get-tuple-element.36), channel_id=1, source_target_pairs={{0,7},{1,2},{2,1},{3,0},{4,3},{5,6},{6,5},{7,4},{8,15},{9,10},{10,... | collective-permute-start | bytes 172040 | tf_op jit(solution)/shard_map/ppermute | solution.py:241
  14.1 0.0 collective-permute-done.5.refs_1_
  14.2 0.2 %shard_map.86 = (bf16[32,16]{1,0:T(8,128)(2,1)S(1)}, f32[16,3584]{1,0:T(8,128)S(1)}) custom-call(bf16[32,32]{1,0:T(8,128)(2,1)S(1)} %get-tuple-element.22.weight_ref, bf16[8,3584]{1,0:T(8,128)(2,1)S(1)} %get-tuple-element.31.refs_0_, bf16[8,3584]{1,0:T(8,128)(2,1)S(1)} %collective-permute-done.5.refs_1_), custom_call_target="tpu_custom_call" | custom-call | flops 3670016 | bytes 347136 | tf_op jit(solution)/shard_map/pallas_call | solution.py:203
  14.3 1.7 %collective-permute-done.6.refs_1_ = bf16[8,3584]{1,0:T(8,128)(2,1)S(1)} collective-permute-done((bf16[8,3584]{1,0:T(8,128)(2,1)S(1)}, bf16[8,3584]{1,0:T(8,128)(2,1)S(1)}, u32[]{:S(2)}, u32[]{:S(2)}) %collective-permute-start.6) | collective-permute-done | bytes 57376 | tf_op jit(solution)/shard_map/ppermute | solution.py:241
  16.0 0.0 collective-permute-done.7.refs_2_
  16.0 0.8 %shard_map.87 = bf16[16,3584]{1,0:T(8,128)(2,1)} custom-call(bf16[32,16]{1,0:T(8,128)(2,1)S(1)} %get-tuple-element.33.weight_ref, f32[16,3584]{1,0:T(8,128)S(1)} %get-tuple-element.34.refs_0_, bf16[8,3584]{1,0:T(8,128)(2,1)S(1)} %collective-permute-done.6.refs_1_, bf16[8,3584]{1,0:T(8,128)(2,1)S(1)} %collective-permute-done.7.refs_2_), custom_call_target="tpu_custom_call" | custom-call | flops 7340032 | bytes 459776 | tf_op jit(solution)/shard_map/pallas_call | solution.py:203
Async XLA Ops:
  1.2 8.3 %collective-permute-start = (bf16[2,3584,128]{2,1,0:T(8,128)(2,1)}, bf16[2,3584,128]{2,1,0:T(8,128)(2,1)S(1)}, u32[]{:S(2)}, u32[]{:S(2)}) collective-permute-start(bf16[2,3584,128]{2,1,0:T(8,128)(2,1)} %in_hbm.1), channel_id=1, source_target_pairs={{0,1},{1,0},{2,3},{3,2},{4,5},{5,4},{6,7},{7,6},{8,9},{9,8},{10,11... | collective-permute-start | bytes 5505032 | tf_op jit(solution)/shard_map/ppermute | solution.py:247
  1.7 7.1 %collective-permute-start.1 = (bf16[8,3584]{1,0:T(8,128)(2,1)S(1)}, bf16[8,3584]{1,0:T(8,128)(2,1)S(1)}, u32[]{:S(2)}, u32[]{:S(2)}) collective-permute-start(bf16[8,3584]{1,0:T(8,128)(2,1)S(1)} %get-tuple-element.26), channel_id=1, source_target_pairs={{0,7},{1,2},{2,5},{3,4},{4,1},{5,6},{6,3},{7,0},{8,15},{9,10},{10,... | collective-permute-start | bytes 172040 | tf_op jit(solution)/shard_map/ppermute | solution.py:241
  5.2 4.2 %collective-permute-start.2 = (bf16[8,3584]{1,0:T(8,128)(2,1)S(1)}, bf16[8,3584]{1,0:T(8,128)(2,1)S(1)}, u32[]{:S(2)}, u32[]{:S(2)}) collective-permute-start(bf16[8,3584]{1,0:T(8,128)(2,1)S(1)} %get-tuple-element.27), channel_id=1, source_target_pairs={{0,5},{1,4},{2,7},{3,6},{4,3},{5,0},{6,1},{7,2},{8,13},{9,12},{10,... | collective-permute-start | bytes 172040 | tf_op jit(solution)/shard_map/ppermute | solution.py:241
  5.5 4.0 %collective-permute-start.3 = (bf16[8,3584]{1,0:T(8,128)(2,1)S(1)}, bf16[8,3584]{1,0:T(8,128)(2,1)S(1)}, u32[]{:S(2)}, u32[]{:S(2)}) collective-permute-start(bf16[8,3584]{1,0:T(8,128)(2,1)S(1)} %get-tuple-element.28), channel_id=1, source_target_pairs={{0,3},{1,6},{2,1},{3,0},{4,7},{5,2},{6,5},{7,4},{8,11},{9,14},{10,... | collective-permute-start | bytes 172040 | tf_op jit(solution)/shard_map/ppermute | solution.py:241
  6.0 4.1 %collective-permute-start.4 = (bf16[128,3584]{1,0:T(8,128)(2,1)}, bf16[128,3584]{1,0:T(8,128)(2,1)S(1)}, u32[]{:S(2)}, u32[]{:S(2)}) collective-permute-start(bf16[128,3584]{1,0:T(8,128)(2,1)} %down_hbm.1), channel_id=1, source_target_pairs={{0,1},{1,0},{2,3},{3,2},{4,5},{5,4},{6,7},{7,6},{8,9},{9,8},{10,11... | collective-permute-start | bytes 2752520 | tf_op jit(solution)/shard_map/ppermute | solution.py:247
  10.5 3.7 %collective-permute-start.5 = (bf16[8,3584]{1,0:T(8,128)(2,1)S(1)}, bf16[8,3584]{1,0:T(8,128)(2,1)S(1)}, u32[]{:S(2)}, u32[]{:S(2)}) collective-permute-start(bf16[8,3584]{1,0:T(8,128)(2,1)S(1)} %get-tuple-element.32), channel_id=1, source_target_pairs={{0,3},{1,6},{2,5},{3,4},{4,7},{5,0},{6,1},{7,2},{8,11},{9,14},{10,... | collective-permute-start | bytes 172040 | tf_op jit(solution)/shard_map/ppermute | solution.py:241
  11.5 4.5 %collective-permute-start.6 = (bf16[8,3584]{1,0:T(8,128)(2,1)S(1)}, bf16[8,3584]{1,0:T(8,128)(2,1)S(1)}, u32[]{:S(2)}, u32[]{:S(2)}) collective-permute-start(bf16[8,3584]{1,0:T(8,128)(2,1)S(1)} %get-tuple-element.35), channel_id=1, source_target_pairs={{0,5},{1,4},{2,7},{3,6},{4,1},{5,2},{6,3},{7,0},{8,13},{9,12},{10,... | collective-permute-start | bytes 172040 | tf_op jit(solution)/shard_map/ppermute | solution.py:241
  12.3 3.7 %collective-permute-start.7 = (bf16[8,3584]{1,0:T(8,128)(2,1)S(1)}, bf16[8,3584]{1,0:T(8,128)(2,1)S(1)}, u32[]{:S(2)}, u32[]{:S(2)}) collective-permute-start(bf16[8,3584]{1,0:T(8,128)(2,1)S(1)} %get-tuple-element.36), channel_id=1, source_target_pairs={{0,7},{1,2},{2,1},{3,0},{4,3},{5,6},{6,5},{7,4},{8,15},{9,10},{10,... | collective-permute-start | bytes 172040 | tf_op jit(solution)/shard_map/ppermute | solution.py:241
